TPU v7x, 32 devices: a whole 2x2x4 slice. The times are simulated.
32 devices in a mesh: fsdp: 32 (over z, y, x, core).
Axes of the slice: x: 2, y: 2, z: 4, core: 2. Of those that a mesh axis runs over, the one named last changes fastest.
Arguments:
- images: bfloat16 [64, 208, 768], P('fsdp'), may hold values from -6 to 6
- lengths: int32 [64], P('fsdp'), may hold values from 98 to 197, as said below
- norm_scale: bfloat16 [768], P('fsdp'), may hold values from 0.5 to 1.5
- norm_shift: bfloat16 [768], P('fsdp'), may hold values from -1 to 1
- attend_in: bfloat16 [768, 2304], P('fsdp'), may hold values from -0.21875 to 0.21875
- attend_out: bfloat16 [768, 768], P('fsdp'), may hold values from -1.5 to 1.5
- mixer_scale: bfloat16 [768], P('fsdp'), may hold values from 0.5 to 1.5
- mixer_shift: bfloat16 [768], P('fsdp'), may hold values from -1 to 1
- slot_params: bfloat16 [768, 4], P('fsdp'), may hold values from -0.15625 to 0.15625
- expert_in: bfloat16 [4, 768, 3072], P(None, None, 'fsdp'), may hold values from -0.875 to 0.875
- expert_out: bfloat16 [4, 3072, 768], P(None, 'fsdp'), may hold values from -0.21875 to 0.21875
- cotangent: bfloat16 [64, 208, 768], P('fsdp'), may hold values from -6 to 6
Outputs:
- block_out: bfloat16 [64, 208, 768], P('fsdp')
- images_grad: float32 [64, 208, 768], P('fsdp')
- nscale_grad: float32 [768], P('fsdp')
- nshift_grad: float32 [768], P('fsdp')
- attin_grad: float32 [768, 2304], P('fsdp')
- attout_grad: float32 [768, 768], P('fsdp')
- mscale_grad: float32 [768], P('fsdp')
- mshift_grad: float32 [768], P('fsdp')
- slots_grad: float32 [768, 4], P('fsdp')
- expin_grad: float32 [4, 768, 3072], P(None, None, 'fsdp')
- expout_grad: float32 [4, 3072, 768], P(None, 'fsdp')
Inputs may be any that keep to these rules, and one draw needn't show every extreme that they name: `lengths`: each image's live rows are its first ones; some image in every draw has exactly 197 live rows.
All inputs are finite; a program needn't handle non-finite values.
Results may differ from a plain program's by a relative error of at most 0.017.
Values may be sent and summed in bfloat16 or wider, within the bound.
No kernel may reach another device: no remote copies, remote signals or barrier semaphores. Data moves between devices by JAX's collectives and lax.ppermute only.
A program may use at most 192 MiB of HBM per device.

v0:
```python
from functools import partial

import jax
import jax.numpy as jnp
from jax import lax
from jax.sharding import PartitionSpec as P

HEADS = 12
IMG_MB = 1
MB = 2


NEGATIVE = -1e30
EPSILON = 1e-06


def layer_norm(inputs, gain_row, shift_row):
    centre = inputs - jnp.mean(inputs, axis=-1, keepdims=True)
    spread = jnp.mean(centre * centre, axis=-1, keepdims=True)
    return centre * lax.rsqrt(spread + EPSILON) * gain_row + shift_row


def router(logits, live):
    dispatch = jax.nn.softmax(jnp.where(live[..., None], logits, NEGATIVE), axis=1)
    combine = jax.nn.softmax(logits, axis=2)
    return (dispatch, combine)


def split_heads(joint, groups, row_count, model_width):
    head_dim = model_width // HEADS
    query_rows = joint[..., :model_width].reshape(groups, row_count, HEADS, head_dim)
    key_rows = joint[..., model_width : 2 * model_width].reshape(groups, row_count, HEADS, head_dim)
    value_rows = joint[..., 2 * model_width :].reshape(groups, row_count, HEADS, head_dim)
    return (query_rows, key_rows, value_rows)


def masked_scores(query_rows, key_rows, live):
    factor = query_rows.shape[-1] ** (-0.5)
    scores = (
        jnp.einsum("gqhd,gkhd->ghqk", query_rows, key_rows, preferred_element_type=jnp.float32)
        * factor
    )
    return jnp.where(live[:, None, None, :], scores, NEGATIVE)


def forward(gathered, x_part, live):
    gain_a, shift_a, w_attend, w_out, gain_m, shift_m, w_slot, w_hidden, w_back = gathered
    groups, row_count, model_width = x_part.shape
    x_float = x_part.astype(jnp.float32)
    normed = layer_norm(x_float, gain_a.astype(jnp.float32), shift_a.astype(jnp.float32)).astype(
        jnp.bfloat16
    )
    joint = jnp.einsum("grd,de->gre", normed, w_attend, preferred_element_type=jnp.float32).astype(
        jnp.bfloat16
    )
    query_rows, key_rows, value_rows = split_heads(joint, groups, row_count, model_width)
    masked = masked_scores(query_rows, key_rows, live)
    row_top = jnp.max(masked, axis=-1, keepdims=True)
    log_total = row_top + jnp.log(jnp.sum(jnp.exp(masked - row_top), axis=-1, keepdims=True))
    soft_probs = jnp.exp(masked - log_total).astype(jnp.bfloat16)
    mixed = jnp.einsum(
        "ghqk,gkhd->gqhd", soft_probs, value_rows, preferred_element_type=jnp.float32
    )
    mixed = mixed.reshape(groups, row_count, model_width).astype(jnp.bfloat16)
    branch = jnp.einsum("grd,de->gre", mixed, w_out, preferred_element_type=jnp.float32)
    residual = x_float + branch
    normed2 = layer_norm(residual, gain_m.astype(jnp.float32), shift_m.astype(jnp.float32)).astype(
        jnp.bfloat16
    )
    logits = jnp.einsum("grd,de->gre", normed2, w_slot, preferred_element_type=jnp.float32)
    dispatch, combine = router(logits, live)
    dispatch_low = dispatch.astype(jnp.bfloat16)
    combine_low = combine.astype(jnp.bfloat16)
    slot_in = jnp.einsum(
        "gre,grd->ged", dispatch_low, normed2, preferred_element_type=jnp.float32
    ).astype(jnp.bfloat16)
    pre_act = jnp.einsum("ged,edf->gef", slot_in, w_hidden, preferred_element_type=jnp.float32)
    active = jax.nn.gelu(pre_act, approximate=True).astype(jnp.bfloat16)
    slot_out = jnp.einsum(
        "gef,efd->ged", active, w_back, preferred_element_type=jnp.float32
    ).astype(jnp.bfloat16)
    expert_sum = jnp.einsum(
        "gre,ged->grd", combine_low, slot_out, preferred_element_type=jnp.float32
    )
    result = jnp.where(live[..., None], residual + expert_sum, 0.0).astype(jnp.bfloat16)
    saved = (
        x_float,
        normed,
        joint,
        log_total,
        mixed,
        residual,
        normed2,
        logits,
        dispatch_low,
        combine_low,
        slot_in,
        pre_act,
        slot_out,
    )
    return (result, saved)


def backward(gathered, saved, cot_part, live):
    gain_a, shift_a, w_attend, w_out, gain_m, shift_m, w_slot, w_hidden, w_back = gathered
    (
        x_float,
        normed,
        joint,
        log_total,
        mixed,
        residual,
        normed2,
        logits,
        dispatch_low,
        combine_low,
        slot_in,
        pre_act,
        slot_out,
    ) = saved
    groups, row_count, model_width = x_float.shape
    back_rows = jnp.where(live[..., None], cot_part, jnp.zeros_like(cot_part))
    grad_comb = jnp.einsum("grd,ged->gre", back_rows, slot_out, preferred_element_type=jnp.float32)
    grad_slot_out = jnp.einsum(
        "gre,grd->ged", combine_low, back_rows, preferred_element_type=jnp.float32
    ).astype(jnp.bfloat16)
    grad_active = jnp.einsum(
        "ged,efd->gef", grad_slot_out, w_back, preferred_element_type=jnp.float32
    )
    gelu_value, gelu_pull = jax.vjp(partial(jax.nn.gelu, approximate=True), pre_act)
    grad_pre = gelu_pull(grad_active)[0].astype(jnp.bfloat16)
    grad_slot_in = jnp.einsum(
        "gef,edf->ged", grad_pre, w_hidden, preferred_element_type=jnp.float32
    ).astype(jnp.bfloat16)
    grad_normed2 = jnp.einsum(
        "gre,ged->grd", dispatch_low, grad_slot_in, preferred_element_type=jnp.float32
    )
    grad_disp = jnp.einsum(
        "grd,ged->gre", normed2, grad_slot_in, preferred_element_type=jnp.float32
    )
    router_value, router_pull = jax.vjp(lambda value_in: router(value_in, live), logits)
    grad_logits = router_pull((grad_disp, grad_comb))[0].astype(jnp.bfloat16)
    grad_slot = jnp.einsum("grd,gre->de", normed2, grad_logits, preferred_element_type=jnp.float32)
    grad_normed2 = grad_normed2 + jnp.einsum(
        "gre,de->grd", grad_logits, w_slot, preferred_element_type=jnp.float32
    )
    norm_value, norm_pull = jax.vjp(
        layer_norm, residual, gain_m.astype(jnp.float32), shift_m.astype(jnp.float32)
    )
    grad_residual, grad_gain_m, grad_shift_m = norm_pull(grad_normed2)
    grad_residual = grad_residual + back_rows.astype(jnp.float32)
    grad_branch = grad_residual.astype(jnp.bfloat16)
    grad_out = jnp.einsum("grd,gre->de", mixed, grad_branch, preferred_element_type=jnp.float32)
    grad_mixed = jnp.einsum(
        "gre,de->grd", grad_branch, w_out, preferred_element_type=jnp.float32
    ).astype(jnp.bfloat16)
    head_dim = model_width // HEADS
    grad_mixed = grad_mixed.reshape(groups, row_count, HEADS, head_dim)
    query_rows, key_rows, value_rows = split_heads(joint, groups, row_count, model_width)
    masked = masked_scores(query_rows, key_rows, live)
    soft_probs = jnp.exp(masked - log_total)
    probs_low = soft_probs.astype(jnp.bfloat16)
    grad_values = jnp.einsum(
        "ghqk,gqhd->gkhd", probs_low, grad_mixed, preferred_element_type=jnp.float32
    )
    grad_probs = jnp.einsum(
        "gqhd,gkhd->ghqk", grad_mixed, value_rows, preferred_element_type=jnp.float32
    )
    row_dot = jnp.sum(soft_probs * grad_probs, axis=-1, keepdims=True)
    grad_scores = (soft_probs * (grad_probs - row_dot)).astype(jnp.bfloat16)
    factor = head_dim ** (-0.5)
    grad_query = (
        jnp.einsum("ghqk,gkhd->gqhd", grad_scores, key_rows, preferred_element_type=jnp.float32)
        * factor
    )
    grad_keys = (
        jnp.einsum("ghqk,gqhd->gkhd", grad_scores, query_rows, preferred_element_type=jnp.float32)
        * factor
    )
    grad_joint = jnp.concatenate(
        [
            grad_query.reshape(groups, row_count, model_width),
            grad_keys.reshape(groups, row_count, model_width),
            grad_values.reshape(groups, row_count, model_width),
        ],
        axis=-1,
    ).astype(jnp.bfloat16)
    grad_attend = jnp.einsum("grd,gre->de", normed, grad_joint, preferred_element_type=jnp.float32)
    grad_normed = jnp.einsum(
        "gre,de->grd", grad_joint, w_attend, preferred_element_type=jnp.float32
    )
    first_value, first_pull = jax.vjp(
        layer_norm, x_float, gain_a.astype(jnp.float32), shift_a.astype(jnp.float32)
    )
    grad_x_norm, grad_gain_a, grad_shift_a = first_pull(grad_normed)
    images_part = grad_residual + grad_x_norm
    grads = (grad_gain_a, grad_shift_a, grad_attend, grad_out, grad_gain_m, grad_shift_m, grad_slot)
    return (images_part, grads, slot_in, grad_slot_out)


def expert_folder(hidden_part, back_part):

    def fold(carry, pieces, start):
        slot_piece, grad_piece = pieces
        pre_part = jnp.einsum(
            "ged,edf->gef", slot_piece, hidden_part, preferred_element_type=jnp.float32
        )
        gelu_value, gelu_pull = jax.vjp(partial(jax.nn.gelu, approximate=True), pre_part)
        active_part = gelu_value.astype(jnp.bfloat16)
        grad_active = jnp.einsum(
            "ged,efd->gef", grad_piece, back_part, preferred_element_type=jnp.float32
        )
        grad_pre = gelu_pull(grad_active)[0].astype(jnp.bfloat16)
        hidden_total = carry[0] + jnp.einsum(
            "ged,gef->edf", slot_piece, grad_pre, preferred_element_type=jnp.float32
        )
        back_total = carry[1] + jnp.einsum(
            "gef,ged->efd", active_part, grad_piece, preferred_element_type=jnp.float32
        )
        return (hidden_total, back_total)

    return fold


def shards(
    images,
    lengths,
    norm_scale,
    norm_shift,
    attend_in,
    attend_out,
    mixer_scale,
    mixer_shift,
    slot_params,
    expert_in,
    expert_out,
    cotangent,
):
    img_count, row_count, model_width = images.shape
    live_all = lax.broadcasted_iota(jnp.int32, (img_count, row_count), 1) < lengths[:, None]
    outputs = []
    image_grads = []
    totals = None
    fold = expert_folder(expert_in, expert_out)
    expert_totals = (
        jnp.zeros(expert_in.shape, jnp.float32),
        jnp.zeros(expert_out.shape, jnp.float32),
    )
    for micro_step in range(MB):
        first_img = micro_step * IMG_MB
        x_part = images[first_img : first_img + IMG_MB]
        live = live_all[first_img : first_img + IMG_MB]
        cot_part = cotangent[first_img : first_img + IMG_MB]
        gathered = (
            lax.all_gather(norm_scale, "fsdp", axis=0, tiled=True),
            lax.all_gather(norm_shift, "fsdp", axis=0, tiled=True),
            lax.all_gather(attend_in, "fsdp", axis=0, tiled=True),
            lax.all_gather(attend_out, "fsdp", axis=0, tiled=True),
            lax.all_gather(mixer_scale, "fsdp", axis=0, tiled=True),
            lax.all_gather(mixer_shift, "fsdp", axis=0, tiled=True),
            lax.all_gather(slot_params, "fsdp", axis=0, tiled=True),
            lax.all_gather(expert_in, "fsdp", axis=2, tiled=True),
            lax.all_gather(expert_out, "fsdp", axis=1, tiled=True),
        )
        result, saved = forward(gathered, x_part, live)
        gathered = (
            lax.all_gather(norm_scale, "fsdp", axis=0, tiled=True),
            lax.all_gather(norm_shift, "fsdp", axis=0, tiled=True),
            lax.all_gather(attend_in, "fsdp", axis=0, tiled=True),
            lax.all_gather(attend_out, "fsdp", axis=0, tiled=True),
            lax.all_gather(mixer_scale, "fsdp", axis=0, tiled=True),
            lax.all_gather(mixer_shift, "fsdp", axis=0, tiled=True),
            lax.all_gather(slot_params, "fsdp", axis=0, tiled=True),
            lax.all_gather(expert_in, "fsdp", axis=2, tiled=True),
            lax.all_gather(expert_out, "fsdp", axis=1, tiled=True),
        )
        images_part, grads, slot_in, grad_slot_out = backward(gathered, saved, cot_part, live)
        expert_totals = fold(
            expert_totals,
            (
                lax.all_gather(slot_in, "fsdp", axis=0, tiled=True),
                lax.all_gather(grad_slot_out, "fsdp", axis=0, tiled=True),
            ),
            jnp.int32(0),
        )
        outputs.append(result)
        image_grads.append(images_part)
        if totals is None:
            totals = tuple(grads)
        else:
            totals = tuple((left + right for left, right in zip(totals, grads)))
    totals = (
        lax.psum_scatter(totals[0], "fsdp", scatter_dimension=0, tiled=True),
        lax.psum_scatter(totals[1], "fsdp", scatter_dimension=0, tiled=True),
        lax.psum_scatter(totals[2], "fsdp", scatter_dimension=0, tiled=True),
        lax.psum_scatter(totals[3], "fsdp", scatter_dimension=0, tiled=True),
        lax.psum_scatter(totals[4], "fsdp", scatter_dimension=0, tiled=True),
        lax.psum_scatter(totals[5], "fsdp", scatter_dimension=0, tiled=True),
        lax.psum_scatter(totals[6], "fsdp", scatter_dimension=0, tiled=True),
    )
    block_out = jnp.concatenate(outputs, axis=0)
    images_grad = jnp.concatenate(image_grads, axis=0)
    return (
        block_out,
        images_grad,
        totals[0],
        totals[1],
        totals[2],
        totals[3],
        totals[4],
        totals[5],
        totals[6],
        expert_totals[0],
        expert_totals[1],
    )


def solution(mesh):
    return jax.shard_map(
        shards,
        mesh=mesh,
        in_specs=(
            P("fsdp", None, None),
            P("fsdp"),
            P("fsdp"),
            P("fsdp"),
            P("fsdp", None),
            P("fsdp", None),
            P("fsdp"),
            P("fsdp"),
            P("fsdp", None),
            P(None, None, "fsdp"),
            P(None, "fsdp", None),
            P("fsdp", None, None),
        ),
        out_specs=(
            P("fsdp", None, None),
            P("fsdp", None, None),
            P("fsdp"),
            P("fsdp"),
            P("fsdp", None),
            P("fsdp", None),
            P("fsdp"),
            P("fsdp"),
            P("fsdp", None),
            P(None, None, "fsdp"),
            P(None, "fsdp", None),
        ),
        check_vma=False,
    )
```

profile of v0, /device:TPU:0, one launch (start us, length us, event | category | flops | bytes accessed | tf_op | source)
XLA Modules:
  0.0 720.1 jit_solution(7910979592185596845)
XLA Ops:
  13.4 42.2 %all-reduce.10 = (bf16[768]{0:T(1024)(128)(2,1)S(1)}, bf16[768]{0:T(1024)(128)(2,1)S(1)}, bf16[768]{0:T(1024)(128)(2,1)S(1)}, bf16[768]{0:T(1024)(128)(2,1)S(1)}) all-reduce(bf16[768]{0:T(1024)(128)(2,1)S(1)} %dynamic-update-slice.1, bf16[768]{0:T(1024)(128)(2,1)S(1)} %dynamic-update-slice, ...), channel_id=1, replica_groups=mesh['fsdp'=32] {'fsdp'}, use_global_device_ids=true, to_apply=%add.1 | all-reduce | flops 3072 | bytes 12288
  56.2 40.5 %all-gather.4 = bf16[32,24,4]{1,2,0:T(4,128)(2,1)S(1)} all-gather(bf16[1,24,4]{1,2,0:T(4,128)(2,1)} %bitcast.371), channel_id=1, replica_groups=mesh['fsdp'=32] {'fsdp'}, dimensions={0}, use_global_device_ids=true | all-gather | bytes 6336 | tf_op jit(solution)/shard_map/all_gather | solution.py:261
  97.6 1.2 convert_reduce_fusion.1
  99.8 3.0 fusion.1
  105.7 3.0 fusion
  111.5 1.9 fusion.2
  114.1 1.5 convolution_convert_fusion.5
  115.6 14.2 %all-gather.16.cloned.1.call-done = bf16[768,768]{1,0:T(8,128)(2,1)} async-done(((bf16[24,768]{1,0:T(8,128)(2,1)}), bf16[768,768]{1,0:T(8,128)(2,1)}) %all-gather.16.cloned.1.call-update) | async-done | bytes 1179664 | tf_op jit(solution)/shard_map/all_gather | solution.py:258
  129.8 2.0 fusion.214
  142.1 1.4 convolution_convert_fusion.9
  143.5 112.8 %all-gather.18.cloned.1.call-done = bf16[4,768,3072]{1,2,0:T(8,128)(2,1)} async-done(((bf16[4,768,96]{1,2,0:T(8,128)(2,1)}), bf16[4,768,3072]{1,2,0:T(8,128)(2,1)}) %all-gather.18.cloned.1.call-update) | async-done | bytes 18874384 | tf_op jit(solution)/shard_map/all_gather | solution.py:262
  256.3 11.9 %fusion.157 = f32[4,1,3072]{2,1,0:T(1,128)} fusion(bf16[4,768,3072]{1,2,0:T(8,128)(2,1)} %all-gather.18.cloned.1.call-done, bf16[4,768,1]{1,0,2:T(4,128)(2,1)S(1)} %bitcast.363), kind=kOutput, calls=%fused_computation.236 | convolution fusion | flops 18874368 | bytes 18929664 | tf_op jit(solution)/shard_map/ged,edf->gef/dot_general | solution.py:77
  268.3 113.7 %all-gather.20.cloned.1.call-done = bf16[4,3072,768]{2,1,0:T(8,128)(2,1)} async-done(((bf16[4,96,768]{2,1,0:T(8,128)(2,1)}), bf16[4,3072,768]{2,1,0:T(8,128)(2,1)}) %all-gather.20.cloned.1.call-update) | async-done | bytes 18874384 | tf_op jit(solution)/shard_map/all_gather | solution.py:263
  382.0 12.4 %fusion.153 = f32[4,1,3072]{2,1,0:T(1,128)} fusion(bf16[4,3072,768]{2,1,0:T(8,128)(2,1)} %all-gather.20.cloned.1.call-done, bf16[4,768,1]{1,0,2:T(4,128)(2,1)S(1)} %bitcast.365), kind=kOutput, calls=%fused_computation.232 | convolution fusion | flops 18874368 | bytes 18929664 | tf_op jit(solution)/shard_map/ged,efd->gef/dot_general | solution.py:127
  395.3 8.9 %fusion.119 = bf16[4,1,768]{2,1,0:T(2,128)(2,1)S(1)} fusion(bf16[4,768,3072]{1,2,0:T(8,128)(2,1)} %all-gather.18.cloned.1.call-done, bf16[4,3072,1]{1,0,2:T(4,128)(2,1)S(1)} %get-tuple-element.64), kind=kOutput, calls=%fused_computation.194 | convolution fusion | flops 18874368 | bytes 18905088 | tf_op jit(solution)/shard_map/gef,edf->ged/dot_general | solution.py:132
  405.1 1.2 fusion.164
  406.3 12.0 %fusion.159 = f32[4,1,3072]{2,1,0:T(1,128)} fusion(bf16[4,768,3072]{1,2,0:T(8,128)(2,1)} %all-gather.18.cloned.1.call-done, bf16[4,768,1]{1,0,2:T(4,128)(2,1)} %bitcast.367), kind=kOutput, calls=%fused_computation.238 | convolution fusion | flops 18874368 | bytes 18929664 | tf_op jit(solution)/shard_map/ged,edf->gef/dot_general | solution.py:77
  418.2 12.0 %fusion.155 = f32[4,1,3072]{2,1,0:T(1,128)} fusion(bf16[4,3072,768]{2,1,0:T(8,128)(2,1)} %all-gather.20.cloned.1.call-done, bf16[4,768,1]{1,0,2:T(4,128)(2,1)} %bitcast.369), kind=kOutput, calls=%fused_computation.234 | convolution fusion | flops 18874368 | bytes 18929664 | tf_op jit(solution)/shard_map/ged,efd->gef/dot_general | solution.py:127
  431.2 9.1 %fusion.121 = bf16[4,1,768]{2,1,0:T(2,128)(2,1)S(1)} fusion(bf16[4,768,3072]{1,2,0:T(8,128)(2,1)} %all-gather.18.cloned.1.call-done, bf16[4,3072,1]{1,0,2:T(4,128)(2,1)S(1)} %get-tuple-element.62), kind=kOutput, calls=%fused_computation.196 | convolution fusion | flops 18874368 | bytes 18905088 | tf_op jit(solution)/shard_map/gef,edf->ged/dot_general | solution.py:132
  441.0 9.2 %fusion.125 = bf16[4,1,768]{2,1,0:T(2,128)(2,1)S(1)} fusion(bf16[4,3072,768]{2,1,0:T(8,128)(2,1)} %all-gather.20.cloned.1.call-done, bf16[4,3072,1]{1,0,2:T(4,128)(2,1)S(1)} %get-tuple-element.63), kind=kOutput, calls=%fused_computation.200 | convolution fusion | flops 18874368 | bytes 18905088 | tf_op jit(solution)/shard_map/gef,efd->ged/dot_general | solution.py:79
  451.0 2.5 fusion.123
  455.1 1.3 fusion.41
  458.1 1.9 fusion.218
  460.0 1.3 convolution_convert_fusion.7
  461.3 1.9 copy.89
  463.2 2.6 convolution_convert_fusion.6
  465.8 1.9 copy.93
  467.7 3.8 convolution_add_fusion.1
  471.9 2.1 multiply_reduce_fusion.1
  481.8 1.3 fusion.45
  483.1 4.2 convolution_add_fusion
  488.0 39.2 %all-gather.5 = bf16[32,4,768]{2,1,0:T(4,128)(2,1)S(1)} all-gather(bf16[1,4,768]{2,1,0:T(4,128)(2,1)S(1)} %bitcast.368), channel_id=2, replica_groups=mesh['fsdp'=32] {'fsdp'}, dimensions={0}, use_global_device_ids=true | all-gather | bytes 202752 | tf_op jit(solution)/shard_map/all_gather | solution.py:281
  527.2 37.1 %all-gather.6 = bf16[32,4,768]{2,1,0:T(4,128)(2,1)S(1)} all-gather(bf16[1,4,768]{2,1,0:T(4,128)(2,1)S(1)} %bitcast.370), channel_id=3, replica_groups=mesh['fsdp'=32] {'fsdp'}, dimensions={0}, use_global_device_ids=true | all-gather | bytes 202752 | tf_op jit(solution)/shard_map/all_gather | solution.py:282
  564.3 38.6 %all-gather.7 = bf16[32,4,768]{2,1,0:T(4,128)(2,1)S(1)} all-gather(bf16[1,4,768]{2,1,0:T(4,128)(2,1)S(1)} %bitcast.364), channel_id=4, replica_groups=mesh['fsdp'=32] {'fsdp'}, dimensions={0}, use_global_device_ids=true | all-gather | bytes 202752 | tf_op jit(solution)/shard_map/all_gather | solution.py:281
  602.9 40.5 %all-gather.8 = bf16[32,4,768]{2,1,0:T(4,128)(2,1)} all-gather(bf16[1,4,768]{2,1,0:T(4,128)(2,1)S(1)} %bitcast.366), channel_id=5, replica_groups=mesh['fsdp'=32] {'fsdp'}, dimensions={0}, use_global_device_ids=true | all-gather | bytes 202752 | tf_op jit(solution)/shard_map/all_gather | solution.py:282
  644.1 1.4 fusion.68
  645.5 1.6 fusion.66
  647.1 2.8 convolution_add_fusion.2
  649.9 2.6 convolution_add_fusion.3
  652.7 3.9 fusion.216
  656.7 1.5 fusion.37
  660.2 2.4 fusion.35
  663.2 1.2 fusion.197
  664.4 1.5 convolution_add_fusion.6
  666.0 38.2 %all-reduce.9 = (f32[768]{0:T(1024)S(1)}, f32[768]{0:T(1024)S(1)}, f32[768]{0:T(1024)S(1)}, f32[768]{0:T(1024)S(1)}, f32[768,4]{0,1:T(4,128)S(1)}) all-reduce(f32[768]{0:T(1024)} %add.231, f32[768]{0:T(1024)} %add.232, f32[768]{0:T(1024)} %add.237, f32[768]{0:T(1024)} %add.238, ...), channel_id=6, replica_groups=mesh['fsdp'=32] {'fsdp'}, use_global_device_ids=true, to_apply=%region_36.37.clone | all-reduce | flops 6144 | bytes 49152
  708.2 1.1 fusion.17
  710.2 1.0 add_add_fusion.5
  711.7 1.1 pad_maximum_fusion
  (434 shorter events, 48.6 us)
Async XLA Ops:
  7.2 91.7 %copy-start.2 = (bf16[2,208,768]{2,1,0:T(8,128)(2,1)S(1)}, bf16[2,208,768]{2,1,0:T(8,128)(2,1)}, u32[]{:S(2)}) copy-start(bf16[2,208,768]{2,1,0:T(8,128)(2,1)} %param.12) | copy-start | bytes 1916932
  7.2 92.6 %all-gather.14.cloned.1.call-start = ((), (), s32[]{:S(2)}) async-start(), calls=%async_computation.2 | async-start | bytes 3649536 | tf_op jit(solution)/shard_map/all_gather | solution.py:257
  7.9 121.8 %all-gather.16.cloned.1.call-start = ((), (), s32[]{:S(2)}) async-start(), calls=%async_computation.3 | async-start | bytes 1216512 | tf_op jit(solution)/shard_map/all_gather | solution.py:258
  8.7 247.7 %all-gather.18.cloned.1.call-start = ((), (), s32[]{:S(2)}) async-start(), calls=%async_computation.4 | async-start | bytes 19464192 | tf_op jit(solution)/shard_map/all_gather | solution.py:262
  9.4 372.5 %all-gather.20.cloned.1.call-start = ((), (), s32[]{:S(2)}) async-start(), calls=%async_computation.5 | async-start | bytes 19464192 | tf_op jit(solution)/shard_map/all_gather | solution.py:263
  10.0 702.8 %reduce-scatter.6.cloned.1.call-start = ((), (), s32[]{:S(2)}) async-start(), calls=%async_computation.7 | async-start | bytes 2433024 | tf_op jit(solution)/shard_map/reduce_scatter | solution.py:296
  55.6 80.7 %copy-start.80 = (f32[768]{0:T(1024)}, f32[768]{0:T(1024)S(1)}, u32[]{:S(2)}) copy-start(f32[768]{0:T(1024)S(1)} %convert_element_type.245) | copy-start | bytes 9220
  97.5 42.5 %copy-start.73 = (pred[208]{0:T(512)(128)(4,1)}, pred[208]{0:T(512)(128)(4,1)S(1)}, u32[]{:S(2)}) copy-start(pred[208]{0:T(512)(128)(4,1)S(1)} %get-tuple-element.40) | copy-start | bytes 628
  97.6 42.7 %copy-start.77 = (pred[208]{0:T(512)(128)(4,1)}, pred[208]{0:T(512)(128)(4,1)S(1)}, u32[]{:S(2)}) copy-start(pred[208]{0:T(512)(128)(4,1)S(1)} %get-tuple-element.39) | copy-start | bytes 628
  114.0 17.7 %copy-start.56 = (f32[12,208]{1,0:T(8,128)}, f32[12,208]{1,0:T(8,128)S(1)}, u32[]{:S(2)}) copy-start(f32[12,208]{1,0:T(8,128)S(1)} %log_add_fusion.1) | copy-start | bytes 29956
  137.0 131.3 %copy-start.60 = (f32[208,4]{0,1:T(4,128)}, f32[208,4]{0,1:T(4,128)S(1)}, u32[]{:S(2)}) copy-start(f32[208,4]{0,1:T(4,128)S(1)} %get-tuple-element.81) | copy-start | bytes 9988
  137.6 130.7 %copy-start.63 = (f32[208,4]{0,1:T(4,128)}, f32[208,4]{0,1:T(4,128)S(1)}, u32[]{:S(2)}) copy-start(f32[208,4]{0,1:T(4,128)S(1)} %get-tuple-element.80) | copy-start | bytes 9988
  140.3 128.0 %copy-start.67 = (bf16[4,768]{1,0:T(4,128)(2,1)}, bf16[4,768]{1,0:T(4,128)(2,1)S(1)}, u32[]{:S(2)}) copy-start(bf16[4,768]{1,0:T(4,128)(2,1)S(1)} %convolution_convert_fusion.10) | copy-start | bytes 18436
  142.1 239.9 %copy-start.69 = (bf16[4,768]{1,0:T(4,128)(2,1)}, bf16[4,768]{1,0:T(4,128)(2,1)S(1)}, u32[]{:S(2)}) copy-start(bf16[4,768]{1,0:T(4,128)(2,1)S(1)} %convolution_convert_fusion.8) | copy-start | bytes 18436
  395.3 9.8 %copy-start.64 = (f32[208,4]{0,1:T(4,128)S(1)}, f32[208,4]{0,1:T(4,128)}, u32[]{:S(2)}) copy-start(f32[208,4]{0,1:T(4,128)} %copy-done.63) | copy-start | bytes 9988
  395.3 9.8 %copy-start.74 = (pred[208]{0:T(512)(128)(4,1)S(1)}, pred[208]{0:T(512)(128)(4,1)}, u32[]{:S(2)}) copy-start(pred[208]{0:T(512)(128)(4,1)} %copy-done.73) | copy-start | bytes 628
  395.3 9.8 %copy-start.134 = (f32[4]{0:T(128)S(1)}, f32[4]{0:T(128)}, u32[]{:S(2)}) copy-start(f32[4]{0:T(128)} %copy-done.133) | copy-start | bytes 52
  395.3 9.8 %copy-start.139 = (f32[4]{0:T(128)S(1)}, f32[4]{0:T(128)}, u32[]{:S(2)}) copy-start(f32[4]{0:T(128)} %copy-done.138) | copy-start | bytes 52
  431.1 9.3 %copy-start.61 = (f32[208,4]{0,1:T(4,128)S(1)}, f32[208,4]{0,1:T(4,128)}, u32[]{:S(2)}) copy-start(f32[208,4]{0,1:T(4,128)} %copy-done.60) | copy-start | bytes 9988
  431.1 9.3 %copy-start.132 = (f32[4]{0:T(128)S(1)}, f32[4]{0:T(128)}, u32[]{:S(2)}) copy-start(f32[4]{0:T(128)} %copy-done.131) | copy-start | bytes 52
  431.1 9.3 %copy-start.137 = (f32[4]{0:T(128)S(1)}, f32[4]{0:T(128)}, u32[]{:S(2)}) copy-start(f32[4]{0:T(128)} %copy-done.136) | copy-start | bytes 52
  431.2 19.6 %slice-start = ((s8[18874368]{0:T(1024)(128)(4,1)}), s8[4194304]{0:T(1024)(128)(4,1)S(1)}, s32[]{:S(2)}) async-start(s8[18874368]{0:T(1024)(128)(4,1)} %bitcast.329), calls=%async_computation.8 | async-start | bytes 8388608
  431.2 19.6 %slice-start.1 = ((s8[18874368]{0:T(1024)(128)(4,1)}), s8[4194304]{0:T(1024)(128)(4,1)S(1)}, s32[]{:S(2)}) async-start(s8[18874368]{0:T(1024)(128)(4,1)} %bitcast.329), calls=%async_computation.9 | async-start | bytes 8388608
  431.2 19.6 %slice-start.2 = ((s8[18874368]{0:T(1024)(128)(4,1)}), s8[4194304]{0:T(1024)(128)(4,1)S(1)}, s32[]{:S(2)}) async-start(s8[18874368]{0:T(1024)(128)(4,1)} %bitcast.329), calls=%async_computation.10 | async-start | bytes 8388608
  440.5 14.5 %copy-start.99 = (f32[208,4]{0,1:T(4,128)}, f32[208,4]{0,1:T(4,128)S(1)}, u32[]{:S(2)}) copy-start(f32[208,4]{0,1:T(4,128)S(1)} %fusion.161) | copy-start | bytes 9988
  440.9 9.3 %copy-start.31 = (bf16[2,208,768]{2,1,0:T(8,128)(2,1)S(1)}, bf16[2,208,768]{2,1,0:T(8,128)(2,1)}, u32[]{:S(2)}) copy-start(bf16[2,208,768]{2,1,0:T(8,128)(2,1)} %param.23) | copy-start | bytes 1916932
  440.9 9.3 %copy-start.111 = (f32[208]{0:T(256)S(1)}, f32[208]{0:T(256)}, u32[]{:S(2)}) copy-start(f32[208]{0:T(256)} %copy-done.110) | copy-start | bytes 2500
  440.9 9.3 %copy-start.148 = (f32[208]{0:T(256)S(1)}, f32[208]{0:T(256)}, u32[]{:S(2)}) copy-start(f32[208]{0:T(256)} %multiply_divide_fusion.1) | copy-start | bytes 2500
  440.9 9.3 %copy-start.153 = (f32[4]{0:T(128)S(1)}, f32[4]{0:T(128)}, u32[]{:S(2)}) copy-start(f32[4]{0:T(128)} %multiply_divide_fusion.3) | copy-start | bytes 52
  440.9 9.9 %slice-start.3 = ((s8[18874368]{0:T(1024)(128)(4,1)}), s8[4194304]{0:T(1024)(128)(4,1)S(1)}, s32[]{:S(2)}) async-start(s8[18874368]{0:T(1024)(128)(4,1)} %bitcast.329), calls=%async_computation.11 | async-start | bytes 8388608
  440.9 9.9 %slice-start.4 = ((s8[18874368]{0:T(1024)(128)(4,1)}), s8[2097152]{0:T(1024)(128)(4,1)S(1)}, s32[]{:S(2)}) async-start(s8[18874368]{0:T(1024)(128)(4,1)} %bitcast.329), calls=%async_computation.12 | async-start | bytes 4194304
  471.6 241.2 %reduce-scatter.4.cloned.1.call-start = ((), (), s32[]{:S(2)}) async-start(), calls=%async_computation.6 | async-start | bytes 7299072 | tf_op jit(solution)/shard_map/reduce_scatter | solution.py:295
  487.3 39.9 %copy-start.72 = (bf16[4,768]{1,0:T(4,128)(2,1)S(1)}, bf16[4,768]{1,0:T(4,128)(2,1)}, u32[]{:S(2)}) copy-start(bf16[4,768]{1,0:T(4,128)(2,1)} %convolution_convert_fusion.9) | copy-start | bytes 18436
  487.3 77.0 %copy-start.68 = (bf16[4,768]{1,0:T(4,128)(2,1)S(1)}, bf16[4,768]{1,0:T(4,128)(2,1)}, u32[]{:S(2)}) copy-start(bf16[4,768]{1,0:T(4,128)(2,1)} %copy-done.67) | copy-start | bytes 18436
  487.3 115.6 %copy-start.70 = (bf16[4,768]{1,0:T(4,128)(2,1)S(1)}, bf16[4,768]{1,0:T(4,128)(2,1)}, u32[]{:S(2)}) copy-start(bf16[4,768]{1,0:T(4,128)(2,1)} %copy-done.69) | copy-start | bytes 18436
  487.3 156.1 %copy-start.17 = (bf16[4,768,96]{1,2,0:T(8,128)(2,1)S(1)}, bf16[4,768,96]{1,2,0:T(8,128)(2,1)}, u32[]{:S(2)}) copy-start(bf16[4,768,96]{1,2,0:T(8,128)(2,1)} %param.21) | copy-start | bytes 1769476
  487.3 158.1 %copy-start.18 = (bf16[4,96,768]{2,1,0:T(8,128)(2,1)S(1)}, bf16[4,96,768]{2,1,0:T(8,128)(2,1)}, u32[]{:S(2)}) copy-start(bf16[4,96,768]{2,1,0:T(8,128)(2,1)} %param.22) | copy-start | bytes 1769476
  527.2 116.8 %copy-start.33 = (bf16[32,4,768]{2,1,0:T(4,128)(2,1)}, bf16[32,4,768]{2,1,0:T(4,128)(2,1)S(1)}, u32[]{:S(2)}) copy-start(bf16[32,4,768]{2,1,0:T(4,128)(2,1)S(1)} %all-gather.5) | copy-start | bytes 589828
  564.3 79.7 %copy-start.34 = (bf16[32,4,768]{2,1,0:T(4,128)(2,1)}, bf16[32,4,768]{2,1,0:T(4,128)(2,1)S(1)}, u32[]{:S(2)}) copy-start(bf16[32,4,768]{2,1,0:T(4,128)(2,1)S(1)} %all-gather.6) | copy-start | bytes 589828
  602.9 41.2 %copy-start.35 = (bf16[32,4,768]{2,1,0:T(4,128)(2,1)}, bf16[32,4,768]{2,1,0:T(4,128)(2,1)S(1)}, u32[]{:S(2)}) copy-start(bf16[32,4,768]{2,1,0:T(4,128)(2,1)S(1)} %all-gather.7) | copy-start | bytes 589828
  658.2 49.0 %copy-start.8 = (f32[1,208,768]{2,1,0:T(8,128)S(1)}, f32[1,208,768]{2,1,0:T(8,128)}, u32[]{:S(2)}) copy-start(f32[1,208,768]{2,1,0:T(8,128)} %copy-done.6) | copy-start | bytes 1916932
  658.2 49.0 %copy-start.55 = (bf16[4,1,768]{2,1,0:T(2,128)(2,1)S(1)}, bf16[4,1,768]{2,1,0:T(2,128)(2,1)}, u32[]{:S(2)}) copy-start(bf16[4,1,768]{2,1,0:T(2,128)(2,1)} %copy-done.54) | copy-start | bytes 18436
  658.2 49.9 %copy-start.5 = (f32[1,208,768]{2,1,0:T(8,128)S(1)}, f32[1,208,768]{2,1,0:T(8,128)}, u32[]{:S(2)}) copy-start(f32[1,208,768]{2,1,0:T(8,128)} %copy-done.3) | copy-start | bytes 1916932
  658.2 49.9 %copy-start.53 = (bf16[4,1,768]{2,1,0:T(2,128)(2,1)S(1)}, bf16[4,1,768]{2,1,0:T(2,128)(2,1)}, u32[]{:S(2)}) copy-start(bf16[4,1,768]{2,1,0:T(2,128)(2,1)} %copy-done.52) | copy-start | bytes 18436
  660.2 50.1 %copy-start.14 = (f32[1,208,768]{2,1,0:T(8,128)S(1)}, f32[1,208,768]{2,1,0:T(8,128)}, u32[]{:S(2)}) copy-start(f32[1,208,768]{2,1,0:T(8,128)} %copy-done.13) | copy-start | bytes 1916932
  666.0 44.2 %copy-start.145 = (f32[208]{0:T(256)S(1)}, f32[208]{0:T(256)}, u32[]{:S(2)}) copy-start(f32[208]{0:T(256)} %get-tuple-element.14) | copy-start | bytes 2500
  666.0 44.2 %copy-start.144 = (f32[208]{0:T(256)S(1)}, f32[208]{0:T(256)}, u32[]{:S(2)}) copy-start(f32[208]{0:T(256)} %get-tuple-element.19) | copy-start | bytes 2500
  666.0 44.2 %copy-start.119 = (f32[208]{0:T(256)S(1)}, f32[208]{0:T(256)}, u32[]{:S(2)}) copy-start(f32[208]{0:T(256)} %copy-done.118) | copy-start | bytes 2500
  (117 other events, 381.6 us)
Sparse Core Ops, SparseCore 0:
  10.9 63.0 all-gather.13
  76.9 52.7 all-gather.15
  132.7 123.5 all-gather.17
  259.1 122.7 all-gather.19
  471.7 97.2 reduce-scatter.5
  576.0 118.5 reduce-scatter.3
where the time goes:
time: 732 us; the launch traced here: 720 us
  blocking collectives  276 us (38%)
  waiting for transfers between devices  243 us (33%)
  matrix products  142 us (19%)
  local copies, waits for them, and re-layouts  21.1 us (3%)
  other arithmetic  20.9 us (3%)
  between operations  16.7 us (2%)
    all_gather x1, waiting for transfers between devices, shards(): lax.all_gather(expert_out, 'fsdp', axis=1, tiled=True)  114 us
    all_gather x1, waiting for transfers between devices, shards(): lax.all_gather(expert_in, 'fsdp', axis=2, tiled=True)  113 us
    unnamed x2, blocking collectives  80.3 us
    all_gather x2, blocking collectives, shards(): lax.all_gather(slot_in, 'fsdp', axis=0, tiled=True)  77.8 us
    all_gather x2, blocking collectives, shards(): lax.all_gather(grad_slot_out, 'fsdp', axis=0, tiled=True)  77.7 us
    all_gather x1, blocking collectives, shards(): lax.all_gather(slot_params, 'fsdp', axis=0, tiled=True)  40.5 us
    dot_general x2, matrix products, backward(): jnp.einsum('ged,efd->gef', grad_slot_out, w_back, preferred_element_type=...  24.4 us
    dot_general x2, matrix products, forward(): jnp.einsum('ged,edf->gef', slot_in, w_hidden, preferred_element_type=jnp....  23.9 us
  transfers between devices with their start and end apart: 6, of which 3 were waited for; matrix products, arithmetic and copies ran while one was open for 13% of the time, Pallas kernels for 0%

commit v1 on v0

v1 whole, which is shorter than its diff:
```python
import jax
import jax.numpy as jnp
from jax import lax
from jax.experimental import pallas as pl
from jax.experimental.pallas import tpu as pltpu
from jax.sharding import PartitionSpec as P

HEADS = 12
NEGATIVE = -1e30
EPSILON = 1e-06
GELU_C = 0.7978845608
GELU_A = 0.044715
LANES = 128
CHUNK = 16
MIB = 1 << 20

bf16 = jnp.bfloat16
f32 = jnp.float32


def dot(a, b, ca, cb):
    return lax.dot_general(a, b, (((ca,), (cb,)), ((), ())), preferred_element_type=f32)


def nn(a, b):
    return dot(a, b, 1, 0)


def nt(a, b):
    return dot(a, b, 1, 1)


def tn(a, b):
    return dot(a, b, 0, 0)


def vmem():
    return pl.BlockSpec(memory_space=pltpu.VMEM)


def smem():
    return pl.BlockSpec(memory_space=pltpu.SMEM)


def call(body, outs, scratch, limit_mib, flops=0, bytes_accessed=0):
    def run(scalars, *args):
        return pl.pallas_call(
            body,
            out_shape=[jax.ShapeDtypeStruct(s, d) for s, d in outs],
            in_specs=[smem()] + [vmem()] * len(args),
            out_specs=[vmem()] * len(outs),
            scratch_shapes=[pltpu.VMEM(s, d) for s, d in scratch],
            compiler_params=pltpu.CompilerParams(vmem_limit_bytes=limit_mib * MIB),
            cost_estimate=pl.CostEstimate(
                flops=flops, bytes_accessed=bytes_accessed, transcendentals=0
            ),
        )(scalars, *args)

    return run


def rows_at(step, count):
    return pl.ds(pl.multiple_of(step * count, count), count)


def fold_rows(value):
    return value[:8] + value[8:]


def head_masks():
    lane = lax.broadcasted_iota(jnp.int32, (1, LANES), 1)
    return lane < LANES // 2


def stacked(pair):
    first = head_masks()
    zero = jnp.zeros_like(pair)
    return jnp.concatenate([jnp.where(first, pair, zero), jnp.where(first, zero, pair)], axis=0)


def unstacked(both):
    rows = both.shape[0] // 2
    return jnp.where(head_masks(), both[:rows], both[rows:])


def routing(logits, live):
    masked = jnp.where(live, logits, NEGATIVE)
    weight = jnp.exp(masked - jnp.max(masked, axis=1, keepdims=True))
    dispatch = weight / jnp.sum(weight, axis=1, keepdims=True)
    share = jnp.exp(logits - jnp.max(logits, axis=0, keepdims=True))
    combine = share / jnp.sum(share, axis=0, keepdims=True)
    return dispatch, combine


def forward_kernel(sizes):
    images, rows, width, experts, chips, part_rows, packed = sizes
    total = images * rows
    pairs = HEADS // 2
    pieces = packed is not None

    def body(meta, x_ref, cot_ref, *refs):
        if pieces:
            own_ref, oth_ref, *refs = refs
            (w_ref, par_ref, n1_ref, joint_ref, probs_ref, mixed_ref, res_ref, n2_ref, log_ref,
             slots_ref, small) = refs
            core = meta[images]

            @pl.loop(0, chips)
            def _(f):
                target = meta[images + 1 + f]
                for c0 in range(0, packed, 640):
                    c1 = min(packed, c0 + 640)
                    a = own_ref[f, :, c0:c1].astype(f32)
                    b = oth_ref[f, :, c0:c1].astype(f32)
                    both = jnp.concatenate(
                        [jnp.where(core == 0, a, b), jnp.where(core == 0, b, a)], axis=0
                    )
                    w_ref[rows_at(target, 2 * part_rows), c0:c1] = both.astype(bf16)
        else:
            w_ref, *refs = refs
            (par_ref, n1_ref, joint_ref, probs_ref, mixed_ref, res_ref, n2_ref, log_ref,
             slots_ref, small) = refs

        par_ref[...] = w_ref[:, 4 * width : 4 * width + LANES].astype(f32).T[:8]
        gain_a, shift_a = par_ref[0:1], par_ref[1:2]
        gain_m, shift_m = par_ref[2:3], par_ref[3:4]

        @pl.loop(0, total // CHUNK)
        def _(i):
            at = rows_at(i, CHUNK)
            x = x_ref[at].astype(f32)
            x = x - jnp.mean(x, axis=-1, keepdims=True)
            rstd = lax.rsqrt(jnp.mean(x * x, axis=-1, keepdims=True) + EPSILON)
            n1_ref[at] = (x * rstd * gain_a + shift_a).astype(bf16)

        @pl.loop(0, 3)
        def _(i):
            at = rows_at(i, width)
            joint_ref[:, at] = nn(n1_ref[...], w_ref[:, at]).astype(bf16)

        column = lax.broadcasted_iota(jnp.int32, (1, rows), 1)

        @pl.loop(0, pairs)
        def _(p):
            at_q = pl.ds(pl.multiple_of(p * LANES, LANES), LANES)
            at_k = pl.ds(pl.multiple_of(width + p * LANES, LANES), LANES)
            at_v = pl.ds(pl.multiple_of(2 * width + p * LANES, LANES), LANES)
            for img in range(images):
                span = slice(img * rows, (img + 1) * rows)
                query, key, value = joint_ref[span, at_q], joint_ref[span, at_k], joint_ref[span, at_v]
                scores = nt(stacked(query), key) * 0.125
                scores = jnp.where(column < meta[img], scores, NEGATIVE)
                weight = jnp.exp(scores - jnp.max(scores, axis=-1, keepdims=True))
                probs = weight * (1.0 / jnp.sum(weight, axis=-1, keepdims=True))
                probs = probs.astype(bf16)
                probs_ref[img, p] = probs
                mixed_ref[span, at_q] = unstacked(nn(probs, value)).astype(bf16)

        res_ref[...] = x_ref[...].astype(f32) + nn(mixed_ref[...], w_ref[:, 3 * width : 4 * width])

        @pl.loop(0, total // CHUNK)
        def _(i):
            at = rows_at(i, CHUNK)
            x = res_ref[at]
            x = x - jnp.mean(x, axis=-1, keepdims=True)
            rstd = lax.rsqrt(jnp.mean(x * x, axis=-1, keepdims=True) + EPSILON)
            n2_ref[at] = (x * rstd * gain_m + shift_m).astype(bf16)

        slot_w = par_ref[4 : 4 + experts].astype(bf16)
        for img in range(images):
            span = slice(img * rows, (img + 1) * rows)
            logits = nt(slot_w, n2_ref[span])
            log_ref[img] = logits
            live = column < meta[img]
            dispatch, combine = routing(logits, live)
            small[img * experts : (img + 1) * experts] = nn(dispatch.astype(bf16), n2_ref[span])
            combine = jnp.where(live, combine, 0.0).astype(bf16)
            small[(images + img) * experts : (images + img + 1) * experts] = nn(combine, cot_ref[span])
        slots_ref[...] = small[...].astype(bf16)

    return body


def expert_kernel(images, experts, width, hidden, chips):
    lanes = -(-hidden // LANES) * LANES
    per = images * experts
    half = chips * per

    def body(_, own_ref, oth_ref, in_ref, out_ref, mine_ref, other_ref, s_ref, g_ref, act_ref, gpre_ref,
             win, wout, so, gs):
        win[...] = jnp.zeros(win.shape, bf16)
        wout[...] = jnp.zeros(wout.shape, bf16)
        for e in range(experts):
            win[:, e * lanes : e * lanes + hidden] = in_ref[e]
            wout[e * lanes : e * lanes + hidden, :] = out_ref[e]

        for side, ref in enumerate((own_ref, oth_ref)):

            @pl.loop(0, chips // 2)
            def _(i):
                first, second = ref[2 * i].astype(f32), ref[2 * i + 1].astype(f32)
                at = pl.ds(pl.multiple_of(side * half + i * 2 * per, 2 * per), 2 * per)
                s_ref[at] = jnp.concatenate([first[:per], second[:per]], axis=0).astype(bf16)
                g_ref[at] = jnp.concatenate([first[per:], second[per:]], axis=0).astype(bf16)

        block = 2 * half if 2 * half <= 256 else 256

        @pl.loop(0, 2 * half // block)
        def _(i):
            at = rows_at(i, block)
            so[at, : experts * lanes] = nn(s_ref[at], win[...])
            gs[at, : experts * lanes] = nt(g_ref[at], wout[...])

        @pl.loop(0, 2 * half // CHUNK)
        def _(i):
            at = rows_at(i, CHUNK)
            shape = (CHUNK, experts * lanes)
            keep = (lax.broadcasted_iota(jnp.int32, shape, 0) % experts) == (
                lax.broadcasted_iota(jnp.int32, shape, 1) // lanes
            )
            v = so[at, : experts * lanes]
            grad = gs[at, : experts * lanes]
            tanh = jnp.tanh(GELU_C * (v + GELU_A * v * v * v))
            act = 0.5 * v * (1.0 + tanh)
            slope = 0.5 * (1.0 + tanh) + 0.5 * v * (1.0 - tanh * tanh) * (
                GELU_C * (1.0 + 3.0 * GELU_A * v * v)
            )
            act_ref[at] = jnp.where(keep, act, 0.0).astype(bf16)
            gpre_ref[at] = jnp.where(keep, slope * grad, 0.0).astype(bf16)

        @pl.loop(0, 2 * half // block)
        def _(i):
            at = rows_at(i, block)
            so[at, :width] = nn(act_ref[at], wout[...])
            gs[at, :width] = nt(gpre_ref[at], win[...])

        for side, ref in enumerate((mine_ref, other_ref)):

            @pl.loop(0, chips)
            def _(f):
                at = pl.ds(pl.multiple_of(side * half + f * per, per), per)
                ref[f] = jnp.concatenate([so[at, :width], gs[at, :width]], axis=0).astype(bf16)

    return body


def expert_grad_kernel(experts, hidden):
    lanes = -(-hidden // LANES) * LANES

    def body(_, s_ref, g_ref, act_ref, gpre_ref, in_ref, out_ref):
        for e in range(experts):
            at = slice(e * lanes, (e + 1) * lanes)
            in_ref[e] = tn(s_ref[...], gpre_ref[:, at])[:, :hidden]
            out_ref[e] = tn(act_ref[:, at], g_ref[...])[:hidden]

    return body


def norm_pull(x, gain, grad):
    x = x - jnp.mean(x, axis=-1, keepdims=True)
    rstd = lax.rsqrt(jnp.mean(x * x, axis=-1, keepdims=True) + EPSILON)
    x = x * rstd
    scaled = grad * gain
    first = jnp.mean(scaled, axis=-1, keepdims=True)
    second = jnp.mean(scaled * x, axis=-1, keepdims=True)
    return x, rstd * (scaled - first - x * second)


def backward_kernel(sizes):
    images, rows, width, experts, chips, part_rows, packed = sizes
    total = images * rows
    pairs = HEADS // 2
    pieces = packed is not None

    def body(meta, x_ref, cot_ref, w_ref, par_ref, n1_ref, joint_ref, probs_ref, mixed_ref, res_ref,
             n2_ref, log_ref, sum_ref, r1_ref, r2_ref, r3_ref, *refs):
        if pieces:
            block_ref, xgrad_ref, mine_ref, other_ref, gn, gb, gm, gj, tile, small, grads = refs
        else:
            block_ref, xgrad_ref, whole_ref, gn, gb, gm, gj, tile, small, grads = refs

        def put(first, count):
            if not pieces:
                whole_ref[:, first : first + count] = tile[:, :count]
                return
            core = meta[images]

            @pl.loop(0, chips)
            def _(f):
                at = rows_at(meta[images + 1 + f], 2 * part_rows)
                both = tile[at, :count]
                low, high = both[:part_rows], both[part_rows:]
                mine_ref[f, :, first : first + count] = jnp.where(core == 0, low, high).astype(bf16)
                other_ref[f, :, first : first + count] = jnp.where(core == 0, high, low).astype(bf16)

        sums = sum_ref[0].astype(f32) + r1_ref[0].astype(f32) + r2_ref[0].astype(f32) + r3_ref[0].astype(f32)
        small[...] = sums.astype(bf16).astype(f32)
        slot_w = par_ref[4 : 4 + experts]
        column = lax.broadcasted_iota(jnp.int32, (1, rows), 1)
        slot_grad = jnp.zeros((experts, width), f32)
        for img in range(images):
            span = slice(img * rows, (img + 1) * rows)
            live = column < meta[img]
            dispatch, combine = routing(log_ref[img], live)
            out32 = small[img * experts : (img + 1) * experts]
            grad32 = small[(images + img) * experts : (images + img + 1) * experts]
            slot_out = out32.astype(bf16)
            grad_comb = jnp.where(live, nt(slot_out, cot_ref[span]), 0.0)
            grad_disp = nt(grad32.astype(bf16), n2_ref[span])
            grad_log = combine * (grad_comb - jnp.sum(combine * grad_comb, axis=0, keepdims=True))
            grad_log = grad_log + dispatch * (
                grad_disp - jnp.sum(dispatch * grad_disp, axis=1, keepdims=True)
            )
            slot_grad = slot_grad + nn(grad_log.astype(bf16), n2_ref[span])
            left = jnp.concatenate([dispatch, grad_log], axis=0).astype(bf16)
            right = jnp.concatenate([grad32, slot_w], axis=0).astype(bf16)
            gn[span] = tn(left, right)
            live_row = lax.broadcasted_iota(jnp.int32, (rows, 1), 0) < meta[img]
            expert_sum = tn(combine.astype(bf16), slot_out)
            block_ref[span] = jnp.where(live_row, res_ref[span] + expert_sum, 0.0).astype(bf16)
        grads[4 : 4 + experts] = slot_grad

        gain_a, gain_m = par_ref[0:1], par_ref[2:3]
        zero = jnp.zeros((8, width), f32)
        for img in range(images):

            def step(i, carry):
                at = pl.ds(pl.multiple_of(img * rows + i * CHUNK, CHUNK), CHUNK)
                grad = gn[at]
                x, pulled = norm_pull(res_ref[at], gain_m, grad)
                row = i * CHUNK + lax.broadcasted_iota(jnp.int32, (CHUNK, 1), 0)
                pulled = pulled + jnp.where(row < meta[img], cot_ref[at].astype(f32), 0.0)
                xgrad_ref[at] = pulled
                gb[at] = pulled.astype(bf16)
                return carry[0] + fold_rows(grad * x), carry[1] + fold_rows(grad)

            sums = lax.fori_loop(0, rows // CHUNK, step, (zero, zero) if img == 0 else sums)
        grads[2:3] = jnp.sum(sums[0], axis=0, keepdims=True)
        grads[3:4] = jnp.sum(sums[1], axis=0, keepdims=True)

        tile[...] = tn(mixed_ref[...], gb[...])
        put(3 * width, width)
        gm[...] = nt(gb[...], w_ref[:, 3 * width : 4 * width]).astype(bf16)

        @pl.loop(0, pairs)
        def _(p):
            at_q = pl.ds(pl.multiple_of(p * LANES, LANES), LANES)
            at_k = pl.ds(pl.multiple_of(width + p * LANES, LANES), LANES)
            at_v = pl.ds(pl.multiple_of(2 * width + p * LANES, LANES), LANES)
            for img in range(images):
                span = slice(img * rows, (img + 1) * rows)
                query, key, value = joint_ref[span, at_q], joint_ref[span, at_k], joint_ref[span, at_v]
                grad = stacked(gm[span, at_q])
                low = probs_ref[img, p]
                probs = low.astype(f32)
                grad_probs = nt(grad, value)
                row_dot = jnp.sum(probs * grad_probs, axis=-1, keepdims=True)
                grad_scores = (probs * (grad_probs - row_dot)).astype(bf16)
                gj[span, at_q] = (unstacked(nn(grad_scores, key)) * 0.125).astype(bf16)
                gj[span, at_k] = (tn(grad_scores, stacked(query)) * 0.125).astype(bf16)
                gj[span, at_v] = tn(low, grad).astype(bf16)

        for i in range(3):
            at = slice(i * width, (i + 1) * width)
            tile[...] = tn(n1_ref[...], gj[:, at])
            put(i * width, width)
        gn[...] = nt(gj[...], w_ref[:, : 3 * width])

        def step(i, carry):
            at = rows_at(i, CHUNK)
            grad = gn[at]
            x, pulled = norm_pull(x_ref[at].astype(f32), gain_a, grad)
            xgrad_ref[at] = xgrad_ref[at] + pulled
            return carry[0] + fold_rows(grad * x), carry[1] + fold_rows(grad)

        sums = lax.fori_loop(0, total // CHUNK, step, (zero, zero))
        grads[0:1] = jnp.sum(sums[0], axis=0, keepdims=True)
        grads[1:2] = jnp.sum(sums[1], axis=0, keepdims=True)
        filled = jnp.concatenate([grads[...], jnp.zeros((LANES - 8, width), f32)], axis=0)
        tile[:, :LANES] = filled.T
        put(4 * width, LANES)

    return body


def split_sum(parts, first_type=f32):
    def run(*args):
        count, rest = args[0].shape[0], args[0].shape[1:]
        share = count // parts

        def body(*refs):
            ins, outs = refs[: len(args)], refs[len(args) :]
            for part in range(parts):

                @pl.loop(0, share)
                def _(i):
                    total = ins[0][part * share + i].astype(f32)
                    for ref in ins[1:]:
                        total = total + ref[part * share + i].astype(f32)
                    outs[part][i] = total.astype(outs[part].dtype)

        types = [first_type] + [bf16] * (parts - 1)
        return pl.pallas_call(
            body,
            out_shape=[jax.ShapeDtypeStruct((share,) + rest, t) for t in types],
            in_specs=[vmem()] * len(args),
            out_specs=[vmem()] * parts,
            compiler_params=pltpu.CompilerParams(vmem_limit_bytes=32 * MIB),
        )(*args)

    return run


def stages_of(devices):
    chips = devices // 2
    groups, bit = [], 1
    while bit < chips:
        count = min(4, chips // bit)
        groups.append([bit * i for i in range(count)])
        bit *= count
    return groups


def swap(value, devices, chip_offset, core_offset):
    mask = 2 * chip_offset + core_offset
    return lax.ppermute(value, "fsdp", [(i, i ^ mask) for i in range(devices)])


def gather_chips(block, devices):
    for group in reversed(stages_of(devices)):
        block = jnp.concatenate(
            [block] + [swap(block, devices, o, 0) for o in group[1:]], axis=0
        )
    return block, swap(block, devices, 0, 1)


def scatter_chips(mine, other, devices):
    terms = [mine, swap(other, devices, 0, 1)]
    for group in stages_of(devices):
        parts = split_sum(len(group))(*terms)
        terms = [parts[0]] + [swap(p, devices, o, 0) for p, o in zip(parts[1:], group[1:])]
    return terms


def build(devices):
    def shards(images, lengths, norm_scale, norm_shift, attend_in, attend_out, mixer_scale, mixer_shift,
               slot_params, expert_in, expert_out, cotangent):
        count, rows, width = images.shape
        experts, _, hidden = expert_in.shape
        part_rows = attend_in.shape[0]
        chips = devices // 2
        total = count * rows
        pairs = HEADS // 2
        packed = 4 * width + LANES
        pieces = part_rows % 8 == 0
        sizes = (count, rows, width, experts, chips, part_rows, packed if pieces else None)
        me = lax.axis_index("fsdp")

        offsets = jnp.zeros((1,), jnp.int32)
        for group in reversed(stages_of(devices)):
            offsets = (jnp.array(group, jnp.int32)[:, None] ^ offsets[None, :]).reshape(-1)
        meta = jnp.concatenate(
            [lengths, jnp.reshape(me % 2, (1,)).astype(jnp.int32), (me // 2).astype(jnp.int32) ^ offsets]
        )

        small = jnp.stack([norm_scale, norm_shift, mixer_scale, mixer_shift], axis=1)
        small = jnp.concatenate([small, slot_params], axis=1)
        small = jnp.pad(small, ((0, 0), (0, LANES - small.shape[1])))
        pack = jnp.concatenate([attend_in, attend_out, small], axis=1)
        x = images.reshape(total, width)
        cot = cotangent.reshape(total, width)

        outs = [
            ((8, width), f32),
            ((total, width), bf16),
            ((total, 3 * width), bf16),
            ((count, pairs, 2 * rows, rows), bf16),
            ((total, width), bf16),
            ((total, width), f32),
            ((total, width), bf16),
            ((count, experts, rows), f32),
            ((2 * count * experts, width), bf16),
        ]
        scratch = [((2 * count * experts, width), f32)]
        if pieces:
            own, oth = gather_chips(pack[None], devices)
            w, par, n1, joint, probs, mixed, res, n2, logs, slots = call(
                forward_kernel(sizes), [((width, packed), bf16)] + outs, scratch, 48
            )(meta, x, cot, own, oth)
        else:
            w = lax.all_gather(pack, "fsdp", axis=0, tiled=True)
            par, n1, joint, probs, mixed, res, n2, logs, slots = call(
                forward_kernel(sizes), outs, scratch, 48
            )(meta, x, cot, w)

        own, oth = gather_chips(slots[None], devices)
        lanes = -(-hidden // LANES) * LANES
        held = devices * count * experts
        wide = max(width, experts * lanes)
        mine, other, s_all, g_all, act, gpre = call(
            expert_kernel(count, experts, width, hidden, chips),
            [
                ((chips, 2 * count * experts, width), bf16),
                ((chips, 2 * count * experts, width), bf16),
                ((held, width), bf16),
                ((held, width), bf16),
                ((held, experts * lanes), bf16),
                ((held, experts * lanes), bf16),
            ],
            [
                ((width, experts * lanes), bf16),
                ((experts * lanes, width), bf16),
                ((held, wide), f32),
                ((held, wide), f32),
            ],
            40,
        )(meta, own, oth, expert_in, expert_out)
        expin_grad, expout_grad = call(
            expert_grad_kernel(experts, hidden),
            [((experts, width, hidden), f32), ((experts, hidden, width), f32)],
            [],
            32,
        )(meta, s_all, g_all, act, gpre)
        terms = scatter_chips(mine, other, devices)
        if len(terms) < 4:
            terms = terms + [jnp.zeros_like(terms[-1])] * (4 - len(terms))

        results = [((total, width), bf16), ((total, width), f32)]
        if pieces:
            results += [((chips, part_rows, packed), bf16)] * 2
        else:
            results += [((width, packed), f32)]
        block, xgrad, *weight_grads = call(
            backward_kernel(sizes),
            results,
            [
                ((total, width), f32),
                ((total, width), bf16),
                ((total, width), bf16),
                ((total, 3 * width), bf16),
                ((width, width), f32),
                ((2 * count * experts, width), f32),
                ((8, width), f32),
            ],
            56,
        )(meta, x, cot, w, par, n1, joint, probs, mixed, res, n2, logs, *terms)
        if pieces:
            grad = split_sum(1)(*scatter_chips(*weight_grads, devices))[0][0]
        else:
            grad = lax.psum_scatter(weight_grads[0], "fsdp", scatter_dimension=0, tiled=True)
        at = 4 * width
        return (
            block.reshape(images.shape),
            xgrad.reshape(images.shape),
            grad[:, at],
            grad[:, at + 1],
            grad[:, : 3 * width],
            grad[:, 3 * width : at],
            grad[:, at + 2],
            grad[:, at + 3],
            grad[:, at + 4 : at + 4 + experts],
            expin_grad,
            expout_grad,
        )

    return shards


def solution(mesh):
    rows = P("fsdp", None, None)
    cols = P(None, None, "fsdp")
    mids = P(None, "fsdp", None)
    flat = P("fsdp", None)
    vec = P("fsdp")
    return jax.shard_map(
        build(mesh.shape["fsdp"]),
        mesh=mesh,
        in_specs=(rows, vec, vec, vec, flat, flat, vec, vec, flat, cols, mids, rows),
        out_specs=(rows, rows, vec, vec, flat, flat, vec, vec, flat, cols, mids),
        check_vma=False,
    )
```

time: 732 us -> 217 us (0.30); the launches traced: 720 us -> 217 us
  blocking collectives: 276 us -> 0 us
  waiting for transfers between devices: 243 us -> 93.3 us
  matrix products: 142 us -> 0 us
  Pallas kernels: 0 us -> 70.4 us
  starting transfers between devices: 0.44 us -> 33.5 us
  other arithmetic: 20.9 us -> 2.73 us
  between operations: 16.7 us -> 0.88 us
    all_gather x4 -> x0, waiting for transfers between devices: 241 us -> none  [the longest x1 114 us: shards(): lax.all_gather(expert_out, 'fsdp', axis=1, tiled=True)]
    all_gather x5 -> x0, blocking collectives: 196 us -> none  [the longest x2 77.8 us: shards(): lax.all_gather(slot_in, 'fsdp', axis=0, tiled=True)]
    dot_general x56 -> x0, matrix products: 142 us -> none  [the longest x2 24.4 us: backward(): jnp.einsum('ged,efd->gef', grad_slot_out, w_back, preferred_element_type=...]
    ppermute x0 -> x28, waiting for transfers between devices: none -> 93.3 us  [swap(): return lax.ppermute(value, 'fsdp', [(i, i ^ mask) for i in range(devices)])]
    unnamed x2 -> x0, blocking collectives: 80.3 us -> none
    pallas_call x0 -> x9, Pallas kernels: none -> 70.4 us  [the longest x4 69.2 us: run(): pl.pallas_call(body, out_shape=[jax.ShapeDtypeStruct(s, d) for s, d in ou...]
    ppermute x0 -> x28, starting transfers between devices: none -> 33.5 us  [swap(): return lax.ppermute(value, 'fsdp', [(i, i ^ mask) for i in range(devices)])]
  transfers between devices with their start and end apart: 6 -> 28, of which waited for: 3 -> 17; matrix products, arithmetic and copies ran while one was open for 13% -> 3% of each run, Pallas kernels for 0% -> 1%
where the time goes in v1:
time: 217 us
  waiting for transfers between devices  93.3 us (43%)
  Pallas kernels  70.4 us (32%)
  starting transfers between devices  33.5 us (15%)
  local copies, waits for them, and re-layouts  16 us (7%)
  other arithmetic  2.73 us (1%)
    ppermute x28, waiting for transfers between devices, swap(): return lax.ppermute(value, 'fsdp', [(i, i ^ mask) for i in range(devices)])  93.3 us
    pallas_call x4, Pallas kernels, run(): pl.pallas_call(body, out_shape=[jax.ShapeDtypeStruct(s, d) for s, d in ou...  69.2 us
    ppermute x28, starting transfers between devices, swap(): return lax.ppermute(value, 'fsdp', [(i, i ^ mask) for i in range(devices)])  33.5 us
    unnamed x50, local copies, waits for them, and re-layouts  12 us
  transfers between devices with their start and end apart: 28, of which 17 were waited for; matrix products, arithmetic and copies ran while one was open for 3% of the time, Pallas kernels for 1%

profile of v1, /device:TPU:0, one launch (start us, length us, event | category | flops | bytes accessed | tf_op | source)
XLA Modules:
  0.0 216.8 jit_solution(7061776696062114592)
XLA Ops:
  0.6 0.8 concatenate.24
  1.5 0.9 fusion.2
  2.4 5.1 %collective-permute-start.2 = (bf16[1,24,3200]{2,1,0:T(8,128)(2,1)S(1)}, bf16[1,24,3200]{2,1,0:T(8,128)(2,1)S(1)}, u32[]{:S(2)}, u32[]{:S(2)}) collective-permute-start(bf16[1,24,3200]{2,1,0:T(8,128)(2,1)S(1)} %fusion.2), channel_id=1, source_target_pairs={{0,24},{1,25},{2,26},{3,27},{4,28},{5,29},{6,30},{7,31},{8,16},{9,... | collective-permute-start | bytes 460808 | tf_op jit(solution)/shard_map/ppermute | solution.py:426
  8.2 1.6 constant_dynamic-update-slice_fusion.6
  9.8 2.7 %collective-permute-done.2 = bf16[1,24,3200]{2,1,0:T(8,128)(2,1)S(1)} collective-permute-done((bf16[1,24,3200]{2,1,0:T(8,128)(2,1)S(1)}, bf16[1,24,3200]{2,1,0:T(8,128)(2,1)S(1)}, u32[]{:S(2)}, u32[]{:S(2)}) %collective-permute-start.2) | collective-permute-done | bytes 153632 | tf_op jit(solution)/shard_map/ppermute | solution.py:426
  12.5 8.1 %collective-permute-done.1 = bf16[1,24,3200]{2,1,0:T(8,128)(2,1)S(1)} collective-permute-done((bf16[1,24,3200]{2,1,0:T(8,128)(2,1)S(1)}, bf16[1,24,3200]{2,1,0:T(8,128)(2,1)S(1)}, u32[]{:S(2)}, u32[]{:S(2)}) %collective-permute-start.1) | collective-permute-done | bytes 153632 | tf_op jit(solution)/shard_map/ppermute | solution.py:426
  20.7 2.5 %collective-permute-start.5 = (bf16[4,24,3200]{2,1,0:T(8,128)(2,1)S(1)}, bf16[4,24,3200]{2,1,0:T(8,128)(2,1)S(1)}, u32[]{:S(2)}, u32[]{:S(2)}) collective-permute-start(bf16[4,24,3200]{2,1,0:T(8,128)(2,1)S(1)} %pad_maximum_fusion), channel_id=1, source_target_pairs={{0,6},{1,7},{2,4},{3,5},{4,2},{5,3},{6,0},{7,1},{8,14},{9,15},{10,... | collective-permute-start | bytes 1843208 | tf_op jit(solution)/shard_map/ppermute | solution.py:426
  26.3 23.6 %collective-permute-done.3 = bf16[4,24,3200]{2,1,0:T(8,128)(2,1)S(1)} collective-permute-done((bf16[4,24,3200]{2,1,0:T(8,128)(2,1)S(1)}, bf16[4,24,3200]{2,1,0:T(8,128)(2,1)S(1)}, u32[]{:S(2)}, u32[]{:S(2)}) %collective-permute-start.3) | collective-permute-done | bytes 614432 | tf_op jit(solution)/shard_map/ppermute | solution.py:426
  49.8 0.9 constant_dynamic-update-slice_fusion.2
  50.7 0.9 constant_dynamic-update-slice_fusion.1
  51.6 0.9 constant_dynamic-update-slice_fusion.refs_0_
  52.7 4.8 %collective-permute-done.6.refs_1_ = bf16[16,24,3200]{2,1,0:T(8,128)(2,1)} collective-permute-done((bf16[16,24,3200]{2,1,0:T(8,128)(2,1)}, bf16[16,24,3200]{2,1,0:T(8,128)(2,1)}, u32[]{:S(2)}, u32[]{:S(2)}) %collective-permute-start.6) | collective-permute-done | bytes 2457632 | tf_op jit(solution)/shard_map/ppermute | solution.py:426
  57.5 25.7 %shard_map.221 = (bf16[768,3200]{1,0:T(8,128)(2,1)}, f32[8,768]{1,0:T(8,128)S(1)}, bf16[416,768]{1,0:T(8,128)(2,1)S(1)}, bf16[416,2304]{1,0:T(8,128)(2,1)}, bf16...) custom-call(s32[19]{0:T(128)S(1)} %pad_add_fusion.meta._, ...), custom_call_target="tpu_custom_call" | custom-call | tf_op jit(solution)/shard_map/pallas_call | solution.py:47
  83.2 1.1 copy-done.3
  84.3 0.8 copy-done.5
  85.1 0.8 copy-done.6
  86.0 2.4 %collective-permute-start.9 = (bf16[1,16,768]{2,1,0:T(8,128)(2,1)S(1)}, bf16[1,16,768]{2,1,0:T(8,128)(2,1)S(1)}, u32[]{:S(2)}, u32[]{:S(2)}) collective-permute-start(bf16[1,16,768]{2,1,0:T(8,128)(2,1)S(1)} %bitcast.24), channel_id=1, source_target_pairs={{0,24},{1,25},{2,26},{3,27},{4,28},{5,29},{6,30},{7,31},{8,16},{9,... | collective-permute-start | bytes 73736 | tf_op jit(solution)/shard_map/ppermute | solution.py:426
  88.4 2.1 collective-permute-start.7
  90.4 1.2 collective-permute-done.9
  91.7 1.4 collective-permute-done.8
  93.1 1.5 collective-permute-start.12
  94.6 1.5 collective-permute-start.11
  96.7 4.1 %collective-permute-done.10 = bf16[4,16,768]{2,1,0:T(8,128)(2,1)S(1)} collective-permute-done((bf16[4,16,768]{2,1,0:T(8,128)(2,1)S(1)}, bf16[4,16,768]{2,1,0:T(8,128)(2,1)S(1)}, u32[]{:S(2)}, u32[]{:S(2)}) %collective-permute-start.10) | collective-permute-done | bytes 98336 | tf_op jit(solution)/shard_map/ppermute | solution.py:426
  101.3 1.3 collective-permute-done.13.oth_ref
  102.6 2.8 %shard_map.222 = (bf16[16,16,768]{2,1,0:T(8,128)(2,1)S(1)}, bf16[16,16,768]{2,1,0:T(8,128)(2,1)S(1)}, bf16[256,768]{1,0:T(8,128)(2,1)S(1)}, bf16[256,768]{1,0:T(...) custom-call(s32[19]{0:T(128)S(1)} %pad_add_fusion.meta._, ...), custom_call_target="tpu_custom_call" | custom-call | tf_op jit(solution)/shard_map/pallas_call | solution.py:47
  105.6 1.6 collective-permute-done.14.refs_1_
  108.7 2.3 %collective-permute-start.17 = (bf16[4,16,768]{2,1,0:T(8,128)(2,1)S(1)}, bf16[4,16,768]{2,1,0:T(8,128)(2,1)S(1)}, u32[]{:S(2)}, u32[]{:S(2)}) collective-permute-start(bf16[4,16,768]{2,1,0:T(8,128)(2,1)S(1)} %get-tuple-element.64), channel_id=1, source_target_pairs={{0,6},{1,7},{2,4},{3,5},{4,2},{5,3},{6,0},{7,1},{8,14},{9,15},{10,... | collective-permute-start | bytes 294920 | tf_op jit(solution)/shard_map/ppermute | solution.py:426
  110.9 2.1 collective-permute-done.15.refs_1_
  113.0 1.7 collective-permute-done.16.refs_2_
  115.4 1.2 collective-permute-start.18
  116.6 1.1 collective-permute-start.19
  117.6 2.1 collective-permute-start.20
  119.8 1.5 collective-permute-done.19.r2_ref
  121.3 2.0 collective-permute-done.20.r3_ref
  123.9 38.4 %shard_map.225 = (bf16[416,768]{1,0:T(8,128)(2,1)}, f32[416,768]{1,0:T(8,128)}, bf16[16,24,3200]{2,1,0:T(8,128)(2,1)}, bf16[16,24,3200]{2,1,0:T(8,128)(2,1)}) custom-call(s32[19]{0:T(128)} %copy-done.10, bf16[416,768]{1,0:T(8,128)(2,1)} %bitcast.16, bf16[416,768]{1,0:T(8,128)(2,1)} %bitcast.18, bf16[768,3200]{1,0:T(8,128)(2,1)} %get-tuple-element.49.w_ref, ...), custom_call_target="tpu_custom_call" | custom-call | tf_op jit(solution)/shard_map/pallas_call | solution.py:47
  162.3 4.9 %collective-permute-done.21.refs_1_ = bf16[16,24,3200]{2,1,0:T(8,128)(2,1)S(1)} collective-permute-done((bf16[16,24,3200]{2,1,0:T(8,128)(2,1)}, bf16[16,24,3200]{2,1,0:T(8,128)(2,1)S(1)}, u32[]{:S(2)}, u32[]{:S(2)}) %collective-permute-start.21) | collective-permute-done | bytes 2457632 | tf_op jit(solution)/shard_map/ppermute | solution.py:426
  167.1 1.7 copy-done.2
  169.5 1.6 collective-permute-start.22
  171.0 0.8 collective-permute-start.23
  171.8 1.2 collective-permute-start.24
  173.0 13.2 %collective-permute-done.22.refs_1_ = bf16[4,24,3200]{2,1,0:T(8,128)(2,1)S(1)} collective-permute-done((bf16[4,24,3200]{2,1,0:T(8,128)(2,1)S(1)}, bf16[4,24,3200]{2,1,0:T(8,128)(2,1)S(1)}, u32[]{:S(2)}, u32[]{:S(2)}) %collective-permute-start.22) | collective-permute-done | bytes 614432 | tf_op jit(solution)/shard_map/ppermute | solution.py:426
  186.2 13.6 %collective-permute-done.23.refs_2_ = bf16[4,24,3200]{2,1,0:T(8,128)(2,1)S(1)} collective-permute-done((bf16[4,24,3200]{2,1,0:T(8,128)(2,1)S(1)}, bf16[4,24,3200]{2,1,0:T(8,128)(2,1)S(1)}, u32[]{:S(2)}, u32[]{:S(2)}) %collective-permute-start.23) | collective-permute-done | bytes 614432 | tf_op jit(solution)/shard_map/ppermute | solution.py:426
  200.2 2.7 %collective-permute-start.26 = (bf16[1,24,3200]{2,1,0:T(8,128)(2,1)S(1)}, bf16[1,24,3200]{2,1,0:T(8,128)(2,1)S(1)}, u32[]{:S(2)}, u32[]{:S(2)}) collective-permute-start(bf16[1,24,3200]{2,1,0:T(8,128)(2,1)S(1)} %get-tuple-element.79), channel_id=1, source_target_pairs={{0,16},{1,17},{2,18},{3,19},{4,20},{5,21},{6,22},{7,23},{8,24},{9,... | collective-permute-start | bytes 460808 | tf_op jit(solution)/shard_map/ppermute | solution.py:426
  202.8 1.7 collective-permute-start.27
  204.6 2.4 %shard_map.229 = (f32[4,768,96]{2,1,0:T(8,128)S(1)}, f32[4,96,768]{2,1,0:T(8,128)}) custom-call(s32[19]{0:T(128)S(1)} %copy-done.11, bf16[256,768]{1,0:T(8,128)(2,1)S(1)} %get-tuple-element.81.s_ref, bf16[256,768]{1,0:T(8,128)(2,1)S(1)} %get-tuple-element.82.g_ref, bf16[256,512]{1,0:T(8,128)(2,1)S(1)} %get-tuple-element.83.act_ref, ...), custom_call_target="tpu_custom_call" | custom-call | tf_op jit(solution)/shard_map/pallas_call | solution.py:47
  206.9 1.5 copy.44
  208.4 5.6 %collective-permute-done.26.refs_2_ = bf16[1,24,3200]{2,1,0:T(8,128)(2,1)S(1)} collective-permute-done((bf16[1,24,3200]{2,1,0:T(8,128)(2,1)S(1)}, bf16[1,24,3200]{2,1,0:T(8,128)(2,1)S(1)}, u32[]{:S(2)}, u32[]{:S(2)}) %collective-permute-start.26) | collective-permute-done | bytes 153632 | tf_op jit(solution)/shard_map/ppermute | solution.py:426
  214.0 0.7 slice_reduce_fusion
  (83 shorter events, 11.2 us)
Async XLA Ops:
  2.4 10.0 %collective-permute-start.2 = (bf16[1,24,3200]{2,1,0:T(8,128)(2,1)S(1)}, bf16[1,24,3200]{2,1,0:T(8,128)(2,1)S(1)}, u32[]{:S(2)}, u32[]{:S(2)}) collective-permute-start(bf16[1,24,3200]{2,1,0:T(8,128)(2,1)S(1)} %fusion.2), channel_id=1, source_target_pairs={{0,24},{1,25},{2,26},{3,27},{4,28},{5,29},{6,30},{7,31},{8,16},{9,... | collective-permute-start | bytes 460808 | tf_op jit(solution)/shard_map/ppermute | solution.py:426
  7.6 13.0 %collective-permute-start.1 = (bf16[1,24,3200]{2,1,0:T(8,128)(2,1)S(1)}, bf16[1,24,3200]{2,1,0:T(8,128)(2,1)S(1)}, u32[]{:S(2)}, u32[]{:S(2)}) collective-permute-start(bf16[1,24,3200]{2,1,0:T(8,128)(2,1)S(1)} %fusion.2), channel_id=1, source_target_pairs={{0,16},{1,17},{2,18},{3,19},{4,20},{5,21},{6,22},{7,23},{8,24},{9,... | collective-permute-start | bytes 460808 | tf_op jit(solution)/shard_map/ppermute | solution.py:426
  7.6 13.0 %collective-permute-start = (bf16[1,24,3200]{2,1,0:T(8,128)(2,1)S(1)}, bf16[1,24,3200]{2,1,0:T(8,128)(2,1)S(1)}, u32[]{:S(2)}, u32[]{:S(2)}) collective-permute-start(bf16[1,24,3200]{2,1,0:T(8,128)(2,1)S(1)} %fusion.2), channel_id=1, source_target_pairs={{0,8},{1,9},{2,10},{3,11},{4,12},{5,13},{6,14},{7,15},{8,0},{9,1},... | collective-permute-start | bytes 460808 | tf_op jit(solution)/shard_map/ppermute | solution.py:426
  20.7 31.9 %copy-start.17 = (s32[2]{0:T(128)S(1)}, s32[2]{0:T(128)}, u32[]{:S(2)}) copy-start(s32[2]{0:T(128)} %param.15) | copy-start | bytes 28
  20.7 36.8 %copy-start = (bf16[2,208,768]{2,1,0:T(8,128)(2,1)S(1)}, bf16[2,208,768]{2,1,0:T(8,128)(2,1)}, u32[]{:S(2)}) copy-start(bf16[2,208,768]{2,1,0:T(8,128)(2,1)} %param.14) | copy-start | bytes 1916932
  20.7 36.8 %copy-start.1 = (bf16[2,208,768]{2,1,0:T(8,128)(2,1)S(1)}, bf16[2,208,768]{2,1,0:T(8,128)(2,1)}, u32[]{:S(2)}) copy-start(bf16[2,208,768]{2,1,0:T(8,128)(2,1)} %param.25) | copy-start | bytes 1916932
  20.7 30.9 %collective-permute-start.5 = (bf16[4,24,3200]{2,1,0:T(8,128)(2,1)S(1)}, bf16[4,24,3200]{2,1,0:T(8,128)(2,1)S(1)}, u32[]{:S(2)}, u32[]{:S(2)}) collective-permute-start(bf16[4,24,3200]{2,1,0:T(8,128)(2,1)S(1)} %pad_maximum_fusion), channel_id=1, source_target_pairs={{0,6},{1,7},{2,4},{3,5},{4,2},{5,3},{6,0},{7,1},{8,14},{9,15},{10,... | collective-permute-start | bytes 1843208 | tf_op jit(solution)/shard_map/ppermute | solution.py:426
  23.2 27.5 %collective-permute-start.4 = (bf16[4,24,3200]{2,1,0:T(8,128)(2,1)S(1)}, bf16[4,24,3200]{2,1,0:T(8,128)(2,1)S(1)}, u32[]{:S(2)}, u32[]{:S(2)}) collective-permute-start(bf16[4,24,3200]{2,1,0:T(8,128)(2,1)S(1)} %pad_maximum_fusion), channel_id=1, source_target_pairs={{0,4},{1,5},{2,6},{3,7},{4,0},{5,1},{6,2},{7,3},{8,12},{9,13},{10,... | collective-permute-start | bytes 1843208 | tf_op jit(solution)/shard_map/ppermute | solution.py:426
  23.7 26.1 %collective-permute-start.3 = (bf16[4,24,3200]{2,1,0:T(8,128)(2,1)S(1)}, bf16[4,24,3200]{2,1,0:T(8,128)(2,1)S(1)}, u32[]{:S(2)}, u32[]{:S(2)}) collective-permute-start(bf16[4,24,3200]{2,1,0:T(8,128)(2,1)S(1)} %pad_maximum_fusion), channel_id=1, source_target_pairs={{0,2},{1,3},{2,0},{3,1},{4,6},{5,7},{6,4},{7,5},{8,10},{9,11},{10,... | collective-permute-start | bytes 1843208 | tf_op jit(solution)/shard_map/ppermute | solution.py:426
  52.5 5.0 %collective-permute-start.6 = (bf16[16,24,3200]{2,1,0:T(8,128)(2,1)}, bf16[16,24,3200]{2,1,0:T(8,128)(2,1)}, u32[]{:S(2)}, u32[]{:S(2)}) collective-permute-start(bf16[16,24,3200]{2,1,0:T(8,128)(2,1)} %constant_dynamic-update-slice_fusion.refs_0_), channel_id=1, source_target_pairs={{0,1},{1,0},{2,3},{3,2},{4,5},{5,4},{6,7},{7,6},{8,9},{9,8},{10,11... | collective-permute-start | bytes 7372808 | tf_op jit(solution)/shard_map/ppermute | solution.py:426
  52.7 50.0 %copy-start.10 = (s32[19]{0:T(128)}, s32[19]{0:T(128)S(1)}, u32[]{:S(2)}) copy-start(s32[19]{0:T(128)S(1)} %pad_add_fusion.meta._) | copy-start | bytes 232
  57.5 43.4 %copy-start.13 = (bf16[4,768,96]{1,2,0:T(8,128)(2,1)S(1)}, bf16[4,768,96]{1,2,0:T(8,128)(2,1)}, u32[]{:S(2)}) copy-start(bf16[4,768,96]{1,2,0:T(8,128)(2,1)} %param.23) | copy-start | bytes 1769476
  83.2 1.1 copy-start.3
  84.3 0.8 copy-start.5
  85.1 0.8 copy-start.6
  86.0 14.8 %copy-start.12 = (f32[2,4,208]{2,1,0:T(4,128)}, f32[2,4,208]{2,1,0:T(4,128)S(1)}, u32[]{:S(2)}) copy-start(f32[2,4,208]{2,1,0:T(4,128)S(1)} %get-tuple-element.57.log_ref) | copy-start | bytes 19972
  86.0 14.8 %copy-start.4 = (bf16[416,768]{1,0:T(8,128)(2,1)}, bf16[416,768]{1,0:T(8,128)(2,1)S(1)}, u32[]{:S(2)}) copy-start(bf16[416,768]{1,0:T(8,128)(2,1)S(1)} %get-tuple-element.51.n1_ref) | copy-start | bytes 1916932
  86.0 14.8 %copy-start.9 = (f32[8,768]{1,0:T(8,128)}, f32[8,768]{1,0:T(8,128)S(1)}, u32[]{:S(2)}) copy-start(f32[8,768]{1,0:T(8,128)S(1)} %get-tuple-element.50.par_ref) | copy-start | bytes 73732
  86.0 16.6 %copy-start.7 = (bf16[4,96,768]{2,1,0:T(8,128)(2,1)S(1)}, bf16[4,96,768]{2,1,0:T(8,128)(2,1)}, u32[]{:S(2)}) copy-start(bf16[4,96,768]{2,1,0:T(8,128)(2,1)} %out_ref.1) | copy-start | bytes 1769476
  86.0 5.7 %collective-permute-start.9 = (bf16[1,16,768]{2,1,0:T(8,128)(2,1)S(1)}, bf16[1,16,768]{2,1,0:T(8,128)(2,1)S(1)}, u32[]{:S(2)}, u32[]{:S(2)}) collective-permute-start(bf16[1,16,768]{2,1,0:T(8,128)(2,1)S(1)} %bitcast.24), channel_id=1, source_target_pairs={{0,24},{1,25},{2,26},{3,27},{4,28},{5,29},{6,30},{7,31},{8,16},{9,... | collective-permute-start | bytes 73736 | tf_op jit(solution)/shard_map/ppermute | solution.py:426
  88.3 4.7 %collective-permute-start.8 = (bf16[1,16,768]{2,1,0:T(8,128)(2,1)S(1)}, bf16[1,16,768]{2,1,0:T(8,128)(2,1)S(1)}, u32[]{:S(2)}, u32[]{:S(2)}) collective-permute-start(bf16[1,16,768]{2,1,0:T(8,128)(2,1)S(1)} %bitcast.25), channel_id=1, source_target_pairs={{0,16},{1,17},{2,18},{3,19},{4,20},{5,21},{6,22},{7,23},{8,24},{9,... | collective-permute-start | bytes 73736 | tf_op jit(solution)/shard_map/ppermute | solution.py:426
  88.4 4.7 %collective-permute-start.7 = (bf16[1,16,768]{2,1,0:T(8,128)(2,1)S(1)}, bf16[1,16,768]{2,1,0:T(8,128)(2,1)S(1)}, u32[]{:S(2)}, u32[]{:S(2)}) collective-permute-start(bf16[1,16,768]{2,1,0:T(8,128)(2,1)S(1)} %bitcast.26), channel_id=1, source_target_pairs={{0,8},{1,9},{2,10},{3,11},{4,12},{5,13},{6,14},{7,15},{8,0},{9,1},... | collective-permute-start | bytes 73736 | tf_op jit(solution)/shard_map/ppermute | solution.py:426
  93.1 7.7 %collective-permute-start.12 = (bf16[4,16,768]{2,1,0:T(8,128)(2,1)S(1)}, bf16[4,16,768]{2,1,0:T(8,128)(2,1)S(1)}, u32[]{:S(2)}, u32[]{:S(2)}) collective-permute-start(bf16[4,16,768]{2,1,0:T(8,128)(2,1)S(1)} %pad_maximum_fusion.1), channel_id=1, source_target_pairs={{0,6},{1,7},{2,4},{3,5},{4,2},{5,3},{6,0},{7,1},{8,14},{9,15},{10,... | collective-permute-start | bytes 294920 | tf_op jit(solution)/shard_map/ppermute | solution.py:426
  94.6 6.2 %collective-permute-start.11 = (bf16[4,16,768]{2,1,0:T(8,128)(2,1)S(1)}, bf16[4,16,768]{2,1,0:T(8,128)(2,1)S(1)}, u32[]{:S(2)}, u32[]{:S(2)}) collective-permute-start(bf16[4,16,768]{2,1,0:T(8,128)(2,1)S(1)} %pad_maximum_fusion.1), channel_id=1, source_target_pairs={{0,4},{1,5},{2,6},{3,7},{4,0},{5,1},{6,2},{7,3},{8,12},{9,13},{10,... | collective-permute-start | bytes 294920 | tf_op jit(solution)/shard_map/ppermute | solution.py:426
  96.1 4.6 %collective-permute-start.10 = (bf16[4,16,768]{2,1,0:T(8,128)(2,1)S(1)}, bf16[4,16,768]{2,1,0:T(8,128)(2,1)S(1)}, u32[]{:S(2)}, u32[]{:S(2)}) collective-permute-start(bf16[4,16,768]{2,1,0:T(8,128)(2,1)S(1)} %pad_maximum_fusion.1), channel_id=1, source_target_pairs={{0,2},{1,3},{2,0},{3,1},{4,6},{5,7},{6,4},{7,5},{8,10},{9,11},{10,... | collective-permute-start | bytes 294920 | tf_op jit(solution)/shard_map/ppermute | solution.py:426
  100.8 1.8 collective-permute-start.13
  105.4 1.8 collective-permute-start.14
  107.4 5.6 %collective-permute-start.15 = (bf16[4,16,768]{2,1,0:T(8,128)(2,1)S(1)}, bf16[4,16,768]{2,1,0:T(8,128)(2,1)S(1)}, u32[]{:S(2)}, u32[]{:S(2)}) collective-permute-start(bf16[4,16,768]{2,1,0:T(8,128)(2,1)S(1)} %get-tuple-element.62), channel_id=1, source_target_pairs={{0,2},{1,3},{2,0},{3,1},{4,6},{5,7},{6,4},{7,5},{8,10},{9,11},{10,... | collective-permute-start | bytes 294920 | tf_op jit(solution)/shard_map/ppermute | solution.py:426
  108.0 6.7 %collective-permute-start.16 = (bf16[4,16,768]{2,1,0:T(8,128)(2,1)S(1)}, bf16[4,16,768]{2,1,0:T(8,128)(2,1)S(1)}, u32[]{:S(2)}, u32[]{:S(2)}) collective-permute-start(bf16[4,16,768]{2,1,0:T(8,128)(2,1)S(1)} %get-tuple-element.63), channel_id=1, source_target_pairs={{0,4},{1,5},{2,6},{3,7},{4,0},{5,1},{6,2},{7,3},{8,12},{9,13},{10,... | collective-permute-start | bytes 294920 | tf_op jit(solution)/shard_map/ppermute | solution.py:426
  108.7 6.0 %collective-permute-start.17 = (bf16[4,16,768]{2,1,0:T(8,128)(2,1)S(1)}, bf16[4,16,768]{2,1,0:T(8,128)(2,1)S(1)}, u32[]{:S(2)}, u32[]{:S(2)}) collective-permute-start(bf16[4,16,768]{2,1,0:T(8,128)(2,1)S(1)} %get-tuple-element.64), channel_id=1, source_target_pairs={{0,6},{1,7},{2,4},{3,5},{4,2},{5,3},{6,0},{7,1},{8,14},{9,15},{10,... | collective-permute-start | bytes 294920 | tf_op jit(solution)/shard_map/ppermute | solution.py:426
  114.7 0.6 copy-start.8
  115.4 4.4 %collective-permute-start.18 = (bf16[1,16,768]{2,1,0:T(8,128)(2,1)S(1)}, bf16[1,16,768]{2,1,0:T(8,128)(2,1)S(1)}, u32[]{:S(2)}, u32[]{:S(2)}) collective-permute-start(bf16[1,16,768]{2,1,0:T(8,128)(2,1)S(1)} %get-tuple-element.66), channel_id=1, source_target_pairs={{0,8},{1,9},{2,10},{3,11},{4,12},{5,13},{6,14},{7,15},{8,0},{9,1},... | collective-permute-start | bytes 73736 | tf_op jit(solution)/shard_map/ppermute | solution.py:426
  116.6 4.7 %collective-permute-start.19 = (bf16[1,16,768]{2,1,0:T(8,128)(2,1)S(1)}, bf16[1,16,768]{2,1,0:T(8,128)(2,1)S(1)}, u32[]{:S(2)}, u32[]{:S(2)}) collective-permute-start(bf16[1,16,768]{2,1,0:T(8,128)(2,1)S(1)} %get-tuple-element.67), channel_id=1, source_target_pairs={{0,16},{1,17},{2,18},{3,19},{4,20},{5,21},{6,22},{7,23},{8,24},{9,... | collective-permute-start | bytes 73736 | tf_op jit(solution)/shard_map/ppermute | solution.py:426
  117.6 5.6 %collective-permute-start.20 = (bf16[1,16,768]{2,1,0:T(8,128)(2,1)S(1)}, bf16[1,16,768]{2,1,0:T(8,128)(2,1)S(1)}, u32[]{:S(2)}, u32[]{:S(2)}) collective-permute-start(bf16[1,16,768]{2,1,0:T(8,128)(2,1)S(1)} %get-tuple-element.68), channel_id=1, source_target_pairs={{0,24},{1,25},{2,26},{3,27},{4,28},{5,29},{6,30},{7,31},{8,16},{9,... | collective-permute-start | bytes 73736 | tf_op jit(solution)/shard_map/ppermute | solution.py:426
  119.8 3.5 %copy-start.14 = (bf16[1,16,768]{2,1,0:T(8,128)(2,1)}, bf16[1,16,768]{2,1,0:T(8,128)(2,1)S(1)}, u32[]{:S(2)}) copy-start(bf16[1,16,768]{2,1,0:T(8,128)(2,1)S(1)} %collective-permute-done.18.r1_ref) | copy-start | bytes 73732
  121.3 2.0 copy-start.15
  123.3 0.6 copy-start.16
  162.3 4.9 %collective-permute-start.21 = (bf16[16,24,3200]{2,1,0:T(8,128)(2,1)}, bf16[16,24,3200]{2,1,0:T(8,128)(2,1)S(1)}, u32[]{:S(2)}, u32[]{:S(2)}) collective-permute-start(bf16[16,24,3200]{2,1,0:T(8,128)(2,1)} %get-tuple-element.72), channel_id=1, source_target_pairs={{0,1},{1,0},{2,3},{3,2},{4,5},{5,4},{6,7},{7,6},{8,9},{9,8},{10,11... | collective-permute-start | bytes 7372808 | tf_op jit(solution)/shard_map/ppermute | solution.py:426
  167.1 1.7 copy-start.2
  169.4 35.1 %copy-start.11 = (s32[19]{0:T(128)S(1)}, s32[19]{0:T(128)}, u32[]{:S(2)}) copy-start(s32[19]{0:T(128)} %copy-done.10) | copy-start | bytes 232
  169.5 16.8 %collective-permute-start.22 = (bf16[4,24,3200]{2,1,0:T(8,128)(2,1)S(1)}, bf16[4,24,3200]{2,1,0:T(8,128)(2,1)S(1)}, u32[]{:S(2)}, u32[]{:S(2)}) collective-permute-start(bf16[4,24,3200]{2,1,0:T(8,128)(2,1)S(1)} %get-tuple-element.74), channel_id=1, source_target_pairs={{0,2},{1,3},{2,0},{3,1},{4,6},{5,7},{6,4},{7,5},{8,10},{9,11},{10,... | collective-permute-start | bytes 1843208 | tf_op jit(solution)/shard_map/ppermute | solution.py:426
  171.0 28.8 %collective-permute-start.23 = (bf16[4,24,3200]{2,1,0:T(8,128)(2,1)S(1)}, bf16[4,24,3200]{2,1,0:T(8,128)(2,1)S(1)}, u32[]{:S(2)}, u32[]{:S(2)}) collective-permute-start(bf16[4,24,3200]{2,1,0:T(8,128)(2,1)S(1)} %get-tuple-element.75), channel_id=1, source_target_pairs={{0,4},{1,5},{2,6},{3,7},{4,0},{5,1},{6,2},{7,3},{8,12},{9,13},{10,... | collective-permute-start | bytes 1843208 | tf_op jit(solution)/shard_map/ppermute | solution.py:426
  171.8 28.0 %collective-permute-start.24 = (bf16[4,24,3200]{2,1,0:T(8,128)(2,1)S(1)}, bf16[4,24,3200]{2,1,0:T(8,128)(2,1)S(1)}, u32[]{:S(2)}, u32[]{:S(2)}) collective-permute-start(bf16[4,24,3200]{2,1,0:T(8,128)(2,1)S(1)} %get-tuple-element.76), channel_id=1, source_target_pairs={{0,6},{1,7},{2,4},{3,5},{4,2},{5,3},{6,0},{7,1},{8,14},{9,15},{10,... | collective-permute-start | bytes 1843208 | tf_op jit(solution)/shard_map/ppermute | solution.py:426
  200.1 8.3 %collective-permute-start.25 = (bf16[1,24,3200]{2,1,0:T(8,128)(2,1)S(1)}, bf16[1,24,3200]{2,1,0:T(8,128)(2,1)S(1)}, u32[]{:S(2)}, u32[]{:S(2)}) collective-permute-start(bf16[1,24,3200]{2,1,0:T(8,128)(2,1)S(1)} %get-tuple-element.78), channel_id=1, source_target_pairs={{0,8},{1,9},{2,10},{3,11},{4,12},{5,13},{6,14},{7,15},{8,0},{9,1},... | collective-permute-start | bytes 460808 | tf_op jit(solution)/shard_map/ppermute | solution.py:426
  200.2 13.8 %collective-permute-start.26 = (bf16[1,24,3200]{2,1,0:T(8,128)(2,1)S(1)}, bf16[1,24,3200]{2,1,0:T(8,128)(2,1)S(1)}, u32[]{:S(2)}, u32[]{:S(2)}) collective-permute-start(bf16[1,24,3200]{2,1,0:T(8,128)(2,1)S(1)} %get-tuple-element.79), channel_id=1, source_target_pairs={{0,16},{1,17},{2,18},{3,19},{4,20},{5,21},{6,22},{7,23},{8,24},{9,... | collective-permute-start | bytes 460808 | tf_op jit(solution)/shard_map/ppermute | solution.py:426
  202.8 11.1 %collective-permute-start.27 = (bf16[1,24,3200]{2,1,0:T(8,128)(2,1)S(1)}, bf16[1,24,3200]{2,1,0:T(8,128)(2,1)S(1)}, u32[]{:S(2)}, u32[]{:S(2)}) collective-permute-start(bf16[1,24,3200]{2,1,0:T(8,128)(2,1)S(1)} %get-tuple-element.80), channel_id=1, source_target_pairs={{0,24},{1,25},{2,26},{3,27},{4,28},{5,29},{6,30},{7,31},{8,16},{9,... | collective-permute-start | bytes 460808 | tf_op jit(solution)/shard_map/ppermute | solution.py:426

commit v2 on v1

v2 whole, which is shorter than its diff:
```python
import jax
import jax.numpy as jnp
from jax import lax
from jax.experimental import pallas as pl
from jax.experimental.pallas import tpu as pltpu
from jax.sharding import PartitionSpec as P

HEADS = 12
NEGATIVE = -1e30
EPSILON = 1e-06
GELU_C = 0.7978845608
GELU_A = 0.044715
LANES = 128
CHUNK = 16
UNROLL = 13
VMEM_MIB = 28
MIB = 1 << 20

bf16 = jnp.bfloat16
f32 = jnp.float32


def dot(a, b, ca, cb):
    return lax.dot_general(a, b, (((ca,), (cb,)), ((), ())), preferred_element_type=f32)


def nn(a, b):
    return dot(a, b, 1, 0)


def nt(a, b):
    return dot(a, b, 1, 1)


def tn(a, b):
    return dot(a, b, 0, 0)


def vmem():
    return pl.BlockSpec(memory_space=pltpu.VMEM)


def hbm():
    return pl.BlockSpec(memory_space=pltpu.HBM)


def smem():
    return pl.BlockSpec(memory_space=pltpu.SMEM)


def call(body, outs, scratch, limit_mib, flops=0, far_in=(), far_out=(), sems=0):
    def run(scalars, *args):
        return pl.pallas_call(
            body,
            out_shape=[
                pltpu.HBM(s, d) if i in far_out else jax.ShapeDtypeStruct(s, d)
                for i, (s, d) in enumerate(outs)
            ],
            in_specs=[smem()] + [hbm() if i in far_in else vmem() for i in range(len(args))],
            out_specs=[hbm() if i in far_out else vmem() for i in range(len(outs))],
            scratch_shapes=[pltpu.VMEM(s, d) for s, d in scratch]
            + ([pltpu.SemaphoreType.DMA((sems,))] if sems else []),
            compiler_params=pltpu.CompilerParams(vmem_limit_bytes=limit_mib * MIB),
            cost_estimate=pl.CostEstimate(flops=flops, bytes_accessed=0, transcendentals=0),
        )(
            scalars,
            *[pltpu.with_memory_space_constraint(a, pltpu.HBM) if i in far_in else a for i, a in enumerate(args)],
        )

    return run


def rows_at(step, count):
    return pl.ds(pl.multiple_of(step * count, count), count)


def fold_rows(value):
    return value[:8] + value[8:]


def head_masks():
    lane = lax.broadcasted_iota(jnp.int32, (1, LANES), 1)
    return lane < LANES // 2


def stacked(pair):
    first = head_masks()
    zero = jnp.zeros_like(pair)
    return jnp.concatenate([jnp.where(first, pair, zero), jnp.where(first, zero, pair)], axis=0)


def unstacked(both):
    rows = both.shape[0] // 2
    return jnp.where(head_masks(), both[:rows], both[rows:])


def routing(logits, live):
    masked = jnp.where(live, logits, NEGATIVE)
    weight = jnp.exp(masked - jnp.max(masked, axis=1, keepdims=True))
    dispatch = weight / jnp.sum(weight, axis=1, keepdims=True)
    share = jnp.exp(logits - jnp.max(logits, axis=0, keepdims=True))
    combine = share / jnp.sum(share, axis=0, keepdims=True)
    return dispatch, combine


def pack_kernel(width, experts):
    def body(in_ref, out_ref, ns_ref, nb_ref, ms_ref, mb_ref, slot_ref, pack_ref, square):
        pack_ref[:, : 3 * width] = in_ref[...]
        pack_ref[:, 3 * width : 4 * width] = out_ref[...]
        rows = in_ref.shape[0]
        square[...] = jnp.zeros_like(square)
        for i, ref in enumerate((ns_ref, nb_ref, ms_ref, mb_ref)):
            square[i : i + 1, :rows] = ref[...].astype(f32)
        square[4 : 4 + experts, :rows] = slot_ref[...].astype(f32)
        pack_ref[:, 4 * width :] = square[...].T[:rows].astype(bf16)

    return body


def block_chip(f, chips):
    k = f % 4
    return (lax.axis_index("fsdp") // 2) ^ (f // 4 + (k % 2) * (chips // 2) + (k // 2) * (chips // 4))


def assemble(meta, images, part_rows, own_ref, oth_ref, w_ref):
    columns = w_ref.shape[1]
    for own_first in (True, False):

        @pl.when(lax.axis_index("fsdp") % 2 == (0 if own_first else 1))
        def _():
            @pl.loop(0, own_ref.shape[0], unroll=2)
            def _(f):
                at = rows_at(block_chip(f, own_ref.shape[0]), 2 * part_rows)
                low_ref, high_ref = (own_ref, oth_ref) if own_first else (oth_ref, own_ref)
                for c0 in range(0, columns, 640):
                    c1 = min(columns, c0 + 640)
                    both = [low_ref[f, :, c0:c1].astype(f32), high_ref[f, :, c0:c1].astype(f32)]
                    w_ref[at, c0:c1] = jnp.concatenate(both, axis=0).astype(bf16)


def cut(meta, images, chips, part_rows, tile, count, mine_ref, other_ref, first):
    for own_first in (True, False):

        @pl.when(lax.axis_index("fsdp") % 2 == (0 if own_first else 1))
        def _():
            @pl.loop(0, chips, unroll=4)
            def _(f):
                at = rows_at(block_chip(f, chips), 2 * part_rows)
                for c0 in range(0, count, 384):
                    c1 = min(count, c0 + 384)
                    both = tile[at, c0:c1]
                    low, high = both[:part_rows].astype(bf16), both[part_rows:].astype(bf16)
                    mine_ref[f, :, first + c0 : first + c1] = low if own_first else high
                    other_ref[f, :, first + c0 : first + c1] = high if own_first else low


def forward_kernel(sizes):
    images, rows, width, experts, chips, part_rows, shares = sizes
    total = images * rows
    pairs = HEADS // 2
    pieces = len(shares)

    def body(meta, x_ref, cot_ref, *refs):
        ins, refs = refs[: 2 * pieces or 1], refs[2 * pieces or 1 :]
        par_ref, log_ref, slots_ref, n1_out, mixed_out, joint_out, probs_out, res_out, n2_out, *refs = refs
        if pieces:
            w_out, *refs = refs
        n1_ref, mixed_ref, joint_ref, probs_ref, res_ref, n2_ref, small, *refs = refs
        if pieces:
            w_ref, own_ref, oth_ref, sems = refs
            loads = []
            for side, stage in enumerate((own_ref, oth_ref)):
                first = 0
                for i, share in enumerate(shares):
                    ref = ins[side * pieces + i]
                    loads.append(
                        pltpu.make_async_copy(
                            ref, stage.at[first : first + share], sems.at[8 + pairs + side * pieces + i]
                        )
                    )
                    first += share
            for load in loads:
                load.start()
            for load in loads:
                load.wait()
            assemble(meta, images, part_rows, own_ref, oth_ref, w_ref)
        else:
            (sems,) = refs
            w_ref = ins[0]
        stores = []

        def store(ref, out):
            stores.append(pltpu.make_async_copy(ref, out, sems.at[len(stores)]))
            stores[-1].start()

        if pieces:
            store(w_ref, w_out)
        par_ref[...] = w_ref[:, 4 * width : 4 * width + LANES].astype(f32).T[:8]
        gain_a, shift_a = par_ref[0:1], par_ref[1:2]
        gain_m, shift_m = par_ref[2:3], par_ref[3:4]

        @pl.loop(0, total // CHUNK, unroll=UNROLL)
        def _(i):
            at = rows_at(i, CHUNK)
            x = x_ref[at].astype(f32)
            x = x - jnp.mean(x, axis=-1, keepdims=True)
            rstd = lax.rsqrt(jnp.mean(x * x, axis=-1, keepdims=True) + EPSILON)
            n1_ref[at] = (x * rstd * gain_a + shift_a).astype(bf16)

        store(n1_ref, n1_out)

        @pl.loop(0, 3)
        def _(i):
            at = rows_at(i, width)
            joint_ref[:, at] = nn(n1_ref[...], w_ref[:, at]).astype(bf16)

        store(joint_ref, joint_out)
        column = lax.broadcasted_iota(jnp.int32, (1, rows), 1)
        for p in range(pairs):
            at_q, at_k, at_v = [slice(i * width + p * LANES, i * width + (p + 1) * LANES) for i in range(3)]
            for img in range(images):
                span = slice(img * rows, (img + 1) * rows)
                query, key, value = joint_ref[span, at_q], joint_ref[span, at_k], joint_ref[span, at_v]
                scores = nt(stacked(query), key) * 0.125
                scores = jnp.where(column < meta[img], scores, NEGATIVE)
                weight = jnp.exp(scores - jnp.max(scores, axis=-1, keepdims=True))
                probs = weight * (1.0 / jnp.sum(weight, axis=-1, keepdims=True))
                probs = probs.astype(bf16)
                probs_ref[p, img] = probs
                mixed_ref[span, at_q] = unstacked(nn(probs, value)).astype(bf16)
            store(probs_ref.at[p], probs_out.at[p])
        store(mixed_ref, mixed_out)

        res_ref[...] = x_ref[...].astype(f32) + nn(mixed_ref[...], w_ref[:, 3 * width : 4 * width])
        store(res_ref, res_out)

        @pl.loop(0, total // CHUNK, unroll=UNROLL)
        def _(i):
            at = rows_at(i, CHUNK)
            x = res_ref[at]
            x = x - jnp.mean(x, axis=-1, keepdims=True)
            rstd = lax.rsqrt(jnp.mean(x * x, axis=-1, keepdims=True) + EPSILON)
            n2_ref[at] = (x * rstd * gain_m + shift_m).astype(bf16)

        store(n2_ref, n2_out)
        slot_w = par_ref[4 : 4 + experts].astype(bf16)
        for img in range(images):
            span = slice(img * rows, (img + 1) * rows)
            logits = nt(slot_w, n2_ref[span])
            log_ref[img] = logits
            live = column < meta[img]
            dispatch, combine = routing(logits, live)
            small[img * experts : (img + 1) * experts] = nn(dispatch.astype(bf16), n2_ref[span])
            combine = jnp.where(live, combine, 0.0).astype(bf16)
            small[(images + img) * experts : (images + img + 1) * experts] = nn(combine, cot_ref[span])
        slots_ref[...] = small[...].astype(bf16)
        for copy in stores:
            copy.wait()

    return body


def stack_kernel(count):
    def body(*refs):
        ins, out = refs[:count], refs[count]
        share = ins[0].shape[0]
        for i, ref in enumerate(ins):
            out[i * share : (i + 1) * share] = ref[...]

    return body


def expert_kernel(images, experts, width, hidden, chips, pieces):
    lanes = -(-hidden // LANES) * LANES
    per = images * experts
    half = chips * per

    def body(_, *refs):
        own_refs, oth_refs, refs = refs[:pieces], refs[pieces : 2 * pieces], refs[2 * pieces :]
        in_ref, out_ref, mine_ref, other_ref, s_ref, g_ref, act_ref, gpre_ref, win, wout, so, gs = refs
        win[...] = jnp.zeros(win.shape, bf16)
        wout[...] = jnp.zeros(wout.shape, bf16)
        for e in range(experts):
            win[e * lanes : e * lanes + hidden, :] = in_ref[e]
            wout[e * lanes : e * lanes + hidden, :] = out_ref[e]

        for side, group in enumerate((own_refs, oth_refs)):
            for j, ref in enumerate(group):
                share = ref.shape[0] // 2

                @pl.loop(0, share)
                def _(i):
                    first, second = ref[2 * i].astype(f32), ref[2 * i + 1].astype(f32)
                    at = pl.ds(pl.multiple_of(side * half + (j * share + i) * 2 * per, 2 * per), 2 * per)
                    s_ref[at] = jnp.concatenate([first[:per], second[:per]], axis=0).astype(bf16)
                    g_ref[at] = jnp.concatenate([first[per:], second[per:]], axis=0).astype(bf16)

        block = 2 * half if 2 * half <= 256 else 256

        @pl.loop(0, 2 * half // block)
        def _(i):
            at = rows_at(i, block)
            so[at, : experts * lanes] = nt(s_ref[at], win[...])
            gs[at, : experts * lanes] = nt(g_ref[at], wout[...])

        @pl.loop(0, 2 * half // CHUNK, unroll=4)
        def _(i):
            at = rows_at(i, CHUNK)
            shape = (CHUNK, experts * lanes)
            keep = (lax.broadcasted_iota(jnp.int32, shape, 0) % experts) == (
                lax.broadcasted_iota(jnp.int32, shape, 1) // lanes
            )
            v = so[at, : experts * lanes]
            grad = gs[at, : experts * lanes]
            tanh = jnp.tanh(GELU_C * (v + GELU_A * v * v * v))
            act = 0.5 * v * (1.0 + tanh)
            slope = 0.5 * (1.0 + tanh) + 0.5 * v * (1.0 - tanh * tanh) * (
                GELU_C * (1.0 + 3.0 * GELU_A * v * v)
            )
            act_ref[at] = jnp.where(keep, act, 0.0).astype(bf16)
            gpre_ref[at] = jnp.where(keep, slope * grad, 0.0).astype(bf16)

        @pl.loop(0, 2 * half // block)
        def _(i):
            at = rows_at(i, block)
            so[at, :width] = nn(act_ref[at], wout[...])
            gs[at, :width] = nn(gpre_ref[at], win[...])

        for side, ref in enumerate((mine_ref, other_ref)):

            @pl.loop(0, chips)
            def _(f):
                at = pl.ds(pl.multiple_of(side * half + f * per, per), per)
                ref[f] = jnp.concatenate([so[at, :width], gs[at, :width]], axis=0).astype(bf16)

    return body


def expert_grad_kernel(experts, hidden):
    lanes = -(-hidden // LANES) * LANES

    def body(_, s_ref, g_ref, act_ref, gpre_ref, in_ref, out_ref):
        for e in range(experts):
            at = slice(e * lanes, (e + 1) * lanes)
            in_ref[e] = tn(gpre_ref[:, at], s_ref[...])[:hidden]
            out_ref[e] = tn(act_ref[:, at], g_ref[...])[:hidden]

    return body


def norm_pull(x, gain, grad):
    x = x - jnp.mean(x, axis=-1, keepdims=True)
    rstd = lax.rsqrt(jnp.mean(x * x, axis=-1, keepdims=True) + EPSILON)
    x = x * rstd
    scaled = grad * gain
    first = jnp.mean(scaled, axis=-1, keepdims=True)
    second = jnp.mean(scaled * x, axis=-1, keepdims=True)
    return x, rstd * (scaled - first - x * second)


def attend_pull(meta, sizes, half, joint_ref, probs_ref, gm_ref, gj):
    images, rows, width, *_ = sizes
    share = HEADS // 4
    for q in range(share):
        at_q, at_k, at_v = [slice(i * width // 2 + q * LANES, i * width // 2 + (q + 1) * LANES) for i in range(3)]
        for img in range(images):
            span = slice(img * rows, (img + 1) * rows)
            query, key, value = joint_ref[span, at_q], joint_ref[span, at_k], joint_ref[span, at_v]
            p = half * share + q
            grad = stacked(gm_ref[span, p * LANES : (p + 1) * LANES])
            low = probs_ref[q, img]
            probs = low.astype(f32)
            grad_probs = nt(grad, value)
            row_dot = jnp.sum(probs * grad_probs, axis=-1, keepdims=True)
            grad_scores = (probs * (grad_probs - row_dot)).astype(bf16)
            gj[span, at_q] = (unstacked(nn(grad_scores, key)) * 0.125).astype(bf16)
            gj[span, at_k] = (tn(grad_scores, stacked(query)) * 0.125).astype(bf16)
            gj[span, at_v] = tn(low, grad).astype(bf16)


def half_loads(width, half, joint_in, joint_ref, probs_in, probs_ref, sems):
    part, share = width // 2, HEADS // 4
    loads = [
        pltpu.make_async_copy(
            joint_in.at[:, i * width + half * part : i * width + (half + 1) * part],
            joint_ref.at[:, i * part : (i + 1) * part],
            sems.at[i],
        )
        for i in range(3)
    ]
    loads.append(pltpu.make_async_copy(probs_in.at[half * share : (half + 1) * share], probs_ref, sems.at[3]))
    return loads


def slots_pull_kernel(sizes):
    images, rows, width, experts, chips, part_rows, shares = sizes
    pieces = len(shares)
    total = images * rows
    share = HEADS // 4

    def body(meta, cot_ref, par_ref, log_ref, sum_ref, r1_ref, r2_ref, r3_ref, w_in, n1_in, joint_in, probs_in,
             mixed_in, res_in, n2_in, block_ref, xgrad_ref, gm, gj, grads, *refs):
        outs, refs = refs[:-13], refs[-13:]
        gn, gb, tile, small, w_ref, n1_ref, joint_ref, probs_ref, mixed_ref, res_ref, n2_ref, _, sems = refs
        early = [
            pltpu.make_async_copy(n2_in, n2_ref, sems.at[0]),
            pltpu.make_async_copy(res_in, res_ref, sems.at[1]),
        ]
        late = [
            pltpu.make_async_copy(mixed_in, mixed_ref, sems.at[2]),
            pltpu.make_async_copy(w_in.at[:, 3 * width : 4 * width], w_ref, sems.at[3]),
            pltpu.make_async_copy(n1_in, n1_ref, sems.at[4]),
        ]
        loads = half_loads(width, 0, joint_in, joint_ref, probs_in, probs_ref, sems.at[5:9])
        for load in early + late + loads:
            load.start()

        def put(first, count):
            if pieces:
                cut(meta, images, chips, part_rows, tile, count, *outs, first)
            else:
                outs[0][:, first : first + count] = tile[:, :count]

        for load in early:
            load.wait()
        sums = sum_ref[0].astype(f32) + r1_ref[0].astype(f32) + r2_ref[0].astype(f32) + r3_ref[0].astype(f32)
        small[...] = sums.astype(bf16).astype(f32)
        slot_w = par_ref[4 : 4 + experts]
        column = lax.broadcasted_iota(jnp.int32, (1, rows), 1)
        slot_grad = jnp.zeros((experts, width), f32)
        for img in range(images):
            span = slice(img * rows, (img + 1) * rows)
            live = column < meta[img]
            dispatch, combine = routing(log_ref[img], live)
            out32 = small[img * experts : (img + 1) * experts]
            grad32 = small[(images + img) * experts : (images + img + 1) * experts]
            slot_out = out32.astype(bf16)
            grad_comb = jnp.where(live, nt(slot_out, cot_ref[span]), 0.0)
            grad_disp = nt(grad32.astype(bf16), n2_ref[span])
            grad_log = combine * (grad_comb - jnp.sum(combine * grad_comb, axis=0, keepdims=True))
            grad_log = grad_log + dispatch * (
                grad_disp - jnp.sum(dispatch * grad_disp, axis=1, keepdims=True)
            )
            slot_grad = slot_grad + nn(grad_log.astype(bf16), n2_ref[span])
            left = jnp.concatenate([dispatch, grad_log], axis=0).astype(bf16)
            right = jnp.concatenate([grad32, slot_w], axis=0).astype(bf16)
            gn[span] = tn(left, right)
            live_row = lax.broadcasted_iota(jnp.int32, (rows, 1), 0) < meta[img]
            expert_sum = tn(combine.astype(bf16), slot_out)
            block_ref[span] = jnp.where(live_row, res_ref[span] + expert_sum, 0.0).astype(bf16)
        grads[0:2] = jnp.zeros((2, width), f32)
        grads[4 : 4 + experts] = slot_grad

        gain_m = par_ref[2:3]
        zero = jnp.zeros((8, width), f32)
        for img in range(images):

            def step(i, carry):
                at = pl.ds(pl.multiple_of(img * rows + i * CHUNK, CHUNK), CHUNK)
                grad = gn[at]
                x, pulled = norm_pull(res_ref[at], gain_m, grad)
                row = i * CHUNK + lax.broadcasted_iota(jnp.int32, (CHUNK, 1), 0)
                pulled = pulled + jnp.where(row < meta[img], cot_ref[at].astype(f32), 0.0)
                xgrad_ref[at] = pulled
                gb[at] = pulled.astype(bf16)
                return carry[0] + fold_rows(grad * x), carry[1] + fold_rows(grad)

            sums = lax.fori_loop(0, rows // CHUNK, step, (zero, zero) if img == 0 else sums, unroll=UNROLL)
        grads[2:3] = jnp.sum(sums[0], axis=0, keepdims=True)
        grads[3:4] = jnp.sum(sums[1], axis=0, keepdims=True)

        for load in late:
            load.wait()
        tile[:, :width] = tn(mixed_ref[...], gb[...])
        put(0, width)
        gm[...] = nt(gb[...], w_ref[...]).astype(bf16)
        for load in loads:
            load.wait()
        attend_pull(meta, sizes, 0, joint_ref, probs_ref, gm, gj)
        tile[...] = tn(n1_ref[...], gj[...])
        put(width, 3 * width // 2)

    return body


def inputs_pull_kernel(sizes):
    images, rows, width, experts, chips, part_rows, shares = sizes
    pieces = len(shares)
    total = images * rows
    share = HEADS // 4
    half = 3 * width // 2

    def body(meta, x_ref, par_ref, gm_ref, gj_ref, part_ref, early_ref, w_in, n1_in, joint_in, probs_in,
             xgrad_ref, *refs):
        outs, (gn, gj, tile, grads, n1_ref, joint_ref, probs_ref, w_ref, sems) = refs[:-9], refs[-9:]
        loads = half_loads(width, 1, joint_in, joint_ref, probs_in, probs_ref, sems.at[0:4])
        late = [pltpu.make_async_copy(n1_in, n1_ref, sems.at[4])]
        part = width // 2
        for i in range(6):
            first = (i % 3) * width + (i // 3) * part
            late.append(
                pltpu.make_async_copy(
                    w_in.at[:, first : first + part], w_ref.at[:, i * part : (i + 1) * part], sems.at[5 + i]
                )
            )
        for load in loads + late:
            load.start()

        def put(first, count):
            if pieces:
                cut(meta, images, chips, part_rows, tile, count, *outs, first)
            else:
                outs[0][:, first : first + count] = tile[:, :count]

        for load in loads:
            load.wait()
        attend_pull(meta, sizes, 1, joint_ref, probs_ref, gm_ref, gj)
        for load in late:
            load.wait()
        tile[...] = tn(n1_ref[...], gj[...])
        put(0, half)
        gn[...] = nt(gj_ref[...], w_ref[:, :half]) + nt(gj[...], w_ref[:, half : 2 * half])
        gain_a = par_ref[0:1]
        zero = jnp.zeros((8, width), f32)

        def step(i, carry):
            at = rows_at(i, CHUNK)
            grad = gn[at]
            x, pulled = norm_pull(x_ref[at].astype(f32), gain_a, grad)
            xgrad_ref[at] = part_ref[at] + pulled
            return carry[0] + fold_rows(grad * x), carry[1] + fold_rows(grad)

        sums = lax.fori_loop(0, total // CHUNK, step, (zero, zero), unroll=UNROLL)
        grads[...] = early_ref[...]
        grads[0:1] = jnp.sum(sums[0], axis=0, keepdims=True)
        grads[1:2] = jnp.sum(sums[1], axis=0, keepdims=True)
        filled = jnp.concatenate([grads[...], jnp.zeros((LANES - 8, width), f32)], axis=0)
        tile[:, :LANES] = filled.T
        put(half, LANES)

    return body


def split_sum(parts, first_type=f32):
    def run(*args):
        count, rest = args[0].shape[0], args[0].shape[1:]
        share = count // parts

        def body(*refs):
            ins, outs = refs[: len(args)], refs[len(args) :]
            for part in range(parts):

                @pl.loop(0, share)
                def _(i):
                    total = ins[0][part * share + i].astype(f32)
                    for ref in ins[1:]:
                        total = total + ref[part * share + i].astype(f32)
                    outs[part][i] = total.astype(outs[part].dtype)

        types = [first_type] + [bf16] * (parts - 1)
        return pl.pallas_call(
            body,
            out_shape=[jax.ShapeDtypeStruct((share,) + rest, t) for t in types],
            in_specs=[vmem()] * len(args),
            out_specs=[vmem()] * parts,
            compiler_params=pltpu.CompilerParams(vmem_limit_bytes=32 * MIB),
        )(*args)

    return run


def add_kernel(groups, terms, types):
    def run(*args):
        rest = args[0].shape[1:]

        def body(*refs):
            ins, outs = refs[: len(args)], refs[len(args) :]
            for out, count, parts in zip(outs, groups, terms):
                for i in range(count):
                    total = ins[parts[0][0]][parts[0][1] + i].astype(f32)
                    for a, first in parts[1:]:
                        total = total + ins[a][first + i].astype(f32)
                    out[i] = total.astype(out.dtype)

        return pl.pallas_call(
            body,
            out_shape=[jax.ShapeDtypeStruct((c,) + rest, t) for c, t in zip(groups, types)],
            in_specs=[vmem()] * len(args),
            out_specs=[vmem()] * len(groups),
            compiler_params=pltpu.CompilerParams(vmem_limit_bytes=16 * MIB),
        )(*args)

    return run


def finish_kernel(width, experts):
    half = width // 2

    def body(a0, a1, b0, b1, out_ref, in_ref, ns_ref, nb_ref, ms_ref, mb_ref, slot_ref, square):
        first = a0[0] + a1[0].astype(f32)
        second = b0[0] + b1[0].astype(f32)
        rows = first.shape[0]
        out_ref[...] = first[:, :width]
        for i in range(3):
            in_ref[:, i * width : i * width + half] = first[:, width + i * half : width + (i + 1) * half]
            in_ref[:, i * width + half : (i + 1) * width] = second[:, i * half : (i + 1) * half]
        small = second[:, 3 * half : 3 * half + LANES]
        square[...] = jnp.zeros_like(square)
        square[:rows] = small
        turned = square[...].T
        for i, ref in enumerate((ns_ref, nb_ref, ms_ref, mb_ref)):
            ref[...] = turned[i : i + 1, :rows]
        slot_ref[...] = turned[4 : 4 + experts, :rows]

    return body


def stages_of(devices):
    chips = devices // 2
    groups, bit = [], 1
    while bit < chips:
        count = min(4, chips // bit)
        groups.append([bit * i for i in range(count)])
        bit *= count
    return groups


def swap(value, devices, chip_offset, core_offset):
    mask = 2 * chip_offset + core_offset
    return lax.ppermute(value, "fsdp", [(i, i ^ mask) for i in range(devices)])


def gather_slots(block, devices):
    *lower, last = stages_of(devices)[::-1]
    for group in lower:
        parts = [block] + [swap(block, devices, o, 0) for o in group[1:]]
        block = pl.pallas_call(
            stack_kernel(len(parts)),
            out_shape=jax.ShapeDtypeStruct((len(parts) * block.shape[0],) + block.shape[1:], block.dtype),
            in_specs=[vmem()] * len(parts),
            out_specs=vmem(),
        )(*parts)
    own = [block] + [swap(block, devices, o, 0) for o in last[1:]]
    return own, [swap(part, devices, 0, 1) for part in own]


def scatter_chips(mine, other, devices):
    terms = [mine, swap(other, devices, 0, 1)]
    for group in stages_of(devices):
        parts = split_sum(len(group))(*terms)
        terms = [parts[0]] + [swap(p, devices, o, 0) for p, o in zip(parts[1:], group[1:])]
    return terms


SHARES = (2,) * 8


def gather_pieces(block, devices):
    z0 = block[None]
    z0 = jnp.concatenate([z0, swap(z0, devices, 8, 0)], axis=0)
    z1 = swap(z0, devices, 4, 0)
    x0, y0 = swap(z0, devices, 1, 0), swap(z0, devices, 2, 0)
    x1, y1 = swap(z1, devices, 1, 0), swap(z1, devices, 2, 0)
    d0, d1 = swap(y0, devices, 1, 0), swap(x1, devices, 2, 0)
    own = [z0, z1, x0, x1, y0, y1, d0, d1]
    return own + [swap(piece, devices, 0, 1) for piece in own]


def scatter_pieces(mine, other, devices):
    got = swap(other, devices, 0, 1)
    two = [[(0, 2 * g), (1, 2 * g)] for g in range(8)]
    z0, z1, x0, x1, y0, y1, d0, d1 = add_kernel([2] * 8, two, [f32, f32] + [bf16] * 6)(mine, got)
    to_y0, to_x1 = swap(d0, devices, 1, 0), swap(d1, devices, 2, 0)
    x1, y0 = add_kernel([2, 2], [[(0, 0), (1, 0)], [(2, 0), (3, 0)]], [bf16, bf16])(x1, to_x1, y0, to_y0)
    from_x1, from_y1 = swap(x1, devices, 1, 0), swap(y1, devices, 2, 0)
    from_x0, from_y0 = swap(x0, devices, 1, 0), swap(y0, devices, 2, 0)
    (z1,) = add_kernel([2], [[(0, 0), (1, 0), (2, 0)]], [bf16])(z1, from_x1, from_y1)
    from_z1 = swap(z1, devices, 4, 0)
    keep, send = add_kernel(
        [1, 1], [[(a, i) for a in range(4)] for i in range(2)], [f32, bf16]
    )(z0, from_x0, from_y0, from_z1)
    return keep, swap(send, devices, 8, 0)


def build(devices):
    def shards(images, lengths, norm_scale, norm_shift, attend_in, attend_out, mixer_scale, mixer_shift,
               slot_params, expert_in, expert_out, cotangent):
        count, rows, width = images.shape
        experts, _, hidden = expert_in.shape
        part_rows = attend_in.shape[0]
        chips = devices // 2
        total = count * rows
        pairs = HEADS // 2
        half = width // 2
        wide = 4 * width + LANES
        shares = SHARES if part_rows % 8 == 0 and chips == 16 else ()
        sizes = (count, rows, width, experts, chips, part_rows, shares)
        meta = lengths
        x = images.reshape(total, width)
        cot = cotangent.reshape(total, width)
        vectors = [v.reshape(1, part_rows) for v in (norm_scale, norm_shift, mixer_scale, mixer_shift)]
        pack = pl.pallas_call(
            pack_kernel(width, experts),
            out_shape=jax.ShapeDtypeStruct((part_rows, wide), bf16),
            in_specs=[vmem()] * 7,
            out_specs=vmem(),
            scratch_shapes=[pltpu.VMEM((LANES, LANES), f32)],
        )(attend_in, attend_out, *vectors, slot_params.T)
        if shares:
            weights = gather_pieces(pack, devices)
        else:
            weights = [lax.all_gather(pack, "fsdp", axis=0, tiled=True)]
        kept = [
            ((total, width), bf16),
            ((total, width), bf16),
            ((total, 3 * width), bf16),
            ((pairs, count, 2 * rows, rows), bf16),
            ((total, width), f32),
            ((total, width), bf16),
        ]
        outs = [
            ((8, width), f32),
            ((count, experts, rows), f32),
            ((2 * count * experts, width), bf16),
        ] + kept
        scratch = kept + [((2 * count * experts, width), f32)]
        if shares:
            outs.append(((width, wide), bf16))
            scratch += [outs[-1]] + [((chips, part_rows, wide), bf16)] * 2
        par, logs, slots, n1, mixed, joint, probs, res, n2, *more = call(
            forward_kernel(sizes),
            outs,
            scratch,
            40,
            far_in=range(2, 2 + 2 * len(shares)),
            far_out=range(3, len(outs)),
            sems=8 + pairs + 2 * len(shares),
        )(meta, x, cot, *weights)
        w = more[0] if shares else weights[0]

        own, oth = gather_slots(slots[None], devices)
        lanes = -(-hidden // LANES) * LANES
        held = devices * count * experts
        most = max(width, experts * lanes)
        mine, other, s_all, g_all, act, gpre = call(
            expert_kernel(count, experts, width, hidden, chips, len(own)),
            [
                ((chips, 2 * count * experts, width), bf16),
                ((chips, 2 * count * experts, width), bf16),
                ((held, width), bf16),
                ((held, width), bf16),
                ((held, experts * lanes), bf16),
                ((held, experts * lanes), bf16),
            ],
            [
                ((experts * lanes, width), bf16),
                ((experts * lanes, width), bf16),
                ((held, most), f32),
                ((held, most), f32),
            ],
            24 if held <= 256 else 56,
        )(meta, *own, *oth, jnp.swapaxes(expert_in, 1, 2), expert_out)
        expin_grad, expout_grad = call(
            expert_grad_kernel(experts, hidden),
            [((experts, hidden, width), f32), ((experts, hidden, width), f32)],
            [],
            24 if held <= 256 else 56,
            flops=2 * 10**9,
        )(meta, s_all, g_all, act, gpre)
        terms = scatter_chips(mine, other, devices)
        if len(terms) < 4:
            terms = terms + [jnp.zeros_like(terms[-1])] * (4 - len(terms))
        terms[0], expin_grad, expout_grad = lax.optimization_barrier((terms[0], expin_grad, expout_grad))

        def blocks(columns):
            if shares:
                return [((chips, part_rows, columns), bf16)] * 2
            return [((width, columns), f32)]

        halves = [((total, 3 * half), bf16), ((pairs // 2, count, 2 * rows, rows), bf16)]
        block, part, gm, gj, early, *first = call(
            slots_pull_kernel(sizes),
            [
                ((total, width), bf16),
                ((total, width), f32),
                ((total, width), bf16),
                ((total, 3 * half), bf16),
                ((8, width), f32),
            ]
            + blocks(width + 3 * half),
            [
                ((total, width), f32),
                ((total, width), bf16),
                ((width, 3 * half), f32),
                ((2 * count * experts, width), f32),
                ((width, width), bf16),
                ((total, width), bf16),
            ]
            + halves
            + [
                ((total, width), bf16),
                ((total, width), f32),
                ((total, width), bf16),
                ((8, LANES), f32),
            ],
            VMEM_MIB,
            far_in=range(7, 14),
            sems=9,
        )(meta, cot, par, logs, *terms, w, n1, joint, probs, mixed, res, n2)
        xgrad, *second = call(
            inputs_pull_kernel(sizes),
            [((total, width), f32)] + blocks(3 * half + LANES),
            [
                ((total, width), f32),
                ((total, 3 * half), bf16),
                ((width, 3 * half), f32),
                ((8, width), f32),
                ((total, width), bf16),
            ]
            + halves
            + [((width, 3 * width), bf16)],
            VMEM_MIB,
            flops=8 * 10**9,
            far_in=range(6, 10),
            sems=11,
        )(meta, x, par, gm, gj, part, early, w, n1, joint, probs)
        if shares:
            ends = [*scatter_pieces(*first, devices), *scatter_pieces(*second, devices)]
        else:
            ends = []
            for full in (first[0], second[0]):
                full = lax.psum_scatter(full, "fsdp", scatter_dimension=0, tiled=True)[None]
                ends += [full, jnp.zeros_like(full)]
        out_grad, in_grad, ns, nb, ms, mb, slot_grad = pl.pallas_call(
            finish_kernel(width, experts),
            out_shape=[jax.ShapeDtypeStruct((part_rows, c), f32) for c in (width, 3 * width)]
            + [jax.ShapeDtypeStruct((1, part_rows), f32)] * 4
            + [jax.ShapeDtypeStruct((experts, part_rows), f32)],
            in_specs=[vmem()] * 4,
            out_specs=[vmem()] * 7,
            scratch_shapes=[pltpu.VMEM((LANES, LANES), f32)],
        )(*ends)
        return (
            block.reshape(images.shape),
            xgrad.reshape(images.shape),
            ns.reshape(part_rows),
            nb.reshape(part_rows),
            in_grad,
            out_grad,
            ms.reshape(part_rows),
            mb.reshape(part_rows),
            slot_grad.T,
            jnp.swapaxes(expin_grad, 1, 2),
            expout_grad,
        )

    return shards


def solution(mesh):
    rows = P("fsdp", None, None)
    cols = P(None, None, "fsdp")
    mids = P(None, "fsdp", None)
    flat = P("fsdp", None)
    vec = P("fsdp")
    return jax.shard_map(
        build(mesh.shape["fsdp"]),
        mesh=mesh,
        in_specs=(rows, vec, vec, vec, flat, flat, vec, vec, flat, cols, mids, rows),
        out_specs=(rows, rows, vec, vec, flat, flat, vec, vec, flat, cols, mids),
        check_vma=False,
    )
```

time: 217 us -> 164 us (0.76)
  waiting for transfers between devices: 93.3 us -> 62.6 us
  Pallas kernels: 70.4 us -> 47.6 us
  starting transfers between devices: 33.5 us -> 44.9 us
  local copies, waits for them, and re-layouts: 16 us -> 6.89 us
    ppermute x28 -> x51, waiting for transfers between devices: 93.3 us -> 62.6 us  [swap(): return lax.ppermute(value, 'fsdp', [(i, i ^ mask) for i in range(devices)])]
    pallas_call x4 -> x16, Pallas kernels: 69.2 us -> 47.4 us  [the longest x5 41.5 us: run(): pl.pallas_call(body, out_shape=[pltpu.HBM(s, d) if i in far_out else jax....]
    ppermute x28 -> x51, starting transfers between devices: 33.5 us -> 44.9 us  [swap(): return lax.ppermute(value, 'fsdp', [(i, i ^ mask) for i in range(devices)])]
    unnamed x50 -> x66, local copies, waits for them, and re-layouts: 12 us -> 6.89 us
  transfers between devices with their start and end apart: 28 -> 51, of which waited for: 17 -> 27; matrix products, arithmetic and copies ran while one was open for 3% -> 0% of each run, Pallas kernels for 1% -> 10%
where the time goes in v2:
time: 164 us
  waiting for transfers between devices  62.6 us (38%)
  Pallas kernels  47.6 us (29%)
  starting transfers between devices  44.9 us (27%)
  local copies, waits for them, and re-layouts  6.89 us (4%)
    ppermute x51, waiting for transfers between devices, swap(): return lax.ppermute(value, 'fsdp', [(i, i ^ mask) for i in range(devices)])  62.6 us
    ppermute x51, starting transfers between devices, swap(): return lax.ppermute(value, 'fsdp', [(i, i ^ mask) for i in range(devices)])  44.9 us
    pallas_call x5, Pallas kernels, run(): pl.pallas_call(body, out_shape=[pltpu.HBM(s, d) if i in far_out else jax....  41.5 us
    unnamed x66, local copies, waits for them, and re-layouts  6.89 us
  transfers between devices with their start and end apart: 51, of which 27 were waited for; matrix products, arithmetic and copies ran while one was open for 0% of the time, Pallas kernels for 10%

profile of v2, /device:TPU:0, one launch (start us, length us, event | category | flops | bytes accessed | tf_op | source)
XLA Modules:
  0.0 164.0 jit_solution(1199130311340902418)
XLA Ops:
  0.6 1.7 %shard_map.203 = bf16[24,3200]{1,0:T(8,128)(2,1)} custom-call(bf16[24,2304]{1,0:T(8,128)(2,1)} %in_ref.1, bf16[24,768]{1,0:T(8,128)(2,1)} %out_ref.1, bf16[1,24]{1,0:T(2,128)(2,1)} %bitcast.30, bf16[1,24]{1,0:T(2,128)(2,1)} %bitcast.31, bf16[1,24]{1,0:T(2,128)(2,1)} %bitcast.32, bf16[1,24]{1,0:T(2,128)(2,1)} %bitcast.33, bf16[4,24]{1,0:T(4,128)(2,1)} %bitcast.29), custom_call_target="tpu_custom_call" | custom-call | tf_op jit(solution)/shard_map/pallas_call | solution.py:702
  2.3 4.0 %collective-permute-start = (bf16[1,24,3200]{2,1,0:T(8,128)(2,1)}, bf16[1,24,3200]{2,1,0:T(8,128)(2,1)S(1)}, u32[]{:S(2)}, u32[]{:S(2)}) collective-permute-start(bf16[1,24,3200]{2,1,0:T(8,128)(2,1)} %bitcast.27), channel_id=1, source_target_pairs={{0,16},{1,17},{2,18},{3,19},{4,20},{5,21},{6,22},{7,23},{8,24},{9,... | collective-permute-start | bytes 460808 | tf_op jit(solution)/shard_map/ppermute | solution.py:630
  6.4 7.5 %collective-permute-done = bf16[1,24,3200]{2,1,0:T(8,128)(2,1)S(1)} collective-permute-done((bf16[1,24,3200]{2,1,0:T(8,128)(2,1)}, bf16[1,24,3200]{2,1,0:T(8,128)(2,1)S(1)}, u32[]{:S(2)}, u32[]{:S(2)}) %collective-permute-start) | collective-permute-done | bytes 153632 | tf_op jit(solution)/shard_map/ppermute | solution.py:630
  15.7 1.5 collective-permute-start.4
  17.2 1.5 collective-permute-start.2
  18.7 4.6 %collective-permute-done.1.refs_1_ = bf16[2,24,3200]{2,1,0:T(8,128)(2,1)S(1)} collective-permute-done((bf16[2,24,3200]{2,1,0:T(8,128)(2,1)S(1)}, bf16[2,24,3200]{2,1,0:T(8,128)(2,1)S(1)}, u32[]{:S(2)}, u32[]{:S(2)}) %collective-permute-start.1) | collective-permute-done | bytes 307232 | tf_op jit(solution)/shard_map/ppermute | solution.py:630
  23.4 1.3 collective-permute-start.3
  24.7 1.5 collective-permute-start.6
  26.1 1.2 collective-permute-done.2.refs_2_
  27.9 6.1 %collective-permute-done.3.refs_3_ = bf16[2,24,3200]{2,1,0:T(8,128)(2,1)S(1)} collective-permute-done((bf16[2,24,3200]{2,1,0:T(8,128)(2,1)S(1)}, bf16[2,24,3200]{2,1,0:T(8,128)(2,1)S(1)}, u32[]{:S(2)}, u32[]{:S(2)}) %collective-permute-start.3) | collective-permute-done | bytes 307232 | tf_op jit(solution)/shard_map/ppermute | solution.py:630
  34.9 4.1 %collective-permute-done.6.refs_6_ = bf16[2,24,3200]{2,1,0:T(8,128)(2,1)S(1)} collective-permute-done((bf16[2,24,3200]{2,1,0:T(8,128)(2,1)S(1)}, bf16[2,24,3200]{2,1,0:T(8,128)(2,1)S(1)}, u32[]{:S(2)}, u32[]{:S(2)}) %collective-permute-start.6) | collective-permute-done | bytes 307232 | tf_op jit(solution)/shard_map/ppermute | solution.py:630
  39.7 4.0 %collective-permute-done.7.refs_7_ = bf16[2,24,3200]{2,1,0:T(8,128)(2,1)S(1)} collective-permute-done((bf16[2,24,3200]{2,1,0:T(8,128)(2,1)S(1)}, bf16[2,24,3200]{2,1,0:T(8,128)(2,1)S(1)}, u32[]{:S(2)}, u32[]{:S(2)}) %collective-permute-start.7) | collective-permute-done | bytes 307232 | tf_op jit(solution)/shard_map/ppermute | solution.py:630
  43.8 1.5 collective-permute-done.15.refs_15_
  46.0 1.1 copy-done
  48.8 11.5 %shard_map.204 = (f32[8,768]{1,0:T(8,128)S(1)}, f32[2,4,208]{2,1,0:T(4,128)S(1)}, bf16[16,768]{1,0:T(8,128)(2,1)S(1)}, bf16[416,768]{1,0:T(8,128)(2,1)}, bf16[41...) custom-call(s32[2]{0:T(128)S(1)} %copy-done.10, ...), custom_call_target="tpu_custom_call" | custom-call | tf_op jit(solution)/shard_map/pallas_call | solution.py:53
  60.3 2.4 %collective-permute-start.18 = (bf16[1,16,768]{2,1,0:T(8,128)(2,1)S(1)}, bf16[1,16,768]{2,1,0:T(8,128)(2,1)S(1)}, u32[]{:S(2)}, u32[]{:S(2)}) collective-permute-start(bf16[1,16,768]{2,1,0:T(8,128)(2,1)S(1)} %bitcast.23), channel_id=1, source_target_pairs={{0,24},{1,25},{2,26},{3,27},{4,28},{5,29},{6,30},{7,31},{8,16},{9,... | collective-permute-start | bytes 73736 | tf_op jit(solution)/shard_map/ppermute | solution.py:630
  62.8 2.0 %collective-permute-start.16 = (bf16[1,16,768]{2,1,0:T(8,128)(2,1)S(1)}, bf16[1,16,768]{2,1,0:T(8,128)(2,1)S(1)}, u32[]{:S(2)}, u32[]{:S(2)}) collective-permute-start(bf16[1,16,768]{2,1,0:T(8,128)(2,1)S(1)} %bitcast.25), channel_id=1, source_target_pairs={{0,8},{1,9},{2,10},{3,11},{4,12},{5,13},{6,14},{7,15},{8,0},{9,1},... | collective-permute-start | bytes 73736 | tf_op jit(solution)/shard_map/ppermute | solution.py:630
  64.8 1.2 collective-permute-done.18.refs_3_
  66.0 1.7 %collective-permute-done.17.refs_2_ = bf16[1,16,768]{2,1,0:T(8,128)(2,1)S(1)} collective-permute-done((bf16[1,16,768]{2,1,0:T(8,128)(2,1)S(1)}, bf16[1,16,768]{2,1,0:T(8,128)(2,1)S(1)}, u32[]{:S(2)}, u32[]{:S(2)}) %collective-permute-start.17) | collective-permute-done | bytes 24608 | tf_op jit(solution)/shard_map/ppermute | solution.py:630
  68.9 1.4 shard_map.205.refs_0_
  70.3 2.2 %collective-permute-start.21 = (bf16[4,16,768]{2,1,0:T(8,128)(2,1)}, bf16[4,16,768]{2,1,0:T(8,128)(2,1)S(1)}, u32[]{:S(2)}, u32[]{:S(2)}) collective-permute-start(bf16[4,16,768]{2,1,0:T(8,128)(2,1)} %shard_map.205.refs_0_), channel_id=1, source_target_pairs={{0,6},{1,7},{2,4},{3,5},{4,2},{5,3},{6,0},{7,1},{8,14},{9,15},{10,... | collective-permute-start | bytes 294920 | tf_op jit(solution)/shard_map/ppermute | solution.py:630
  73.8 3.0 %collective-permute-done.21.refs_3_ = bf16[4,16,768]{2,1,0:T(8,128)(2,1)S(1)} collective-permute-done((bf16[4,16,768]{2,1,0:T(8,128)(2,1)}, bf16[4,16,768]{2,1,0:T(8,128)(2,1)S(1)}, u32[]{:S(2)}, u32[]{:S(2)}) %collective-permute-start.21) | collective-permute-done | bytes 98336 | tf_op jit(solution)/shard_map/ppermute | solution.py:630
  80.3 2.6 %shard_map.206 = (bf16[16,16,768]{2,1,0:T(8,128)(2,1)S(1)}, bf16[16,16,768]{2,1,0:T(8,128)(2,1)S(1)}, bf16[256,768]{1,0:T(8,128)(2,1)S(1)}, bf16[256,768]{1,0:T(...) custom-call(s32[2]{0:T(128)S(1)} %copy-done.11, bf16[4,16,768]{2,1,0:T(8,128)(2,1)S(1)} %copy-done.6, ...), custom_call_target="tpu_custom_call" | custom-call | tf_op jit(solution)/shard_map/pallas_call | solution.py:53
  83.1 1.6 collective-permute-done.26.refs_1_
  86.8 1.7 %collective-permute-start.29 = (bf16[4,16,768]{2,1,0:T(8,128)(2,1)S(1)}, bf16[4,16,768]{2,1,0:T(8,128)(2,1)S(1)}, u32[]{:S(2)}, u32[]{:S(2)}) collective-permute-start(bf16[4,16,768]{2,1,0:T(8,128)(2,1)S(1)} %get-tuple-element.89), channel_id=1, source_target_pairs={{0,6},{1,7},{2,4},{3,5},{4,2},{5,3},{6,0},{7,1},{8,14},{9,15},{10,... | collective-permute-start | bytes 294920 | tf_op jit(solution)/shard_map/ppermute | solution.py:630
  88.4 1.6 collective-permute-done.27.refs_1_
  91.0 1.6 collective-permute-done.29.refs_3_
  93.1 1.6 collective-permute-start.31
  94.6 2.5 %collective-permute-start.32 = (bf16[1,16,768]{2,1,0:T(8,128)(2,1)S(1)}, bf16[1,16,768]{2,1,0:T(8,128)(2,1)S(1)}, u32[]{:S(2)}, u32[]{:S(2)}) collective-permute-start(bf16[1,16,768]{2,1,0:T(8,128)(2,1)S(1)} %get-tuple-element.100), channel_id=1, source_target_pairs={{0,24},{1,25},{2,26},{3,27},{4,28},{5,29},{6,30},{7,31},{8,16},{9,... | collective-permute-start | bytes 73736 | tf_op jit(solution)/shard_map/ppermute | solution.py:630
  97.1 2.5 %shard_map.209 = (f32[4,96,768]{2,1,0:T(8,128)}, f32[4,96,768]{2,1,0:T(8,128)}) custom-call(s32[2]{0:T(128)S(1)} %copy-done.11, bf16[256,768]{1,0:T(8,128)(2,1)S(1)} %get-tuple-element.91.s_ref, bf16[256,768]{1,0:T(8,128)(2,1)S(1)} %get-tuple-element.92.g_ref, bf16[256,512]{1,0:T(8,128)(2,1)S(1)} %get-tuple-element.93.act_ref, ...), custom_call_target="tpu_custom_call" | custom-call | flops 2000000000 | tf_op jit(solution)/shard_map/pallas_call | solution.py:53
  100.3 12.7 %shard_map.210 = (bf16[416,768]{1,0:T(8,128)(2,1)}, f32[416,768]{1,0:T(8,128)S(1)}, bf16[416,768]{1,0:T(8,128)(2,1)S(1)}, bf16[416,1152]{1,0:T(8,128)(2,1)S(1)},...) custom-call(s32[2]{0:T(128)S(1)} %copy-done.11, ...), custom_call_target="tpu_custom_call" | custom-call | tf_op jit(solution)/shard_map/pallas_call | solution.py:53
  113.1 12.3 %shard_map.211 = (f32[416,768]{1,0:T(8,128)}, bf16[16,24,1280]{2,1,0:T(8,128)(2,1)S(1)}, bf16[16,24,1280]{2,1,0:T(8,128)(2,1)S(1)}) custom-call(s32[2]{0:T(128)S(1)} %copy-done.11, bf16[416,768]{1,0:T(8,128)(2,1)S(1)} %bitcast.21, f32[8,768]{1,0:T(8,128)S(1)} %get-tuple-element.81.par_ref, bf16[416,768]{1,0:T(8,128)(2,1)S(1)} %get-tuple-element.109.gm_ref, ...), custom_call_target="tpu_custom_call" | custom-call | flops 8000000000 | tf_op jit(solution)/shard_map/pallas_call | solution.py:53
  127.1 1.1 collective-permute-start.36
  128.2 1.2 collective-permute-start.39
  129.4 4.3 %collective-permute-done.35.refs_1_ = bf16[2,24,1920]{2,1,0:T(8,128)(2,1)S(1)} collective-permute-done((bf16[2,24,1920]{2,1,0:T(8,128)(2,1)S(1)}, bf16[2,24,1920]{2,1,0:T(8,128)(2,1)S(1)}, u32[]{:S(2)}, u32[]{:S(2)}) %collective-permute-start.35) | collective-permute-done | bytes 184352 | tf_op jit(solution)/shard_map/ppermute | solution.py:630
  133.9 1.2 collective-permute-start.38
  137.1 1.1 collective-permute-start.34
  138.2 2.0 %collective-permute-done.44.refs_1_ = bf16[2,24,1280]{2,1,0:T(8,128)(2,1)S(1)} collective-permute-done((bf16[2,24,1280]{2,1,0:T(8,128)(2,1)S(1)}, bf16[2,24,1280]{2,1,0:T(8,128)(2,1)S(1)}, u32[]{:S(2)}, u32[]{:S(2)}) %collective-permute-start.44) | collective-permute-done | bytes 122912 | tf_op jit(solution)/shard_map/ppermute | solution.py:630
  141.1 2.9 %collective-permute-done.45.refs_3_ = bf16[2,24,1280]{2,1,0:T(8,128)(2,1)S(1)} collective-permute-done((bf16[2,24,1280]{2,1,0:T(8,128)(2,1)S(1)}, bf16[2,24,1280]{2,1,0:T(8,128)(2,1)S(1)}, u32[]{:S(2)}, u32[]{:S(2)}) %collective-permute-start.45) | collective-permute-done | bytes 122912 | tf_op jit(solution)/shard_map/ppermute | solution.py:630
  144.1 1.3 collective-permute-start.47
  147.4 2.2 %collective-permute-done.47.refs_1_ = bf16[2,24,1280]{2,1,0:T(8,128)(2,1)S(1)} collective-permute-done((bf16[2,24,1280]{2,1,0:T(8,128)(2,1)S(1)}, bf16[2,24,1280]{2,1,0:T(8,128)(2,1)S(1)}, u32[]{:S(2)}, u32[]{:S(2)}) %collective-permute-start.47) | collective-permute-done | bytes 122912 | tf_op jit(solution)/shard_map/ppermute | solution.py:630
  149.6 1.1 collective-permute-start.46
  150.9 1.1 collective-permute-done.37.refs_2_
  152.0 2.1 %collective-permute-done.40.refs_3_ = bf16[2,24,1920]{2,1,0:T(8,128)(2,1)S(1)} collective-permute-done((bf16[2,24,1920]{2,1,0:T(8,128)(2,1)S(1)}, bf16[2,24,1920]{2,1,0:T(8,128)(2,1)S(1)}, u32[]{:S(2)}, u32[]{:S(2)}) %collective-permute-start.40) | collective-permute-done | bytes 184352 | tf_op jit(solution)/shard_map/ppermute | solution.py:630
  154.2 1.3 collective-permute-start.41
  156.5 1.4 collective-permute-start.50
  157.9 3.7 %collective-permute-done.50.b1 = bf16[1,24,1280]{2,1,0:T(8,128)(2,1)S(1)} collective-permute-done((bf16[1,24,1280]{2,1,0:T(8,128)(2,1)S(1)}, bf16[1,24,1280]{2,1,0:T(8,128)(2,1)S(1)}, u32[]{:S(2)}, u32[]{:S(2)}) %collective-permute-start.50) | collective-permute-done | bytes 61472 | tf_op jit(solution)/shard_map/ppermute | solution.py:630
  162.3 1.8 %shard_map.220 = (f32[24,768]{1,0:T(8,128)}, f32[24,2304]{1,0:T(8,128)}, f32[1,24]{1,0:T(1,128)}, f32[1,24]{1,0:T(1,128)}, f32[1,24]{1,0:T(1,128)}, /*index=5*/f32[1,24]{1,0:T(1,128)}, f32[4,24]{1,0:T(4,128)}) custom-call(f32[1,24,1920]{2,1,0:T(8,128)} %copy-done.7, bf16[1,24,1920]{2,1,0:T(8,128)(2,1)} %copy-done.28, f32[1,24,1280]{2,1,0:T(8,128)} %copy-done.8, ...), custom_call_target="tpu_custom_call" | custom-call | tf_op jit(solution)/shard_map/pallas_call | solution.py:834
  (139 shorter events, 25.4 us)
Async XLA Ops:
  2.3 11.5 %collective-permute-start = (bf16[1,24,3200]{2,1,0:T(8,128)(2,1)}, bf16[1,24,3200]{2,1,0:T(8,128)(2,1)S(1)}, u32[]{:S(2)}, u32[]{:S(2)}) collective-permute-start(bf16[1,24,3200]{2,1,0:T(8,128)(2,1)} %bitcast.27), channel_id=1, source_target_pairs={{0,16},{1,17},{2,18},{3,19},{4,20},{5,21},{6,22},{7,23},{8,24},{9,... | collective-permute-start | bytes 460808 | tf_op jit(solution)/shard_map/ppermute | solution.py:630
  14.8 8.5 %collective-permute-start.1 = (bf16[2,24,3200]{2,1,0:T(8,128)(2,1)S(1)}, bf16[2,24,3200]{2,1,0:T(8,128)(2,1)S(1)}, u32[]{:S(2)}, u32[]{:S(2)}) collective-permute-start(bf16[2,24,3200]{2,1,0:T(8,128)(2,1)S(1)} %pad_maximum_fusion.refs_0_), channel_id=1, source_target_pairs={{0,8},{1,9},{2,10},{3,11},{4,12},{5,13},{6,14},{7,15},{8,0},{9,1},... | collective-permute-start | bytes 921608 | tf_op jit(solution)/shard_map/ppermute | solution.py:630
  15.7 9.0 %collective-permute-start.4 = (bf16[2,24,3200]{2,1,0:T(8,128)(2,1)S(1)}, bf16[2,24,3200]{2,1,0:T(8,128)(2,1)S(1)}, u32[]{:S(2)}, u32[]{:S(2)}) collective-permute-start(bf16[2,24,3200]{2,1,0:T(8,128)(2,1)S(1)} %pad_maximum_fusion.refs_0_), channel_id=1, source_target_pairs={{0,4},{1,5},{2,6},{3,7},{4,0},{5,1},{6,2},{7,3},{8,12},{9,13},{10,... | collective-permute-start | bytes 921608 | tf_op jit(solution)/shard_map/ppermute | solution.py:630
  17.2 10.1 %collective-permute-start.2 = (bf16[2,24,3200]{2,1,0:T(8,128)(2,1)S(1)}, bf16[2,24,3200]{2,1,0:T(8,128)(2,1)S(1)}, u32[]{:S(2)}, u32[]{:S(2)}) collective-permute-start(bf16[2,24,3200]{2,1,0:T(8,128)(2,1)S(1)} %pad_maximum_fusion.refs_0_), channel_id=1, source_target_pairs={{0,2},{1,3},{2,0},{3,1},{4,6},{5,7},{6,4},{7,5},{8,10},{9,11},{10,... | collective-permute-start | bytes 921608 | tf_op jit(solution)/shard_map/ppermute | solution.py:630
  18.7 8.7 %collective-permute-start.8 = (bf16[2,24,3200]{2,1,0:T(8,128)(2,1)S(1)}, bf16[2,24,3200]{2,1,0:T(8,128)(2,1)S(1)}, u32[]{:S(2)}, u32[]{:S(2)}) collective-permute-start(bf16[2,24,3200]{2,1,0:T(8,128)(2,1)S(1)} %pad_maximum_fusion.refs_0_), channel_id=1, source_target_pairs={{0,1},{1,0},{2,3},{3,2},{4,5},{5,4},{6,7},{7,6},{8,9},{9,8},{10,11... | collective-permute-start | bytes 921608 | tf_op jit(solution)/shard_map/ppermute | solution.py:630
  23.4 10.6 %collective-permute-start.3 = (bf16[2,24,3200]{2,1,0:T(8,128)(2,1)S(1)}, bf16[2,24,3200]{2,1,0:T(8,128)(2,1)S(1)}, u32[]{:S(2)}, u32[]{:S(2)}) collective-permute-start(bf16[2,24,3200]{2,1,0:T(8,128)(2,1)S(1)} %collective-permute-done.1.refs_1_), channel_id=1, source_target_pairs={{0,2},{1,3},{2,0},{3,1},{4,6},{5,7},{6,4},{7,5},{8,10},{9,11},{10,... | collective-permute-start | bytes 921608 | tf_op jit(solution)/shard_map/ppermute | solution.py:630
  24.7 10.2 %collective-permute-start.12 = (bf16[2,24,3200]{2,1,0:T(8,128)(2,1)S(1)}, bf16[2,24,3200]{2,1,0:T(8,128)(2,1)S(1)}, u32[]{:S(2)}, u32[]{:S(2)}) collective-permute-start(bf16[2,24,3200]{2,1,0:T(8,128)(2,1)S(1)} %collective-permute-done.4.refs_4_), channel_id=1, source_target_pairs={{0,1},{1,0},{2,3},{3,2},{4,5},{5,4},{6,7},{7,6},{8,9},{9,8},{10,11... | collective-permute-start | bytes 921608 | tf_op jit(solution)/shard_map/ppermute | solution.py:630
  24.7 14.4 %collective-permute-start.6 = (bf16[2,24,3200]{2,1,0:T(8,128)(2,1)S(1)}, bf16[2,24,3200]{2,1,0:T(8,128)(2,1)S(1)}, u32[]{:S(2)}, u32[]{:S(2)}) collective-permute-start(bf16[2,24,3200]{2,1,0:T(8,128)(2,1)S(1)} %collective-permute-done.4.refs_4_), channel_id=1, source_target_pairs={{0,2},{1,3},{2,0},{3,1},{4,6},{5,7},{6,4},{7,5},{8,10},{9,11},{10,... | collective-permute-start | bytes 921608 | tf_op jit(solution)/shard_map/ppermute | solution.py:630
  27.4 11.7 %collective-permute-start.10 = (bf16[2,24,3200]{2,1,0:T(8,128)(2,1)S(1)}, bf16[2,24,3200]{2,1,0:T(8,128)(2,1)S(1)}, u32[]{:S(2)}, u32[]{:S(2)}) collective-permute-start(bf16[2,24,3200]{2,1,0:T(8,128)(2,1)S(1)} %collective-permute-done.2.refs_2_), channel_id=1, source_target_pairs={{0,1},{1,0},{2,3},{3,2},{4,5},{5,4},{6,7},{7,6},{8,9},{9,8},{10,11... | collective-permute-start | bytes 921608 | tf_op jit(solution)/shard_map/ppermute | solution.py:630
  27.4 12.2 %collective-permute-start.5 = (bf16[2,24,3200]{2,1,0:T(8,128)(2,1)S(1)}, bf16[2,24,3200]{2,1,0:T(8,128)(2,1)S(1)}, u32[]{:S(2)}, u32[]{:S(2)}) collective-permute-start(bf16[2,24,3200]{2,1,0:T(8,128)(2,1)S(1)} %collective-permute-done.1.refs_1_), channel_id=1, source_target_pairs={{0,4},{1,5},{2,6},{3,7},{4,0},{5,1},{6,2},{7,3},{8,12},{9,13},{10,... | collective-permute-start | bytes 921608 | tf_op jit(solution)/shard_map/ppermute | solution.py:630
  34.0 9.7 %collective-permute-start.7 = (bf16[2,24,3200]{2,1,0:T(8,128)(2,1)S(1)}, bf16[2,24,3200]{2,1,0:T(8,128)(2,1)S(1)}, u32[]{:S(2)}, u32[]{:S(2)}) collective-permute-start(bf16[2,24,3200]{2,1,0:T(8,128)(2,1)S(1)} %collective-permute-done.3.refs_3_), channel_id=1, source_target_pairs={{0,4},{1,5},{2,6},{3,7},{4,0},{5,1},{6,2},{7,3},{8,12},{9,13},{10,... | collective-permute-start | bytes 921608 | tf_op jit(solution)/shard_map/ppermute | solution.py:630
  34.9 8.8 %collective-permute-start.9 = (bf16[2,24,3200]{2,1,0:T(8,128)(2,1)S(1)}, bf16[2,24,3200]{2,1,0:T(8,128)(2,1)S(1)}, u32[]{:S(2)}, u32[]{:S(2)}) collective-permute-start(bf16[2,24,3200]{2,1,0:T(8,128)(2,1)S(1)} %collective-permute-done.1.refs_1_), channel_id=1, source_target_pairs={{0,1},{1,0},{2,3},{3,2},{4,5},{5,4},{6,7},{7,6},{8,9},{9,8},{10,11... | collective-permute-start | bytes 921608 | tf_op jit(solution)/shard_map/ppermute | solution.py:630
  39.0 4.7 %collective-permute-start.11 = (bf16[2,24,3200]{2,1,0:T(8,128)(2,1)S(1)}, bf16[2,24,3200]{2,1,0:T(8,128)(2,1)S(1)}, u32[]{:S(2)}, u32[]{:S(2)}) collective-permute-start(bf16[2,24,3200]{2,1,0:T(8,128)(2,1)S(1)} %collective-permute-done.3.refs_3_), channel_id=1, source_target_pairs={{0,1},{1,0},{2,3},{3,2},{4,5},{5,4},{6,7},{7,6},{8,9},{9,8},{10,11... | collective-permute-start | bytes 921608 | tf_op jit(solution)/shard_map/ppermute | solution.py:630
  39.1 4.6 %collective-permute-start.14 = (bf16[2,24,3200]{2,1,0:T(8,128)(2,1)S(1)}, bf16[2,24,3200]{2,1,0:T(8,128)(2,1)S(1)}, u32[]{:S(2)}, u32[]{:S(2)}) collective-permute-start(bf16[2,24,3200]{2,1,0:T(8,128)(2,1)S(1)} %collective-permute-done.6.refs_6_), channel_id=1, source_target_pairs={{0,1},{1,0},{2,3},{3,2},{4,5},{5,4},{6,7},{7,6},{8,9},{9,8},{10,11... | collective-permute-start | bytes 921608 | tf_op jit(solution)/shard_map/ppermute | solution.py:630
  39.6 4.2 %collective-permute-start.13 = (bf16[2,24,3200]{2,1,0:T(8,128)(2,1)S(1)}, bf16[2,24,3200]{2,1,0:T(8,128)(2,1)S(1)}, u32[]{:S(2)}, u32[]{:S(2)}) collective-permute-start(bf16[2,24,3200]{2,1,0:T(8,128)(2,1)S(1)} %collective-permute-done.5.refs_5_), channel_id=1, source_target_pairs={{0,1},{1,0},{2,3},{3,2},{4,5},{5,4},{6,7},{7,6},{8,9},{9,8},{10,11... | collective-permute-start | bytes 921608 | tf_op jit(solution)/shard_map/ppermute | solution.py:630
  43.7 1.6 collective-permute-start.15
  60.3 5.7 %collective-permute-start.18 = (bf16[1,16,768]{2,1,0:T(8,128)(2,1)S(1)}, bf16[1,16,768]{2,1,0:T(8,128)(2,1)S(1)}, u32[]{:S(2)}, u32[]{:S(2)}) collective-permute-start(bf16[1,16,768]{2,1,0:T(8,128)(2,1)S(1)} %bitcast.23), channel_id=1, source_target_pairs={{0,24},{1,25},{2,26},{3,27},{4,28},{5,29},{6,30},{7,31},{8,16},{9,... | collective-permute-start | bytes 73736 | tf_op jit(solution)/shard_map/ppermute | solution.py:630
  62.7 5.0 %collective-permute-start.17 = (bf16[1,16,768]{2,1,0:T(8,128)(2,1)S(1)}, bf16[1,16,768]{2,1,0:T(8,128)(2,1)S(1)}, u32[]{:S(2)}, u32[]{:S(2)}) collective-permute-start(bf16[1,16,768]{2,1,0:T(8,128)(2,1)S(1)} %bitcast.24), channel_id=1, source_target_pairs={{0,16},{1,17},{2,18},{3,19},{4,20},{5,21},{6,22},{7,23},{8,24},{9,... | collective-permute-start | bytes 73736 | tf_op jit(solution)/shard_map/ppermute | solution.py:630
  62.8 4.9 %collective-permute-start.16 = (bf16[1,16,768]{2,1,0:T(8,128)(2,1)S(1)}, bf16[1,16,768]{2,1,0:T(8,128)(2,1)S(1)}, u32[]{:S(2)}, u32[]{:S(2)}) collective-permute-start(bf16[1,16,768]{2,1,0:T(8,128)(2,1)S(1)} %bitcast.25), channel_id=1, source_target_pairs={{0,8},{1,9},{2,10},{3,11},{4,12},{5,13},{6,14},{7,15},{8,0},{9,1},... | collective-permute-start | bytes 73736 | tf_op jit(solution)/shard_map/ppermute | solution.py:630
  70.3 6.5 %collective-permute-start.21 = (bf16[4,16,768]{2,1,0:T(8,128)(2,1)}, bf16[4,16,768]{2,1,0:T(8,128)(2,1)S(1)}, u32[]{:S(2)}, u32[]{:S(2)}) collective-permute-start(bf16[4,16,768]{2,1,0:T(8,128)(2,1)} %shard_map.205.refs_0_), channel_id=1, source_target_pairs={{0,6},{1,7},{2,4},{3,5},{4,2},{5,3},{6,0},{7,1},{8,14},{9,15},{10,... | collective-permute-start | bytes 294920 | tf_op jit(solution)/shard_map/ppermute | solution.py:630
  72.5 5.1 %collective-permute-start.20 = (bf16[4,16,768]{2,1,0:T(8,128)(2,1)}, bf16[4,16,768]{2,1,0:T(8,128)(2,1)S(1)}, u32[]{:S(2)}, u32[]{:S(2)}) collective-permute-start(bf16[4,16,768]{2,1,0:T(8,128)(2,1)} %shard_map.205.refs_0_), channel_id=1, source_target_pairs={{0,4},{1,5},{2,6},{3,7},{4,0},{5,1},{6,2},{7,3},{8,12},{9,13},{10,... | collective-permute-start | bytes 294920 | tf_op jit(solution)/shard_map/ppermute | solution.py:630
  73.3 4.8 %collective-permute-start.19 = (bf16[4,16,768]{2,1,0:T(8,128)(2,1)}, bf16[4,16,768]{2,1,0:T(8,128)(2,1)S(1)}, u32[]{:S(2)}, u32[]{:S(2)}) collective-permute-start(bf16[4,16,768]{2,1,0:T(8,128)(2,1)} %shard_map.205.refs_0_), channel_id=1, source_target_pairs={{0,2},{1,3},{2,0},{3,1},{4,6},{5,7},{6,4},{7,5},{8,10},{9,11},{10,... | collective-permute-start | bytes 294920 | tf_op jit(solution)/shard_map/ppermute | solution.py:630
  73.8 4.3 %collective-permute-start.22 = (bf16[4,16,768]{2,1,0:T(8,128)(2,1)}, bf16[4,16,768]{2,1,0:T(8,128)(2,1)S(1)}, u32[]{:S(2)}, u32[]{:S(2)}) collective-permute-start(bf16[4,16,768]{2,1,0:T(8,128)(2,1)} %shard_map.205.refs_0_), channel_id=1, source_target_pairs={{0,1},{1,0},{2,3},{3,2},{4,5},{5,4},{6,7},{7,6},{8,9},{9,8},{10,11... | collective-permute-start | bytes 294920 | tf_op jit(solution)/shard_map/ppermute | solution.py:630
  82.9 1.8 %collective-permute-start.26 = (bf16[16,16,768]{2,1,0:T(8,128)(2,1)S(1)}, bf16[16,16,768]{2,1,0:T(8,128)(2,1)S(1)}, u32[]{:S(2)}, u32[]{:S(2)}) collective-permute-start(bf16[16,16,768]{2,1,0:T(8,128)(2,1)S(1)} %get-tuple-element.85), channel_id=1, source_target_pairs={{0,1},{1,0},{2,3},{3,2},{4,5},{5,4},{6,7},{7,6},{8,9},{9,8},{10,11... | collective-permute-start | bytes 1179656 | tf_op jit(solution)/shard_map/ppermute | solution.py:630
  84.9 5.1 %collective-permute-start.27 = (bf16[4,16,768]{2,1,0:T(8,128)(2,1)S(1)}, bf16[4,16,768]{2,1,0:T(8,128)(2,1)S(1)}, u32[]{:S(2)}, u32[]{:S(2)}) collective-permute-start(bf16[4,16,768]{2,1,0:T(8,128)(2,1)S(1)} %get-tuple-element.87), channel_id=1, source_target_pairs={{0,2},{1,3},{2,0},{3,1},{4,6},{5,7},{6,4},{7,5},{8,10},{9,11},{10,... | collective-permute-start | bytes 294920 | tf_op jit(solution)/shard_map/ppermute | solution.py:630
  85.7 5.3 %collective-permute-start.28 = (bf16[4,16,768]{2,1,0:T(8,128)(2,1)S(1)}, bf16[4,16,768]{2,1,0:T(8,128)(2,1)S(1)}, u32[]{:S(2)}, u32[]{:S(2)}) collective-permute-start(bf16[4,16,768]{2,1,0:T(8,128)(2,1)S(1)} %get-tuple-element.88), channel_id=1, source_target_pairs={{0,4},{1,5},{2,6},{3,7},{4,0},{5,1},{6,2},{7,3},{8,12},{9,13},{10,... | collective-permute-start | bytes 294920 | tf_op jit(solution)/shard_map/ppermute | solution.py:630
  86.8 5.8 %collective-permute-start.29 = (bf16[4,16,768]{2,1,0:T(8,128)(2,1)S(1)}, bf16[4,16,768]{2,1,0:T(8,128)(2,1)S(1)}, u32[]{:S(2)}, u32[]{:S(2)}) collective-permute-start(bf16[4,16,768]{2,1,0:T(8,128)(2,1)S(1)} %get-tuple-element.89), channel_id=1, source_target_pairs={{0,6},{1,7},{2,4},{3,5},{4,2},{5,3},{6,0},{7,1},{8,14},{9,15},{10,... | collective-permute-start | bytes 294920 | tf_op jit(solution)/shard_map/ppermute | solution.py:630
  92.7 7.0 %collective-permute-start.30 = (bf16[1,16,768]{2,1,0:T(8,128)(2,1)S(1)}, bf16[1,16,768]{2,1,0:T(8,128)(2,1)S(1)}, u32[]{:S(2)}, u32[]{:S(2)}) collective-permute-start(bf16[1,16,768]{2,1,0:T(8,128)(2,1)S(1)} %get-tuple-element.98), channel_id=1, source_target_pairs={{0,8},{1,9},{2,10},{3,11},{4,12},{5,13},{6,14},{7,15},{8,0},{9,1},... | collective-permute-start | bytes 73736 | tf_op jit(solution)/shard_map/ppermute | solution.py:630
  93.1 6.6 %collective-permute-start.31 = (bf16[1,16,768]{2,1,0:T(8,128)(2,1)S(1)}, bf16[1,16,768]{2,1,0:T(8,128)(2,1)S(1)}, u32[]{:S(2)}, u32[]{:S(2)}) collective-permute-start(bf16[1,16,768]{2,1,0:T(8,128)(2,1)S(1)} %get-tuple-element.99), channel_id=1, source_target_pairs={{0,16},{1,17},{2,18},{3,19},{4,20},{5,21},{6,22},{7,23},{8,24},{9,... | collective-permute-start | bytes 73736 | tf_op jit(solution)/shard_map/ppermute | solution.py:630
  94.6 5.6 %collective-permute-start.32 = (bf16[1,16,768]{2,1,0:T(8,128)(2,1)S(1)}, bf16[1,16,768]{2,1,0:T(8,128)(2,1)S(1)}, u32[]{:S(2)}, u32[]{:S(2)}) collective-permute-start(bf16[1,16,768]{2,1,0:T(8,128)(2,1)S(1)} %get-tuple-element.100), channel_id=1, source_target_pairs={{0,24},{1,25},{2,26},{3,27},{4,28},{5,29},{6,30},{7,31},{8,16},{9,... | collective-permute-start | bytes 73736 | tf_op jit(solution)/shard_map/ppermute | solution.py:630
  113.0 12.9 %collective-permute-start.33 = (bf16[16,24,1920]{2,1,0:T(8,128)(2,1)S(1)}, bf16[16,24,1920]{2,1,0:T(8,128)(2,1)S(1)}, u32[]{:S(2)}, u32[]{:S(2)}) collective-permute-start(bf16[16,24,1920]{2,1,0:T(8,128)(2,1)S(1)} %get-tuple-element.115), channel_id=1, source_target_pairs={{0,1},{1,0},{2,3},{3,2},{4,5},{5,4},{6,7},{7,6},{8,9},{9,8},{10,11... | collective-permute-start | bytes 4423688 | tf_op jit(solution)/shard_map/ppermute | solution.py:630
  125.4 9.7 %collective-permute-start.42 = (bf16[16,24,1280]{2,1,0:T(8,128)(2,1)S(1)}, bf16[16,24,1280]{2,1,0:T(8,128)(2,1)S(1)}, u32[]{:S(2)}, u32[]{:S(2)}) collective-permute-start(bf16[16,24,1280]{2,1,0:T(8,128)(2,1)S(1)} %get-tuple-element.129), channel_id=1, source_target_pairs={{0,1},{1,0},{2,3},{3,2},{4,5},{5,4},{6,7},{7,6},{8,9},{9,8},{10,11... | collective-permute-start | bytes 2949128 | tf_op jit(solution)/shard_map/ppermute | solution.py:630
  126.2 7.6 %collective-permute-start.35 = (bf16[2,24,1920]{2,1,0:T(8,128)(2,1)S(1)}, bf16[2,24,1920]{2,1,0:T(8,128)(2,1)S(1)}, u32[]{:S(2)}, u32[]{:S(2)}) collective-permute-start(bf16[2,24,1920]{2,1,0:T(8,128)(2,1)S(1)} %get-tuple-element.119), channel_id=1, source_target_pairs={{0,4},{1,5},{2,6},{3,7},{4,0},{5,1},{6,2},{7,3},{8,12},{9,13},{10,... | collective-permute-start | bytes 552968 | tf_op jit(solution)/shard_map/ppermute | solution.py:630
  127.1 6.7 %collective-permute-start.36 = (bf16[2,24,1920]{2,1,0:T(8,128)(2,1)S(1)}, bf16[2,24,1920]{2,1,0:T(8,128)(2,1)S(1)}, u32[]{:S(2)}, u32[]{:S(2)}) collective-permute-start(bf16[2,24,1920]{2,1,0:T(8,128)(2,1)S(1)} %get-tuple-element.121), channel_id=1, source_target_pairs={{0,2},{1,3},{2,0},{3,1},{4,6},{5,7},{6,4},{7,5},{8,10},{9,11},{10,... | collective-permute-start | bytes 552968 | tf_op jit(solution)/shard_map/ppermute | solution.py:630
  128.2 17.2 %collective-permute-start.39 = (bf16[2,24,1920]{2,1,0:T(8,128)(2,1)S(1)}, bf16[2,24,1920]{2,1,0:T(8,128)(2,1)S(1)}, u32[]{:S(2)}, u32[]{:S(2)}) collective-permute-start(bf16[2,24,1920]{2,1,0:T(8,128)(2,1)S(1)} %get-tuple-element.125), channel_id=1, source_target_pairs={{0,4},{1,5},{2,6},{3,7},{4,0},{5,1},{6,2},{7,3},{8,12},{9,13},{10,... | collective-permute-start | bytes 552968 | tf_op jit(solution)/shard_map/ppermute | solution.py:630
  133.9 12.4 %collective-permute-start.38 = (bf16[2,24,1920]{2,1,0:T(8,128)(2,1)S(1)}, bf16[2,24,1920]{2,1,0:T(8,128)(2,1)S(1)}, u32[]{:S(2)}, u32[]{:S(2)}) collective-permute-start(bf16[2,24,1920]{2,1,0:T(8,128)(2,1)S(1)} %get-tuple-element.124), channel_id=1, source_target_pairs={{0,2},{1,3},{2,0},{3,1},{4,6},{5,7},{6,4},{7,5},{8,10},{9,11},{10,... | collective-permute-start | bytes 552968 | tf_op jit(solution)/shard_map/ppermute | solution.py:630
  135.3 4.9 %collective-permute-start.44 = (bf16[2,24,1280]{2,1,0:T(8,128)(2,1)S(1)}, bf16[2,24,1280]{2,1,0:T(8,128)(2,1)S(1)}, u32[]{:S(2)}, u32[]{:S(2)}) collective-permute-start(bf16[2,24,1280]{2,1,0:T(8,128)(2,1)S(1)} %get-tuple-element.133), channel_id=1, source_target_pairs={{0,4},{1,5},{2,6},{3,7},{4,0},{5,1},{6,2},{7,3},{8,12},{9,13},{10,... | collective-permute-start | bytes 368648 | tf_op jit(solution)/shard_map/ppermute | solution.py:630
  136.2 7.8 %collective-permute-start.45 = (bf16[2,24,1280]{2,1,0:T(8,128)(2,1)S(1)}, bf16[2,24,1280]{2,1,0:T(8,128)(2,1)S(1)}, u32[]{:S(2)}, u32[]{:S(2)}) collective-permute-start(bf16[2,24,1280]{2,1,0:T(8,128)(2,1)S(1)} %get-tuple-element.135), channel_id=1, source_target_pairs={{0,2},{1,3},{2,0},{3,1},{4,6},{5,7},{6,4},{7,5},{8,10},{9,11},{10,... | collective-permute-start | bytes 368648 | tf_op jit(solution)/shard_map/ppermute | solution.py:630
  137.1 13.7 %collective-permute-start.34 = (bf16[2,24,1920]{2,1,0:T(8,128)(2,1)S(1)}, bf16[2,24,1920]{2,1,0:T(8,128)(2,1)S(1)}, u32[]{:S(2)}, u32[]{:S(2)}) collective-permute-start(bf16[2,24,1920]{2,1,0:T(8,128)(2,1)S(1)} %get-tuple-element.117), channel_id=1, source_target_pairs={{0,2},{1,3},{2,0},{3,1},{4,6},{5,7},{6,4},{7,5},{8,10},{9,11},{10,... | collective-permute-start | bytes 552968 | tf_op jit(solution)/shard_map/ppermute | solution.py:630
  140.3 6.3 %collective-permute-start.48 = (bf16[2,24,1280]{2,1,0:T(8,128)(2,1)S(1)}, bf16[2,24,1280]{2,1,0:T(8,128)(2,1)S(1)}, u32[]{:S(2)}, u32[]{:S(2)}) collective-permute-start(bf16[2,24,1280]{2,1,0:T(8,128)(2,1)S(1)} %get-tuple-element.139), channel_id=1, source_target_pairs={{0,4},{1,5},{2,6},{3,7},{4,0},{5,1},{6,2},{7,3},{8,12},{9,13},{10,... | collective-permute-start | bytes 368648 | tf_op jit(solution)/shard_map/ppermute | solution.py:630
  144.1 5.5 %collective-permute-start.47 = (bf16[2,24,1280]{2,1,0:T(8,128)(2,1)S(1)}, bf16[2,24,1280]{2,1,0:T(8,128)(2,1)S(1)}, u32[]{:S(2)}, u32[]{:S(2)}) collective-permute-start(bf16[2,24,1280]{2,1,0:T(8,128)(2,1)S(1)} %get-tuple-element.138), channel_id=1, source_target_pairs={{0,2},{1,3},{2,0},{3,1},{4,6},{5,7},{6,4},{7,5},{8,10},{9,11},{10,... | collective-permute-start | bytes 368648 | tf_op jit(solution)/shard_map/ppermute | solution.py:630
  145.4 6.5 %collective-permute-start.37 = (bf16[2,24,1920]{2,1,0:T(8,128)(2,1)S(1)}, bf16[2,24,1920]{2,1,0:T(8,128)(2,1)S(1)}, u32[]{:S(2)}, u32[]{:S(2)}) collective-permute-start(bf16[2,24,1920]{2,1,0:T(8,128)(2,1)S(1)} %get-tuple-element.122), channel_id=1, source_target_pairs={{0,4},{1,5},{2,6},{3,7},{4,0},{5,1},{6,2},{7,3},{8,12},{9,13},{10,... | collective-permute-start | bytes 552968 | tf_op jit(solution)/shard_map/ppermute | solution.py:630
  146.3 7.7 %collective-permute-start.40 = (bf16[2,24,1920]{2,1,0:T(8,128)(2,1)S(1)}, bf16[2,24,1920]{2,1,0:T(8,128)(2,1)S(1)}, u32[]{:S(2)}, u32[]{:S(2)}) collective-permute-start(bf16[2,24,1920]{2,1,0:T(8,128)(2,1)S(1)} %shard_map.214), channel_id=1, source_target_pairs={{0,8},{1,9},{2,10},{3,11},{4,12},{5,13},{6,14},{7,15},{8,0},{9,1},... | collective-permute-start | bytes 552968 | tf_op jit(solution)/shard_map/ppermute | solution.py:630
  146.5 9.0 %collective-permute-start.43 = (bf16[2,24,1280]{2,1,0:T(8,128)(2,1)S(1)}, bf16[2,24,1280]{2,1,0:T(8,128)(2,1)S(1)}, u32[]{:S(2)}, u32[]{:S(2)}) collective-permute-start(bf16[2,24,1280]{2,1,0:T(8,128)(2,1)S(1)} %get-tuple-element.131), channel_id=1, source_target_pairs={{0,2},{1,3},{2,0},{3,1},{4,6},{5,7},{6,4},{7,5},{8,10},{9,11},{10,... | collective-permute-start | bytes 368648 | tf_op jit(solution)/shard_map/ppermute | solution.py:630
  149.6 5.9 %collective-permute-start.46 = (bf16[2,24,1280]{2,1,0:T(8,128)(2,1)S(1)}, bf16[2,24,1280]{2,1,0:T(8,128)(2,1)S(1)}, u32[]{:S(2)}, u32[]{:S(2)}) collective-permute-start(bf16[2,24,1280]{2,1,0:T(8,128)(2,1)S(1)} %get-tuple-element.136), channel_id=1, source_target_pairs={{0,4},{1,5},{2,6},{3,7},{4,0},{5,1},{6,2},{7,3},{8,12},{9,13},{10,... | collective-permute-start | bytes 368648 | tf_op jit(solution)/shard_map/ppermute | solution.py:630
  150.8 4.9 %collective-permute-start.49 = (bf16[2,24,1280]{2,1,0:T(8,128)(2,1)S(1)}, bf16[2,24,1280]{2,1,0:T(8,128)(2,1)S(1)}, u32[]{:S(2)}, u32[]{:S(2)}) collective-permute-start(bf16[2,24,1280]{2,1,0:T(8,128)(2,1)S(1)} %shard_map.218), channel_id=1, source_target_pairs={{0,8},{1,9},{2,10},{3,11},{4,12},{5,13},{6,14},{7,15},{8,0},{9,1},... | collective-permute-start | bytes 368648 | tf_op jit(solution)/shard_map/ppermute | solution.py:630
  154.2 7.4 %collective-permute-start.41 = (bf16[1,24,1920]{2,1,0:T(8,128)(2,1)S(1)}, bf16[1,24,1920]{2,1,0:T(8,128)(2,1)S(1)}, u32[]{:S(2)}, u32[]{:S(2)}) collective-permute-start(bf16[1,24,1920]{2,1,0:T(8,128)(2,1)S(1)} %get-tuple-element.127), channel_id=1, source_target_pairs={{0,16},{1,17},{2,18},{3,19},{4,20},{5,21},{6,22},{7,23},{8,24},{9,... | collective-permute-start | bytes 276488 | tf_op jit(solution)/shard_map/ppermute | solution.py:630
  156.5 5.1 %collective-permute-start.50 = (bf16[1,24,1280]{2,1,0:T(8,128)(2,1)S(1)}, bf16[1,24,1280]{2,1,0:T(8,128)(2,1)S(1)}, u32[]{:S(2)}, u32[]{:S(2)}) collective-permute-start(bf16[1,24,1280]{2,1,0:T(8,128)(2,1)S(1)} %get-tuple-element.141), channel_id=1, source_target_pairs={{0,16},{1,17},{2,18},{3,19},{4,20},{5,21},{6,22},{7,23},{8,24},{9,... | collective-permute-start | bytes 184328 | tf_op jit(solution)/shard_map/ppermute | solution.py:630
  (36 other events, 287.3 us)

commit v3 on v2

--- a/solution.py
+++ b/solution.py
@@ -117,21 +117,24 @@
     return body
 
 
-def block_chip(f, chips):
+def gathered_chip(f, chips):
+    return (lax.axis_index("fsdp") // 2) ^ (f // 4 + (f % 4) * (chips // 4))
+
+
+def scattered_chip(f, chips):
     k = f % 4
     return (lax.axis_index("fsdp") // 2) ^ (f // 4 + (k % 2) * (chips // 2) + (k // 2) * (chips // 4))
 
 
-def assemble(meta, images, part_rows, own_ref, oth_ref, w_ref):
+def assemble(first, share, chips, part_rows, own_ref, oth_ref, w_ref):
     columns = w_ref.shape[1]
     for own_first in (True, False):
 
         @pl.when(lax.axis_index("fsdp") % 2 == (0 if own_first else 1))
         def _():
-            @pl.loop(0, own_ref.shape[0], unroll=2)
-            def _(f):
-                at = rows_at(block_chip(f, own_ref.shape[0]), 2 * part_rows)
-                low_ref, high_ref = (own_ref, oth_ref) if own_first else (oth_ref, own_ref)
+            low_ref, high_ref = (own_ref, oth_ref) if own_first else (oth_ref, own_ref)
+            for f in range(first, first + share):
+                at = rows_at(gathered_chip(f, chips), 2 * part_rows)
                 for c0 in range(0, columns, 640):
                     c1 = min(columns, c0 + 640)
                     both = [low_ref[f, :, c0:c1].astype(f32), high_ref[f, :, c0:c1].astype(f32)]
@@ -145,7 +148,7 @@
         def _():
             @pl.loop(0, chips, unroll=4)
             def _(f):
-                at = rows_at(block_chip(f, chips), 2 * part_rows)
+                at = rows_at(scattered_chip(f, chips), 2 * part_rows)
                 for c0 in range(0, count, 384):
                     c1 = min(count, c0 + 384)
                     both = tile[at, c0:c1]
@@ -154,36 +157,117 @@
                     other_ref[f, :, first + c0 : first + c1] = high if own_first else low
 
 
+def column_sums(ref):
+    total = jnp.zeros((CHUNK, ref.shape[1]), f32)
+    for i in range(ref.shape[0] // CHUNK):
+        total = total + ref[i * CHUNK : (i + 1) * CHUNK].astype(f32)
+    return jnp.sum(total, axis=0, keepdims=True)
+
+
+def cut_scaled(chips, part_rows, tile, sums, w_ref, col_ref, small_ref, outs, first):
+    count = tile.shape[1]
+    rows = 2 * part_rows if len(outs) == 2 else 48
+    lane = lax.broadcasted_iota(jnp.int32, (1, LANES), 1)
+
+    def step(at, write):
+        gain = col_ref[at, 0:1].astype(f32)
+        shift = col_ref[at, 1:2].astype(f32)
+        by_gain = jnp.zeros((rows, LANES), f32)
+        by_shift = jnp.zeros((rows, LANES), f32)
+        for c0 in range(0, count, LANES):
+            c1 = c0 + LANES
+            value, weight = tile[at, c0:c1], w_ref[at, c0:c1].astype(f32)
+            by_gain = by_gain + value * weight
+            by_shift = by_shift + sums[:, c0:c1] * weight
+            write(c0, c1, value * gain + shift * sums[:, c0:c1])
+        by_gain = jnp.sum(by_gain, axis=1, keepdims=True)
+        by_shift = jnp.sum(by_shift, axis=1, keepdims=True)
+        small_ref[at] = small_ref[at] + jnp.where(lane == 0, by_gain, jnp.where(lane == 1, by_shift, 0.0))
+
+    if len(outs) == 1:
+
+        @pl.loop(0, tile.shape[0] // rows)
+        def _(i):
+            at = rows_at(i, rows)
+
+            def write(c0, c1, value):
+                outs[0][at, first + c0 : first + c1] = value
+
+            step(at, write)
+
+        return
+    for own_first in (True, False):
+
+        @pl.when(lax.axis_index("fsdp") % 2 == (0 if own_first else 1))
+        def _():
+            low_ref, high_ref = outs if own_first else outs[::-1]
+
+            @pl.loop(0, chips, unroll=2)
+            def _(f):
+                at = rows_at(scattered_chip(f, chips), rows)
+
+                def write(c0, c1, value):
+                    low_ref[f, :, first + c0 : first + c1] = value[:part_rows].astype(bf16)
+                    high_ref[f, :, first + c0 : first + c1] = value[part_rows:].astype(bf16)
+
+                step(at, write)
+
+
+def weight_loads(width, half, w_in, w_ref, col_ref, sems):
+    part = width // 2
+    loads = [
+        pltpu.make_async_copy(
+            w_in.at[:, i * width + half * part : i * width + (half + 1) * part],
+            w_ref.at[:, i * part : (i + 1) * part],
+            sems.at[i],
+        )
+        for i in range(3)
+    ]
+    loads.append(pltpu.make_async_copy(w_in.at[:, 4 * width : 4 * width + LANES], col_ref, sems.at[3]))
+    return loads
+
+
 def forward_kernel(sizes):
     images, rows, width, experts, chips, part_rows, shares = sizes
     total = images * rows
     pairs = HEADS // 2
     pieces = len(shares)
 
-    def body(meta, x_ref, cot_ref, *refs):
+    def body(meta, x_in, cot_in, *refs):
         ins, refs = refs[: 2 * pieces or 1], refs[2 * pieces or 1 :]
-        par_ref, log_ref, slots_ref, n1_out, mixed_out, joint_out, probs_out, res_out, n2_out, *refs = refs
+        par_ref, log_ref, slots_ref, xh_out, mixed_out, joint_out, probs_out, res_out, n2_out, *refs = refs
         if pieces:
             w_out, *refs = refs
-        n1_ref, mixed_ref, joint_ref, probs_ref, res_ref, n2_ref, small, *refs = refs
+        xh_ref, mixed_ref, joint_ref, probs_ref, res_ref, n2_ref, small, x_ref, cot_ref, n1_ref, *refs = refs
+        given = [
+            pltpu.make_async_copy(x_in, x_ref, refs[-1].at[8 + pairs + 2 * pieces]),
+            pltpu.make_async_copy(cot_in, cot_ref, refs[-1].at[9 + pairs + 2 * pieces]),
+        ]
+        for load in given:
+            load.start()
         if pieces:
             w_ref, own_ref, oth_ref, sems = refs
-            loads = []
-            for side, stage in enumerate((own_ref, oth_ref)):
-                first = 0
-                for i, share in enumerate(shares):
-                    ref = ins[side * pieces + i]
-                    loads.append(
+            loads, first = [], 0
+            for i, share in enumerate(shares):
+                loads.append(
+                    [
                         pltpu.make_async_copy(
-                            ref, stage.at[first : first + share], sems.at[8 + pairs + side * pieces + i]
+                            ins[side * pieces + i],
+                            stage.at[first : first + share],
+                            sems.at[8 + pairs + side * pieces + i],
                         )
-                    )
-                    first += share
-            for load in loads:
+                        for side, stage in enumerate((own_ref, oth_ref))
+                    ]
+                )
+                first += share
+            for load in sum(loads, []):
                 load.start()
-            for load in loads:
-                load.wait()
-            assemble(meta, images, part_rows, own_ref, oth_ref, w_ref)
+            first = 0
+            for pair, share in zip(loads, shares):
+                for load in pair:
+                    load.wait()
+                assemble(first, share, chips, part_rows, own_ref, oth_ref, w_ref)
+                first += share
         else:
             (sems,) = refs
             w_ref = ins[0]
@@ -198,6 +282,8 @@
         par_ref[...] = w_ref[:, 4 * width : 4 * width + LANES].astype(f32).T[:8]
         gain_a, shift_a = par_ref[0:1], par_ref[1:2]
         gain_m, shift_m = par_ref[2:3], par_ref[3:4]
+        for load in given:
+            load.wait()
 
         @pl.loop(0, total // CHUNK, unroll=UNROLL)
         def _(i):
@@ -205,9 +291,11 @@
             x = x_ref[at].astype(f32)
             x = x - jnp.mean(x, axis=-1, keepdims=True)
             rstd = lax.rsqrt(jnp.mean(x * x, axis=-1, keepdims=True) + EPSILON)
-            n1_ref[at] = (x * rstd * gain_a + shift_a).astype(bf16)
-
-        store(n1_ref, n1_out)
+            x = x * rstd
+            xh_ref[at] = x.astype(bf16)
+            n1_ref[at] = (x * gain_a + shift_a).astype(bf16)
+
+        store(xh_ref, xh_out)
 
         @pl.loop(0, 3)
         def _(i):
@@ -260,16 +348,6 @@
     return body
 
 
-def stack_kernel(count):
-    def body(*refs):
-        ins, out = refs[:count], refs[count]
-        share = ins[0].shape[0]
-        for i, ref in enumerate(ins):
-            out[i * share : (i + 1) * share] = ref[...]
-
-    return body
-
-
 def expert_kernel(images, experts, width, hidden, chips, pieces):
     lanes = -(-hidden // LANES) * LANES
     per = images * experts
@@ -348,14 +426,11 @@
     return body
 
 
-def norm_pull(x, gain, grad):
-    x = x - jnp.mean(x, axis=-1, keepdims=True)
-    rstd = lax.rsqrt(jnp.mean(x * x, axis=-1, keepdims=True) + EPSILON)
-    x = x * rstd
+def norm_pull(x, rstd, gain, grad):
     scaled = grad * gain
     first = jnp.mean(scaled, axis=-1, keepdims=True)
     second = jnp.mean(scaled * x, axis=-1, keepdims=True)
-    return x, rstd * (scaled - first - x * second)
+    return rstd * (scaled - first - x * second)
 
 
 def attend_pull(meta, sizes, half, joint_ref, probs_ref, gm_ref, gj):
@@ -392,27 +467,49 @@
     return loads
 
 
+def second_norm_kernel(sizes):
+    images, rows, width, *_ = sizes
+
+    def body(meta, res_in, n2_in, xn_ref, dev_ref, n2_ref, res_ref, sems):
+        loads = [pltpu.make_async_copy(res_in, res_ref, sems.at[0]), pltpu.make_async_copy(n2_in, n2_ref, sems.at[1])]
+        for load in loads:
+            load.start()
+        loads[0].wait()
+
+        @pl.loop(0, images * rows // CHUNK, unroll=UNROLL)
+        def _(i):
+            at = rows_at(i, CHUNK)
+            x = res_ref[at]
+            x = x - jnp.mean(x, axis=-1, keepdims=True)
+            rstd = lax.rsqrt(jnp.mean(x * x, axis=-1, keepdims=True) + EPSILON)
+            xn_ref[at] = x * rstd
+            dev_ref[at] = jnp.broadcast_to(rstd, (CHUNK, LANES))
+
+        loads[1].wait()
+
+    return body
+
+
 def slots_pull_kernel(sizes):
     images, rows, width, experts, chips, part_rows, shares = sizes
     pieces = len(shares)
     total = images * rows
     share = HEADS // 4
 
-    def body(meta, cot_ref, par_ref, log_ref, sum_ref, r1_ref, r2_ref, r3_ref, w_in, n1_in, joint_in, probs_in,
-             mixed_in, res_in, n2_in, block_ref, xgrad_ref, gm, gj, grads, *refs):
-        outs, refs = refs[:-13], refs[-13:]
-        gn, gb, tile, small, w_ref, n1_ref, joint_ref, probs_ref, mixed_ref, res_ref, n2_ref, _, sems = refs
-        early = [
-            pltpu.make_async_copy(n2_in, n2_ref, sems.at[0]),
-            pltpu.make_async_copy(res_in, res_ref, sems.at[1]),
+    def body(meta, cot_ref, par_ref, log_ref, sum_ref, r1_ref, r2_ref, r3_ref, xn_ref, dev_ref, n2_ref, w_in, xh_in,
+             joint_in, probs_in, mixed_in, res_in, block_ref, xgrad_ref, gm, gj, grads, part_ref, xh_ref, w_half,
+             joint_late, probs_late, *refs):
+        outs, (gn, gb, tile, small, w_ref, joint_ref, probs_ref, mixed_ref, res_ref, col_ref, sems) = refs[:-11], refs[-11:]
+        early = [pltpu.make_async_copy(res_in, res_ref, sems.at[0])]
+        late = [
+            pltpu.make_async_copy(mixed_in, mixed_ref, sems.at[1]),
+            pltpu.make_async_copy(w_in.at[:, 3 * width : 4 * width], w_ref, sems.at[2]),
         ]
-        late = [
-            pltpu.make_async_copy(mixed_in, mixed_ref, sems.at[2]),
-            pltpu.make_async_copy(w_in.at[:, 3 * width : 4 * width], w_ref, sems.at[3]),
-            pltpu.make_async_copy(n1_in, n1_ref, sems.at[4]),
-        ]
-        loads = half_loads(width, 0, joint_in, joint_ref, probs_in, probs_ref, sems.at[5:9])
-        for load in early + late + loads:
+        loads = half_loads(width, 0, joint_in, joint_ref, probs_in, probs_ref, sems.at[3:7])
+        last = [pltpu.make_async_copy(xh_in, xh_ref, sems.at[7])]
+        last += weight_loads(width, 0, w_in, w_half, col_ref, sems.at[8:12])
+        ahead = half_loads(width, 1, joint_in, joint_late, probs_in, probs_late, sems.at[12:16])
+        for load in early + late + loads + last + ahead:
             load.start()
 
         def put(first, count):
@@ -421,8 +518,6 @@
             else:
                 outs[0][:, first : first + count] = tile[:, :count]
 
-        for load in early:
-            load.wait()
         sums = sum_ref[0].astype(f32) + r1_ref[0].astype(f32) + r2_ref[0].astype(f32) + r3_ref[0].astype(f32)
         small[...] = sums.astype(bf16).astype(f32)
         slot_w = par_ref[4 : 4 + experts]
@@ -447,6 +542,8 @@
             gn[span] = tn(left, right)
             live_row = lax.broadcasted_iota(jnp.int32, (rows, 1), 0) < meta[img]
             expert_sum = tn(combine.astype(bf16), slot_out)
+            for load in early if img == 0 else []:
+                load.wait()
             block_ref[span] = jnp.where(live_row, res_ref[span] + expert_sum, 0.0).astype(bf16)
         grads[0:2] = jnp.zeros((2, width), f32)
         grads[4 : 4 + experts] = slot_grad
@@ -458,7 +555,8 @@
             def step(i, carry):
                 at = pl.ds(pl.multiple_of(img * rows + i * CHUNK, CHUNK), CHUNK)
                 grad = gn[at]
-                x, pulled = norm_pull(res_ref[at], gain_m, grad)
+                x = xn_ref[at]
+                pulled = norm_pull(x, dev_ref[at, 0:1], gain_m, grad)
                 row = i * CHUNK + lax.broadcasted_iota(jnp.int32, (CHUNK, 1), 0)
                 pulled = pulled + jnp.where(row < meta[img], cot_ref[at].astype(f32), 0.0)
                 xgrad_ref[at] = pulled
@@ -477,66 +575,65 @@
         for load in loads:
             load.wait()
         attend_pull(meta, sizes, 0, joint_ref, probs_ref, gm, gj)
-        tile[...] = tn(n1_ref[...], gj[...])
-        put(width, 3 * width // 2)
+        for load in last:
+            load.wait()
+        tile[...] = tn(xh_ref[...], gj[...])
+        part_ref[...] = jnp.zeros_like(part_ref)
+        cut_scaled(chips, part_rows, tile, column_sums(gj), w_half, col_ref, part_ref, outs, width)
+        for load in ahead:
+            load.wait()
+
+    return body
+
+
+def heads_pull_kernel(sizes):
+    width = sizes[2]
+
+    def body(meta, gm_ref, joint_ref, probs_ref, w_in, gj, w_half, col_ref, sems):
+        loads = weight_loads(width, 1, w_in, w_half, col_ref, sems)
+        for load in loads:
+            load.start()
+        attend_pull(meta, sizes, 1, joint_ref, probs_ref, gm_ref, gj)
+        for load in loads:
+            load.wait()
+
+    return body
+
+
+def heads_grad_kernel(sizes):
+    images, rows, width, experts, chips, part_rows, shares = sizes
+    half = 3 * width // 2
+
+    def body(meta, gj, grads, part_ref, w_half, col_ref, xh_ref, *refs):
+        outs, (tile, small) = refs[:-2], refs[-2:]
+        filled = jnp.concatenate([grads[...], jnp.zeros((LANES - 8, width), f32)], axis=0)
+        small[...] = part_ref[...] + filled.T
+        tile[...] = tn(xh_ref[...], gj[...])
+        cut_scaled(chips, part_rows, tile, column_sums(gj), w_half, col_ref, small, outs, 0)
+        if shares:
+            cut(meta, images, chips, part_rows, small, LANES, *outs, half)
+        else:
+            outs[0][:, half : half + LANES] = small[...]
 
     return body
 
 
 def inputs_pull_kernel(sizes):
     images, rows, width, experts, chips, part_rows, shares = sizes
-    pieces = len(shares)
     total = images * rows
-    share = HEADS // 4
     half = 3 * width // 2
 
-    def body(meta, x_ref, par_ref, gm_ref, gj_ref, part_ref, early_ref, w_in, n1_in, joint_in, probs_in,
-             xgrad_ref, *refs):
-        outs, (gn, gj, tile, grads, n1_ref, joint_ref, probs_ref, w_ref, sems) = refs[:-9], refs[-9:]
-        loads = half_loads(width, 1, joint_in, joint_ref, probs_in, probs_ref, sems.at[0:4])
-        late = [pltpu.make_async_copy(n1_in, n1_ref, sems.at[4])]
-        part = width // 2
-        for i in range(6):
-            first = (i % 3) * width + (i // 3) * part
-            late.append(
-                pltpu.make_async_copy(
-                    w_in.at[:, first : first + part], w_ref.at[:, i * part : (i + 1) * part], sems.at[5 + i]
-                )
-            )
-        for load in loads + late:
-            load.start()
-
-        def put(first, count):
-            if pieces:
-                cut(meta, images, chips, part_rows, tile, count, *outs, first)
-            else:
-                outs[0][:, first : first + count] = tile[:, :count]
-
-        for load in loads:
-            load.wait()
-        attend_pull(meta, sizes, 1, joint_ref, probs_ref, gm_ref, gj)
-        for load in late:
-            load.wait()
-        tile[...] = tn(n1_ref[...], gj[...])
-        put(0, half)
-        gn[...] = nt(gj_ref[...], w_ref[:, :half]) + nt(gj[...], w_ref[:, half : 2 * half])
+    def body(meta, x_ref, par_ref, gj0_ref, gj1_ref, w0_ref, w1_ref, part_ref, xgrad_ref, gn):
+        gn[...] = nt(gj0_ref[...], w0_ref[...]) + nt(gj1_ref[...], w1_ref[...])
         gain_a = par_ref[0:1]
-        zero = jnp.zeros((8, width), f32)
-
-        def step(i, carry):
+
+        @pl.loop(0, total // CHUNK, unroll=UNROLL)
+        def _(i):
             at = rows_at(i, CHUNK)
-            grad = gn[at]
-            x, pulled = norm_pull(x_ref[at].astype(f32), gain_a, grad)
-            xgrad_ref[at] = part_ref[at] + pulled
-            return carry[0] + fold_rows(grad * x), carry[1] + fold_rows(grad)
-
-        sums = lax.fori_loop(0, total // CHUNK, step, (zero, zero), unroll=UNROLL)
-        grads[...] = early_ref[...]
-        grads[0:1] = jnp.sum(sums[0], axis=0, keepdims=True)
-        grads[1:2] = jnp.sum(sums[1], axis=0, keepdims=True)
-        filled = jnp.concatenate([grads[...], jnp.zeros((LANES - 8, width), f32)], axis=0)
-        tile[:, :LANES] = filled.T
-        put(half, LANES)
+            x = x_ref[at].astype(f32)
+            x = x - jnp.mean(x, axis=-1, keepdims=True)
+            rstd = lax.rsqrt(jnp.mean(x * x, axis=-1, keepdims=True) + EPSILON)
+            xgrad_ref[at] = part_ref[at] + norm_pull(x * rstd, rstd, gain_a, gn[at])
 
     return body
 
@@ -569,22 +666,24 @@
     return run
 
 
-def add_kernel(groups, terms, types):
+def add_kernel(groups, types, share=2):
     def run(*args):
         rest = args[0].shape[1:]
+        sizes = [share * len(g) for g in groups]
 
         def body(*refs):
             ins, outs = refs[: len(args)], refs[len(args) :]
-            for out, count, parts in zip(outs, groups, terms):
-                for i in range(count):
-                    total = ins[parts[0][0]][parts[0][1] + i].astype(f32)
-                    for a, first in parts[1:]:
-                        total = total + ins[a][first + i].astype(f32)
-                    out[i] = total.astype(out.dtype)
+            for out, group in zip(outs, groups):
+                for j, terms in enumerate(group):
+                    for i in range(share):
+                        total = ins[terms[0][0]][terms[0][1] + i].astype(f32)
+                        for a, first in terms[1:]:
+                            total = total + ins[a][first + i].astype(f32)
+                        out[j * share + i] = total.astype(out.dtype)
 
         return pl.pallas_call(
             body,
-            out_shape=[jax.ShapeDtypeStruct((c,) + rest, t) for c, t in zip(groups, types)],
+            out_shape=[jax.ShapeDtypeStruct((c,) + rest, t) for c, t in zip(sizes, types)],
             in_specs=[vmem()] * len(args),
             out_specs=[vmem()] * len(groups),
             compiler_params=pltpu.CompilerParams(vmem_limit_bytes=16 * MIB),
@@ -634,12 +733,7 @@
     *lower, last = stages_of(devices)[::-1]
     for group in lower:
         parts = [block] + [swap(block, devices, o, 0) for o in group[1:]]
-        block = pl.pallas_call(
-            stack_kernel(len(parts)),
-            out_shape=jax.ShapeDtypeStruct((len(parts) * block.shape[0],) + block.shape[1:], block.dtype),
-            in_specs=[vmem()] * len(parts),
-            out_specs=vmem(),
-        )(*parts)
+        block = jnp.concatenate(parts, axis=0)
     own = [block] + [swap(block, devices, o, 0) for o in last[1:]]
     return own, [swap(part, devices, 0, 1) for part in own]
 
@@ -656,29 +750,52 @@
 
 
 def gather_pieces(block, devices):
-    z0 = block[None]
-    z0 = jnp.concatenate([z0, swap(z0, devices, 8, 0)], axis=0)
-    z1 = swap(z0, devices, 4, 0)
+    block = block[None]
+    far = swap(block, devices, 8, 0)
+    z0 = jnp.concatenate([block, swap(block, devices, 4, 0)], axis=0)
     x0, y0 = swap(z0, devices, 1, 0), swap(z0, devices, 2, 0)
+    z1 = jnp.concatenate([far, swap(far, devices, 4, 0)], axis=0)
     x1, y1 = swap(z1, devices, 1, 0), swap(z1, devices, 2, 0)
     d0, d1 = swap(y0, devices, 1, 0), swap(x1, devices, 2, 0)
     own = [z0, z1, x0, x1, y0, y1, d0, d1]
     return own + [swap(piece, devices, 0, 1) for piece in own]
 
 
-def scatter_pieces(mine, other, devices):
+def after(values, events):
+    return lax.optimization_barrier((*values, *events))[: len(values)]
+
+
+def scatter_begin(mine, other, devices, events=()):
     got = swap(other, devices, 0, 1)
-    two = [[(0, 2 * g), (1, 2 * g)] for g in range(8)]
-    z0, z1, x0, x1, y0, y1, d0, d1 = add_kernel([2] * 8, two, [f32, f32] + [bf16] * 6)(mine, got)
-    to_y0, to_x1 = swap(d0, devices, 1, 0), swap(d1, devices, 2, 0)
-    x1, y0 = add_kernel([2, 2], [[(0, 0), (1, 0)], [(2, 0), (3, 0)]], [bf16, bf16])(x1, to_x1, y0, to_y0)
-    from_x1, from_y1 = swap(x1, devices, 1, 0), swap(y1, devices, 2, 0)
-    from_x0, from_y0 = swap(x0, devices, 1, 0), swap(y0, devices, 2, 0)
-    (z1,) = add_kernel([2], [[(0, 0), (1, 0), (2, 0)]], [bf16])(z1, from_x1, from_y1)
-    from_z1 = swap(z1, devices, 4, 0)
+    if events:
+        (got,) = after([got], events)
+    z0, z1, x0, x1, y0, y1, d0, d1 = [[(0, i), (1, i)] for i in range(0, 16, 2)]
+    return add_kernel(
+        [[z0], [z1], [d0, x0], [d1, y1], [x1], [y0]], [f32, f32, bf16, bf16, bf16, bf16]
+    )(mine, got)
+
+
+def scatter_middle(parts, devices, events=()):
+    z0, z1, to_x, to_y, x1, y0 = parts
+    from_x, from_y = swap(to_x, devices, 1, 0), swap(to_y, devices, 2, 0)
+    if events:
+        x1, y0 = after([x1, y0], events)
+    x1, y0 = add_kernel([[[(0, 0), (2, 0)]], [[(1, 0), (3, 0)]]], [bf16, bf16])(x1, y0, from_y, from_x)
+    return z0, z1, x1, y0, from_x, from_y
+
+
+def scatter_near(parts, devices):
+    z0, z1, x1, y0, from_x, from_y = parts
+    from_x1, from_y0 = swap(x1, devices, 1, 0), swap(y0, devices, 2, 0)
+    (z1,) = add_kernel([[[(0, 0), (1, 0), (2, 2)]]], [bf16])(z1, from_x1, from_y)
+    return z0, from_x, from_y0, swap(z1, devices, 4, 0)
+
+
+def scatter_end(parts, devices):
+    z0, from_x, from_y0, from_z1 = parts
     keep, send = add_kernel(
-        [1, 1], [[(a, i) for a in range(4)] for i in range(2)], [f32, bf16]
-    )(z0, from_x0, from_y0, from_z1)
+        [[[(0, i), (1, 2 + i), (2, i), (3, i)]] for i in range(2)], [f32, bf16], 1
+    )(z0, from_x, from_y0, from_z1)
     return keep, swap(send, devices, 8, 0)
 
 
@@ -723,18 +840,18 @@
             ((count, experts, rows), f32),
             ((2 * count * experts, width), bf16),
         ] + kept
-        scratch = kept + [((2 * count * experts, width), f32)]
+        scratch = kept + [((2 * count * experts, width), f32)] + [((total, width), bf16)] * 3
         if shares:
             outs.append(((width, wide), bf16))
             scratch += [outs[-1]] + [((chips, part_rows, wide), bf16)] * 2
-        par, logs, slots, n1, mixed, joint, probs, res, n2, *more = call(
+        par, logs, slots, xh, mixed, joint, probs, res, n2, *more = call(
             forward_kernel(sizes),
             outs,
             scratch,
             40,
-            far_in=range(2, 2 + 2 * len(shares)),
+            far_in=range(0, 2 + 2 * len(shares)),
             far_out=range(3, len(outs)),
-            sems=8 + pairs + 2 * len(shares),
+            sems=10 + pairs + 2 * len(shares),
         )(meta, x, cot, *weights)
         w = more[0] if shares else weights[0]
 
@@ -778,7 +895,17 @@
             return [((width, columns), f32)]
 
         halves = [((total, 3 * half), bf16), ((pairs // 2, count, 2 * rows, rows), bf16)]
-        block, part, gm, gj, early, *first = call(
+        xn, dev, n2 = call(
+            second_norm_kernel(sizes),
+            [((total, width), f32), ((total, LANES), f32), ((total, width), bf16)],
+            [((total, width), f32)],
+            16,
+            flops=10**9,
+            far_in=range(2),
+            sems=2,
+        )(meta, res, n2)
+        columns = ((width, 3 * half), bf16)
+        block, part, gm, gj, early, tiny, xh, w0, joint1, probs1, *first = call(
             slots_pull_kernel(sizes),
             [
                 ((total, width), bf16),
@@ -786,7 +913,11 @@
                 ((total, width), bf16),
                 ((total, 3 * half), bf16),
                 ((8, width), f32),
+                ((width, LANES), f32),
+                ((total, width), bf16),
+                columns,
             ]
+            + halves
             + blocks(width + 3 * half),
             [
                 ((total, width), f32),
@@ -794,38 +925,53 @@
                 ((width, 3 * half), f32),
                 ((2 * count * experts, width), f32),
                 ((width, width), bf16),
-                ((total, width), bf16),
             ]
             + halves
             + [
                 ((total, width), bf16),
                 ((total, width), f32),
-                ((total, width), bf16),
-                ((8, LANES), f32),
+                ((width, LANES), bf16),
             ],
             VMEM_MIB,
-            far_in=range(7, 14),
-            sems=9,
-        )(meta, cot, par, logs, *terms, w, n1, joint, probs, mixed, res, n2)
-        xgrad, *second = call(
+            far_in=range(10, 16),
+            sems=16,
+        )(meta, cot, par, logs, *terms, xn, dev, n2, w, xh, joint, probs, mixed, res)
+        gj1, w1, tail = call(
+            heads_pull_kernel(sizes),
+            [((total, 3 * half), bf16), columns, ((width, LANES), bf16)],
+            [],
+            VMEM_MIB,
+            flops=3 * 10**9,
+            far_in=range(3, 4),
+            sems=4,
+        )(meta, gm, joint1, probs1, w)
+        gj_late = gj1
+        if shares:
+            first = scatter_begin(*first, devices)
+            gj_late = after([gj1], first)[0]
+        second = call(
+            heads_grad_kernel(sizes),
+            blocks(3 * half + LANES),
+            [((width, 3 * half), f32), ((width, LANES), f32)],
+            VMEM_MIB,
+            flops=4 * 10**9,
+        )(meta, gj_late, early, tiny, w1, tail, xh)
+        if shares:
+            first = scatter_middle(first, devices)
+            second = scatter_begin(*after(second, first[2:4]), devices)
+            part = after([part], [*second, first[2]])[0]
+            first = scatter_near(first, devices)
+        xgrad = call(
             inputs_pull_kernel(sizes),
-            [((total, width), f32)] + blocks(3 * half + LANES),
-            [
-                ((total, width), f32),
-                ((total, 3 * half), bf16),
-                ((width, 3 * half), f32),
-                ((8, width), f32),
-                ((total, width), bf16),
-            ]
-            + halves
-            + [((width, 3 * width), bf16)],
+            [((total, width), f32)],
+            [((total, width), f32)],
             VMEM_MIB,
-            flops=8 * 10**9,
-            far_in=range(6, 10),
-            sems=11,
-        )(meta, x, par, gm, gj, part, early, w, n1, joint, probs)
+            flops=5 * 10**9,
+        )(meta, x, par, gj, gj1, w0, w1, part)[0]
         if shares:
-            ends = [*scatter_pieces(*first, devices), *scatter_pieces(*second, devices)]
+            second = scatter_middle(second, devices, [xgrad, first[2]])
+            second = scatter_near(second, devices)
+            ends = [*scatter_end(first, devices), *scatter_end(second, devices)]
         else:
             ends = []
             for full in (first[0], second[0]):

time: 164 us -> 152 us (0.927)
  starting transfers between devices: 44.9 us -> 39.4 us
  local copies, waits for them, and re-layouts: 6.89 us -> 2 us
  waiting for transfers between devices: 62.6 us -> 59.4 us
    ppermute x51 -> x48, starting transfers between devices: 44.9 us -> 39.4 us  [swap(): return lax.ppermute(value, 'fsdp', [(i, i ^ mask) for i in range(devices)])]
    unnamed x66 -> x51, local copies, waits for them, and re-layouts: 6.89 us -> 1.98 us
    ppermute x51 -> x48, waiting for transfers between devices: 62.6 us -> 59.4 us  [swap(): return lax.ppermute(value, 'fsdp', [(i, i ^ mask) for i in range(devices)])]
    pallas_call x5 -> x8, Pallas kernels: 41.5 us -> 44.6 us  [run(): pl.pallas_call(body, out_shape=[pltpu.HBM(s, d) if i in far_out else jax....]
  transfers between devices with their start and end apart: 51 -> 48, of which waited for: 27 -> 26; matrix products, arithmetic and copies ran while one was open for 0% -> 1% of each run, Pallas kernels for 10% -> 12%
where the time goes in v3:
time: 152 us
  waiting for transfers between devices  59.4 us (39%)
  Pallas kernels  49.2 us (32%)
  starting transfers between devices  39.4 us (26%)
  local copies, waits for them, and re-layouts  2 us (1%)
    ppermute x48, waiting for transfers between devices, swap(): return lax.ppermute(value, 'fsdp', [(i, i ^ mask) for i in range(devices)])  59.4 us
    pallas_call x8, Pallas kernels, run(): pl.pallas_call(body, out_shape=[pltpu.HBM(s, d) if i in far_out else jax....  44.6 us
    ppermute x48, starting transfers between devices, swap(): return lax.ppermute(value, 'fsdp', [(i, i ^ mask) for i in range(devices)])  39.4 us
  transfers between devices with their start and end apart: 48, of which 26 were waited for; matrix products, arithmetic and copies ran while one was open for 1% of the time, Pallas kernels for 12%

profile of v3, /device:TPU:0, one launch (start us, length us, event | category | flops | bytes accessed | tf_op | source)
XLA Modules:
  0.0 152.1 jit_solution(11188248380926183491)
XLA Ops:
  0.7 1.7 %shard_map.203 = bf16[24,3200]{1,0:T(8,128)(2,1)} custom-call(bf16[24,2304]{1,0:T(8,128)(2,1)} %in_ref.1, bf16[24,768]{1,0:T(8,128)(2,1)} %out_ref.1, bf16[1,24]{1,0:T(2,128)(2,1)} %bitcast.31, bf16[1,24]{1,0:T(2,128)(2,1)} %bitcast.32, bf16[1,24]{1,0:T(2,128)(2,1)} %bitcast.33, bf16[1,24]{1,0:T(2,128)(2,1)} %bitcast.34, bf16[4,24]{1,0:T(4,128)(2,1)} %bitcast.30), custom_call_target="tpu_custom_call" | custom-call | tf_op jit(solution)/shard_map/pallas_call | solution.py:819
  2.4 3.0 %collective-permute-start = (bf16[1,24,3200]{2,1,0:T(8,128)(2,1)}, bf16[1,24,3200]{2,1,0:T(8,128)(2,1)S(1)}, u32[]{:S(2)}, u32[]{:S(2)}) collective-permute-start(bf16[1,24,3200]{2,1,0:T(8,128)(2,1)} %bitcast.27), channel_id=1, source_target_pairs={{0,8},{1,9},{2,10},{3,11},{4,12},{5,13},{6,14},{7,15},{8,0},{9,1},... | collective-permute-start | bytes 460808 | tf_op jit(solution)/shard_map/ppermute | solution.py:729
  5.4 2.6 %collective-permute-start.1 = (bf16[1,24,3200]{2,1,0:T(8,128)(2,1)}, bf16[1,24,3200]{2,1,0:T(8,128)(2,1)S(1)}, u32[]{:S(2)}, u32[]{:S(2)}) collective-permute-start(bf16[1,24,3200]{2,1,0:T(8,128)(2,1)} %bitcast.28), channel_id=1, source_target_pairs={{0,16},{1,17},{2,18},{3,19},{4,20},{5,21},{6,22},{7,23},{8,24},{9,... | collective-permute-start | bytes 460808 | tf_op jit(solution)/shard_map/ppermute | solution.py:729
  8.0 4.4 %collective-permute-done = bf16[1,24,3200]{2,1,0:T(8,128)(2,1)S(1)} collective-permute-done((bf16[1,24,3200]{2,1,0:T(8,128)(2,1)}, bf16[1,24,3200]{2,1,0:T(8,128)(2,1)S(1)}, u32[]{:S(2)}, u32[]{:S(2)}) %collective-permute-start) | collective-permute-done | bytes 153632 | tf_op jit(solution)/shard_map/ppermute | solution.py:729
  12.3 0.9 pad_maximum_fusion.refs_0_
  13.4 1.9 %collective-permute-start.5 = (bf16[2,24,3200]{2,1,0:T(8,128)(2,1)S(1)}, bf16[2,24,3200]{2,1,0:T(8,128)(2,1)S(1)}, u32[]{:S(2)}, u32[]{:S(2)}) collective-permute-start(bf16[2,24,3200]{2,1,0:T(8,128)(2,1)S(1)} %pad_maximum_fusion.refs_0_), channel_id=1, source_target_pairs={{0,4},{1,5},{2,6},{3,7},{4,0},{5,1},{6,2},{7,3},{8,12},{9,13},{10,... | collective-permute-start | bytes 921608 | tf_op jit(solution)/shard_map/ppermute | solution.py:729
  15.3 1.5 collective-permute-start.3
  16.8 5.8 %collective-permute-done.2 = bf16[1,24,3200]{2,1,0:T(8,128)(2,1)S(1)} collective-permute-done((bf16[1,24,3200]{2,1,0:T(8,128)(2,1)S(1)}, bf16[1,24,3200]{2,1,0:T(8,128)(2,1)S(1)}, u32[]{:S(2)}, u32[]{:S(2)}) %collective-permute-start.2) | collective-permute-done | bytes 153632 | tf_op jit(solution)/shard_map/ppermute | solution.py:729
  23.9 1.1 collective-permute-done.3.refs_2_
  25.0 2.0 %collective-permute-start.7 = (bf16[2,24,3200]{2,1,0:T(8,128)(2,1)S(1)}, bf16[2,24,3200]{2,1,0:T(8,128)(2,1)S(1)}, u32[]{:S(2)}, u32[]{:S(2)}) collective-permute-start(bf16[2,24,3200]{2,1,0:T(8,128)(2,1)S(1)} %collective-permute-done.5.refs_4_), channel_id=1, source_target_pairs={{0,2},{1,3},{2,0},{3,1},{4,6},{5,7},{6,4},{7,5},{8,10},{9,11},{10,... | collective-permute-start | bytes 921608 | tf_op jit(solution)/shard_map/ppermute | solution.py:729
  26.9 6.0 %collective-permute-done.4.refs_3_ = bf16[2,24,3200]{2,1,0:T(8,128)(2,1)S(1)} collective-permute-done((bf16[2,24,3200]{2,1,0:T(8,128)(2,1)S(1)}, bf16[2,24,3200]{2,1,0:T(8,128)(2,1)S(1)}, u32[]{:S(2)}, u32[]{:S(2)}) %collective-permute-start.4) | collective-permute-done | bytes 307232 | tf_op jit(solution)/shard_map/ppermute | solution.py:729
  34.0 3.8 %collective-permute-done.7.refs_6_ = bf16[2,24,3200]{2,1,0:T(8,128)(2,1)S(1)} collective-permute-done((bf16[2,24,3200]{2,1,0:T(8,128)(2,1)S(1)}, bf16[2,24,3200]{2,1,0:T(8,128)(2,1)S(1)}, u32[]{:S(2)}, u32[]{:S(2)}) %collective-permute-start.7) | collective-permute-done | bytes 307232 | tf_op jit(solution)/shard_map/ppermute | solution.py:729
  37.8 1.9 %collective-permute-done.8.refs_7_ = bf16[2,24,3200]{2,1,0:T(8,128)(2,1)S(1)} collective-permute-done((bf16[2,24,3200]{2,1,0:T(8,128)(2,1)S(1)}, bf16[2,24,3200]{2,1,0:T(8,128)(2,1)S(1)}, u32[]{:S(2)}, u32[]{:S(2)}) %collective-permute-start.8) | collective-permute-done | bytes 307232 | tf_op jit(solution)/shard_map/ppermute | solution.py:729
  39.8 1.5 collective-permute-done.16.refs_15_
  42.1 11.5 %shard_map.204 = (f32[8,768]{1,0:T(8,128)S(1)}, f32[2,4,208]{2,1,0:T(4,128)S(1)}, bf16[16,768]{1,0:T(8,128)(2,1)S(1)}, bf16[416,768]{1,0:T(8,128)(2,1)}, bf16[41...) custom-call(s32[2]{0:T(128)S(1)} %copy-done.6, ...), custom_call_target="tpu_custom_call" | custom-call | tf_op jit(solution)/shard_map/pallas_call | solution.py:53
  53.6 2.8 %collective-permute-start.19 = (bf16[1,16,768]{2,1,0:T(8,128)(2,1)S(1)}, bf16[1,16,768]{2,1,0:T(8,128)(2,1)S(1)}, u32[]{:S(2)}, u32[]{:S(2)}) collective-permute-start(bf16[1,16,768]{2,1,0:T(8,128)(2,1)S(1)} %bitcast.23), channel_id=1, source_target_pairs={{0,24},{1,25},{2,26},{3,27},{4,28},{5,29},{6,30},{7,31},{8,16},{9,... | collective-permute-start | bytes 73736 | tf_op jit(solution)/shard_map/ppermute | solution.py:729
  56.4 1.7 %collective-permute-start.17 = (bf16[1,16,768]{2,1,0:T(8,128)(2,1)S(1)}, bf16[1,16,768]{2,1,0:T(8,128)(2,1)S(1)}, u32[]{:S(2)}, u32[]{:S(2)}) collective-permute-start(bf16[1,16,768]{2,1,0:T(8,128)(2,1)S(1)} %bitcast.25), channel_id=1, source_target_pairs={{0,8},{1,9},{2,10},{3,11},{4,12},{5,13},{6,14},{7,15},{8,0},{9,1},... | collective-permute-start | bytes 73736 | tf_op jit(solution)/shard_map/ppermute | solution.py:729
  58.1 1.3 collective-permute-done.19
  59.4 1.8 %collective-permute-done.18 = bf16[1,16,768]{2,1,0:T(8,128)(2,1)S(1)} collective-permute-done((bf16[1,16,768]{2,1,0:T(8,128)(2,1)S(1)}, bf16[1,16,768]{2,1,0:T(8,128)(2,1)S(1)}, u32[]{:S(2)}, u32[]{:S(2)}) %collective-permute-start.18) | collective-permute-done | bytes 24608 | tf_op jit(solution)/shard_map/ppermute | solution.py:729
  61.2 1.5 collective-permute-start.22
  62.7 1.5 %collective-permute-start.21 = (bf16[4,16,768]{2,1,0:T(8,128)(2,1)S(1)}, bf16[4,16,768]{2,1,0:T(8,128)(2,1)S(1)}, u32[]{:S(2)}, u32[]{:S(2)}) collective-permute-start(bf16[4,16,768]{2,1,0:T(8,128)(2,1)S(1)} %pad_maximum_fusion.1.refs_0_), channel_id=1, source_target_pairs={{0,4},{1,5},{2,6},{3,7},{4,0},{5,1},{6,2},{7,3},{8,12},{9,13},{10,... | collective-permute-start | bytes 294920 | tf_op jit(solution)/shard_map/ppermute | solution.py:729
  64.7 2.3 %collective-permute-done.22.refs_3_ = bf16[4,16,768]{2,1,0:T(8,128)(2,1)S(1)} collective-permute-done((bf16[4,16,768]{2,1,0:T(8,128)(2,1)S(1)}, bf16[4,16,768]{2,1,0:T(8,128)(2,1)S(1)}, u32[]{:S(2)}, u32[]{:S(2)}) %collective-permute-start.22) | collective-permute-done | bytes 98336 | tf_op jit(solution)/shard_map/ppermute | solution.py:729
  67.1 1.0 collective-permute-done.21.refs_2_
  70.1 2.6 %shard_map.205 = (bf16[16,16,768]{2,1,0:T(8,128)(2,1)S(1)}, bf16[16,16,768]{2,1,0:T(8,128)(2,1)S(1)}, bf16[256,768]{1,0:T(8,128)(2,1)S(1)}, bf16[256,768]{1,0:T(...) custom-call(s32[2]{0:T(128)S(1)} %copy-done.6, ...), custom_call_target="tpu_custom_call" | custom-call | tf_op jit(solution)/shard_map/pallas_call | solution.py:53
  72.9 1.6 %collective-permute-done.27.refs_1_ = bf16[16,16,768]{2,1,0:T(8,128)(2,1)S(1)} collective-permute-done((bf16[16,16,768]{2,1,0:T(8,128)(2,1)S(1)}, bf16[16,16,768]{2,1,0:T(8,128)(2,1)S(1)}, u32[]{:S(2)}, u32[]{:S(2)}) %collective-permute-start.27) | collective-permute-done | bytes 393248 | tf_op jit(solution)/shard_map/ppermute | solution.py:729
  76.2 2.1 %collective-permute-start.30 = (bf16[4,16,768]{2,1,0:T(8,128)(2,1)S(1)}, bf16[4,16,768]{2,1,0:T(8,128)(2,1)S(1)}, u32[]{:S(2)}, u32[]{:S(2)}) collective-permute-start(bf16[4,16,768]{2,1,0:T(8,128)(2,1)S(1)} %get-tuple-element.101), channel_id=1, source_target_pairs={{0,6},{1,7},{2,4},{3,5},{4,2},{5,3},{6,0},{7,1},{8,14},{9,15},{10,... | collective-permute-start | bytes 294920 | tf_op jit(solution)/shard_map/ppermute | solution.py:729
  78.2 2.4 %shard_map.209 = (f32[416,768]{1,0:T(8,128)S(1)}, f32[416,128]{1,0:T(8,128)S(1)}, bf16[416,768]{1,0:T(8,128)(2,1)S(1)}) custom-call(s32[2]{0:T(128)S(1)} %copy-done.6, f32[416,768]{1,0:T(8,128)} %get-tuple-element.113.res_in, bf16[416,768]{1,0:T(8,128)(2,1)} %get-tuple-element.114.n2_in), custom_call_target="tpu_custom_call" | custom-call | flops 1000000000 | tf_op jit(solution)/shard_map/pallas_call | solution.py:53
  80.6 1.4 collective-permute-done.29.refs_2_
  82.9 1.4 collective-permute-start.32
  84.2 2.2 %collective-permute-start.33 = (bf16[1,16,768]{2,1,0:T(8,128)(2,1)S(1)}, bf16[1,16,768]{2,1,0:T(8,128)(2,1)S(1)}, u32[]{:S(2)}, u32[]{:S(2)}) collective-permute-start(bf16[1,16,768]{2,1,0:T(8,128)(2,1)S(1)} %get-tuple-element.112), channel_id=1, source_target_pairs={{0,24},{1,25},{2,26},{3,27},{4,28},{5,29},{6,30},{7,31},{8,16},{9,... | collective-permute-start | bytes 73736 | tf_op jit(solution)/shard_map/ppermute | solution.py:729
  86.5 2.5 %shard_map.208 = (f32[4,96,768]{2,1,0:T(8,128)}, f32[4,96,768]{2,1,0:T(8,128)}) custom-call(s32[2]{0:T(128)S(1)} %copy-done.6, bf16[256,768]{1,0:T(8,128)(2,1)S(1)} %get-tuple-element.103.s_ref, bf16[256,768]{1,0:T(8,128)(2,1)S(1)} %get-tuple-element.104.g_ref, bf16[256,512]{1,0:T(8,128)(2,1)S(1)} %get-tuple-element.105.act_ref, ...), custom_call_target="tpu_custom_call" | custom-call | flops 2000000000 | tf_op jit(solution)/shard_map/pallas_call | solution.py:53
  89.9 12.8 %shard_map.210 = (bf16[416,768]{1,0:T(8,128)(2,1)}, f32[416,768]{1,0:T(8,128)S(1)}, bf16[416,768]{1,0:T(8,128)(2,1)S(1)}, bf16[416,1152]{1,0:T(8,128)(2,1)S(1)},...) custom-call(s32[2]{0:T(128)S(1)} %copy-done.6, ...), custom_call_target="tpu_custom_call" | custom-call | tf_op jit(solution)/shard_map/pallas_call | solution.py:53
  102.8 4.2 %shard_map.211 = (bf16[416,1152]{1,0:T(8,128)(2,1)S(1)}, bf16[768,1152]{1,0:T(8,128)(2,1)S(1)}, bf16[768,128]{1,0:T(8,128)(2,1)S(1)}) custom-call(s32[2]{0:T(128)S(1)} %copy-done.6, bf16[416,768]{1,0:T(8,128)(2,1)S(1)} %get-tuple-element.125.gm_ref, bf16[416,1152]{1,0:T(8,128)(2,1)S(1)} %get-tuple-element.126.joint_ref, ...), custom_call_target="tpu_custom_call" | custom-call | flops 3000000000 | tf_op jit(solution)/shard_map/pallas_call | solution.py:53
  107.3 1.6 %collective-permute-start.36 = (bf16[4,24,1920]{2,1,0:T(8,128)(2,1)S(1)}, bf16[4,24,1920]{2,1,0:T(8,128)(2,1)S(1)}, u32[]{:S(2)}, u32[]{:S(2)}) collective-permute-start(bf16[4,24,1920]{2,1,0:T(8,128)(2,1)S(1)} %get-tuple-element.136), channel_id=1, source_target_pairs={{0,2},{1,3},{2,0},{3,1},{4,6},{5,7},{6,4},{7,5},{8,10},{9,11},{10,... | collective-permute-start | bytes 1105928 | tf_op jit(solution)/shard_map/ppermute | solution.py:729
  109.7 4.3 %shard_map.213 = (bf16[16,24,1280]{2,1,0:T(8,128)(2,1)S(1)}, bf16[16,24,1280]{2,1,0:T(8,128)(2,1)S(1)}) custom-call(s32[2]{0:T(128)S(1)} %copy-done.6, bf16[416,1152]{1,0:T(8,128)(2,1)S(1)} %get-tuple-element.140.gj.gj1_ref, f32[8,768]{1,0:T(8,128)S(1)} %get-tuple-element.141.grads, f32[768,128]{1,0:T(8,128)S(1)} %get-tuple-element.142.part_ref, ...), custom_call_target="tpu_custom_call" | custom-call | flops 4000000000 | tf_op jit(solution)/shard_map/pallas_call | solution.py:53
  114.0 4.4 %collective-permute-done.36.refs_3_.refs_1_ = bf16[4,24,1920]{2,1,0:T(8,128)(2,1)S(1)} collective-permute-done((bf16[4,24,1920]{2,1,0:T(8,128)(2,1)S(1)}, bf16[4,24,1920]{2,1,0:T(8,128)(2,1)S(1)}, u32[]{:S(2)}, u32[]{:S(2)}) %collective-permute-start.36) | collective-permute-done | bytes 368672 | tf_op jit(solution)/shard_map/ppermute | solution.py:729
  118.4 1.2 collective-permute-done.35.refs_2_
  123.1 1.2 collective-permute-start.43
  124.3 4.3 %shard_map.216 = f32[416,768]{1,0:T(8,128)} custom-call(s32[2]{0:T(128)S(1)} %copy-done.6, bf16[416,768]{1,0:T(8,128)(2,1)S(1)} %bitcast.21, f32[8,768]{1,0:T(8,128)S(1)} %get-tuple-element.93.par_ref, bf16[416,1152]{1,0:T(8,128)(2,1)S(1)} %get-tuple-element.124.gj0_ref, bf16[416,1152]{1,0:T(8,128)(2,1)S(1)} %get-tuple-element.140.gj.gj1_ref, ...), custom_call_target="tpu_custom_call" | custom-call | flops 5000000000 | tf_op jit(solution)/shard_map/pallas_call | solution.py:53
  128.6 4.0 %collective-permute-done.42.refs_3_.refs_1_ = bf16[4,24,1280]{2,1,0:T(8,128)(2,1)S(1)} collective-permute-done((bf16[4,24,1280]{2,1,0:T(8,128)(2,1)S(1)}, bf16[4,24,1280]{2,1,0:T(8,128)(2,1)S(1)}, u32[]{:S(2)}, u32[]{:S(2)}) %collective-permute-start.42) | collective-permute-done | bytes 245792 | tf_op jit(solution)/shard_map/ppermute | solution.py:729
  132.7 0.9 collective-permute-start.45
  134.8 2.9 %collective-permute-done.45.refs_1_ = bf16[2,24,1280]{2,1,0:T(8,128)(2,1)S(1)} collective-permute-done((bf16[2,24,1280]{2,1,0:T(8,128)(2,1)S(1)}, bf16[2,24,1280]{2,1,0:T(8,128)(2,1)S(1)}, u32[]{:S(2)}, u32[]{:S(2)}) %collective-permute-start.45) | collective-permute-done | bytes 122912 | tf_op jit(solution)/shard_map/ppermute | solution.py:729
  137.9 2.3 %collective-permute-done.40.refs_3_ = bf16[2,24,1920]{2,1,0:T(8,128)(2,1)S(1)} collective-permute-done((bf16[2,24,1920]{2,1,0:T(8,128)(2,1)S(1)}, bf16[2,24,1920]{2,1,0:T(8,128)(2,1)S(1)}, u32[]{:S(2)}, u32[]{:S(2)}) %collective-permute-start.40) | collective-permute-done | bytes 184352 | tf_op jit(solution)/shard_map/ppermute | solution.py:729
  140.3 1.1 collective-permute-start.41
  141.4 2.1 %collective-permute-done.46.refs_3_ = bf16[2,24,1280]{2,1,0:T(8,128)(2,1)S(1)} collective-permute-done((bf16[2,24,1280]{2,1,0:T(8,128)(2,1)S(1)}, bf16[2,24,1280]{2,1,0:T(8,128)(2,1)S(1)}, u32[]{:S(2)}, u32[]{:S(2)}) %collective-permute-start.46) | collective-permute-done | bytes 122912 | tf_op jit(solution)/shard_map/ppermute | solution.py:729
  144.8 3.0 %collective-permute-done.41.a1 = bf16[1,24,1920]{2,1,0:T(8,128)(2,1)S(1)} collective-permute-done((bf16[1,24,1920]{2,1,0:T(8,128)(2,1)S(1)}, bf16[1,24,1920]{2,1,0:T(8,128)(2,1)S(1)}, u32[]{:S(2)}, u32[]{:S(2)}) %collective-permute-start.41) | collective-permute-done | bytes 92192 | tf_op jit(solution)/shard_map/ppermute | solution.py:729
  147.7 1.9 %collective-permute-done.47.b1 = bf16[1,24,1280]{2,1,0:T(8,128)(2,1)S(1)} collective-permute-done((bf16[1,24,1280]{2,1,0:T(8,128)(2,1)S(1)}, bf16[1,24,1280]{2,1,0:T(8,128)(2,1)S(1)}, u32[]{:S(2)}, u32[]{:S(2)}) %collective-permute-start.47) | collective-permute-done | bytes 61472 | tf_op jit(solution)/shard_map/ppermute | solution.py:729
  150.3 1.8 %shard_map.222 = (f32[24,768]{1,0:T(8,128)}, f32[24,2304]{1,0:T(8,128)}, f32[1,24]{1,0:T(1,128)}, f32[1,24]{1,0:T(1,128)}, f32[1,24]{1,0:T(1,128)}, /*index=5*/f32[1,24]{1,0:T(1,128)}, f32[4,24]{1,0:T(4,128)}) custom-call(f32[1,24,1920]{2,1,0:T(8,128)} %copy-done.4, bf16[1,24,1920]{2,1,0:T(8,128)(2,1)} %copy-done.23, f32[1,24,1280]{2,1,0:T(8,128)} %copy-done.5, ...), custom_call_target="tpu_custom_call" | custom-call | tf_op jit(solution)/shard_map/pallas_call | solution.py:980
  (122 shorter events, 17.5 us)
Async XLA Ops:
  2.4 10.0 %collective-permute-start = (bf16[1,24,3200]{2,1,0:T(8,128)(2,1)}, bf16[1,24,3200]{2,1,0:T(8,128)(2,1)S(1)}, u32[]{:S(2)}, u32[]{:S(2)}) collective-permute-start(bf16[1,24,3200]{2,1,0:T(8,128)(2,1)} %bitcast.27), channel_id=1, source_target_pairs={{0,8},{1,9},{2,10},{3,11},{4,12},{5,13},{6,14},{7,15},{8,0},{9,1},... | collective-permute-start | bytes 460808 | tf_op jit(solution)/shard_map/ppermute | solution.py:729
  5.4 11.4 %collective-permute-start.1 = (bf16[1,24,3200]{2,1,0:T(8,128)(2,1)}, bf16[1,24,3200]{2,1,0:T(8,128)(2,1)S(1)}, u32[]{:S(2)}, u32[]{:S(2)}) collective-permute-start(bf16[1,24,3200]{2,1,0:T(8,128)(2,1)} %bitcast.28), channel_id=1, source_target_pairs={{0,16},{1,17},{2,18},{3,19},{4,20},{5,21},{6,22},{7,23},{8,24},{9,... | collective-permute-start | bytes 460808 | tf_op jit(solution)/shard_map/ppermute | solution.py:729
  13.3 9.9 %collective-permute-start.9 = (bf16[2,24,3200]{2,1,0:T(8,128)(2,1)S(1)}, bf16[2,24,3200]{2,1,0:T(8,128)(2,1)S(1)}, u32[]{:S(2)}, u32[]{:S(2)}) collective-permute-start(bf16[2,24,3200]{2,1,0:T(8,128)(2,1)S(1)} %pad_maximum_fusion.refs_0_), channel_id=1, source_target_pairs={{0,1},{1,0},{2,3},{3,2},{4,5},{5,4},{6,7},{7,6},{8,9},{9,8},{10,11... | collective-permute-start | bytes 921608 | tf_op jit(solution)/shard_map/ppermute | solution.py:729
  13.4 10.3 %collective-permute-start.5 = (bf16[2,24,3200]{2,1,0:T(8,128)(2,1)S(1)}, bf16[2,24,3200]{2,1,0:T(8,128)(2,1)S(1)}, u32[]{:S(2)}, u32[]{:S(2)}) collective-permute-start(bf16[2,24,3200]{2,1,0:T(8,128)(2,1)S(1)} %pad_maximum_fusion.refs_0_), channel_id=1, source_target_pairs={{0,4},{1,5},{2,6},{3,7},{4,0},{5,1},{6,2},{7,3},{8,12},{9,13},{10,... | collective-permute-start | bytes 921608 | tf_op jit(solution)/shard_map/ppermute | solution.py:729
  15.3 9.6 %collective-permute-start.3 = (bf16[2,24,3200]{2,1,0:T(8,128)(2,1)S(1)}, bf16[2,24,3200]{2,1,0:T(8,128)(2,1)S(1)}, u32[]{:S(2)}, u32[]{:S(2)}) collective-permute-start(bf16[2,24,3200]{2,1,0:T(8,128)(2,1)S(1)} %pad_maximum_fusion.refs_0_), channel_id=1, source_target_pairs={{0,2},{1,3},{2,0},{3,1},{4,6},{5,7},{6,4},{7,5},{8,10},{9,11},{10,... | collective-permute-start | bytes 921608 | tf_op jit(solution)/shard_map/ppermute | solution.py:729
  16.8 5.8 %collective-permute-start.2 = (bf16[1,24,3200]{2,1,0:T(8,128)(2,1)S(1)}, bf16[1,24,3200]{2,1,0:T(8,128)(2,1)S(1)}, u32[]{:S(2)}, u32[]{:S(2)}) collective-permute-start(bf16[1,24,3200]{2,1,0:T(8,128)(2,1)S(1)} %collective-permute-done.1), channel_id=1, source_target_pairs={{0,8},{1,9},{2,10},{3,11},{4,12},{5,13},{6,14},{7,15},{8,0},{9,1},... | collective-permute-start | bytes 460808 | tf_op jit(solution)/shard_map/ppermute | solution.py:729
  22.6 10.3 %collective-permute-start.4 = (bf16[2,24,3200]{2,1,0:T(8,128)(2,1)S(1)}, bf16[2,24,3200]{2,1,0:T(8,128)(2,1)S(1)}, u32[]{:S(2)}, u32[]{:S(2)}) collective-permute-start(bf16[2,24,3200]{2,1,0:T(8,128)(2,1)S(1)} %constant_dynamic-update-slice_fusion.refs_1_), channel_id=1, source_target_pairs={{0,2},{1,3},{2,0},{3,1},{4,6},{5,7},{6,4},{7,5},{8,10},{9,11},{10,... | collective-permute-start | bytes 921608 | tf_op jit(solution)/shard_map/ppermute | solution.py:729
  23.2 10.2 %collective-permute-start.10 = (bf16[2,24,3200]{2,1,0:T(8,128)(2,1)S(1)}, bf16[2,24,3200]{2,1,0:T(8,128)(2,1)S(1)}, u32[]{:S(2)}, u32[]{:S(2)}) collective-permute-start(bf16[2,24,3200]{2,1,0:T(8,128)(2,1)S(1)} %constant_dynamic-update-slice_fusion.refs_1_), channel_id=1, source_target_pairs={{0,1},{1,0},{2,3},{3,2},{4,5},{5,4},{6,7},{7,6},{8,9},{9,8},{10,11... | collective-permute-start | bytes 921608 | tf_op jit(solution)/shard_map/ppermute | solution.py:729
  23.2 10.2 %collective-permute-start.6 = (bf16[2,24,3200]{2,1,0:T(8,128)(2,1)S(1)}, bf16[2,24,3200]{2,1,0:T(8,128)(2,1)S(1)}, u32[]{:S(2)}, u32[]{:S(2)}) collective-permute-start(bf16[2,24,3200]{2,1,0:T(8,128)(2,1)S(1)} %constant_dynamic-update-slice_fusion.refs_1_), channel_id=1, source_target_pairs={{0,4},{1,5},{2,6},{3,7},{4,0},{5,1},{6,2},{7,3},{8,12},{9,13},{10,... | collective-permute-start | bytes 921608 | tf_op jit(solution)/shard_map/ppermute | solution.py:729
  23.7 10.2 %collective-permute-start.13 = (bf16[2,24,3200]{2,1,0:T(8,128)(2,1)S(1)}, bf16[2,24,3200]{2,1,0:T(8,128)(2,1)S(1)}, u32[]{:S(2)}, u32[]{:S(2)}) collective-permute-start(bf16[2,24,3200]{2,1,0:T(8,128)(2,1)S(1)} %collective-permute-done.5.refs_4_), channel_id=1, source_target_pairs={{0,1},{1,0},{2,3},{3,2},{4,5},{5,4},{6,7},{7,6},{8,9},{9,8},{10,11... | collective-permute-start | bytes 921608 | tf_op jit(solution)/shard_map/ppermute | solution.py:729
  25.0 12.9 %collective-permute-start.7 = (bf16[2,24,3200]{2,1,0:T(8,128)(2,1)S(1)}, bf16[2,24,3200]{2,1,0:T(8,128)(2,1)S(1)}, u32[]{:S(2)}, u32[]{:S(2)}) collective-permute-start(bf16[2,24,3200]{2,1,0:T(8,128)(2,1)S(1)} %collective-permute-done.5.refs_4_), channel_id=1, source_target_pairs={{0,2},{1,3},{2,0},{3,1},{4,6},{5,7},{6,4},{7,5},{8,10},{9,11},{10,... | collective-permute-start | bytes 921608 | tf_op jit(solution)/shard_map/ppermute | solution.py:729
  32.9 6.9 %collective-permute-start.8 = (bf16[2,24,3200]{2,1,0:T(8,128)(2,1)S(1)}, bf16[2,24,3200]{2,1,0:T(8,128)(2,1)S(1)}, u32[]{:S(2)}, u32[]{:S(2)}) collective-permute-start(bf16[2,24,3200]{2,1,0:T(8,128)(2,1)S(1)} %collective-permute-done.4.refs_3_), channel_id=1, source_target_pairs={{0,4},{1,5},{2,6},{3,7},{4,0},{5,1},{6,2},{7,3},{8,12},{9,13},{10,... | collective-permute-start | bytes 921608 | tf_op jit(solution)/shard_map/ppermute | solution.py:729
  33.4 6.4 %collective-permute-start.11 = (bf16[2,24,3200]{2,1,0:T(8,128)(2,1)S(1)}, bf16[2,24,3200]{2,1,0:T(8,128)(2,1)S(1)}, u32[]{:S(2)}, u32[]{:S(2)}) collective-permute-start(bf16[2,24,3200]{2,1,0:T(8,128)(2,1)S(1)} %collective-permute-done.3.refs_2_), channel_id=1, source_target_pairs={{0,1},{1,0},{2,3},{3,2},{4,5},{5,4},{6,7},{7,6},{8,9},{9,8},{10,11... | collective-permute-start | bytes 921608 | tf_op jit(solution)/shard_map/ppermute | solution.py:729
  33.4 6.4 %collective-permute-start.12 = (bf16[2,24,3200]{2,1,0:T(8,128)(2,1)S(1)}, bf16[2,24,3200]{2,1,0:T(8,128)(2,1)S(1)}, u32[]{:S(2)}, u32[]{:S(2)}) collective-permute-start(bf16[2,24,3200]{2,1,0:T(8,128)(2,1)S(1)} %collective-permute-done.4.refs_3_), channel_id=1, source_target_pairs={{0,1},{1,0},{2,3},{3,2},{4,5},{5,4},{6,7},{7,6},{8,9},{9,8},{10,11... | collective-permute-start | bytes 921608 | tf_op jit(solution)/shard_map/ppermute | solution.py:729
  33.9 5.8 %collective-permute-start.14 = (bf16[2,24,3200]{2,1,0:T(8,128)(2,1)S(1)}, bf16[2,24,3200]{2,1,0:T(8,128)(2,1)S(1)}, u32[]{:S(2)}, u32[]{:S(2)}) collective-permute-start(bf16[2,24,3200]{2,1,0:T(8,128)(2,1)S(1)} %collective-permute-done.6.refs_5_), channel_id=1, source_target_pairs={{0,1},{1,0},{2,3},{3,2},{4,5},{5,4},{6,7},{7,6},{8,9},{9,8},{10,11... | collective-permute-start | bytes 921608 | tf_op jit(solution)/shard_map/ppermute | solution.py:729
  37.8 2.0 %collective-permute-start.15 = (bf16[2,24,3200]{2,1,0:T(8,128)(2,1)S(1)}, bf16[2,24,3200]{2,1,0:T(8,128)(2,1)S(1)}, u32[]{:S(2)}, u32[]{:S(2)}) collective-permute-start(bf16[2,24,3200]{2,1,0:T(8,128)(2,1)S(1)} %collective-permute-done.7.refs_6_), channel_id=1, source_target_pairs={{0,1},{1,0},{2,3},{3,2},{4,5},{5,4},{6,7},{7,6},{8,9},{9,8},{10,11... | collective-permute-start | bytes 921608 | tf_op jit(solution)/shard_map/ppermute | solution.py:729
  39.7 1.6 %collective-permute-start.16 = (bf16[2,24,3200]{2,1,0:T(8,128)(2,1)S(1)}, bf16[2,24,3200]{2,1,0:T(8,128)(2,1)S(1)}, u32[]{:S(2)}, u32[]{:S(2)}) collective-permute-start(bf16[2,24,3200]{2,1,0:T(8,128)(2,1)S(1)} %collective-permute-done.8.refs_7_), channel_id=1, source_target_pairs={{0,1},{1,0},{2,3},{3,2},{4,5},{5,4},{6,7},{7,6},{8,9},{9,8},{10,11... | collective-permute-start | bytes 921608 | tf_op jit(solution)/shard_map/ppermute | solution.py:729
  53.6 5.8 %collective-permute-start.19 = (bf16[1,16,768]{2,1,0:T(8,128)(2,1)S(1)}, bf16[1,16,768]{2,1,0:T(8,128)(2,1)S(1)}, u32[]{:S(2)}, u32[]{:S(2)}) collective-permute-start(bf16[1,16,768]{2,1,0:T(8,128)(2,1)S(1)} %bitcast.23), channel_id=1, source_target_pairs={{0,24},{1,25},{2,26},{3,27},{4,28},{5,29},{6,30},{7,31},{8,16},{9,... | collective-permute-start | bytes 73736 | tf_op jit(solution)/shard_map/ppermute | solution.py:729
  56.4 4.7 %collective-permute-start.18 = (bf16[1,16,768]{2,1,0:T(8,128)(2,1)S(1)}, bf16[1,16,768]{2,1,0:T(8,128)(2,1)S(1)}, u32[]{:S(2)}, u32[]{:S(2)}) collective-permute-start(bf16[1,16,768]{2,1,0:T(8,128)(2,1)S(1)} %bitcast.24), channel_id=1, source_target_pairs={{0,16},{1,17},{2,18},{3,19},{4,20},{5,21},{6,22},{7,23},{8,24},{9,... | collective-permute-start | bytes 73736 | tf_op jit(solution)/shard_map/ppermute | solution.py:729
  56.4 4.7 %collective-permute-start.17 = (bf16[1,16,768]{2,1,0:T(8,128)(2,1)S(1)}, bf16[1,16,768]{2,1,0:T(8,128)(2,1)S(1)}, u32[]{:S(2)}, u32[]{:S(2)}) collective-permute-start(bf16[1,16,768]{2,1,0:T(8,128)(2,1)S(1)} %bitcast.25), channel_id=1, source_target_pairs={{0,8},{1,9},{2,10},{3,11},{4,12},{5,13},{6,14},{7,15},{8,0},{9,1},... | collective-permute-start | bytes 73736 | tf_op jit(solution)/shard_map/ppermute | solution.py:729
  61.2 5.9 %collective-permute-start.22 = (bf16[4,16,768]{2,1,0:T(8,128)(2,1)S(1)}, bf16[4,16,768]{2,1,0:T(8,128)(2,1)S(1)}, u32[]{:S(2)}, u32[]{:S(2)}) collective-permute-start(bf16[4,16,768]{2,1,0:T(8,128)(2,1)S(1)} %pad_maximum_fusion.1.refs_0_), channel_id=1, source_target_pairs={{0,6},{1,7},{2,4},{3,5},{4,2},{5,3},{6,0},{7,1},{8,14},{9,15},{10,... | collective-permute-start | bytes 294920 | tf_op jit(solution)/shard_map/ppermute | solution.py:729
  62.7 5.4 %collective-permute-start.21 = (bf16[4,16,768]{2,1,0:T(8,128)(2,1)S(1)}, bf16[4,16,768]{2,1,0:T(8,128)(2,1)S(1)}, u32[]{:S(2)}, u32[]{:S(2)}) collective-permute-start(bf16[4,16,768]{2,1,0:T(8,128)(2,1)S(1)} %pad_maximum_fusion.1.refs_0_), channel_id=1, source_target_pairs={{0,4},{1,5},{2,6},{3,7},{4,0},{5,1},{6,2},{7,3},{8,12},{9,13},{10,... | collective-permute-start | bytes 294920 | tf_op jit(solution)/shard_map/ppermute | solution.py:729
  64.2 4.6 %collective-permute-start.20 = (bf16[4,16,768]{2,1,0:T(8,128)(2,1)S(1)}, bf16[4,16,768]{2,1,0:T(8,128)(2,1)S(1)}, u32[]{:S(2)}, u32[]{:S(2)}) collective-permute-start(bf16[4,16,768]{2,1,0:T(8,128)(2,1)S(1)} %pad_maximum_fusion.1.refs_0_), channel_id=1, source_target_pairs={{0,2},{1,3},{2,0},{3,1},{4,6},{5,7},{6,4},{7,5},{8,10},{9,11},{10,... | collective-permute-start | bytes 294920 | tf_op jit(solution)/shard_map/ppermute | solution.py:729
  64.7 4.1 %collective-permute-start.23 = (bf16[4,16,768]{2,1,0:T(8,128)(2,1)S(1)}, bf16[4,16,768]{2,1,0:T(8,128)(2,1)S(1)}, u32[]{:S(2)}, u32[]{:S(2)}) collective-permute-start(bf16[4,16,768]{2,1,0:T(8,128)(2,1)S(1)} %pad_maximum_fusion.1.refs_0_), channel_id=1, source_target_pairs={{0,1},{1,0},{2,3},{3,2},{4,5},{5,4},{6,7},{7,6},{8,9},{9,8},{10,11... | collective-permute-start | bytes 294920 | tf_op jit(solution)/shard_map/ppermute | solution.py:729
  67.0 1.8 %collective-permute-start.26 = (bf16[4,16,768]{2,1,0:T(8,128)(2,1)S(1)}, bf16[4,16,768]{2,1,0:T(8,128)(2,1)S(1)}, u32[]{:S(2)}, u32[]{:S(2)}) collective-permute-start(bf16[4,16,768]{2,1,0:T(8,128)(2,1)S(1)} %collective-permute-done.22.refs_3_), channel_id=1, source_target_pairs={{0,1},{1,0},{2,3},{3,2},{4,5},{5,4},{6,7},{7,6},{8,9},{9,8},{10,11... | collective-permute-start | bytes 294920 | tf_op jit(solution)/shard_map/ppermute | solution.py:729
  68.0 1.3 collective-permute-start.25
  68.8 1.3 collective-permute-start.24
  72.7 1.8 %collective-permute-start.27 = (bf16[16,16,768]{2,1,0:T(8,128)(2,1)S(1)}, bf16[16,16,768]{2,1,0:T(8,128)(2,1)S(1)}, u32[]{:S(2)}, u32[]{:S(2)}) collective-permute-start(bf16[16,16,768]{2,1,0:T(8,128)(2,1)S(1)} %get-tuple-element.97), channel_id=1, source_target_pairs={{0,1},{1,0},{2,3},{3,2},{4,5},{5,4},{6,7},{7,6},{8,9},{9,8},{10,11... | collective-permute-start | bytes 1179656 | tf_op jit(solution)/shard_map/ppermute | solution.py:729
  74.7 5.9 %collective-permute-start.28 = (bf16[4,16,768]{2,1,0:T(8,128)(2,1)S(1)}, bf16[4,16,768]{2,1,0:T(8,128)(2,1)S(1)}, u32[]{:S(2)}, u32[]{:S(2)}) collective-permute-start(bf16[4,16,768]{2,1,0:T(8,128)(2,1)S(1)} %get-tuple-element.99), channel_id=1, source_target_pairs={{0,2},{1,3},{2,0},{3,1},{4,6},{5,7},{6,4},{7,5},{8,10},{9,11},{10,... | collective-permute-start | bytes 294920 | tf_op jit(solution)/shard_map/ppermute | solution.py:729
  75.3 6.7 %collective-permute-start.29 = (bf16[4,16,768]{2,1,0:T(8,128)(2,1)S(1)}, bf16[4,16,768]{2,1,0:T(8,128)(2,1)S(1)}, u32[]{:S(2)}, u32[]{:S(2)}) collective-permute-start(bf16[4,16,768]{2,1,0:T(8,128)(2,1)S(1)} %get-tuple-element.100), channel_id=1, source_target_pairs={{0,4},{1,5},{2,6},{3,7},{4,0},{5,1},{6,2},{7,3},{8,12},{9,13},{10,... | collective-permute-start | bytes 294920 | tf_op jit(solution)/shard_map/ppermute | solution.py:729
  76.2 5.8 %collective-permute-start.30 = (bf16[4,16,768]{2,1,0:T(8,128)(2,1)S(1)}, bf16[4,16,768]{2,1,0:T(8,128)(2,1)S(1)}, u32[]{:S(2)}, u32[]{:S(2)}) collective-permute-start(bf16[4,16,768]{2,1,0:T(8,128)(2,1)S(1)} %get-tuple-element.101), channel_id=1, source_target_pairs={{0,6},{1,7},{2,4},{3,5},{4,2},{5,3},{6,0},{7,1},{8,14},{9,15},{10,... | collective-permute-start | bytes 294920 | tf_op jit(solution)/shard_map/ppermute | solution.py:729
  82.0 7.0 %collective-permute-start.31 = (bf16[1,16,768]{2,1,0:T(8,128)(2,1)S(1)}, bf16[1,16,768]{2,1,0:T(8,128)(2,1)S(1)}, u32[]{:S(2)}, u32[]{:S(2)}) collective-permute-start(bf16[1,16,768]{2,1,0:T(8,128)(2,1)S(1)} %get-tuple-element.110), channel_id=1, source_target_pairs={{0,8},{1,9},{2,10},{3,11},{4,12},{5,13},{6,14},{7,15},{8,0},{9,1},... | collective-permute-start | bytes 73736 | tf_op jit(solution)/shard_map/ppermute | solution.py:729
  82.9 6.1 %collective-permute-start.32 = (bf16[1,16,768]{2,1,0:T(8,128)(2,1)S(1)}, bf16[1,16,768]{2,1,0:T(8,128)(2,1)S(1)}, u32[]{:S(2)}, u32[]{:S(2)}) collective-permute-start(bf16[1,16,768]{2,1,0:T(8,128)(2,1)S(1)} %get-tuple-element.111), channel_id=1, source_target_pairs={{0,16},{1,17},{2,18},{3,19},{4,20},{5,21},{6,22},{7,23},{8,24},{9,... | collective-permute-start | bytes 73736 | tf_op jit(solution)/shard_map/ppermute | solution.py:729
  84.2 5.6 %collective-permute-start.33 = (bf16[1,16,768]{2,1,0:T(8,128)(2,1)S(1)}, bf16[1,16,768]{2,1,0:T(8,128)(2,1)S(1)}, u32[]{:S(2)}, u32[]{:S(2)}) collective-permute-start(bf16[1,16,768]{2,1,0:T(8,128)(2,1)S(1)} %get-tuple-element.112), channel_id=1, source_target_pairs={{0,24},{1,25},{2,26},{3,27},{4,28},{5,29},{6,30},{7,31},{8,16},{9,... | collective-permute-start | bytes 73736 | tf_op jit(solution)/shard_map/ppermute | solution.py:729
  102.7 4.3 %collective-permute-start.34 = (bf16[16,24,1920]{2,1,0:T(8,128)(2,1)S(1)}, bf16[16,24,1920]{2,1,0:T(8,128)(2,1)S(1)}, u32[]{:S(2)}, u32[]{:S(2)}) collective-permute-start(bf16[16,24,1920]{2,1,0:T(8,128)(2,1)S(1)} %get-tuple-element.133), channel_id=1, source_target_pairs={{0,1},{1,0},{2,3},{3,2},{4,5},{5,4},{6,7},{7,6},{8,9},{9,8},{10,11... | collective-permute-start | bytes 4423688 | tf_op jit(solution)/shard_map/ppermute | solution.py:729
  107.3 11.1 %collective-permute-start.36 = (bf16[4,24,1920]{2,1,0:T(8,128)(2,1)S(1)}, bf16[4,24,1920]{2,1,0:T(8,128)(2,1)S(1)}, u32[]{:S(2)}, u32[]{:S(2)}) collective-permute-start(bf16[4,24,1920]{2,1,0:T(8,128)(2,1)S(1)} %get-tuple-element.136), channel_id=1, source_target_pairs={{0,2},{1,3},{2,0},{3,1},{4,6},{5,7},{6,4},{7,5},{8,10},{9,11},{10,... | collective-permute-start | bytes 1105928 | tf_op jit(solution)/shard_map/ppermute | solution.py:729
  108.9 10.7 %collective-permute-start.35 = (bf16[4,24,1920]{2,1,0:T(8,128)(2,1)S(1)}, bf16[4,24,1920]{2,1,0:T(8,128)(2,1)S(1)}, u32[]{:S(2)}, u32[]{:S(2)}) collective-permute-start(bf16[4,24,1920]{2,1,0:T(8,128)(2,1)S(1)} %get-tuple-element.137), channel_id=1, source_target_pairs={{0,4},{1,5},{2,6},{3,7},{4,0},{5,1},{6,2},{7,3},{8,12},{9,13},{10,... | collective-permute-start | bytes 1105928 | tf_op jit(solution)/shard_map/ppermute | solution.py:729
  119.7 2.6 %collective-permute-start.37 = (bf16[16,24,1280]{2,1,0:T(8,128)(2,1)S(1)}, bf16[16,24,1280]{2,1,0:T(8,128)(2,1)S(1)}, u32[]{:S(2)}, u32[]{:S(2)}) collective-permute-start(bf16[16,24,1280]{2,1,0:T(8,128)(2,1)S(1)} %get-tuple-element.150), channel_id=1, source_target_pairs={{0,1},{1,0},{2,3},{3,2},{4,5},{5,4},{6,7},{7,6},{8,9},{9,8},{10,11... | collective-permute-start | bytes 2949128 | tf_op jit(solution)/shard_map/ppermute | solution.py:729
  119.8 8.9 %collective-permute-start.38 = (bf16[2,24,1920]{2,1,0:T(8,128)(2,1)S(1)}, bf16[2,24,1920]{2,1,0:T(8,128)(2,1)S(1)}, u32[]{:S(2)}, u32[]{:S(2)}) collective-permute-start(bf16[2,24,1920]{2,1,0:T(8,128)(2,1)S(1)} %get-tuple-element.148), channel_id=1, source_target_pairs={{0,4},{1,5},{2,6},{3,7},{4,0},{5,1},{6,2},{7,3},{8,12},{9,13},{10,... | collective-permute-start | bytes 552968 | tf_op jit(solution)/shard_map/ppermute | solution.py:729
  120.7 13.0 %collective-permute-start.39 = (bf16[2,24,1920]{2,1,0:T(8,128)(2,1)S(1)}, bf16[2,24,1920]{2,1,0:T(8,128)(2,1)S(1)}, u32[]{:S(2)}, u32[]{:S(2)}) collective-permute-start(bf16[2,24,1920]{2,1,0:T(8,128)(2,1)S(1)} %get-tuple-element.147), channel_id=1, source_target_pairs={{0,2},{1,3},{2,0},{3,1},{4,6},{5,7},{6,4},{7,5},{8,10},{9,11},{10,... | collective-permute-start | bytes 552968 | tf_op jit(solution)/shard_map/ppermute | solution.py:729
  122.6 10.1 %collective-permute-start.42 = (bf16[4,24,1280]{2,1,0:T(8,128)(2,1)S(1)}, bf16[4,24,1280]{2,1,0:T(8,128)(2,1)S(1)}, u32[]{:S(2)}, u32[]{:S(2)}) collective-permute-start(bf16[4,24,1280]{2,1,0:T(8,128)(2,1)S(1)} %get-tuple-element.153), channel_id=1, source_target_pairs={{0,2},{1,3},{2,0},{3,1},{4,6},{5,7},{6,4},{7,5},{8,10},{9,11},{10,... | collective-permute-start | bytes 737288 | tf_op jit(solution)/shard_map/ppermute | solution.py:729
  123.1 9.5 %collective-permute-start.43 = (bf16[4,24,1280]{2,1,0:T(8,128)(2,1)S(1)}, bf16[4,24,1280]{2,1,0:T(8,128)(2,1)S(1)}, u32[]{:S(2)}, u32[]{:S(2)}) collective-permute-start(bf16[4,24,1280]{2,1,0:T(8,128)(2,1)S(1)} %get-tuple-element.154), channel_id=1, source_target_pairs={{0,4},{1,5},{2,6},{3,7},{4,0},{5,1},{6,2},{7,3},{8,12},{9,13},{10,... | collective-permute-start | bytes 737288 | tf_op jit(solution)/shard_map/ppermute | solution.py:729
  132.7 4.9 %collective-permute-start.45 = (bf16[2,24,1280]{2,1,0:T(8,128)(2,1)S(1)}, bf16[2,24,1280]{2,1,0:T(8,128)(2,1)S(1)}, u32[]{:S(2)}, u32[]{:S(2)}) collective-permute-start(bf16[2,24,1280]{2,1,0:T(8,128)(2,1)S(1)} %get-tuple-element.163), channel_id=1, source_target_pairs={{0,2},{1,3},{2,0},{3,1},{4,6},{5,7},{6,4},{7,5},{8,10},{9,11},{10,... | collective-permute-start | bytes 368648 | tf_op jit(solution)/shard_map/ppermute | solution.py:729
  133.7 6.5 %collective-permute-start.40 = (bf16[2,24,1920]{2,1,0:T(8,128)(2,1)S(1)}, bf16[2,24,1920]{2,1,0:T(8,128)(2,1)S(1)}, u32[]{:S(2)}, u32[]{:S(2)}) collective-permute-start(bf16[2,24,1920]{2,1,0:T(8,128)(2,1)S(1)} %shard_map.217), channel_id=1, source_target_pairs={{0,8},{1,9},{2,10},{3,11},{4,12},{5,13},{6,14},{7,15},{8,0},{9,1},... | collective-permute-start | bytes 552968 | tf_op jit(solution)/shard_map/ppermute | solution.py:729
  133.9 7.5 %collective-permute-start.44 = (bf16[2,24,1280]{2,1,0:T(8,128)(2,1)S(1)}, bf16[2,24,1280]{2,1,0:T(8,128)(2,1)S(1)}, u32[]{:S(2)}, u32[]{:S(2)}) collective-permute-start(bf16[2,24,1280]{2,1,0:T(8,128)(2,1)S(1)} %get-tuple-element.162), channel_id=1, source_target_pairs={{0,4},{1,5},{2,6},{3,7},{4,0},{5,1},{6,2},{7,3},{8,12},{9,13},{10,... | collective-permute-start | bytes 368648 | tf_op jit(solution)/shard_map/ppermute | solution.py:729
  137.7 5.8 %collective-permute-start.46 = (bf16[2,24,1280]{2,1,0:T(8,128)(2,1)S(1)}, bf16[2,24,1280]{2,1,0:T(8,128)(2,1)S(1)}, u32[]{:S(2)}, u32[]{:S(2)}) collective-permute-start(bf16[2,24,1280]{2,1,0:T(8,128)(2,1)S(1)} %shard_map.220), channel_id=1, source_target_pairs={{0,8},{1,9},{2,10},{3,11},{4,12},{5,13},{6,14},{7,15},{8,0},{9,1},... | collective-permute-start | bytes 368648 | tf_op jit(solution)/shard_map/ppermute | solution.py:729
  140.3 7.5 %collective-permute-start.41 = (bf16[1,24,1920]{2,1,0:T(8,128)(2,1)S(1)}, bf16[1,24,1920]{2,1,0:T(8,128)(2,1)S(1)}, u32[]{:S(2)}, u32[]{:S(2)}) collective-permute-start(bf16[1,24,1920]{2,1,0:T(8,128)(2,1)S(1)} %get-tuple-element.159), channel_id=1, source_target_pairs={{0,16},{1,17},{2,18},{3,19},{4,20},{5,21},{6,22},{7,23},{8,24},{9,... | collective-permute-start | bytes 276488 | tf_op jit(solution)/shard_map/ppermute | solution.py:729
  144.2 5.4 %collective-permute-start.47 = (bf16[1,24,1280]{2,1,0:T(8,128)(2,1)S(1)}, bf16[1,24,1280]{2,1,0:T(8,128)(2,1)S(1)}, u32[]{:S(2)}, u32[]{:S(2)}) collective-permute-start(bf16[1,24,1280]{2,1,0:T(8,128)(2,1)S(1)} %get-tuple-element.165), channel_id=1, source_target_pairs={{0,16},{1,17},{2,18},{3,19},{4,20},{5,21},{6,22},{7,23},{8,24},{9,... | collective-permute-start | bytes 184328 | tf_op jit(solution)/shard_map/ppermute | solution.py:729
  (25 other events, 261.5 us)

commit v4 on v3

--- a/solution.py
+++ b/solution.py
@@ -40,6 +40,10 @@
     return pl.BlockSpec(memory_space=pltpu.VMEM)
 
 
+def anywhere():
+    return pl.BlockSpec(memory_space=pl.ANY)
+
+
 def hbm():
     return pl.BlockSpec(memory_space=pltpu.HBM)
 
@@ -48,7 +52,7 @@
     return pl.BlockSpec(memory_space=pltpu.SMEM)
 
 
-def call(body, outs, scratch, limit_mib, flops=0, far_in=(), far_out=(), sems=0):
+def call(body, outs, scratch, limit_mib, flops=0, far_in=(), any_in=(), far_out=(), sems=0):
     def run(scalars, *args):
         return pl.pallas_call(
             body,
@@ -56,7 +60,8 @@
                 pltpu.HBM(s, d) if i in far_out else jax.ShapeDtypeStruct(s, d)
                 for i, (s, d) in enumerate(outs)
             ],
-            in_specs=[smem()] + [hbm() if i in far_in else vmem() for i in range(len(args))],
+            in_specs=[smem()]
+            + [hbm() if i in far_in else anywhere() if i in any_in else vmem() for i in range(len(args))],
             out_specs=[hbm() if i in far_out else vmem() for i in range(len(outs))],
             scratch_shapes=[pltpu.VMEM(s, d) for s, d in scratch]
             + ([pltpu.SemaphoreType.DMA((sems,))] if sems else []),
@@ -104,7 +109,14 @@
 
 
 def pack_kernel(width, experts):
-    def body(in_ref, out_ref, ns_ref, nb_ref, ms_ref, mb_ref, slot_ref, pack_ref, square):
+    def body(*refs):
+        given, pack_ref, square, here, sems = refs[:7], refs[7], refs[8], refs[9:16], refs[16]
+        loads = [pltpu.make_async_copy(a, b, sems.at[i]) for i, (a, b) in enumerate(zip(given, here))]
+        for load in loads:
+            load.start()
+        for load in loads:
+            load.wait()
+        in_ref, out_ref, ns_ref, nb_ref, ms_ref, mb_ref, slot_ref = here
         pack_ref[:, : 3 * width] = in_ref[...]
         pack_ref[:, 3 * width : 4 * width] = out_ref[...]
         rows = in_ref.shape[0]
@@ -164,66 +176,16 @@
     return jnp.sum(total, axis=0, keepdims=True)
 
 
-def cut_scaled(chips, part_rows, tile, sums, w_ref, col_ref, small_ref, outs, first):
-    count = tile.shape[1]
-    rows = 2 * part_rows if len(outs) == 2 else 48
-    lane = lax.broadcasted_iota(jnp.int32, (1, LANES), 1)
-
-    def step(at, write):
-        gain = col_ref[at, 0:1].astype(f32)
-        shift = col_ref[at, 1:2].astype(f32)
-        by_gain = jnp.zeros((rows, LANES), f32)
-        by_shift = jnp.zeros((rows, LANES), f32)
-        for c0 in range(0, count, LANES):
-            c1 = c0 + LANES
-            value, weight = tile[at, c0:c1], w_ref[at, c0:c1].astype(f32)
-            by_gain = by_gain + value * weight
-            by_shift = by_shift + sums[:, c0:c1] * weight
-            write(c0, c1, value * gain + shift * sums[:, c0:c1])
-        by_gain = jnp.sum(by_gain, axis=1, keepdims=True)
-        by_shift = jnp.sum(by_shift, axis=1, keepdims=True)
-        small_ref[at] = small_ref[at] + jnp.where(lane == 0, by_gain, jnp.where(lane == 1, by_shift, 0.0))
-
-    if len(outs) == 1:
-
-        @pl.loop(0, tile.shape[0] // rows)
-        def _(i):
-            at = rows_at(i, rows)
-
-            def write(c0, c1, value):
-                outs[0][at, first + c0 : first + c1] = value
-
-            step(at, write)
-
-        return
-    for own_first in (True, False):
-
-        @pl.when(lax.axis_index("fsdp") % 2 == (0 if own_first else 1))
-        def _():
-            low_ref, high_ref = outs if own_first else outs[::-1]
-
-            @pl.loop(0, chips, unroll=2)
-            def _(f):
-                at = rows_at(scattered_chip(f, chips), rows)
-
-                def write(c0, c1, value):
-                    low_ref[f, :, first + c0 : first + c1] = value[:part_rows].astype(bf16)
-                    high_ref[f, :, first + c0 : first + c1] = value[part_rows:].astype(bf16)
-
-                step(at, write)
-
-
-def weight_loads(width, half, w_in, w_ref, col_ref, sems):
+def weight_loads(width, w_in, w_ref, sems):
     part = width // 2
-    loads = [
-        pltpu.make_async_copy(
-            w_in.at[:, i * width + half * part : i * width + (half + 1) * part],
-            w_ref.at[:, i * part : (i + 1) * part],
-            sems.at[i],
+    loads = []
+    for i in range(6):
+        first = (i % 3) * width + (i // 3) * part
+        loads.append(
+            pltpu.make_async_copy(
+                w_in.at[:, first : first + part], w_ref.at[:, i * part : (i + 1) * part], sems.at[i]
+            )
         )
-        for i in range(3)
-    ]
-    loads.append(pltpu.make_async_copy(w_in.at[:, 4 * width : 4 * width + LANES], col_ref, sems.at[3]))
     return loads
 
 
@@ -453,6 +415,14 @@
             gj[span, at_v] = tn(low, grad).astype(bf16)
 
 
+def sums_lanes(width, part_rows):
+    return slice(8, 8 + 3 * width // part_rows)
+
+
+def small_lanes(width, part_rows):
+    return -(-sums_lanes(width, part_rows).stop // LANES) * LANES
+
+
 def half_loads(width, half, joint_in, joint_ref, probs_in, probs_ref, sems):
     part, share = width // 2, HEADS // 4
     loads = [
@@ -497,9 +467,9 @@
     share = HEADS // 4
 
     def body(meta, cot_ref, par_ref, log_ref, sum_ref, r1_ref, r2_ref, r3_ref, xn_ref, dev_ref, n2_ref, w_in, xh_in,
-             joint_in, probs_in, mixed_in, res_in, block_ref, xgrad_ref, gm, gj, grads, part_ref, xh_ref, w_half,
+             joint_in, probs_in, mixed_in, res_in, block_ref, xgrad_ref, gm, gj, grads, sums_ref, xh_ref,
              joint_late, probs_late, *refs):
-        outs, (gn, gb, tile, small, w_ref, joint_ref, probs_ref, mixed_ref, res_ref, col_ref, sems) = refs[:-11], refs[-11:]
+        outs, (gn, gb, tile, small, w_ref, joint_ref, probs_ref, mixed_ref, res_ref, sems) = refs[:-10], refs[-10:]
         early = [pltpu.make_async_copy(res_in, res_ref, sems.at[0])]
         late = [
             pltpu.make_async_copy(mixed_in, mixed_ref, sems.at[1]),
@@ -507,8 +477,7 @@
         ]
         loads = half_loads(width, 0, joint_in, joint_ref, probs_in, probs_ref, sems.at[3:7])
         last = [pltpu.make_async_copy(xh_in, xh_ref, sems.at[7])]
-        last += weight_loads(width, 0, w_in, w_half, col_ref, sems.at[8:12])
-        ahead = half_loads(width, 1, joint_in, joint_late, probs_in, probs_late, sems.at[12:16])
+        ahead = half_loads(width, 1, joint_in, joint_late, probs_in, probs_late, sems.at[8:12])
         for load in early + late + loads + last + ahead:
             load.start()
 
@@ -578,8 +547,8 @@
         for load in last:
             load.wait()
         tile[...] = tn(xh_ref[...], gj[...])
-        part_ref[...] = jnp.zeros_like(part_ref)
-        cut_scaled(chips, part_rows, tile, column_sums(gj), w_half, col_ref, part_ref, outs, width)
+        sums_ref[0:1] = column_sums(gj)
+        put(width, 3 * width // 2)
         for load in ahead:
             load.wait()
 
@@ -589,13 +558,8 @@
 def heads_pull_kernel(sizes):
     width = sizes[2]
 
-    def body(meta, gm_ref, joint_ref, probs_ref, w_in, gj, w_half, col_ref, sems):
-        loads = weight_loads(width, 1, w_in, w_half, col_ref, sems)
-        for load in loads:
-            load.start()
+    def body(meta, gm_ref, joint_ref, probs_ref, gj):
         attend_pull(meta, sizes, 1, joint_ref, probs_ref, gm_ref, gj)
-        for load in loads:
-            load.wait()
 
     return body
 
@@ -604,16 +568,33 @@
     images, rows, width, experts, chips, part_rows, shares = sizes
     half = 3 * width // 2
 
-    def body(meta, gj, grads, part_ref, w_half, col_ref, xh_ref, *refs):
-        outs, (tile, small) = refs[:-2], refs[-2:]
-        filled = jnp.concatenate([grads[...], jnp.zeros((LANES - 8, width), f32)], axis=0)
-        small[...] = part_ref[...] + filled.T
+    def body(meta, gj, grads, sums_ref, xh_ref, w_in, w_ref, *refs):
+        outs, (tile, small, sems) = refs[:-3], refs[-3:]
+        loads = weight_loads(width, w_in, w_ref, sems)
+        for load in loads:
+            load.start()
+        sums = [sums_ref[0:1], column_sums(gj)]
+        wide = sums_lanes(width, part_rows)
+        small[:, :LANES] = jnp.concatenate([grads[...], jnp.zeros((LANES - 8, width), f32)], axis=0).T
+        each = 3 * width // part_rows
+        for r in range(part_rows):
+            row = [s[:, c0 - i * half : c1 - i * half] for i, s in enumerate(sums)
+                   for c0, c1 in [(max(r * each, i * half), min((r + 1) * each, (i + 1) * half))] if c0 < c1]
+            small[r : r + 1, wide] = jnp.concatenate(row, axis=1)
+        for t in range(1, width // part_rows):
+            small[t * part_rows : (t + 1) * part_rows, wide] = small[:part_rows, wide]
         tile[...] = tn(xh_ref[...], gj[...])
-        cut_scaled(chips, part_rows, tile, column_sums(gj), w_half, col_ref, small, outs, 0)
-        if shares:
-            cut(meta, images, chips, part_rows, small, LANES, *outs, half)
-        else:
-            outs[0][:, half : half + LANES] = small[...]
+
+        def put(ref, count, first):
+            if shares:
+                cut(meta, images, chips, part_rows, ref, count, *outs, first)
+            else:
+                outs[0][:, first : first + count] = ref[:, :count]
+
+        put(tile, half, 0)
+        put(small, small.shape[1], half)
+        for load in loads:
+            load.wait()
 
     return body
 
@@ -623,8 +604,8 @@
     total = images * rows
     half = 3 * width // 2
 
-    def body(meta, x_ref, par_ref, gj0_ref, gj1_ref, w0_ref, w1_ref, part_ref, xgrad_ref, gn):
-        gn[...] = nt(gj0_ref[...], w0_ref[...]) + nt(gj1_ref[...], w1_ref[...])
+    def body(meta, x_ref, par_ref, gj0_ref, gj1_ref, w_ref, part_ref, xgrad_ref, gn):
+        gn[...] = nt(gj0_ref[...], w_ref[:, :half]) + nt(gj1_ref[...], w_ref[:, half:])
         gain_a = par_ref[0:1]
 
         @pl.loop(0, total // CHUNK, unroll=UNROLL)
@@ -692,24 +673,42 @@
     return run
 
 
-def finish_kernel(width, experts):
+def finish_kernel(width, experts, part_rows):
     half = width // 2
-
-    def body(a0, a1, b0, b1, out_ref, in_ref, ns_ref, nb_ref, ms_ref, mb_ref, slot_ref, square):
+    wide = sums_lanes(width, part_rows)
+
+    def body(a0, a1, b0, b1, w_ref, gain_ref, shift_ref, out_ref, in_ref, ns_ref, nb_ref, ms_ref, mb_ref, slot_ref,
+             square, sums):
         first = a0[0] + a1[0].astype(f32)
         second = b0[0] + b1[0].astype(f32)
-        rows = first.shape[0]
         out_ref[...] = first[:, :width]
+        small = second[:, 3 * half :]
+        each = 3 * width // part_rows
+        for r in range(part_rows):
+            sums[0:1, r * each : (r + 1) * each] = small[r : r + 1, wide]
+        square[...] = jnp.zeros_like(square)
+        square[0:1, :part_rows] = gain_ref[...].astype(f32)
+        square[1:2, :part_rows] = shift_ref[...].astype(f32)
+        turned = square[...].T
+        gain, shift = turned[:part_rows, 0:1], turned[:part_rows, 1:2]
+        by_gain = jnp.zeros((part_rows, half), f32)
+        by_shift = jnp.zeros((part_rows, half), f32)
         for i in range(3):
-            in_ref[:, i * width : i * width + half] = first[:, width + i * half : width + (i + 1) * half]
-            in_ref[:, i * width + half : (i + 1) * width] = second[:, i * half : (i + 1) * half]
-        small = second[:, 3 * half : 3 * half + LANES]
-        square[...] = jnp.zeros_like(square)
-        square[:rows] = small
+            for j, value in enumerate((first[:, width + i * half : width + (i + 1) * half], second[:, i * half : (i + 1) * half])):
+                at = slice(i * width + j * half, i * width + (j + 1) * half)
+                total = sums[0:1, (j * 3 + i) * half : (j * 3 + i + 1) * half]
+                weight = w_ref[:, at].astype(f32)
+                in_ref[:, at] = value * gain + shift * total
+                by_gain = by_gain + value * weight
+                by_shift = by_shift + total * weight
+        lane = lax.broadcasted_iota(jnp.int32, (1, LANES), 1)
+        small = jnp.where(lane == 0, jnp.sum(by_gain, axis=1, keepdims=True), small[:, :LANES])
+        small = jnp.where(lane == 1, jnp.sum(by_shift, axis=1, keepdims=True), small)
+        square[:part_rows] = small
         turned = square[...].T
         for i, ref in enumerate((ns_ref, nb_ref, ms_ref, mb_ref)):
-            ref[...] = turned[i : i + 1, :rows]
-        slot_ref[...] = turned[4 : 4 + experts, :rows]
+            ref[...] = turned[i : i + 1, :part_rows]
+        slot_ref[...] = turned[4 : 4 + experts, :part_rows]
 
     return body
 
@@ -788,11 +787,11 @@
     z0, z1, x1, y0, from_x, from_y = parts
     from_x1, from_y0 = swap(x1, devices, 1, 0), swap(y0, devices, 2, 0)
     (z1,) = add_kernel([[[(0, 0), (1, 0), (2, 2)]]], [bf16])(z1, from_x1, from_y)
-    return z0, from_x, from_y0, swap(z1, devices, 4, 0)
+    return z0, from_x, from_y0, swap(z1, devices, 4, 0), z1
 
 
 def scatter_end(parts, devices):
-    z0, from_x, from_y0, from_z1 = parts
+    z0, from_x, from_y0, from_z1, _ = parts
     keep, send = add_kernel(
         [[[(0, i), (1, 2 + i), (2, i), (3, i)]] for i in range(2)], [f32, bf16], 1
     )(z0, from_x, from_y0, from_z1)
@@ -816,13 +815,17 @@
         x = images.reshape(total, width)
         cot = cotangent.reshape(total, width)
         vectors = [v.reshape(1, part_rows) for v in (norm_scale, norm_shift, mixer_scale, mixer_shift)]
+        given = [attend_in, attend_out, *vectors, slot_params.T]
         pack = pl.pallas_call(
             pack_kernel(width, experts),
             out_shape=jax.ShapeDtypeStruct((part_rows, wide), bf16),
-            in_specs=[vmem()] * 7,
+            in_specs=[hbm()] * 7,
             out_specs=vmem(),
-            scratch_shapes=[pltpu.VMEM((LANES, LANES), f32)],
-        )(attend_in, attend_out, *vectors, slot_params.T)
+            scratch_shapes=[pltpu.VMEM((LANES, LANES), f32)]
+            + [pltpu.VMEM(a.shape, bf16) for a in given]
+            + [pltpu.SemaphoreType.DMA((7,))],
+            compiler_params=pltpu.CompilerParams(vmem_limit_bytes=8 * MIB),
+        )(*[pltpu.with_memory_space_constraint(a, pltpu.HBM) for a in given])
         if shares:
             weights = gather_pieces(pack, devices)
         else:
@@ -849,7 +852,8 @@
             outs,
             scratch,
             40,
-            far_in=range(0, 2 + 2 * len(shares)),
+            far_in=range(2),
+            any_in=range(2, 2 + 2 * len(shares)),
             far_out=range(3, len(outs)),
             sems=10 + pairs + 2 * len(shares),
         )(meta, x, cot, *weights)
@@ -904,8 +908,7 @@
             far_in=range(2),
             sems=2,
         )(meta, res, n2)
-        columns = ((width, 3 * half), bf16)
-        block, part, gm, gj, early, tiny, xh, w0, joint1, probs1, *first = call(
+        block, part, gm, gj, early, sums, xh, joint1, probs1, *first = call(
             slots_pull_kernel(sizes),
             [
                 ((total, width), bf16),
@@ -913,9 +916,8 @@
                 ((total, width), bf16),
                 ((total, 3 * half), bf16),
                 ((8, width), f32),
-                ((width, LANES), f32),
+                ((8, 3 * half), f32),
                 ((total, width), bf16),
-                columns,
             ]
             + halves
             + blocks(width + 3 * half),
@@ -930,47 +932,42 @@
             + [
                 ((total, width), bf16),
                 ((total, width), f32),
-                ((width, LANES), bf16),
             ],
             VMEM_MIB,
             far_in=range(10, 16),
-            sems=16,
+            sems=12,
         )(meta, cot, par, logs, *terms, xn, dev, n2, w, xh, joint, probs, mixed, res)
-        gj1, w1, tail = call(
-            heads_pull_kernel(sizes),
-            [((total, 3 * half), bf16), columns, ((width, LANES), bf16)],
-            [],
-            VMEM_MIB,
-            flops=3 * 10**9,
-            far_in=range(3, 4),
-            sems=4,
-        )(meta, gm, joint1, probs1, w)
+        gj1 = call(
+            heads_pull_kernel(sizes), [((total, 3 * half), bf16)], [], VMEM_MIB, flops=3 * 10**9
+        )(meta, gm, joint1, probs1)[0]
         gj_late = gj1
         if shares:
             first = scatter_begin(*first, devices)
             gj_late = after([gj1], first)[0]
-        second = call(
+        tiny = small_lanes(width, part_rows)
+        w_all, *second = call(
             heads_grad_kernel(sizes),
-            blocks(3 * half + LANES),
-            [((width, 3 * half), f32), ((width, LANES), f32)],
+            [((width, 3 * width), bf16)] + blocks(3 * half + tiny),
+            [((width, 3 * half), f32), ((width, tiny), f32)],
             VMEM_MIB,
             flops=4 * 10**9,
-        )(meta, gj_late, early, tiny, w1, tail, xh)
+            far_in=range(4, 5),
+            sems=6,
+        )(meta, gj_late, early, sums, xh, w)
         if shares:
-            first = scatter_middle(first, devices)
-            second = scatter_begin(*after(second, first[2:4]), devices)
-            part = after([part], [*second, first[2]])[0]
-            first = scatter_near(first, devices)
+            second = scatter_begin(*second, devices)
+            part = after([part], second)[0]
         xgrad = call(
             inputs_pull_kernel(sizes),
             [((total, width), f32)],
             [((total, width), f32)],
             VMEM_MIB,
             flops=5 * 10**9,
-        )(meta, x, par, gj, gj1, w0, w1, part)[0]
+        )(meta, x, par, gj, gj1, w_all, part)[0]
         if shares:
-            second = scatter_middle(second, devices, [xgrad, first[2]])
-            second = scatter_near(second, devices)
+            first = scatter_middle(first, devices, [xgrad])
+            second = scatter_middle(second, devices, first[2:4])
+            first, second = scatter_near(first, devices), scatter_near(second, devices)
             ends = [*scatter_end(first, devices), *scatter_end(second, devices)]
         else:
             ends = []
@@ -978,14 +975,15 @@
                 full = lax.psum_scatter(full, "fsdp", scatter_dimension=0, tiled=True)[None]
                 ends += [full, jnp.zeros_like(full)]
         out_grad, in_grad, ns, nb, ms, mb, slot_grad = pl.pallas_call(
-            finish_kernel(width, experts),
+            finish_kernel(width, experts, part_rows),
             out_shape=[jax.ShapeDtypeStruct((part_rows, c), f32) for c in (width, 3 * width)]
             + [jax.ShapeDtypeStruct((1, part_rows), f32)] * 4
             + [jax.ShapeDtypeStruct((experts, part_rows), f32)],
-            in_specs=[vmem()] * 4,
+            in_specs=[vmem()] * 7,
             out_specs=[vmem()] * 7,
-            scratch_shapes=[pltpu.VMEM((LANES, LANES), f32)],
-        )(*ends)
+            scratch_shapes=[pltpu.VMEM((LANES, LANES), f32), pltpu.VMEM((8, 3 * width), f32)],
+            compiler_params=pltpu.CompilerParams(vmem_limit_bytes=8 * MIB),
+        )(*ends, attend_in, *vectors[:2])
         return (
             block.reshape(images.shape),
             xgrad.reshape(images.shape),

time: 152 us -> 143 us (0.941)
  Pallas kernels: 49.2 us -> 43.8 us
  waiting for transfers between devices: 59.4 us -> 55.1 us
  starting transfers between devices: 39.4 us -> 42.9 us
  local copies, waits for them, and re-layouts: 2 us -> 0.07 us
    ppermute x48, waiting for transfers between devices: 59.4 us -> 55.1 us  [swap(): return lax.ppermute(value, 'fsdp', [(i, i ^ mask) for i in range(devices)])]
    pallas_call x8, Pallas kernels: 44.6 us -> 40.6 us  [run(): pl.pallas_call(body, out_shape=[pltpu.HBM(s, d) if i in far_out else jax....]
    ppermute x48, starting transfers between devices: 39.4 us -> 42.9 us  [swap(): return lax.ppermute(value, 'fsdp', [(i, i ^ mask) for i in range(devices)])]
    unnamed x51 -> x17, local copies, waits for them, and re-layouts: 1.98 us -> 0.05 us
  transfers between devices with their start and end apart: 48 -> 48, of which waited for: 26 -> 29; matrix products, arithmetic and copies ran while one was open for 1% -> 0% of each run, Pallas kernels for 12% -> 9%
where the time goes in v4:
time: 143 us
  waiting for transfers between devices  55.1 us (39%)
  Pallas kernels  43.8 us (31%)
  starting transfers between devices  42.9 us (30%)
    ppermute x48, waiting for transfers between devices, swap(): return lax.ppermute(value, 'fsdp', [(i, i ^ mask) for i in range(devices)])  55.1 us
    ppermute x48, starting transfers between devices, swap(): return lax.ppermute(value, 'fsdp', [(i, i ^ mask) for i in range(devices)])  42.9 us
    pallas_call x8, Pallas kernels, run(): pl.pallas_call(body, out_shape=[pltpu.HBM(s, d) if i in far_out else jax....  40.6 us
  transfers between devices with their start and end apart: 48, of which 29 were waited for; matrix products, arithmetic and copies ran while one was open for 0% of the time, Pallas kernels for 9%

profile of v4, /device:TPU:0, one launch (start us, length us, event | category | flops | bytes accessed | tf_op | source)
XLA Modules:
  0.0 142.8 jit_solution(3412825943504932014)
XLA Ops:
  0.7 1.1 shard_map.203
  1.7 3.1 %collective-permute-start = (bf16[1,24,3200]{2,1,0:T(8,128)(2,1)S(1)}, bf16[1,24,3200]{2,1,0:T(8,128)(2,1)S(1)}, u32[]{:S(2)}, u32[]{:S(2)}) collective-permute-start(bf16[1,24,3200]{2,1,0:T(8,128)(2,1)S(1)} %bitcast.22), channel_id=1, source_target_pairs={{0,8},{1,9},{2,10},{3,11},{4,12},{5,13},{6,14},{7,15},{8,0},{9,1},... | collective-permute-start | bytes 460808 | tf_op jit(solution)/shard_map/ppermute | solution.py:728
  4.8 2.6 %collective-permute-start.1 = (bf16[1,24,3200]{2,1,0:T(8,128)(2,1)S(1)}, bf16[1,24,3200]{2,1,0:T(8,128)(2,1)S(1)}, u32[]{:S(2)}, u32[]{:S(2)}) collective-permute-start(bf16[1,24,3200]{2,1,0:T(8,128)(2,1)S(1)} %bitcast.23), channel_id=1, source_target_pairs={{0,16},{1,17},{2,18},{3,19},{4,20},{5,21},{6,22},{7,23},{8,24},{9,... | collective-permute-start | bytes 460808 | tf_op jit(solution)/shard_map/ppermute | solution.py:728
  7.4 4.2 %collective-permute-done = bf16[1,24,3200]{2,1,0:T(8,128)(2,1)S(1)} collective-permute-done((bf16[1,24,3200]{2,1,0:T(8,128)(2,1)S(1)}, bf16[1,24,3200]{2,1,0:T(8,128)(2,1)S(1)}, u32[]{:S(2)}, u32[]{:S(2)}) %collective-permute-start) | collective-permute-done | bytes 153632 | tf_op jit(solution)/shard_map/ppermute | solution.py:728
  11.7 1.9 %collective-permute-start.5 = (bf16[2,24,3200]{2,1,0:T(8,128)(2,1)S(1)}, bf16[2,24,3200]{2,1,0:T(8,128)(2,1)S(1)}, u32[]{:S(2)}, u32[]{:S(2)}) collective-permute-start(bf16[2,24,3200]{2,1,0:T(8,128)(2,1)S(1)} %pad_maximum_fusion.refs_0_), channel_id=1, source_target_pairs={{0,4},{1,5},{2,6},{3,7},{4,0},{5,1},{6,2},{7,3},{8,12},{9,13},{10,... | collective-permute-start | bytes 921608 | tf_op jit(solution)/shard_map/ppermute | solution.py:728
  13.6 1.5 %collective-permute-start.3 = (bf16[2,24,3200]{2,1,0:T(8,128)(2,1)S(1)}, bf16[2,24,3200]{2,1,0:T(8,128)(2,1)S(1)}, u32[]{:S(2)}, u32[]{:S(2)}) collective-permute-start(bf16[2,24,3200]{2,1,0:T(8,128)(2,1)S(1)} %pad_maximum_fusion.refs_0_), channel_id=1, source_target_pairs={{0,2},{1,3},{2,0},{3,1},{4,6},{5,7},{6,4},{7,5},{8,10},{9,11},{10,... | collective-permute-start | bytes 921608 | tf_op jit(solution)/shard_map/ppermute | solution.py:728
  15.2 5.8 %collective-permute-done.2 = bf16[1,24,3200]{2,1,0:T(8,128)(2,1)S(1)} collective-permute-done((bf16[1,24,3200]{2,1,0:T(8,128)(2,1)S(1)}, bf16[1,24,3200]{2,1,0:T(8,128)(2,1)S(1)}, u32[]{:S(2)}, u32[]{:S(2)}) %collective-permute-start.2) | collective-permute-done | bytes 153632 | tf_op jit(solution)/shard_map/ppermute | solution.py:728
  21.5 1.3 collective-permute-start.6
  23.3 2.0 %collective-permute-start.7 = (bf16[2,24,3200]{2,1,0:T(8,128)(2,1)S(1)}, bf16[2,24,3200]{2,1,0:T(8,128)(2,1)S(1)}, u32[]{:S(2)}, u32[]{:S(2)}) collective-permute-start(bf16[2,24,3200]{2,1,0:T(8,128)(2,1)S(1)} %collective-permute-done.5.refs_4_), channel_id=1, source_target_pairs={{0,2},{1,3},{2,0},{3,1},{4,6},{5,7},{6,4},{7,5},{8,10},{9,11},{10,... | collective-permute-start | bytes 921608 | tf_op jit(solution)/shard_map/ppermute | solution.py:728
  25.2 6.0 %collective-permute-done.4.refs_3_ = bf16[2,24,3200]{2,1,0:T(8,128)(2,1)S(1)} collective-permute-done((bf16[2,24,3200]{2,1,0:T(8,128)(2,1)S(1)}, bf16[2,24,3200]{2,1,0:T(8,128)(2,1)S(1)}, u32[]{:S(2)}, u32[]{:S(2)}) %collective-permute-start.4) | collective-permute-done | bytes 307232 | tf_op jit(solution)/shard_map/ppermute | solution.py:728
  32.3 3.9 %collective-permute-done.7.refs_6_ = bf16[2,24,3200]{2,1,0:T(8,128)(2,1)S(1)} collective-permute-done((bf16[2,24,3200]{2,1,0:T(8,128)(2,1)S(1)}, bf16[2,24,3200]{2,1,0:T(8,128)(2,1)S(1)}, u32[]{:S(2)}, u32[]{:S(2)}) %collective-permute-start.7) | collective-permute-done | bytes 307232 | tf_op jit(solution)/shard_map/ppermute | solution.py:728
  36.1 1.9 %collective-permute-done.8.refs_7_ = bf16[2,24,3200]{2,1,0:T(8,128)(2,1)S(1)} collective-permute-done((bf16[2,24,3200]{2,1,0:T(8,128)(2,1)S(1)}, bf16[2,24,3200]{2,1,0:T(8,128)(2,1)S(1)}, u32[]{:S(2)}, u32[]{:S(2)}) %collective-permute-start.8) | collective-permute-done | bytes 307232 | tf_op jit(solution)/shard_map/ppermute | solution.py:728
  38.1 1.6 %collective-permute-done.16.refs_15_ = bf16[2,24,3200]{2,1,0:T(8,128)(2,1)S(1)} collective-permute-done((bf16[2,24,3200]{2,1,0:T(8,128)(2,1)S(1)}, bf16[2,24,3200]{2,1,0:T(8,128)(2,1)S(1)}, u32[]{:S(2)}, u32[]{:S(2)}) %collective-permute-start.16) | collective-permute-done | bytes 307232 | tf_op jit(solution)/shard_map/ppermute | solution.py:728
  39.7 10.6 %shard_map.204 = (f32[8,768]{1,0:T(8,128)S(1)}, f32[2,4,208]{2,1,0:T(4,128)S(1)}, bf16[16,768]{1,0:T(8,128)(2,1)S(1)}, bf16[416,768]{1,0:T(8,128)(2,1)}, bf16[41...) custom-call(s32[2]{0:T(128)S(1)} %copy-done.5, ...), custom_call_target="tpu_custom_call" | custom-call | tf_op jit(solution)/shard_map/pallas_call | solution.py:57
  50.3 2.8 %collective-permute-start.19 = (bf16[1,16,768]{2,1,0:T(8,128)(2,1)S(1)}, bf16[1,16,768]{2,1,0:T(8,128)(2,1)S(1)}, u32[]{:S(2)}, u32[]{:S(2)}) collective-permute-start(bf16[1,16,768]{2,1,0:T(8,128)(2,1)S(1)} %bitcast.26), channel_id=1, source_target_pairs={{0,24},{1,25},{2,26},{3,27},{4,28},{5,29},{6,30},{7,31},{8,16},{9,... | collective-permute-start | bytes 73736 | tf_op jit(solution)/shard_map/ppermute | solution.py:728
  53.0 1.7 %collective-permute-start.17 = (bf16[1,16,768]{2,1,0:T(8,128)(2,1)S(1)}, bf16[1,16,768]{2,1,0:T(8,128)(2,1)S(1)}, u32[]{:S(2)}, u32[]{:S(2)}) collective-permute-start(bf16[1,16,768]{2,1,0:T(8,128)(2,1)S(1)} %bitcast.28), channel_id=1, source_target_pairs={{0,8},{1,9},{2,10},{3,11},{4,12},{5,13},{6,14},{7,15},{8,0},{9,1},... | collective-permute-start | bytes 73736 | tf_op jit(solution)/shard_map/ppermute | solution.py:728
  54.7 1.3 collective-permute-done.19
  56.0 1.7 %collective-permute-done.18 = bf16[1,16,768]{2,1,0:T(8,128)(2,1)S(1)} collective-permute-done((bf16[1,16,768]{2,1,0:T(8,128)(2,1)S(1)}, bf16[1,16,768]{2,1,0:T(8,128)(2,1)S(1)}, u32[]{:S(2)}, u32[]{:S(2)}) %collective-permute-start.18) | collective-permute-done | bytes 24608 | tf_op jit(solution)/shard_map/ppermute | solution.py:728
  57.8 1.3 collective-permute-start.22
  59.1 1.7 %collective-permute-start.21 = (bf16[4,16,768]{2,1,0:T(8,128)(2,1)S(1)}, bf16[4,16,768]{2,1,0:T(8,128)(2,1)S(1)}, u32[]{:S(2)}, u32[]{:S(2)}) collective-permute-start(bf16[4,16,768]{2,1,0:T(8,128)(2,1)S(1)} %pad_maximum_fusion.1.refs_0_), channel_id=1, source_target_pairs={{0,4},{1,5},{2,6},{3,7},{4,0},{5,1},{6,2},{7,3},{8,12},{9,13},{10,... | collective-permute-start | bytes 294920 | tf_op jit(solution)/shard_map/ppermute | solution.py:728
  61.3 2.3 %collective-permute-done.22.refs_3_ = bf16[4,16,768]{2,1,0:T(8,128)(2,1)S(1)} collective-permute-done((bf16[4,16,768]{2,1,0:T(8,128)(2,1)S(1)}, bf16[4,16,768]{2,1,0:T(8,128)(2,1)S(1)}, u32[]{:S(2)}, u32[]{:S(2)}) %collective-permute-start.22) | collective-permute-done | bytes 98336 | tf_op jit(solution)/shard_map/ppermute | solution.py:728
  66.7 2.6 %shard_map.205 = (bf16[16,16,768]{2,1,0:T(8,128)(2,1)S(1)}, bf16[16,16,768]{2,1,0:T(8,128)(2,1)S(1)}, bf16[256,768]{1,0:T(8,128)(2,1)S(1)}, bf16[256,768]{1,0:T(...) custom-call(s32[2]{0:T(128)S(1)} %copy-done.5, ...), custom_call_target="tpu_custom_call" | custom-call | tf_op jit(solution)/shard_map/pallas_call | solution.py:57
  69.5 1.6 %collective-permute-done.27.refs_1_ = bf16[16,16,768]{2,1,0:T(8,128)(2,1)S(1)} collective-permute-done((bf16[16,16,768]{2,1,0:T(8,128)(2,1)S(1)}, bf16[16,16,768]{2,1,0:T(8,128)(2,1)S(1)}, u32[]{:S(2)}, u32[]{:S(2)}) %collective-permute-start.27) | collective-permute-done | bytes 393248 | tf_op jit(solution)/shard_map/ppermute | solution.py:728
  72.7 2.2 %collective-permute-start.30 = (bf16[4,16,768]{2,1,0:T(8,128)(2,1)S(1)}, bf16[4,16,768]{2,1,0:T(8,128)(2,1)S(1)}, u32[]{:S(2)}, u32[]{:S(2)}) collective-permute-start(bf16[4,16,768]{2,1,0:T(8,128)(2,1)S(1)} %get-tuple-element.98), channel_id=1, source_target_pairs={{0,6},{1,7},{2,4},{3,5},{4,2},{5,3},{6,0},{7,1},{8,14},{9,15},{10,... | collective-permute-start | bytes 294920 | tf_op jit(solution)/shard_map/ppermute | solution.py:728
  74.8 2.4 %shard_map.209 = (f32[416,768]{1,0:T(8,128)S(1)}, f32[416,128]{1,0:T(8,128)S(1)}, bf16[416,768]{1,0:T(8,128)(2,1)S(1)}) custom-call(s32[2]{0:T(128)S(1)} %copy-done.5, f32[416,768]{1,0:T(8,128)} %get-tuple-element.110.res_in, bf16[416,768]{1,0:T(8,128)(2,1)} %get-tuple-element.111.n2_in), custom_call_target="tpu_custom_call" | custom-call | flops 1000000000 | tf_op jit(solution)/shard_map/pallas_call | solution.py:57
  77.2 1.5 %collective-permute-done.29.refs_2_ = bf16[4,16,768]{2,1,0:T(8,128)(2,1)S(1)} collective-permute-done((bf16[4,16,768]{2,1,0:T(8,128)(2,1)S(1)}, bf16[4,16,768]{2,1,0:T(8,128)(2,1)S(1)}, u32[]{:S(2)}, u32[]{:S(2)}) %collective-permute-start.29) | collective-permute-done | bytes 98336 | tf_op jit(solution)/shard_map/ppermute | solution.py:728
  79.8 1.3 collective-permute-start.32
  81.1 2.1 %collective-permute-start.33 = (bf16[1,16,768]{2,1,0:T(8,128)(2,1)S(1)}, bf16[1,16,768]{2,1,0:T(8,128)(2,1)S(1)}, u32[]{:S(2)}, u32[]{:S(2)}) collective-permute-start(bf16[1,16,768]{2,1,0:T(8,128)(2,1)S(1)} %get-tuple-element.109), channel_id=1, source_target_pairs={{0,24},{1,25},{2,26},{3,27},{4,28},{5,29},{6,30},{7,31},{8,16},{9,... | collective-permute-start | bytes 73736 | tf_op jit(solution)/shard_map/ppermute | solution.py:728
  83.2 2.5 %shard_map.208 = (f32[4,96,768]{2,1,0:T(8,128)}, f32[4,96,768]{2,1,0:T(8,128)}) custom-call(s32[2]{0:T(128)S(1)} %copy-done.5, bf16[256,768]{1,0:T(8,128)(2,1)S(1)} %get-tuple-element.100.s_ref, bf16[256,768]{1,0:T(8,128)(2,1)S(1)} %get-tuple-element.101.g_ref, bf16[256,512]{1,0:T(8,128)(2,1)S(1)} %get-tuple-element.102.act_ref, ...), custom_call_target="tpu_custom_call" | custom-call | flops 2000000000 | tf_op jit(solution)/shard_map/pallas_call | solution.py:57
  86.7 11.1 %shard_map.210 = (bf16[416,768]{1,0:T(8,128)(2,1)}, f32[416,768]{1,0:T(8,128)S(1)}, bf16[416,768]{1,0:T(8,128)(2,1)S(1)}, bf16[416,1152]{1,0:T(8,128)(2,1)S(1)},...) custom-call(s32[2]{0:T(128)S(1)} %copy-done.5, ...), custom_call_target="tpu_custom_call" | custom-call | tf_op jit(solution)/shard_map/pallas_call | solution.py:57
  97.9 3.4 %shard_map.211.gj.gj1_ref = bf16[416,1152]{1,0:T(8,128)(2,1)S(1)} custom-call(s32[2]{0:T(128)S(1)} %copy-done.5, bf16[416,768]{1,0:T(8,128)(2,1)S(1)} %get-tuple-element.122.gm_ref, bf16[416,1152]{1,0:T(8,128)(2,1)S(1)} %get-tuple-element.123.joint_ref, bf16[3,2,416,208]{3,2,1,0:T(8,128)(2,1)S(1)} %get-tuple-element.124.probs_ref), custom_call_target="tpu_custom_call" | custom-call | flops 3000000000 | tf_op jit(solution)/shard_map/pallas_call | solution.py:57
  101.7 3.7 %shard_map.213 = (bf16[768,2304]{1,0:T(8,128)(2,1)S(1)}, bf16[16,24,1280]{2,1,0:T(8,128)(2,1)S(1)}, bf16[16,24,1280]{2,1,0:T(8,128)(2,1)S(1)}) custom-call(s32[2]{0:T(128)S(1)} %copy-done.5, bf16[416,1152]{1,0:T(8,128)(2,1)S(1)} %shard_map.211.gj.gj1_ref, f32[8,768]{1,0:T(8,128)S(1)} %get-tuple-element.134.grads, f32[8,1152]{1,0:T(8,128)S(1)} %get-tuple-element.135.sums_ref, ...), custom_call_target="tpu_custom_call" | custom-call | flops 4000000000 | tf_op jit(solution)/shard_map/pallas_call | solution.py:57
  106.0 1.3 collective-permute-start.36
  108.4 1.4 collective-permute-start.42
  110.6 4.3 %shard_map.215 = f32[416,768]{1,0:T(8,128)} custom-call(s32[2]{0:T(128)S(1)} %copy-done.5, bf16[416,768]{1,0:T(8,128)(2,1)S(1)} %bitcast.21, f32[8,768]{1,0:T(8,128)S(1)} %get-tuple-element.90.par_ref, bf16[416,1152]{1,0:T(8,128)(2,1)S(1)} %get-tuple-element.121.gj0_ref, bf16[416,1152]{1,0:T(8,128)(2,1)S(1)} %shard_map.211.gj.gj1_ref, ...), custom_call_target="tpu_custom_call" | custom-call | flops 5000000000 | tf_op jit(solution)/shard_map/pallas_call | solution.py:57
  114.9 2.5 %collective-permute-done.36.refs_3_.refs_1_ = bf16[4,24,1920]{2,1,0:T(8,128)(2,1)S(1)} collective-permute-done((bf16[4,24,1920]{2,1,0:T(8,128)(2,1)S(1)}, bf16[4,24,1920]{2,1,0:T(8,128)(2,1)S(1)}, u32[]{:S(2)}, u32[]{:S(2)}) %collective-permute-start.36) | collective-permute-done | bytes 368672 | tf_op jit(solution)/shard_map/ppermute | solution.py:728
  117.4 1.3 collective-permute-done.37.refs_2_
  119.6 3.0 %collective-permute-done.42.refs_3_.refs_1_ = bf16[4,24,1280]{2,1,0:T(8,128)(2,1)S(1)} collective-permute-done((bf16[4,24,1280]{2,1,0:T(8,128)(2,1)S(1)}, bf16[4,24,1280]{2,1,0:T(8,128)(2,1)S(1)}, u32[]{:S(2)}, u32[]{:S(2)}) %collective-permute-start.42) | collective-permute-done | bytes 245792 | tf_op jit(solution)/shard_map/ppermute | solution.py:728
  122.9 1.2 collective-permute-start.45
  124.9 1.7 %collective-permute-done.39.refs_1_ = bf16[2,24,1920]{2,1,0:T(8,128)(2,1)S(1)} collective-permute-done((bf16[2,24,1920]{2,1,0:T(8,128)(2,1)S(1)}, bf16[2,24,1920]{2,1,0:T(8,128)(2,1)S(1)}, u32[]{:S(2)}, u32[]{:S(2)}) %collective-permute-start.39) | collective-permute-done | bytes 184352 | tf_op jit(solution)/shard_map/ppermute | solution.py:728
  126.8 1.0 collective-permute-start.44
  128.5 1.4 %collective-permute-start.46 = (bf16[2,24,1280]{2,1,0:T(8,128)(2,1)S(1)}, bf16[2,24,1280]{2,1,0:T(8,128)(2,1)S(1)}, u32[]{:S(2)}, u32[]{:S(2)}) collective-permute-start(bf16[2,24,1280]{2,1,0:T(8,128)(2,1)S(1)} %shard_map.220), channel_id=1, source_target_pairs={{0,8},{1,9},{2,10},{3,11},{4,12},{5,13},{6,14},{7,15},{8,0},{9,1},... | collective-permute-start | bytes 368648 | tf_op jit(solution)/shard_map/ppermute | solution.py:728
  129.9 1.1 collective-permute-done.38.refs_2_
  131.0 2.8 %collective-permute-done.40.refs_3_ = bf16[2,24,1920]{2,1,0:T(8,128)(2,1)S(1)} collective-permute-done((bf16[2,24,1920]{2,1,0:T(8,128)(2,1)S(1)}, bf16[2,24,1920]{2,1,0:T(8,128)(2,1)S(1)}, u32[]{:S(2)}, u32[]{:S(2)}) %collective-permute-start.40) | collective-permute-done | bytes 184352 | tf_op jit(solution)/shard_map/ppermute | solution.py:728
  133.9 1.1 collective-permute-start.41
  134.9 1.0 collective-permute-done.46.refs_3_
  137.0 3.0 %collective-permute-done.41.a1 = bf16[1,24,1920]{2,1,0:T(8,128)(2,1)S(1)} collective-permute-done((bf16[1,24,1920]{2,1,0:T(8,128)(2,1)S(1)}, bf16[1,24,1920]{2,1,0:T(8,128)(2,1)S(1)}, u32[]{:S(2)}, u32[]{:S(2)}) %collective-permute-start.41) | collective-permute-done | bytes 92192 | tf_op jit(solution)/shard_map/ppermute | solution.py:728
  140.0 1.8 %collective-permute-done.47.b1 = bf16[1,24,1280]{2,1,0:T(8,128)(2,1)S(1)} collective-permute-done((bf16[1,24,1280]{2,1,0:T(8,128)(2,1)S(1)}, bf16[1,24,1280]{2,1,0:T(8,128)(2,1)S(1)}, u32[]{:S(2)}, u32[]{:S(2)}) %collective-permute-start.47) | collective-permute-done | bytes 61472 | tf_op jit(solution)/shard_map/ppermute | solution.py:728
  (88 shorter events, 17.5 us)
Async XLA Ops:
  1.7 9.9 %collective-permute-start = (bf16[1,24,3200]{2,1,0:T(8,128)(2,1)S(1)}, bf16[1,24,3200]{2,1,0:T(8,128)(2,1)S(1)}, u32[]{:S(2)}, u32[]{:S(2)}) collective-permute-start(bf16[1,24,3200]{2,1,0:T(8,128)(2,1)S(1)} %bitcast.22), channel_id=1, source_target_pairs={{0,8},{1,9},{2,10},{3,11},{4,12},{5,13},{6,14},{7,15},{8,0},{9,1},... | collective-permute-start | bytes 460808 | tf_op jit(solution)/shard_map/ppermute | solution.py:728
  4.8 10.3 %collective-permute-start.1 = (bf16[1,24,3200]{2,1,0:T(8,128)(2,1)S(1)}, bf16[1,24,3200]{2,1,0:T(8,128)(2,1)S(1)}, u32[]{:S(2)}, u32[]{:S(2)}) collective-permute-start(bf16[1,24,3200]{2,1,0:T(8,128)(2,1)S(1)} %bitcast.23), channel_id=1, source_target_pairs={{0,16},{1,17},{2,18},{3,19},{4,20},{5,21},{6,22},{7,23},{8,24},{9,... | collective-permute-start | bytes 460808 | tf_op jit(solution)/shard_map/ppermute | solution.py:728
  11.6 9.9 %collective-permute-start.9 = (bf16[2,24,3200]{2,1,0:T(8,128)(2,1)S(1)}, bf16[2,24,3200]{2,1,0:T(8,128)(2,1)S(1)}, u32[]{:S(2)}, u32[]{:S(2)}) collective-permute-start(bf16[2,24,3200]{2,1,0:T(8,128)(2,1)S(1)} %pad_maximum_fusion.refs_0_), channel_id=1, source_target_pairs={{0,1},{1,0},{2,3},{3,2},{4,5},{5,4},{6,7},{7,6},{8,9},{9,8},{10,11... | collective-permute-start | bytes 921608 | tf_op jit(solution)/shard_map/ppermute | solution.py:728
  11.7 11.1 %collective-permute-start.5 = (bf16[2,24,3200]{2,1,0:T(8,128)(2,1)S(1)}, bf16[2,24,3200]{2,1,0:T(8,128)(2,1)S(1)}, u32[]{:S(2)}, u32[]{:S(2)}) collective-permute-start(bf16[2,24,3200]{2,1,0:T(8,128)(2,1)S(1)} %pad_maximum_fusion.refs_0_), channel_id=1, source_target_pairs={{0,4},{1,5},{2,6},{3,7},{4,0},{5,1},{6,2},{7,3},{8,12},{9,13},{10,... | collective-permute-start | bytes 921608 | tf_op jit(solution)/shard_map/ppermute | solution.py:728
  13.6 9.7 %collective-permute-start.3 = (bf16[2,24,3200]{2,1,0:T(8,128)(2,1)S(1)}, bf16[2,24,3200]{2,1,0:T(8,128)(2,1)S(1)}, u32[]{:S(2)}, u32[]{:S(2)}) collective-permute-start(bf16[2,24,3200]{2,1,0:T(8,128)(2,1)S(1)} %pad_maximum_fusion.refs_0_), channel_id=1, source_target_pairs={{0,2},{1,3},{2,0},{3,1},{4,6},{5,7},{6,4},{7,5},{8,10},{9,11},{10,... | collective-permute-start | bytes 921608 | tf_op jit(solution)/shard_map/ppermute | solution.py:728
  15.1 5.8 %collective-permute-start.2 = (bf16[1,24,3200]{2,1,0:T(8,128)(2,1)S(1)}, bf16[1,24,3200]{2,1,0:T(8,128)(2,1)S(1)}, u32[]{:S(2)}, u32[]{:S(2)}) collective-permute-start(bf16[1,24,3200]{2,1,0:T(8,128)(2,1)S(1)} %collective-permute-done.1), channel_id=1, source_target_pairs={{0,8},{1,9},{2,10},{3,11},{4,12},{5,13},{6,14},{7,15},{8,0},{9,1},... | collective-permute-start | bytes 460808 | tf_op jit(solution)/shard_map/ppermute | solution.py:728
  20.9 10.3 %collective-permute-start.4 = (bf16[2,24,3200]{2,1,0:T(8,128)(2,1)S(1)}, bf16[2,24,3200]{2,1,0:T(8,128)(2,1)S(1)}, u32[]{:S(2)}, u32[]{:S(2)}) collective-permute-start(bf16[2,24,3200]{2,1,0:T(8,128)(2,1)S(1)} %constant_dynamic-update-slice_fusion.refs_1_), channel_id=1, source_target_pairs={{0,2},{1,3},{2,0},{3,1},{4,6},{5,7},{6,4},{7,5},{8,10},{9,11},{10,... | collective-permute-start | bytes 921608 | tf_op jit(solution)/shard_map/ppermute | solution.py:728
  21.5 10.2 %collective-permute-start.10 = (bf16[2,24,3200]{2,1,0:T(8,128)(2,1)S(1)}, bf16[2,24,3200]{2,1,0:T(8,128)(2,1)S(1)}, u32[]{:S(2)}, u32[]{:S(2)}) collective-permute-start(bf16[2,24,3200]{2,1,0:T(8,128)(2,1)S(1)} %constant_dynamic-update-slice_fusion.refs_1_), channel_id=1, source_target_pairs={{0,1},{1,0},{2,3},{3,2},{4,5},{5,4},{6,7},{7,6},{8,9},{9,8},{10,11... | collective-permute-start | bytes 921608 | tf_op jit(solution)/shard_map/ppermute | solution.py:728
  21.5 10.2 %collective-permute-start.6 = (bf16[2,24,3200]{2,1,0:T(8,128)(2,1)S(1)}, bf16[2,24,3200]{2,1,0:T(8,128)(2,1)S(1)}, u32[]{:S(2)}, u32[]{:S(2)}) collective-permute-start(bf16[2,24,3200]{2,1,0:T(8,128)(2,1)S(1)} %constant_dynamic-update-slice_fusion.refs_1_), channel_id=1, source_target_pairs={{0,4},{1,5},{2,6},{3,7},{4,0},{5,1},{6,2},{7,3},{8,12},{9,13},{10,... | collective-permute-start | bytes 921608 | tf_op jit(solution)/shard_map/ppermute | solution.py:728
  22.8 9.4 %collective-permute-start.13 = (bf16[2,24,3200]{2,1,0:T(8,128)(2,1)S(1)}, bf16[2,24,3200]{2,1,0:T(8,128)(2,1)S(1)}, u32[]{:S(2)}, u32[]{:S(2)}) collective-permute-start(bf16[2,24,3200]{2,1,0:T(8,128)(2,1)S(1)} %collective-permute-done.5.refs_4_), channel_id=1, source_target_pairs={{0,1},{1,0},{2,3},{3,2},{4,5},{5,4},{6,7},{7,6},{8,9},{9,8},{10,11... | collective-permute-start | bytes 921608 | tf_op jit(solution)/shard_map/ppermute | solution.py:728
  23.3 12.9 %collective-permute-start.7 = (bf16[2,24,3200]{2,1,0:T(8,128)(2,1)S(1)}, bf16[2,24,3200]{2,1,0:T(8,128)(2,1)S(1)}, u32[]{:S(2)}, u32[]{:S(2)}) collective-permute-start(bf16[2,24,3200]{2,1,0:T(8,128)(2,1)S(1)} %collective-permute-done.5.refs_4_), channel_id=1, source_target_pairs={{0,2},{1,3},{2,0},{3,1},{4,6},{5,7},{6,4},{7,5},{8,10},{9,11},{10,... | collective-permute-start | bytes 921608 | tf_op jit(solution)/shard_map/ppermute | solution.py:728
  31.2 6.9 %collective-permute-start.8 = (bf16[2,24,3200]{2,1,0:T(8,128)(2,1)S(1)}, bf16[2,24,3200]{2,1,0:T(8,128)(2,1)S(1)}, u32[]{:S(2)}, u32[]{:S(2)}) collective-permute-start(bf16[2,24,3200]{2,1,0:T(8,128)(2,1)S(1)} %collective-permute-done.4.refs_3_), channel_id=1, source_target_pairs={{0,4},{1,5},{2,6},{3,7},{4,0},{5,1},{6,2},{7,3},{8,12},{9,13},{10,... | collective-permute-start | bytes 921608 | tf_op jit(solution)/shard_map/ppermute | solution.py:728
  31.7 6.4 %collective-permute-start.11 = (bf16[2,24,3200]{2,1,0:T(8,128)(2,1)S(1)}, bf16[2,24,3200]{2,1,0:T(8,128)(2,1)S(1)}, u32[]{:S(2)}, u32[]{:S(2)}) collective-permute-start(bf16[2,24,3200]{2,1,0:T(8,128)(2,1)S(1)} %collective-permute-done.3.refs_2_), channel_id=1, source_target_pairs={{0,1},{1,0},{2,3},{3,2},{4,5},{5,4},{6,7},{7,6},{8,9},{9,8},{10,11... | collective-permute-start | bytes 921608 | tf_op jit(solution)/shard_map/ppermute | solution.py:728
  31.7 6.4 %collective-permute-start.12 = (bf16[2,24,3200]{2,1,0:T(8,128)(2,1)S(1)}, bf16[2,24,3200]{2,1,0:T(8,128)(2,1)S(1)}, u32[]{:S(2)}, u32[]{:S(2)}) collective-permute-start(bf16[2,24,3200]{2,1,0:T(8,128)(2,1)S(1)} %collective-permute-done.4.refs_3_), channel_id=1, source_target_pairs={{0,1},{1,0},{2,3},{3,2},{4,5},{5,4},{6,7},{7,6},{8,9},{9,8},{10,11... | collective-permute-start | bytes 921608 | tf_op jit(solution)/shard_map/ppermute | solution.py:728
  32.2 5.8 %collective-permute-start.14 = (bf16[2,24,3200]{2,1,0:T(8,128)(2,1)S(1)}, bf16[2,24,3200]{2,1,0:T(8,128)(2,1)S(1)}, u32[]{:S(2)}, u32[]{:S(2)}) collective-permute-start(bf16[2,24,3200]{2,1,0:T(8,128)(2,1)S(1)} %collective-permute-done.6.refs_5_), channel_id=1, source_target_pairs={{0,1},{1,0},{2,3},{3,2},{4,5},{5,4},{6,7},{7,6},{8,9},{9,8},{10,11... | collective-permute-start | bytes 921608 | tf_op jit(solution)/shard_map/ppermute | solution.py:728
  36.1 1.9 %collective-permute-start.15 = (bf16[2,24,3200]{2,1,0:T(8,128)(2,1)S(1)}, bf16[2,24,3200]{2,1,0:T(8,128)(2,1)S(1)}, u32[]{:S(2)}, u32[]{:S(2)}) collective-permute-start(bf16[2,24,3200]{2,1,0:T(8,128)(2,1)S(1)} %collective-permute-done.7.refs_6_), channel_id=1, source_target_pairs={{0,1},{1,0},{2,3},{3,2},{4,5},{5,4},{6,7},{7,6},{8,9},{9,8},{10,11... | collective-permute-start | bytes 921608 | tf_op jit(solution)/shard_map/ppermute | solution.py:728
  38.1 1.6 %collective-permute-start.16 = (bf16[2,24,3200]{2,1,0:T(8,128)(2,1)S(1)}, bf16[2,24,3200]{2,1,0:T(8,128)(2,1)S(1)}, u32[]{:S(2)}, u32[]{:S(2)}) collective-permute-start(bf16[2,24,3200]{2,1,0:T(8,128)(2,1)S(1)} %collective-permute-done.8.refs_7_), channel_id=1, source_target_pairs={{0,1},{1,0},{2,3},{3,2},{4,5},{5,4},{6,7},{7,6},{8,9},{9,8},{10,11... | collective-permute-start | bytes 921608 | tf_op jit(solution)/shard_map/ppermute | solution.py:728
  50.3 5.7 %collective-permute-start.19 = (bf16[1,16,768]{2,1,0:T(8,128)(2,1)S(1)}, bf16[1,16,768]{2,1,0:T(8,128)(2,1)S(1)}, u32[]{:S(2)}, u32[]{:S(2)}) collective-permute-start(bf16[1,16,768]{2,1,0:T(8,128)(2,1)S(1)} %bitcast.26), channel_id=1, source_target_pairs={{0,24},{1,25},{2,26},{3,27},{4,28},{5,29},{6,30},{7,31},{8,16},{9,... | collective-permute-start | bytes 73736 | tf_op jit(solution)/shard_map/ppermute | solution.py:728
  53.0 4.7 %collective-permute-start.18 = (bf16[1,16,768]{2,1,0:T(8,128)(2,1)S(1)}, bf16[1,16,768]{2,1,0:T(8,128)(2,1)S(1)}, u32[]{:S(2)}, u32[]{:S(2)}) collective-permute-start(bf16[1,16,768]{2,1,0:T(8,128)(2,1)S(1)} %bitcast.27), channel_id=1, source_target_pairs={{0,16},{1,17},{2,18},{3,19},{4,20},{5,21},{6,22},{7,23},{8,24},{9,... | collective-permute-start | bytes 73736 | tf_op jit(solution)/shard_map/ppermute | solution.py:728
  53.0 4.7 %collective-permute-start.17 = (bf16[1,16,768]{2,1,0:T(8,128)(2,1)S(1)}, bf16[1,16,768]{2,1,0:T(8,128)(2,1)S(1)}, u32[]{:S(2)}, u32[]{:S(2)}) collective-permute-start(bf16[1,16,768]{2,1,0:T(8,128)(2,1)S(1)} %bitcast.28), channel_id=1, source_target_pairs={{0,8},{1,9},{2,10},{3,11},{4,12},{5,13},{6,14},{7,15},{8,0},{9,1},... | collective-permute-start | bytes 73736 | tf_op jit(solution)/shard_map/ppermute | solution.py:728
  57.8 5.8 %collective-permute-start.22 = (bf16[4,16,768]{2,1,0:T(8,128)(2,1)S(1)}, bf16[4,16,768]{2,1,0:T(8,128)(2,1)S(1)}, u32[]{:S(2)}, u32[]{:S(2)}) collective-permute-start(bf16[4,16,768]{2,1,0:T(8,128)(2,1)S(1)} %pad_maximum_fusion.1.refs_0_), channel_id=1, source_target_pairs={{0,6},{1,7},{2,4},{3,5},{4,2},{5,3},{6,0},{7,1},{8,14},{9,15},{10,... | collective-permute-start | bytes 294920 | tf_op jit(solution)/shard_map/ppermute | solution.py:728
  59.1 5.5 %collective-permute-start.21 = (bf16[4,16,768]{2,1,0:T(8,128)(2,1)S(1)}, bf16[4,16,768]{2,1,0:T(8,128)(2,1)S(1)}, u32[]{:S(2)}, u32[]{:S(2)}) collective-permute-start(bf16[4,16,768]{2,1,0:T(8,128)(2,1)S(1)} %pad_maximum_fusion.1.refs_0_), channel_id=1, source_target_pairs={{0,4},{1,5},{2,6},{3,7},{4,0},{5,1},{6,2},{7,3},{8,12},{9,13},{10,... | collective-permute-start | bytes 294920 | tf_op jit(solution)/shard_map/ppermute | solution.py:728
  60.8 4.6 %collective-permute-start.20 = (bf16[4,16,768]{2,1,0:T(8,128)(2,1)S(1)}, bf16[4,16,768]{2,1,0:T(8,128)(2,1)S(1)}, u32[]{:S(2)}, u32[]{:S(2)}) collective-permute-start(bf16[4,16,768]{2,1,0:T(8,128)(2,1)S(1)} %pad_maximum_fusion.1.refs_0_), channel_id=1, source_target_pairs={{0,2},{1,3},{2,0},{3,1},{4,6},{5,7},{6,4},{7,5},{8,10},{9,11},{10,... | collective-permute-start | bytes 294920 | tf_op jit(solution)/shard_map/ppermute | solution.py:728
  61.3 4.1 %collective-permute-start.23 = (bf16[4,16,768]{2,1,0:T(8,128)(2,1)S(1)}, bf16[4,16,768]{2,1,0:T(8,128)(2,1)S(1)}, u32[]{:S(2)}, u32[]{:S(2)}) collective-permute-start(bf16[4,16,768]{2,1,0:T(8,128)(2,1)S(1)} %pad_maximum_fusion.1.refs_0_), channel_id=1, source_target_pairs={{0,1},{1,0},{2,3},{3,2},{4,5},{5,4},{6,7},{7,6},{8,9},{9,8},{10,11... | collective-permute-start | bytes 294920 | tf_op jit(solution)/shard_map/ppermute | solution.py:728
  63.6 1.9 %collective-permute-start.26 = (bf16[4,16,768]{2,1,0:T(8,128)(2,1)S(1)}, bf16[4,16,768]{2,1,0:T(8,128)(2,1)S(1)}, u32[]{:S(2)}, u32[]{:S(2)}) collective-permute-start(bf16[4,16,768]{2,1,0:T(8,128)(2,1)S(1)} %collective-permute-done.22.refs_3_), channel_id=1, source_target_pairs={{0,1},{1,0},{2,3},{3,2},{4,5},{5,4},{6,7},{7,6},{8,9},{9,8},{10,11... | collective-permute-start | bytes 294920 | tf_op jit(solution)/shard_map/ppermute | solution.py:728
  64.5 1.3 collective-permute-start.25
  65.4 1.3 collective-permute-start.24
  69.3 1.8 %collective-permute-start.27 = (bf16[16,16,768]{2,1,0:T(8,128)(2,1)S(1)}, bf16[16,16,768]{2,1,0:T(8,128)(2,1)S(1)}, u32[]{:S(2)}, u32[]{:S(2)}) collective-permute-start(bf16[16,16,768]{2,1,0:T(8,128)(2,1)S(1)} %get-tuple-element.94), channel_id=1, source_target_pairs={{0,1},{1,0},{2,3},{3,2},{4,5},{5,4},{6,7},{7,6},{8,9},{9,8},{10,11... | collective-permute-start | bytes 1179656 | tf_op jit(solution)/shard_map/ppermute | solution.py:728
  71.3 5.9 %collective-permute-start.28 = (bf16[4,16,768]{2,1,0:T(8,128)(2,1)S(1)}, bf16[4,16,768]{2,1,0:T(8,128)(2,1)S(1)}, u32[]{:S(2)}, u32[]{:S(2)}) collective-permute-start(bf16[4,16,768]{2,1,0:T(8,128)(2,1)S(1)} %get-tuple-element.96), channel_id=1, source_target_pairs={{0,2},{1,3},{2,0},{3,1},{4,6},{5,7},{6,4},{7,5},{8,10},{9,11},{10,... | collective-permute-start | bytes 294920 | tf_op jit(solution)/shard_map/ppermute | solution.py:728
  71.8 6.9 %collective-permute-start.29 = (bf16[4,16,768]{2,1,0:T(8,128)(2,1)S(1)}, bf16[4,16,768]{2,1,0:T(8,128)(2,1)S(1)}, u32[]{:S(2)}, u32[]{:S(2)}) collective-permute-start(bf16[4,16,768]{2,1,0:T(8,128)(2,1)S(1)} %get-tuple-element.97), channel_id=1, source_target_pairs={{0,4},{1,5},{2,6},{3,7},{4,0},{5,1},{6,2},{7,3},{8,12},{9,13},{10,... | collective-permute-start | bytes 294920 | tf_op jit(solution)/shard_map/ppermute | solution.py:728
  72.7 6.1 %collective-permute-start.30 = (bf16[4,16,768]{2,1,0:T(8,128)(2,1)S(1)}, bf16[4,16,768]{2,1,0:T(8,128)(2,1)S(1)}, u32[]{:S(2)}, u32[]{:S(2)}) collective-permute-start(bf16[4,16,768]{2,1,0:T(8,128)(2,1)S(1)} %get-tuple-element.98), channel_id=1, source_target_pairs={{0,6},{1,7},{2,4},{3,5},{4,2},{5,3},{6,0},{7,1},{8,14},{9,15},{10,... | collective-permute-start | bytes 294920 | tf_op jit(solution)/shard_map/ppermute | solution.py:728
  78.8 7.0 %collective-permute-start.31 = (bf16[1,16,768]{2,1,0:T(8,128)(2,1)S(1)}, bf16[1,16,768]{2,1,0:T(8,128)(2,1)S(1)}, u32[]{:S(2)}, u32[]{:S(2)}) collective-permute-start(bf16[1,16,768]{2,1,0:T(8,128)(2,1)S(1)} %get-tuple-element.107), channel_id=1, source_target_pairs={{0,8},{1,9},{2,10},{3,11},{4,12},{5,13},{6,14},{7,15},{8,0},{9,1},... | collective-permute-start | bytes 73736 | tf_op jit(solution)/shard_map/ppermute | solution.py:728
  79.8 6.0 %collective-permute-start.32 = (bf16[1,16,768]{2,1,0:T(8,128)(2,1)S(1)}, bf16[1,16,768]{2,1,0:T(8,128)(2,1)S(1)}, u32[]{:S(2)}, u32[]{:S(2)}) collective-permute-start(bf16[1,16,768]{2,1,0:T(8,128)(2,1)S(1)} %get-tuple-element.108), channel_id=1, source_target_pairs={{0,16},{1,17},{2,18},{3,19},{4,20},{5,21},{6,22},{7,23},{8,24},{9,... | collective-permute-start | bytes 73736 | tf_op jit(solution)/shard_map/ppermute | solution.py:728
  81.1 5.6 %collective-permute-start.33 = (bf16[1,16,768]{2,1,0:T(8,128)(2,1)S(1)}, bf16[1,16,768]{2,1,0:T(8,128)(2,1)S(1)}, u32[]{:S(2)}, u32[]{:S(2)}) collective-permute-start(bf16[1,16,768]{2,1,0:T(8,128)(2,1)S(1)} %get-tuple-element.109), channel_id=1, source_target_pairs={{0,24},{1,25},{2,26},{3,27},{4,28},{5,29},{6,30},{7,31},{8,16},{9,... | collective-permute-start | bytes 73736 | tf_op jit(solution)/shard_map/ppermute | solution.py:728
  97.8 3.5 %collective-permute-start.34 = (bf16[16,24,1920]{2,1,0:T(8,128)(2,1)S(1)}, bf16[16,24,1920]{2,1,0:T(8,128)(2,1)S(1)}, u32[]{:S(2)}, u32[]{:S(2)}) collective-permute-start(bf16[16,24,1920]{2,1,0:T(8,128)(2,1)S(1)} %get-tuple-element.126), channel_id=1, source_target_pairs={{0,1},{1,0},{2,3},{3,2},{4,5},{5,4},{6,7},{7,6},{8,9},{9,8},{10,11... | collective-permute-start | bytes 4423688 | tf_op jit(solution)/shard_map/ppermute | solution.py:728
  105.4 2.8 %collective-permute-start.35 = (bf16[16,24,1280]{2,1,0:T(8,128)(2,1)S(1)}, bf16[16,24,1280]{2,1,0:T(8,128)(2,1)S(1)}, u32[]{:S(2)}, u32[]{:S(2)}) collective-permute-start(bf16[16,24,1280]{2,1,0:T(8,128)(2,1)S(1)} %get-tuple-element.140), channel_id=1, source_target_pairs={{0,1},{1,0},{2,3},{3,2},{4,5},{5,4},{6,7},{7,6},{8,9},{9,8},{10,11... | collective-permute-start | bytes 2949128 | tf_op jit(solution)/shard_map/ppermute | solution.py:728
  106.0 11.4 %collective-permute-start.36 = (bf16[4,24,1920]{2,1,0:T(8,128)(2,1)S(1)}, bf16[4,24,1920]{2,1,0:T(8,128)(2,1)S(1)}, u32[]{:S(2)}, u32[]{:S(2)}) collective-permute-start(bf16[4,24,1920]{2,1,0:T(8,128)(2,1)S(1)} %get-tuple-element.129), channel_id=1, source_target_pairs={{0,2},{1,3},{2,0},{3,1},{4,6},{5,7},{6,4},{7,5},{8,10},{9,11},{10,... | collective-permute-start | bytes 1105928 | tf_op jit(solution)/shard_map/ppermute | solution.py:728
  107.3 11.5 %collective-permute-start.37 = (bf16[4,24,1920]{2,1,0:T(8,128)(2,1)S(1)}, bf16[4,24,1920]{2,1,0:T(8,128)(2,1)S(1)}, u32[]{:S(2)}, u32[]{:S(2)}) collective-permute-start(bf16[4,24,1920]{2,1,0:T(8,128)(2,1)S(1)} %get-tuple-element.130), channel_id=1, source_target_pairs={{0,4},{1,5},{2,6},{3,7},{4,0},{5,1},{6,2},{7,3},{8,12},{9,13},{10,... | collective-permute-start | bytes 1105928 | tf_op jit(solution)/shard_map/ppermute | solution.py:728
  108.4 14.3 %collective-permute-start.42 = (bf16[4,24,1280]{2,1,0:T(8,128)(2,1)S(1)}, bf16[4,24,1280]{2,1,0:T(8,128)(2,1)S(1)}, u32[]{:S(2)}, u32[]{:S(2)}) collective-permute-start(bf16[4,24,1280]{2,1,0:T(8,128)(2,1)S(1)} %get-tuple-element.143), channel_id=1, source_target_pairs={{0,2},{1,3},{2,0},{3,1},{4,6},{5,7},{6,4},{7,5},{8,10},{9,11},{10,... | collective-permute-start | bytes 737288 | tf_op jit(solution)/shard_map/ppermute | solution.py:728
  109.8 13.1 %collective-permute-start.43 = (bf16[4,24,1280]{2,1,0:T(8,128)(2,1)S(1)}, bf16[4,24,1280]{2,1,0:T(8,128)(2,1)S(1)}, u32[]{:S(2)}, u32[]{:S(2)}) collective-permute-start(bf16[4,24,1280]{2,1,0:T(8,128)(2,1)S(1)} %get-tuple-element.144), channel_id=1, source_target_pairs={{0,4},{1,5},{2,6},{3,7},{4,0},{5,1},{6,2},{7,3},{8,12},{9,13},{10,... | collective-permute-start | bytes 737288 | tf_op jit(solution)/shard_map/ppermute | solution.py:728
  118.8 7.8 %collective-permute-start.39 = (bf16[2,24,1920]{2,1,0:T(8,128)(2,1)S(1)}, bf16[2,24,1920]{2,1,0:T(8,128)(2,1)S(1)}, u32[]{:S(2)}, u32[]{:S(2)}) collective-permute-start(bf16[2,24,1920]{2,1,0:T(8,128)(2,1)S(1)} %get-tuple-element.151), channel_id=1, source_target_pairs={{0,2},{1,3},{2,0},{3,1},{4,6},{5,7},{6,4},{7,5},{8,10},{9,11},{10,... | collective-permute-start | bytes 552968 | tf_op jit(solution)/shard_map/ppermute | solution.py:728
  122.9 5.5 %collective-permute-start.45 = (bf16[2,24,1280]{2,1,0:T(8,128)(2,1)S(1)}, bf16[2,24,1280]{2,1,0:T(8,128)(2,1)S(1)}, u32[]{:S(2)}, u32[]{:S(2)}) collective-permute-start(bf16[2,24,1280]{2,1,0:T(8,128)(2,1)S(1)} %get-tuple-element.157), channel_id=1, source_target_pairs={{0,2},{1,3},{2,0},{3,1},{4,6},{5,7},{6,4},{7,5},{8,10},{9,11},{10,... | collective-permute-start | bytes 368648 | tf_op jit(solution)/shard_map/ppermute | solution.py:728
  124.1 6.9 %collective-permute-start.38 = (bf16[2,24,1920]{2,1,0:T(8,128)(2,1)S(1)}, bf16[2,24,1920]{2,1,0:T(8,128)(2,1)S(1)}, u32[]{:S(2)}, u32[]{:S(2)}) collective-permute-start(bf16[2,24,1920]{2,1,0:T(8,128)(2,1)S(1)} %get-tuple-element.150), channel_id=1, source_target_pairs={{0,4},{1,5},{2,6},{3,7},{4,0},{5,1},{6,2},{7,3},{8,12},{9,13},{10,... | collective-permute-start | bytes 552968 | tf_op jit(solution)/shard_map/ppermute | solution.py:728
  126.7 7.0 %collective-permute-start.40 = (bf16[2,24,1920]{2,1,0:T(8,128)(2,1)S(1)}, bf16[2,24,1920]{2,1,0:T(8,128)(2,1)S(1)}, u32[]{:S(2)}, u32[]{:S(2)}) collective-permute-start(bf16[2,24,1920]{2,1,0:T(8,128)(2,1)S(1)} %shard_map.217), channel_id=1, source_target_pairs={{0,8},{1,9},{2,10},{3,11},{4,12},{5,13},{6,14},{7,15},{8,0},{9,1},... | collective-permute-start | bytes 552968 | tf_op jit(solution)/shard_map/ppermute | solution.py:728
  126.8 8.1 %collective-permute-start.44 = (bf16[2,24,1280]{2,1,0:T(8,128)(2,1)S(1)}, bf16[2,24,1280]{2,1,0:T(8,128)(2,1)S(1)}, u32[]{:S(2)}, u32[]{:S(2)}) collective-permute-start(bf16[2,24,1280]{2,1,0:T(8,128)(2,1)S(1)} %get-tuple-element.156), channel_id=1, source_target_pairs={{0,4},{1,5},{2,6},{3,7},{4,0},{5,1},{6,2},{7,3},{8,12},{9,13},{10,... | collective-permute-start | bytes 368648 | tf_op jit(solution)/shard_map/ppermute | solution.py:728
  128.5 7.5 %collective-permute-start.46 = (bf16[2,24,1280]{2,1,0:T(8,128)(2,1)S(1)}, bf16[2,24,1280]{2,1,0:T(8,128)(2,1)S(1)}, u32[]{:S(2)}, u32[]{:S(2)}) collective-permute-start(bf16[2,24,1280]{2,1,0:T(8,128)(2,1)S(1)} %shard_map.220), channel_id=1, source_target_pairs={{0,8},{1,9},{2,10},{3,11},{4,12},{5,13},{6,14},{7,15},{8,0},{9,1},... | collective-permute-start | bytes 368648 | tf_op jit(solution)/shard_map/ppermute | solution.py:728
  133.9 6.2 %collective-permute-start.41 = (bf16[1,24,1920]{2,1,0:T(8,128)(2,1)S(1)}, bf16[1,24,1920]{2,1,0:T(8,128)(2,1)S(1)}, u32[]{:S(2)}, u32[]{:S(2)}) collective-permute-start(bf16[1,24,1920]{2,1,0:T(8,128)(2,1)S(1)} %get-tuple-element.153), channel_id=1, source_target_pairs={{0,16},{1,17},{2,18},{3,19},{4,20},{5,21},{6,22},{7,23},{8,24},{9,... | collective-permute-start | bytes 276488 | tf_op jit(solution)/shard_map/ppermute | solution.py:728
  136.0 5.8 %collective-permute-start.47 = (bf16[1,24,1280]{2,1,0:T(8,128)(2,1)S(1)}, bf16[1,24,1280]{2,1,0:T(8,128)(2,1)S(1)}, u32[]{:S(2)}, u32[]{:S(2)}) collective-permute-start(bf16[1,24,1280]{2,1,0:T(8,128)(2,1)S(1)} %get-tuple-element.159), channel_id=1, source_target_pairs={{0,16},{1,17},{2,18},{3,19},{4,20},{5,21},{6,22},{7,23},{8,24},{9,... | collective-permute-start | bytes 184328 | tf_op jit(solution)/shard_map/ppermute | solution.py:728
  (8 other events, 147.2 us)

commit v5 on v4

--- a/solution.py
+++ b/solution.py
@@ -92,6 +92,10 @@
     first = head_masks()
     zero = jnp.zeros_like(pair)
     return jnp.concatenate([jnp.where(first, pair, zero), jnp.where(first, zero, pair)], axis=0)
+
+
+def beside(left, right):
+    return jnp.concatenate([left, right], axis=1)
 
 
 def unstacked(both):
@@ -266,18 +270,22 @@
 
         store(joint_ref, joint_out)
         column = lax.broadcasted_iota(jnp.int32, (1, rows), 1)
+        ones = jnp.ones((rows, LANES), bf16)
+        lane = lax.broadcasted_iota(jnp.int32, (2 * rows, LANES), 1)
+        first_lane = jnp.where(lane == 0, 1.0, 0.0).astype(bf16)
+        row = lax.broadcasted_iota(jnp.int32, (rows, LANES), 0)
+        bias = [jnp.where((row >= meta[i]) & (lane[:rows] == 0), NEGATIVE, 0.0).astype(bf16) for i in range(images)]
         for p in range(pairs):
             at_q, at_k, at_v = [slice(i * width + p * LANES, i * width + (p + 1) * LANES) for i in range(3)]
             for img in range(images):
                 span = slice(img * rows, (img + 1) * rows)
                 query, key, value = joint_ref[span, at_q], joint_ref[span, at_k], joint_ref[span, at_v]
-                scores = nt(stacked(query), key) * 0.125
-                scores = jnp.where(column < meta[img], scores, NEGATIVE)
+                scores = nt(beside(stacked(query * 0.125), first_lane), beside(key, bias[img]))
                 weight = jnp.exp(scores - jnp.max(scores, axis=-1, keepdims=True))
-                probs = weight * (1.0 / jnp.sum(weight, axis=-1, keepdims=True))
-                probs = probs.astype(bf16)
-                probs_ref[p, img] = probs
-                mixed_ref[span, at_q] = unstacked(nn(probs, value)).astype(bf16)
+                sums = nn(weight.astype(bf16), beside(value, ones))
+                share = 1.0 / sums[:, LANES:]
+                probs_ref[p, img] = (weight * jnp.concatenate([share, share[:, : rows - LANES]], axis=1)).astype(bf16)
+                mixed_ref[span, at_q] = unstacked(sums[:, :LANES] * share).astype(bf16)
             store(probs_ref.at[p], probs_out.at[p])
         store(mixed_ref, mixed_out)
 
@@ -395,21 +403,21 @@
     return rstd * (scaled - first - x * second)
 
 
-def attend_pull(meta, sizes, half, joint_ref, probs_ref, gm_ref, gj):
+def attend_pull(meta, sizes, half, joint_ref, probs_ref, mixed_ref, gm_ref, gj):
     images, rows, width, *_ = sizes
     share = HEADS // 4
+    ones = jnp.ones((rows, LANES), bf16)
     for q in range(share):
         at_q, at_k, at_v = [slice(i * width // 2 + q * LANES, i * width // 2 + (q + 1) * LANES) for i in range(3)]
         for img in range(images):
             span = slice(img * rows, (img + 1) * rows)
             query, key, value = joint_ref[span, at_q], joint_ref[span, at_k], joint_ref[span, at_v]
             p = half * share + q
-            grad = stacked(gm_ref[span, p * LANES : (p + 1) * LANES])
+            at = slice(p * LANES, (p + 1) * LANES)
+            grad = stacked(gm_ref[span, at])
+            dots = stacked(-(gm_ref[span, at].astype(f32) * mixed_ref[span, at].astype(f32)).astype(bf16))
             low = probs_ref[q, img]
-            probs = low.astype(f32)
-            grad_probs = nt(grad, value)
-            row_dot = jnp.sum(probs * grad_probs, axis=-1, keepdims=True)
-            grad_scores = (probs * (grad_probs - row_dot)).astype(bf16)
+            grad_scores = (low.astype(f32) * nt(beside(grad, dots), beside(value, ones))).astype(bf16)
             gj[span, at_q] = (unstacked(nn(grad_scores, key)) * 0.125).astype(bf16)
             gj[span, at_k] = (tn(grad_scores, stacked(query)) * 0.125).astype(bf16)
             gj[span, at_v] = tn(low, grad).astype(bf16)
@@ -468,8 +476,8 @@
 
     def body(meta, cot_ref, par_ref, log_ref, sum_ref, r1_ref, r2_ref, r3_ref, xn_ref, dev_ref, n2_ref, w_in, xh_in,
              joint_in, probs_in, mixed_in, res_in, block_ref, xgrad_ref, gm, gj, grads, sums_ref, xh_ref,
-             joint_late, probs_late, *refs):
-        outs, (gn, gb, tile, small, w_ref, joint_ref, probs_ref, mixed_ref, res_ref, sems) = refs[:-10], refs[-10:]
+             mixed_ref, joint_late, probs_late, *refs):
+        outs, (gn, gb, tile, small, w_ref, joint_ref, probs_ref, res_ref, sems) = refs[:-9], refs[-9:]
         early = [pltpu.make_async_copy(res_in, res_ref, sems.at[0])]
         late = [
             pltpu.make_async_copy(mixed_in, mixed_ref, sems.at[1]),
@@ -543,7 +551,7 @@
         gm[...] = nt(gb[...], w_ref[...]).astype(bf16)
         for load in loads:
             load.wait()
-        attend_pull(meta, sizes, 0, joint_ref, probs_ref, gm, gj)
+        attend_pull(meta, sizes, 0, joint_ref, probs_ref, mixed_ref, gm, gj)
         for load in last:
             load.wait()
         tile[...] = tn(xh_ref[...], gj[...])
@@ -558,8 +566,8 @@
 def heads_pull_kernel(sizes):
     width = sizes[2]
 
-    def body(meta, gm_ref, joint_ref, probs_ref, gj):
-        attend_pull(meta, sizes, 1, joint_ref, probs_ref, gm_ref, gj)
+    def body(meta, gm_ref, joint_ref, probs_ref, mixed_ref, gj):
+        attend_pull(meta, sizes, 1, joint_ref, probs_ref, mixed_ref, gm_ref, gj)
 
     return body
 
@@ -908,7 +916,7 @@
             far_in=range(2),
             sems=2,
         )(meta, res, n2)
-        block, part, gm, gj, early, sums, xh, joint1, probs1, *first = call(
+        block, part, gm, gj, early, sums, xh, mixed, joint1, probs1, *first = call(
             slots_pull_kernel(sizes),
             [
                 ((total, width), bf16),
@@ -917,6 +925,7 @@
                 ((total, 3 * half), bf16),
                 ((8, width), f32),
                 ((8, 3 * half), f32),
+                ((total, width), bf16),
                 ((total, width), bf16),
             ]
             + halves
@@ -929,17 +938,14 @@
                 ((width, width), bf16),
             ]
             + halves
-            + [
-                ((total, width), bf16),
-                ((total, width), f32),
-            ],
+            + [((total, width), f32)],
             VMEM_MIB,
             far_in=range(10, 16),
             sems=12,
         )(meta, cot, par, logs, *terms, xn, dev, n2, w, xh, joint, probs, mixed, res)
         gj1 = call(
             heads_pull_kernel(sizes), [((total, 3 * half), bf16)], [], VMEM_MIB, flops=3 * 10**9
-        )(meta, gm, joint1, probs1)[0]
+        )(meta, gm, joint1, probs1, mixed)[0]
         gj_late = gj1
         if shares:
             first = scatter_begin(*first, devices)

time: 143 us -> 141 us (0.986)
  Pallas kernels: 43.8 us -> 41.6 us
    pallas_call x8, Pallas kernels: 40.6 us -> 38.4 us  [run(): pl.pallas_call(body, out_shape=[pltpu.HBM(s, d) if i in far_out else jax....]
  transfers between devices with their start and end apart: 48 -> 48, of which waited for: 29 -> 30; matrix products, arithmetic and copies ran while one was open for 0% -> 0% of each run, Pallas kernels for 9% -> 9%
where the time goes in v5:
time: 141 us
  waiting for transfers between devices  55.9 us (40%)
  starting transfers between devices  42 us (30%)
  Pallas kernels  41.6 us (30%)
    ppermute x48, waiting for transfers between devices, swap(): return lax.ppermute(value, 'fsdp', [(i, i ^ mask) for i in range(devices)])  55.9 us
    ppermute x48, starting transfers between devices, swap(): return lax.ppermute(value, 'fsdp', [(i, i ^ mask) for i in range(devices)])  42 us
    pallas_call x8, Pallas kernels, run(): pl.pallas_call(body, out_shape=[pltpu.HBM(s, d) if i in far_out else jax....  38.4 us
  transfers between devices with their start and end apart: 48, of which 30 were waited for; matrix products, arithmetic and copies ran while one was open for 0% of the time, Pallas kernels for 9%

profile of v5, /device:TPU:0, one launch (start us, length us, event | category | flops | bytes accessed | tf_op | source)
XLA Modules:
  0.0 140.6 jit_solution(6182377700806376066)
XLA Ops:
  0.7 1.1 shard_map.203
  1.7 3.1 %collective-permute-start = (bf16[1,24,3200]{2,1,0:T(8,128)(2,1)S(1)}, bf16[1,24,3200]{2,1,0:T(8,128)(2,1)S(1)}, u32[]{:S(2)}, u32[]{:S(2)}) collective-permute-start(bf16[1,24,3200]{2,1,0:T(8,128)(2,1)S(1)} %bitcast.22), channel_id=1, source_target_pairs={{0,8},{1,9},{2,10},{3,11},{4,12},{5,13},{6,14},{7,15},{8,0},{9,1},... | collective-permute-start | bytes 460808 | tf_op jit(solution)/shard_map/ppermute | solution.py:736
  4.8 2.6 %collective-permute-start.1 = (bf16[1,24,3200]{2,1,0:T(8,128)(2,1)S(1)}, bf16[1,24,3200]{2,1,0:T(8,128)(2,1)S(1)}, u32[]{:S(2)}, u32[]{:S(2)}) collective-permute-start(bf16[1,24,3200]{2,1,0:T(8,128)(2,1)S(1)} %bitcast.23), channel_id=1, source_target_pairs={{0,16},{1,17},{2,18},{3,19},{4,20},{5,21},{6,22},{7,23},{8,24},{9,... | collective-permute-start | bytes 460808 | tf_op jit(solution)/shard_map/ppermute | solution.py:736
  7.4 4.2 %collective-permute-done = bf16[1,24,3200]{2,1,0:T(8,128)(2,1)S(1)} collective-permute-done((bf16[1,24,3200]{2,1,0:T(8,128)(2,1)S(1)}, bf16[1,24,3200]{2,1,0:T(8,128)(2,1)S(1)}, u32[]{:S(2)}, u32[]{:S(2)}) %collective-permute-start) | collective-permute-done | bytes 153632 | tf_op jit(solution)/shard_map/ppermute | solution.py:736
  11.7 1.9 %collective-permute-start.5 = (bf16[2,24,3200]{2,1,0:T(8,128)(2,1)S(1)}, bf16[2,24,3200]{2,1,0:T(8,128)(2,1)S(1)}, u32[]{:S(2)}, u32[]{:S(2)}) collective-permute-start(bf16[2,24,3200]{2,1,0:T(8,128)(2,1)S(1)} %pad_maximum_fusion.refs_0_), channel_id=1, source_target_pairs={{0,4},{1,5},{2,6},{3,7},{4,0},{5,1},{6,2},{7,3},{8,12},{9,13},{10,... | collective-permute-start | bytes 921608 | tf_op jit(solution)/shard_map/ppermute | solution.py:736
  13.6 1.5 %collective-permute-start.3 = (bf16[2,24,3200]{2,1,0:T(8,128)(2,1)S(1)}, bf16[2,24,3200]{2,1,0:T(8,128)(2,1)S(1)}, u32[]{:S(2)}, u32[]{:S(2)}) collective-permute-start(bf16[2,24,3200]{2,1,0:T(8,128)(2,1)S(1)} %pad_maximum_fusion.refs_0_), channel_id=1, source_target_pairs={{0,2},{1,3},{2,0},{3,1},{4,6},{5,7},{6,4},{7,5},{8,10},{9,11},{10,... | collective-permute-start | bytes 921608 | tf_op jit(solution)/shard_map/ppermute | solution.py:736
  15.2 5.8 %collective-permute-done.2 = bf16[1,24,3200]{2,1,0:T(8,128)(2,1)S(1)} collective-permute-done((bf16[1,24,3200]{2,1,0:T(8,128)(2,1)S(1)}, bf16[1,24,3200]{2,1,0:T(8,128)(2,1)S(1)}, u32[]{:S(2)}, u32[]{:S(2)}) %collective-permute-start.2) | collective-permute-done | bytes 153632 | tf_op jit(solution)/shard_map/ppermute | solution.py:736
  21.5 1.3 collective-permute-start.6
  23.3 2.0 %collective-permute-start.7 = (bf16[2,24,3200]{2,1,0:T(8,128)(2,1)S(1)}, bf16[2,24,3200]{2,1,0:T(8,128)(2,1)S(1)}, u32[]{:S(2)}, u32[]{:S(2)}) collective-permute-start(bf16[2,24,3200]{2,1,0:T(8,128)(2,1)S(1)} %collective-permute-done.5.refs_4_), channel_id=1, source_target_pairs={{0,2},{1,3},{2,0},{3,1},{4,6},{5,7},{6,4},{7,5},{8,10},{9,11},{10,... | collective-permute-start | bytes 921608 | tf_op jit(solution)/shard_map/ppermute | solution.py:736
  25.2 6.0 %collective-permute-done.4.refs_3_ = bf16[2,24,3200]{2,1,0:T(8,128)(2,1)S(1)} collective-permute-done((bf16[2,24,3200]{2,1,0:T(8,128)(2,1)S(1)}, bf16[2,24,3200]{2,1,0:T(8,128)(2,1)S(1)}, u32[]{:S(2)}, u32[]{:S(2)}) %collective-permute-start.4) | collective-permute-done | bytes 307232 | tf_op jit(solution)/shard_map/ppermute | solution.py:736
  32.3 3.9 %collective-permute-done.7.refs_6_ = bf16[2,24,3200]{2,1,0:T(8,128)(2,1)S(1)} collective-permute-done((bf16[2,24,3200]{2,1,0:T(8,128)(2,1)S(1)}, bf16[2,24,3200]{2,1,0:T(8,128)(2,1)S(1)}, u32[]{:S(2)}, u32[]{:S(2)}) %collective-permute-start.7) | collective-permute-done | bytes 307232 | tf_op jit(solution)/shard_map/ppermute | solution.py:736
  36.1 1.9 %collective-permute-done.8.refs_7_ = bf16[2,24,3200]{2,1,0:T(8,128)(2,1)S(1)} collective-permute-done((bf16[2,24,3200]{2,1,0:T(8,128)(2,1)S(1)}, bf16[2,24,3200]{2,1,0:T(8,128)(2,1)S(1)}, u32[]{:S(2)}, u32[]{:S(2)}) %collective-permute-start.8) | collective-permute-done | bytes 307232 | tf_op jit(solution)/shard_map/ppermute | solution.py:736
  38.1 1.6 %collective-permute-done.16.refs_15_ = bf16[2,24,3200]{2,1,0:T(8,128)(2,1)S(1)} collective-permute-done((bf16[2,24,3200]{2,1,0:T(8,128)(2,1)S(1)}, bf16[2,24,3200]{2,1,0:T(8,128)(2,1)S(1)}, u32[]{:S(2)}, u32[]{:S(2)}) %collective-permute-start.16) | collective-permute-done | bytes 307232 | tf_op jit(solution)/shard_map/ppermute | solution.py:736
  39.7 9.5 %shard_map.204 = (f32[8,768]{1,0:T(8,128)S(1)}, f32[2,4,208]{2,1,0:T(4,128)S(1)}, bf16[16,768]{1,0:T(8,128)(2,1)S(1)}, bf16[416,768]{1,0:T(8,128)(2,1)}, bf16[41...) custom-call(s32[2]{0:T(128)S(1)} %copy-done.5, ...), custom_call_target="tpu_custom_call" | custom-call | tf_op jit(solution)/shard_map/pallas_call | solution.py:57
  49.1 2.8 %collective-permute-start.19 = (bf16[1,16,768]{2,1,0:T(8,128)(2,1)S(1)}, bf16[1,16,768]{2,1,0:T(8,128)(2,1)S(1)}, u32[]{:S(2)}, u32[]{:S(2)}) collective-permute-start(bf16[1,16,768]{2,1,0:T(8,128)(2,1)S(1)} %bitcast.26), channel_id=1, source_target_pairs={{0,24},{1,25},{2,26},{3,27},{4,28},{5,29},{6,30},{7,31},{8,16},{9,... | collective-permute-start | bytes 73736 | tf_op jit(solution)/shard_map/ppermute | solution.py:736
  51.9 1.7 %collective-permute-start.17 = (bf16[1,16,768]{2,1,0:T(8,128)(2,1)S(1)}, bf16[1,16,768]{2,1,0:T(8,128)(2,1)S(1)}, u32[]{:S(2)}, u32[]{:S(2)}) collective-permute-start(bf16[1,16,768]{2,1,0:T(8,128)(2,1)S(1)} %bitcast.28), channel_id=1, source_target_pairs={{0,8},{1,9},{2,10},{3,11},{4,12},{5,13},{6,14},{7,15},{8,0},{9,1},... | collective-permute-start | bytes 73736 | tf_op jit(solution)/shard_map/ppermute | solution.py:736
  53.6 1.3 collective-permute-done.19
  54.9 1.7 %collective-permute-done.18 = bf16[1,16,768]{2,1,0:T(8,128)(2,1)S(1)} collective-permute-done((bf16[1,16,768]{2,1,0:T(8,128)(2,1)S(1)}, bf16[1,16,768]{2,1,0:T(8,128)(2,1)S(1)}, u32[]{:S(2)}, u32[]{:S(2)}) %collective-permute-start.18) | collective-permute-done | bytes 24608 | tf_op jit(solution)/shard_map/ppermute | solution.py:736
  56.7 1.3 collective-permute-start.22
  57.9 1.7 %collective-permute-start.21 = (bf16[4,16,768]{2,1,0:T(8,128)(2,1)S(1)}, bf16[4,16,768]{2,1,0:T(8,128)(2,1)S(1)}, u32[]{:S(2)}, u32[]{:S(2)}) collective-permute-start(bf16[4,16,768]{2,1,0:T(8,128)(2,1)S(1)} %pad_maximum_fusion.1.refs_0_), channel_id=1, source_target_pairs={{0,4},{1,5},{2,6},{3,7},{4,0},{5,1},{6,2},{7,3},{8,12},{9,13},{10,... | collective-permute-start | bytes 294920 | tf_op jit(solution)/shard_map/ppermute | solution.py:736
  60.2 2.3 %collective-permute-done.22.refs_3_ = bf16[4,16,768]{2,1,0:T(8,128)(2,1)S(1)} collective-permute-done((bf16[4,16,768]{2,1,0:T(8,128)(2,1)S(1)}, bf16[4,16,768]{2,1,0:T(8,128)(2,1)S(1)}, u32[]{:S(2)}, u32[]{:S(2)}) %collective-permute-start.22) | collective-permute-done | bytes 98336 | tf_op jit(solution)/shard_map/ppermute | solution.py:736
  65.6 2.6 %shard_map.205 = (bf16[16,16,768]{2,1,0:T(8,128)(2,1)S(1)}, bf16[16,16,768]{2,1,0:T(8,128)(2,1)S(1)}, bf16[256,768]{1,0:T(8,128)(2,1)S(1)}, bf16[256,768]{1,0:T(...) custom-call(s32[2]{0:T(128)S(1)} %copy-done.5, ...), custom_call_target="tpu_custom_call" | custom-call | tf_op jit(solution)/shard_map/pallas_call | solution.py:57
  68.4 1.6 %collective-permute-done.27.refs_1_ = bf16[16,16,768]{2,1,0:T(8,128)(2,1)S(1)} collective-permute-done((bf16[16,16,768]{2,1,0:T(8,128)(2,1)S(1)}, bf16[16,16,768]{2,1,0:T(8,128)(2,1)S(1)}, u32[]{:S(2)}, u32[]{:S(2)}) %collective-permute-start.27) | collective-permute-done | bytes 393248 | tf_op jit(solution)/shard_map/ppermute | solution.py:736
  71.5 2.2 %collective-permute-start.30 = (bf16[4,16,768]{2,1,0:T(8,128)(2,1)S(1)}, bf16[4,16,768]{2,1,0:T(8,128)(2,1)S(1)}, u32[]{:S(2)}, u32[]{:S(2)}) collective-permute-start(bf16[4,16,768]{2,1,0:T(8,128)(2,1)S(1)} %get-tuple-element.99), channel_id=1, source_target_pairs={{0,6},{1,7},{2,4},{3,5},{4,2},{5,3},{6,0},{7,1},{8,14},{9,15},{10,... | collective-permute-start | bytes 294920 | tf_op jit(solution)/shard_map/ppermute | solution.py:736
  73.7 2.4 %shard_map.209 = (f32[416,768]{1,0:T(8,128)S(1)}, f32[416,128]{1,0:T(8,128)S(1)}, bf16[416,768]{1,0:T(8,128)(2,1)S(1)}) custom-call(s32[2]{0:T(128)S(1)} %copy-done.5, f32[416,768]{1,0:T(8,128)} %get-tuple-element.111.res_in, bf16[416,768]{1,0:T(8,128)(2,1)} %get-tuple-element.112.n2_in), custom_call_target="tpu_custom_call" | custom-call | flops 1000000000 | tf_op jit(solution)/shard_map/pallas_call | solution.py:57
  76.1 1.5 %collective-permute-done.29.refs_2_ = bf16[4,16,768]{2,1,0:T(8,128)(2,1)S(1)} collective-permute-done((bf16[4,16,768]{2,1,0:T(8,128)(2,1)S(1)}, bf16[4,16,768]{2,1,0:T(8,128)(2,1)S(1)}, u32[]{:S(2)}, u32[]{:S(2)}) %collective-permute-start.29) | collective-permute-done | bytes 98336 | tf_op jit(solution)/shard_map/ppermute | solution.py:736
  77.7 1.0 collective-permute-start.31
  78.7 1.3 collective-permute-start.32
  80.0 2.1 %collective-permute-start.33 = (bf16[1,16,768]{2,1,0:T(8,128)(2,1)S(1)}, bf16[1,16,768]{2,1,0:T(8,128)(2,1)S(1)}, u32[]{:S(2)}, u32[]{:S(2)}) collective-permute-start(bf16[1,16,768]{2,1,0:T(8,128)(2,1)S(1)} %get-tuple-element.110), channel_id=1, source_target_pairs={{0,24},{1,25},{2,26},{3,27},{4,28},{5,29},{6,30},{7,31},{8,16},{9,... | collective-permute-start | bytes 73736 | tf_op jit(solution)/shard_map/ppermute | solution.py:736
  82.1 2.5 %shard_map.208 = (f32[4,96,768]{2,1,0:T(8,128)}, f32[4,96,768]{2,1,0:T(8,128)}) custom-call(s32[2]{0:T(128)S(1)} %copy-done.5, bf16[256,768]{1,0:T(8,128)(2,1)S(1)} %get-tuple-element.101.s_ref, bf16[256,768]{1,0:T(8,128)(2,1)S(1)} %get-tuple-element.102.g_ref, bf16[256,512]{1,0:T(8,128)(2,1)S(1)} %get-tuple-element.103.act_ref, ...), custom_call_target="tpu_custom_call" | custom-call | flops 2000000000 | tf_op jit(solution)/shard_map/pallas_call | solution.py:57
  85.6 10.6 %shard_map.210 = (bf16[416,768]{1,0:T(8,128)(2,1)}, f32[416,768]{1,0:T(8,128)S(1)}, bf16[416,768]{1,0:T(8,128)(2,1)S(1)}, bf16[416,1152]{1,0:T(8,128)(2,1)S(1)},...) custom-call(s32[2]{0:T(128)S(1)} %copy-done.5, ...), custom_call_target="tpu_custom_call" | custom-call | tf_op jit(solution)/shard_map/pallas_call | solution.py:57
  96.3 2.8 %shard_map.211.gj.gj1_ref = bf16[416,1152]{1,0:T(8,128)(2,1)S(1)} custom-call(s32[2]{0:T(128)S(1)} %copy-done.5, bf16[416,768]{1,0:T(8,128)(2,1)S(1)} %get-tuple-element.123.gm_ref, bf16[416,1152]{1,0:T(8,128)(2,1)S(1)} %get-tuple-element.124.joint_ref, bf16[3,2,416,208]{3,2,1,0:T(8,128)(2,1)S(1)} %get-tuple-element.125.probs_ref, ...), custom_call_target="tpu_custom_call" | custom-call | flops 3000000000 | tf_op jit(solution)/shard_map/pallas_call | solution.py:57
  99.9 3.7 %shard_map.213 = (bf16[768,2304]{1,0:T(8,128)(2,1)S(1)}, bf16[16,24,1280]{2,1,0:T(8,128)(2,1)S(1)}, bf16[16,24,1280]{2,1,0:T(8,128)(2,1)S(1)}) custom-call(s32[2]{0:T(128)S(1)} %copy-done.5, bf16[416,1152]{1,0:T(8,128)(2,1)S(1)} %shard_map.211.gj.gj1_ref, f32[8,768]{1,0:T(8,128)S(1)} %get-tuple-element.136.grads, f32[8,1152]{1,0:T(8,128)S(1)} %get-tuple-element.137.sums_ref, ...), custom_call_target="tpu_custom_call" | custom-call | flops 4000000000 | tf_op jit(solution)/shard_map/pallas_call | solution.py:57
  103.8 1.3 collective-permute-start.36
  106.5 1.3 collective-permute-start.42
  108.6 4.3 %shard_map.215 = f32[416,768]{1,0:T(8,128)} custom-call(s32[2]{0:T(128)S(1)} %copy-done.5, bf16[416,768]{1,0:T(8,128)(2,1)S(1)} %bitcast.21, f32[8,768]{1,0:T(8,128)S(1)} %get-tuple-element.91.par_ref, bf16[416,1152]{1,0:T(8,128)(2,1)S(1)} %get-tuple-element.122.gj0_ref, bf16[416,1152]{1,0:T(8,128)(2,1)S(1)} %shard_map.211.gj.gj1_ref, ...), custom_call_target="tpu_custom_call" | custom-call | flops 5000000000 | tf_op jit(solution)/shard_map/pallas_call | solution.py:57
  113.0 2.3 %collective-permute-done.36.refs_3_.refs_1_ = bf16[4,24,1920]{2,1,0:T(8,128)(2,1)S(1)} collective-permute-done((bf16[4,24,1920]{2,1,0:T(8,128)(2,1)S(1)}, bf16[4,24,1920]{2,1,0:T(8,128)(2,1)S(1)}, u32[]{:S(2)}, u32[]{:S(2)}) %collective-permute-start.36) | collective-permute-done | bytes 368672 | tf_op jit(solution)/shard_map/ppermute | solution.py:736
  115.2 1.3 collective-permute-done.37.refs_2_
  117.5 3.0 %collective-permute-done.42.refs_3_.refs_1_ = bf16[4,24,1280]{2,1,0:T(8,128)(2,1)S(1)} collective-permute-done((bf16[4,24,1280]{2,1,0:T(8,128)(2,1)S(1)}, bf16[4,24,1280]{2,1,0:T(8,128)(2,1)S(1)}, u32[]{:S(2)}, u32[]{:S(2)}) %collective-permute-start.42) | collective-permute-done | bytes 245792 | tf_op jit(solution)/shard_map/ppermute | solution.py:736
  122.8 1.7 %collective-permute-done.39.refs_1_ = bf16[2,24,1920]{2,1,0:T(8,128)(2,1)S(1)} collective-permute-done((bf16[2,24,1920]{2,1,0:T(8,128)(2,1)S(1)}, bf16[2,24,1920]{2,1,0:T(8,128)(2,1)S(1)}, u32[]{:S(2)}, u32[]{:S(2)}) %collective-permute-start.39) | collective-permute-done | bytes 184352 | tf_op jit(solution)/shard_map/ppermute | solution.py:736
  124.6 1.0 collective-permute-start.44
  126.6 1.1 collective-permute-start.46
  128.6 2.9 %collective-permute-done.40.refs_3_ = bf16[2,24,1920]{2,1,0:T(8,128)(2,1)S(1)} collective-permute-done((bf16[2,24,1920]{2,1,0:T(8,128)(2,1)S(1)}, bf16[2,24,1920]{2,1,0:T(8,128)(2,1)S(1)}, u32[]{:S(2)}, u32[]{:S(2)}) %collective-permute-start.40) | collective-permute-done | bytes 184352 | tf_op jit(solution)/shard_map/ppermute | solution.py:736
  131.6 1.0 collective-permute-start.41
  132.6 1.0 collective-permute-done.46.refs_3_
  133.7 1.2 collective-permute-start.47
  134.9 3.0 %collective-permute-done.41.a1 = bf16[1,24,1920]{2,1,0:T(8,128)(2,1)S(1)} collective-permute-done((bf16[1,24,1920]{2,1,0:T(8,128)(2,1)S(1)}, bf16[1,24,1920]{2,1,0:T(8,128)(2,1)S(1)}, u32[]{:S(2)}, u32[]{:S(2)}) %collective-permute-start.41) | collective-permute-done | bytes 92192 | tf_op jit(solution)/shard_map/ppermute | solution.py:736
  137.9 1.6 %collective-permute-done.47.b1 = bf16[1,24,1280]{2,1,0:T(8,128)(2,1)S(1)} collective-permute-done((bf16[1,24,1280]{2,1,0:T(8,128)(2,1)S(1)}, bf16[1,24,1280]{2,1,0:T(8,128)(2,1)S(1)}, u32[]{:S(2)}, u32[]{:S(2)}) %collective-permute-start.47) | collective-permute-done | bytes 61472 | tf_op jit(solution)/shard_map/ppermute | solution.py:736
  (88 shorter events, 18.3 us)
Async XLA Ops:
  1.7 9.9 %collective-permute-start = (bf16[1,24,3200]{2,1,0:T(8,128)(2,1)S(1)}, bf16[1,24,3200]{2,1,0:T(8,128)(2,1)S(1)}, u32[]{:S(2)}, u32[]{:S(2)}) collective-permute-start(bf16[1,24,3200]{2,1,0:T(8,128)(2,1)S(1)} %bitcast.22), channel_id=1, source_target_pairs={{0,8},{1,9},{2,10},{3,11},{4,12},{5,13},{6,14},{7,15},{8,0},{9,1},... | collective-permute-start | bytes 460808 | tf_op jit(solution)/shard_map/ppermute | solution.py:736
  4.8 10.3 %collective-permute-start.1 = (bf16[1,24,3200]{2,1,0:T(8,128)(2,1)S(1)}, bf16[1,24,3200]{2,1,0:T(8,128)(2,1)S(1)}, u32[]{:S(2)}, u32[]{:S(2)}) collective-permute-start(bf16[1,24,3200]{2,1,0:T(8,128)(2,1)S(1)} %bitcast.23), channel_id=1, source_target_pairs={{0,16},{1,17},{2,18},{3,19},{4,20},{5,21},{6,22},{7,23},{8,24},{9,... | collective-permute-start | bytes 460808 | tf_op jit(solution)/shard_map/ppermute | solution.py:736
  11.6 9.9 %collective-permute-start.9 = (bf16[2,24,3200]{2,1,0:T(8,128)(2,1)S(1)}, bf16[2,24,3200]{2,1,0:T(8,128)(2,1)S(1)}, u32[]{:S(2)}, u32[]{:S(2)}) collective-permute-start(bf16[2,24,3200]{2,1,0:T(8,128)(2,1)S(1)} %pad_maximum_fusion.refs_0_), channel_id=1, source_target_pairs={{0,1},{1,0},{2,3},{3,2},{4,5},{5,4},{6,7},{7,6},{8,9},{9,8},{10,11... | collective-permute-start | bytes 921608 | tf_op jit(solution)/shard_map/ppermute | solution.py:736
  11.7 11.1 %collective-permute-start.5 = (bf16[2,24,3200]{2,1,0:T(8,128)(2,1)S(1)}, bf16[2,24,3200]{2,1,0:T(8,128)(2,1)S(1)}, u32[]{:S(2)}, u32[]{:S(2)}) collective-permute-start(bf16[2,24,3200]{2,1,0:T(8,128)(2,1)S(1)} %pad_maximum_fusion.refs_0_), channel_id=1, source_target_pairs={{0,4},{1,5},{2,6},{3,7},{4,0},{5,1},{6,2},{7,3},{8,12},{9,13},{10,... | collective-permute-start | bytes 921608 | tf_op jit(solution)/shard_map/ppermute | solution.py:736
  13.6 9.7 %collective-permute-start.3 = (bf16[2,24,3200]{2,1,0:T(8,128)(2,1)S(1)}, bf16[2,24,3200]{2,1,0:T(8,128)(2,1)S(1)}, u32[]{:S(2)}, u32[]{:S(2)}) collective-permute-start(bf16[2,24,3200]{2,1,0:T(8,128)(2,1)S(1)} %pad_maximum_fusion.refs_0_), channel_id=1, source_target_pairs={{0,2},{1,3},{2,0},{3,1},{4,6},{5,7},{6,4},{7,5},{8,10},{9,11},{10,... | collective-permute-start | bytes 921608 | tf_op jit(solution)/shard_map/ppermute | solution.py:736
  15.1 5.8 %collective-permute-start.2 = (bf16[1,24,3200]{2,1,0:T(8,128)(2,1)S(1)}, bf16[1,24,3200]{2,1,0:T(8,128)(2,1)S(1)}, u32[]{:S(2)}, u32[]{:S(2)}) collective-permute-start(bf16[1,24,3200]{2,1,0:T(8,128)(2,1)S(1)} %collective-permute-done.1), channel_id=1, source_target_pairs={{0,8},{1,9},{2,10},{3,11},{4,12},{5,13},{6,14},{7,15},{8,0},{9,1},... | collective-permute-start | bytes 460808 | tf_op jit(solution)/shard_map/ppermute | solution.py:736
  20.9 10.3 %collective-permute-start.4 = (bf16[2,24,3200]{2,1,0:T(8,128)(2,1)S(1)}, bf16[2,24,3200]{2,1,0:T(8,128)(2,1)S(1)}, u32[]{:S(2)}, u32[]{:S(2)}) collective-permute-start(bf16[2,24,3200]{2,1,0:T(8,128)(2,1)S(1)} %constant_dynamic-update-slice_fusion.refs_1_), channel_id=1, source_target_pairs={{0,2},{1,3},{2,0},{3,1},{4,6},{5,7},{6,4},{7,5},{8,10},{9,11},{10,... | collective-permute-start | bytes 921608 | tf_op jit(solution)/shard_map/ppermute | solution.py:736
  21.5 10.2 %collective-permute-start.10 = (bf16[2,24,3200]{2,1,0:T(8,128)(2,1)S(1)}, bf16[2,24,3200]{2,1,0:T(8,128)(2,1)S(1)}, u32[]{:S(2)}, u32[]{:S(2)}) collective-permute-start(bf16[2,24,3200]{2,1,0:T(8,128)(2,1)S(1)} %constant_dynamic-update-slice_fusion.refs_1_), channel_id=1, source_target_pairs={{0,1},{1,0},{2,3},{3,2},{4,5},{5,4},{6,7},{7,6},{8,9},{9,8},{10,11... | collective-permute-start | bytes 921608 | tf_op jit(solution)/shard_map/ppermute | solution.py:736
  21.5 10.2 %collective-permute-start.6 = (bf16[2,24,3200]{2,1,0:T(8,128)(2,1)S(1)}, bf16[2,24,3200]{2,1,0:T(8,128)(2,1)S(1)}, u32[]{:S(2)}, u32[]{:S(2)}) collective-permute-start(bf16[2,24,3200]{2,1,0:T(8,128)(2,1)S(1)} %constant_dynamic-update-slice_fusion.refs_1_), channel_id=1, source_target_pairs={{0,4},{1,5},{2,6},{3,7},{4,0},{5,1},{6,2},{7,3},{8,12},{9,13},{10,... | collective-permute-start | bytes 921608 | tf_op jit(solution)/shard_map/ppermute | solution.py:736
  22.8 9.4 %collective-permute-start.13 = (bf16[2,24,3200]{2,1,0:T(8,128)(2,1)S(1)}, bf16[2,24,3200]{2,1,0:T(8,128)(2,1)S(1)}, u32[]{:S(2)}, u32[]{:S(2)}) collective-permute-start(bf16[2,24,3200]{2,1,0:T(8,128)(2,1)S(1)} %collective-permute-done.5.refs_4_), channel_id=1, source_target_pairs={{0,1},{1,0},{2,3},{3,2},{4,5},{5,4},{6,7},{7,6},{8,9},{9,8},{10,11... | collective-permute-start | bytes 921608 | tf_op jit(solution)/shard_map/ppermute | solution.py:736
  23.3 12.9 %collective-permute-start.7 = (bf16[2,24,3200]{2,1,0:T(8,128)(2,1)S(1)}, bf16[2,24,3200]{2,1,0:T(8,128)(2,1)S(1)}, u32[]{:S(2)}, u32[]{:S(2)}) collective-permute-start(bf16[2,24,3200]{2,1,0:T(8,128)(2,1)S(1)} %collective-permute-done.5.refs_4_), channel_id=1, source_target_pairs={{0,2},{1,3},{2,0},{3,1},{4,6},{5,7},{6,4},{7,5},{8,10},{9,11},{10,... | collective-permute-start | bytes 921608 | tf_op jit(solution)/shard_map/ppermute | solution.py:736
  31.2 6.9 %collective-permute-start.8 = (bf16[2,24,3200]{2,1,0:T(8,128)(2,1)S(1)}, bf16[2,24,3200]{2,1,0:T(8,128)(2,1)S(1)}, u32[]{:S(2)}, u32[]{:S(2)}) collective-permute-start(bf16[2,24,3200]{2,1,0:T(8,128)(2,1)S(1)} %collective-permute-done.4.refs_3_), channel_id=1, source_target_pairs={{0,4},{1,5},{2,6},{3,7},{4,0},{5,1},{6,2},{7,3},{8,12},{9,13},{10,... | collective-permute-start | bytes 921608 | tf_op jit(solution)/shard_map/ppermute | solution.py:736
  31.7 6.4 %collective-permute-start.11 = (bf16[2,24,3200]{2,1,0:T(8,128)(2,1)S(1)}, bf16[2,24,3200]{2,1,0:T(8,128)(2,1)S(1)}, u32[]{:S(2)}, u32[]{:S(2)}) collective-permute-start(bf16[2,24,3200]{2,1,0:T(8,128)(2,1)S(1)} %collective-permute-done.3.refs_2_), channel_id=1, source_target_pairs={{0,1},{1,0},{2,3},{3,2},{4,5},{5,4},{6,7},{7,6},{8,9},{9,8},{10,11... | collective-permute-start | bytes 921608 | tf_op jit(solution)/shard_map/ppermute | solution.py:736
  31.7 6.4 %collective-permute-start.12 = (bf16[2,24,3200]{2,1,0:T(8,128)(2,1)S(1)}, bf16[2,24,3200]{2,1,0:T(8,128)(2,1)S(1)}, u32[]{:S(2)}, u32[]{:S(2)}) collective-permute-start(bf16[2,24,3200]{2,1,0:T(8,128)(2,1)S(1)} %collective-permute-done.4.refs_3_), channel_id=1, source_target_pairs={{0,1},{1,0},{2,3},{3,2},{4,5},{5,4},{6,7},{7,6},{8,9},{9,8},{10,11... | collective-permute-start | bytes 921608 | tf_op jit(solution)/shard_map/ppermute | solution.py:736
  32.2 5.8 %collective-permute-start.14 = (bf16[2,24,3200]{2,1,0:T(8,128)(2,1)S(1)}, bf16[2,24,3200]{2,1,0:T(8,128)(2,1)S(1)}, u32[]{:S(2)}, u32[]{:S(2)}) collective-permute-start(bf16[2,24,3200]{2,1,0:T(8,128)(2,1)S(1)} %collective-permute-done.6.refs_5_), channel_id=1, source_target_pairs={{0,1},{1,0},{2,3},{3,2},{4,5},{5,4},{6,7},{7,6},{8,9},{9,8},{10,11... | collective-permute-start | bytes 921608 | tf_op jit(solution)/shard_map/ppermute | solution.py:736
  36.1 1.9 %collective-permute-start.15 = (bf16[2,24,3200]{2,1,0:T(8,128)(2,1)S(1)}, bf16[2,24,3200]{2,1,0:T(8,128)(2,1)S(1)}, u32[]{:S(2)}, u32[]{:S(2)}) collective-permute-start(bf16[2,24,3200]{2,1,0:T(8,128)(2,1)S(1)} %collective-permute-done.7.refs_6_), channel_id=1, source_target_pairs={{0,1},{1,0},{2,3},{3,2},{4,5},{5,4},{6,7},{7,6},{8,9},{9,8},{10,11... | collective-permute-start | bytes 921608 | tf_op jit(solution)/shard_map/ppermute | solution.py:736
  38.1 1.6 %collective-permute-start.16 = (bf16[2,24,3200]{2,1,0:T(8,128)(2,1)S(1)}, bf16[2,24,3200]{2,1,0:T(8,128)(2,1)S(1)}, u32[]{:S(2)}, u32[]{:S(2)}) collective-permute-start(bf16[2,24,3200]{2,1,0:T(8,128)(2,1)S(1)} %collective-permute-done.8.refs_7_), channel_id=1, source_target_pairs={{0,1},{1,0},{2,3},{3,2},{4,5},{5,4},{6,7},{7,6},{8,9},{9,8},{10,11... | collective-permute-start | bytes 921608 | tf_op jit(solution)/shard_map/ppermute | solution.py:736
  49.1 5.7 %collective-permute-start.19 = (bf16[1,16,768]{2,1,0:T(8,128)(2,1)S(1)}, bf16[1,16,768]{2,1,0:T(8,128)(2,1)S(1)}, u32[]{:S(2)}, u32[]{:S(2)}) collective-permute-start(bf16[1,16,768]{2,1,0:T(8,128)(2,1)S(1)} %bitcast.26), channel_id=1, source_target_pairs={{0,24},{1,25},{2,26},{3,27},{4,28},{5,29},{6,30},{7,31},{8,16},{9,... | collective-permute-start | bytes 73736 | tf_op jit(solution)/shard_map/ppermute | solution.py:736
  51.9 4.7 %collective-permute-start.18 = (bf16[1,16,768]{2,1,0:T(8,128)(2,1)S(1)}, bf16[1,16,768]{2,1,0:T(8,128)(2,1)S(1)}, u32[]{:S(2)}, u32[]{:S(2)}) collective-permute-start(bf16[1,16,768]{2,1,0:T(8,128)(2,1)S(1)} %bitcast.27), channel_id=1, source_target_pairs={{0,16},{1,17},{2,18},{3,19},{4,20},{5,21},{6,22},{7,23},{8,24},{9,... | collective-permute-start | bytes 73736 | tf_op jit(solution)/shard_map/ppermute | solution.py:736
  51.9 4.7 %collective-permute-start.17 = (bf16[1,16,768]{2,1,0:T(8,128)(2,1)S(1)}, bf16[1,16,768]{2,1,0:T(8,128)(2,1)S(1)}, u32[]{:S(2)}, u32[]{:S(2)}) collective-permute-start(bf16[1,16,768]{2,1,0:T(8,128)(2,1)S(1)} %bitcast.28), channel_id=1, source_target_pairs={{0,8},{1,9},{2,10},{3,11},{4,12},{5,13},{6,14},{7,15},{8,0},{9,1},... | collective-permute-start | bytes 73736 | tf_op jit(solution)/shard_map/ppermute | solution.py:736
  56.7 5.8 %collective-permute-start.22 = (bf16[4,16,768]{2,1,0:T(8,128)(2,1)S(1)}, bf16[4,16,768]{2,1,0:T(8,128)(2,1)S(1)}, u32[]{:S(2)}, u32[]{:S(2)}) collective-permute-start(bf16[4,16,768]{2,1,0:T(8,128)(2,1)S(1)} %pad_maximum_fusion.1.refs_0_), channel_id=1, source_target_pairs={{0,6},{1,7},{2,4},{3,5},{4,2},{5,3},{6,0},{7,1},{8,14},{9,15},{10,... | collective-permute-start | bytes 294920 | tf_op jit(solution)/shard_map/ppermute | solution.py:736
  57.9 5.5 %collective-permute-start.21 = (bf16[4,16,768]{2,1,0:T(8,128)(2,1)S(1)}, bf16[4,16,768]{2,1,0:T(8,128)(2,1)S(1)}, u32[]{:S(2)}, u32[]{:S(2)}) collective-permute-start(bf16[4,16,768]{2,1,0:T(8,128)(2,1)S(1)} %pad_maximum_fusion.1.refs_0_), channel_id=1, source_target_pairs={{0,4},{1,5},{2,6},{3,7},{4,0},{5,1},{6,2},{7,3},{8,12},{9,13},{10,... | collective-permute-start | bytes 294920 | tf_op jit(solution)/shard_map/ppermute | solution.py:736
  59.7 4.6 %collective-permute-start.20 = (bf16[4,16,768]{2,1,0:T(8,128)(2,1)S(1)}, bf16[4,16,768]{2,1,0:T(8,128)(2,1)S(1)}, u32[]{:S(2)}, u32[]{:S(2)}) collective-permute-start(bf16[4,16,768]{2,1,0:T(8,128)(2,1)S(1)} %pad_maximum_fusion.1.refs_0_), channel_id=1, source_target_pairs={{0,2},{1,3},{2,0},{3,1},{4,6},{5,7},{6,4},{7,5},{8,10},{9,11},{10,... | collective-permute-start | bytes 294920 | tf_op jit(solution)/shard_map/ppermute | solution.py:736
  60.2 4.1 %collective-permute-start.23 = (bf16[4,16,768]{2,1,0:T(8,128)(2,1)S(1)}, bf16[4,16,768]{2,1,0:T(8,128)(2,1)S(1)}, u32[]{:S(2)}, u32[]{:S(2)}) collective-permute-start(bf16[4,16,768]{2,1,0:T(8,128)(2,1)S(1)} %pad_maximum_fusion.1.refs_0_), channel_id=1, source_target_pairs={{0,1},{1,0},{2,3},{3,2},{4,5},{5,4},{6,7},{7,6},{8,9},{9,8},{10,11... | collective-permute-start | bytes 294920 | tf_op jit(solution)/shard_map/ppermute | solution.py:736
  62.5 1.9 %collective-permute-start.26 = (bf16[4,16,768]{2,1,0:T(8,128)(2,1)S(1)}, bf16[4,16,768]{2,1,0:T(8,128)(2,1)S(1)}, u32[]{:S(2)}, u32[]{:S(2)}) collective-permute-start(bf16[4,16,768]{2,1,0:T(8,128)(2,1)S(1)} %collective-permute-done.22.refs_3_), channel_id=1, source_target_pairs={{0,1},{1,0},{2,3},{3,2},{4,5},{5,4},{6,7},{7,6},{8,9},{9,8},{10,11... | collective-permute-start | bytes 294920 | tf_op jit(solution)/shard_map/ppermute | solution.py:736
  63.4 1.3 collective-permute-start.25
  64.3 1.3 collective-permute-start.24
  68.2 1.8 %collective-permute-start.27 = (bf16[16,16,768]{2,1,0:T(8,128)(2,1)S(1)}, bf16[16,16,768]{2,1,0:T(8,128)(2,1)S(1)}, u32[]{:S(2)}, u32[]{:S(2)}) collective-permute-start(bf16[16,16,768]{2,1,0:T(8,128)(2,1)S(1)} %get-tuple-element.95), channel_id=1, source_target_pairs={{0,1},{1,0},{2,3},{3,2},{4,5},{5,4},{6,7},{7,6},{8,9},{9,8},{10,11... | collective-permute-start | bytes 1179656 | tf_op jit(solution)/shard_map/ppermute | solution.py:736
  70.2 5.9 %collective-permute-start.28 = (bf16[4,16,768]{2,1,0:T(8,128)(2,1)S(1)}, bf16[4,16,768]{2,1,0:T(8,128)(2,1)S(1)}, u32[]{:S(2)}, u32[]{:S(2)}) collective-permute-start(bf16[4,16,768]{2,1,0:T(8,128)(2,1)S(1)} %get-tuple-element.97), channel_id=1, source_target_pairs={{0,2},{1,3},{2,0},{3,1},{4,6},{5,7},{6,4},{7,5},{8,10},{9,11},{10,... | collective-permute-start | bytes 294920 | tf_op jit(solution)/shard_map/ppermute | solution.py:736
  70.7 6.9 %collective-permute-start.29 = (bf16[4,16,768]{2,1,0:T(8,128)(2,1)S(1)}, bf16[4,16,768]{2,1,0:T(8,128)(2,1)S(1)}, u32[]{:S(2)}, u32[]{:S(2)}) collective-permute-start(bf16[4,16,768]{2,1,0:T(8,128)(2,1)S(1)} %get-tuple-element.98), channel_id=1, source_target_pairs={{0,4},{1,5},{2,6},{3,7},{4,0},{5,1},{6,2},{7,3},{8,12},{9,13},{10,... | collective-permute-start | bytes 294920 | tf_op jit(solution)/shard_map/ppermute | solution.py:736
  71.5 6.1 %collective-permute-start.30 = (bf16[4,16,768]{2,1,0:T(8,128)(2,1)S(1)}, bf16[4,16,768]{2,1,0:T(8,128)(2,1)S(1)}, u32[]{:S(2)}, u32[]{:S(2)}) collective-permute-start(bf16[4,16,768]{2,1,0:T(8,128)(2,1)S(1)} %get-tuple-element.99), channel_id=1, source_target_pairs={{0,6},{1,7},{2,4},{3,5},{4,2},{5,3},{6,0},{7,1},{8,14},{9,15},{10,... | collective-permute-start | bytes 294920 | tf_op jit(solution)/shard_map/ppermute | solution.py:736
  77.7 7.0 %collective-permute-start.31 = (bf16[1,16,768]{2,1,0:T(8,128)(2,1)S(1)}, bf16[1,16,768]{2,1,0:T(8,128)(2,1)S(1)}, u32[]{:S(2)}, u32[]{:S(2)}) collective-permute-start(bf16[1,16,768]{2,1,0:T(8,128)(2,1)S(1)} %get-tuple-element.108), channel_id=1, source_target_pairs={{0,8},{1,9},{2,10},{3,11},{4,12},{5,13},{6,14},{7,15},{8,0},{9,1},... | collective-permute-start | bytes 73736 | tf_op jit(solution)/shard_map/ppermute | solution.py:736
  78.7 6.0 %collective-permute-start.32 = (bf16[1,16,768]{2,1,0:T(8,128)(2,1)S(1)}, bf16[1,16,768]{2,1,0:T(8,128)(2,1)S(1)}, u32[]{:S(2)}, u32[]{:S(2)}) collective-permute-start(bf16[1,16,768]{2,1,0:T(8,128)(2,1)S(1)} %get-tuple-element.109), channel_id=1, source_target_pairs={{0,16},{1,17},{2,18},{3,19},{4,20},{5,21},{6,22},{7,23},{8,24},{9,... | collective-permute-start | bytes 73736 | tf_op jit(solution)/shard_map/ppermute | solution.py:736
  80.0 5.6 %collective-permute-start.33 = (bf16[1,16,768]{2,1,0:T(8,128)(2,1)S(1)}, bf16[1,16,768]{2,1,0:T(8,128)(2,1)S(1)}, u32[]{:S(2)}, u32[]{:S(2)}) collective-permute-start(bf16[1,16,768]{2,1,0:T(8,128)(2,1)S(1)} %get-tuple-element.110), channel_id=1, source_target_pairs={{0,24},{1,25},{2,26},{3,27},{4,28},{5,29},{6,30},{7,31},{8,16},{9,... | collective-permute-start | bytes 73736 | tf_op jit(solution)/shard_map/ppermute | solution.py:736
  96.2 3.3 %collective-permute-start.34 = (bf16[16,24,1920]{2,1,0:T(8,128)(2,1)S(1)}, bf16[16,24,1920]{2,1,0:T(8,128)(2,1)S(1)}, u32[]{:S(2)}, u32[]{:S(2)}) collective-permute-start(bf16[16,24,1920]{2,1,0:T(8,128)(2,1)S(1)} %get-tuple-element.128), channel_id=1, source_target_pairs={{0,1},{1,0},{2,3},{3,2},{4,5},{5,4},{6,7},{7,6},{8,9},{9,8},{10,11... | collective-permute-start | bytes 4423688 | tf_op jit(solution)/shard_map/ppermute | solution.py:736
  103.6 2.6 %collective-permute-start.35 = (bf16[16,24,1280]{2,1,0:T(8,128)(2,1)S(1)}, bf16[16,24,1280]{2,1,0:T(8,128)(2,1)S(1)}, u32[]{:S(2)}, u32[]{:S(2)}) collective-permute-start(bf16[16,24,1280]{2,1,0:T(8,128)(2,1)S(1)} %get-tuple-element.142), channel_id=1, source_target_pairs={{0,1},{1,0},{2,3},{3,2},{4,5},{5,4},{6,7},{7,6},{8,9},{9,8},{10,11... | collective-permute-start | bytes 2949128 | tf_op jit(solution)/shard_map/ppermute | solution.py:736
  103.8 11.4 %collective-permute-start.36 = (bf16[4,24,1920]{2,1,0:T(8,128)(2,1)S(1)}, bf16[4,24,1920]{2,1,0:T(8,128)(2,1)S(1)}, u32[]{:S(2)}, u32[]{:S(2)}) collective-permute-start(bf16[4,24,1920]{2,1,0:T(8,128)(2,1)S(1)} %get-tuple-element.131), channel_id=1, source_target_pairs={{0,2},{1,3},{2,0},{3,1},{4,6},{5,7},{6,4},{7,5},{8,10},{9,11},{10,... | collective-permute-start | bytes 1105928 | tf_op jit(solution)/shard_map/ppermute | solution.py:736
  105.1 11.4 %collective-permute-start.37 = (bf16[4,24,1920]{2,1,0:T(8,128)(2,1)S(1)}, bf16[4,24,1920]{2,1,0:T(8,128)(2,1)S(1)}, u32[]{:S(2)}, u32[]{:S(2)}) collective-permute-start(bf16[4,24,1920]{2,1,0:T(8,128)(2,1)S(1)} %get-tuple-element.132), channel_id=1, source_target_pairs={{0,4},{1,5},{2,6},{3,7},{4,0},{5,1},{6,2},{7,3},{8,12},{9,13},{10,... | collective-permute-start | bytes 1105928 | tf_op jit(solution)/shard_map/ppermute | solution.py:736
  106.5 14.0 %collective-permute-start.42 = (bf16[4,24,1280]{2,1,0:T(8,128)(2,1)S(1)}, bf16[4,24,1280]{2,1,0:T(8,128)(2,1)S(1)}, u32[]{:S(2)}, u32[]{:S(2)}) collective-permute-start(bf16[4,24,1280]{2,1,0:T(8,128)(2,1)S(1)} %get-tuple-element.145), channel_id=1, source_target_pairs={{0,2},{1,3},{2,0},{3,1},{4,6},{5,7},{6,4},{7,5},{8,10},{9,11},{10,... | collective-permute-start | bytes 737288 | tf_op jit(solution)/shard_map/ppermute | solution.py:736
  107.8 13.1 %collective-permute-start.43 = (bf16[4,24,1280]{2,1,0:T(8,128)(2,1)S(1)}, bf16[4,24,1280]{2,1,0:T(8,128)(2,1)S(1)}, u32[]{:S(2)}, u32[]{:S(2)}) collective-permute-start(bf16[4,24,1280]{2,1,0:T(8,128)(2,1)S(1)} %get-tuple-element.146), channel_id=1, source_target_pairs={{0,4},{1,5},{2,6},{3,7},{4,0},{5,1},{6,2},{7,3},{8,12},{9,13},{10,... | collective-permute-start | bytes 737288 | tf_op jit(solution)/shard_map/ppermute | solution.py:736
  116.7 7.8 %collective-permute-start.39 = (bf16[2,24,1920]{2,1,0:T(8,128)(2,1)S(1)}, bf16[2,24,1920]{2,1,0:T(8,128)(2,1)S(1)}, u32[]{:S(2)}, u32[]{:S(2)}) collective-permute-start(bf16[2,24,1920]{2,1,0:T(8,128)(2,1)S(1)} %get-tuple-element.153), channel_id=1, source_target_pairs={{0,2},{1,3},{2,0},{3,1},{4,6},{5,7},{6,4},{7,5},{8,10},{9,11},{10,... | collective-permute-start | bytes 552968 | tf_op jit(solution)/shard_map/ppermute | solution.py:736
  121.0 5.5 %collective-permute-start.45 = (bf16[2,24,1280]{2,1,0:T(8,128)(2,1)S(1)}, bf16[2,24,1280]{2,1,0:T(8,128)(2,1)S(1)}, u32[]{:S(2)}, u32[]{:S(2)}) collective-permute-start(bf16[2,24,1280]{2,1,0:T(8,128)(2,1)S(1)} %get-tuple-element.159), channel_id=1, source_target_pairs={{0,2},{1,3},{2,0},{3,1},{4,6},{5,7},{6,4},{7,5},{8,10},{9,11},{10,... | collective-permute-start | bytes 368648 | tf_op jit(solution)/shard_map/ppermute | solution.py:736
  121.9 6.7 %collective-permute-start.38 = (bf16[2,24,1920]{2,1,0:T(8,128)(2,1)S(1)}, bf16[2,24,1920]{2,1,0:T(8,128)(2,1)S(1)}, u32[]{:S(2)}, u32[]{:S(2)}) collective-permute-start(bf16[2,24,1920]{2,1,0:T(8,128)(2,1)S(1)} %get-tuple-element.152), channel_id=1, source_target_pairs={{0,4},{1,5},{2,6},{3,7},{4,0},{5,1},{6,2},{7,3},{8,12},{9,13},{10,... | collective-permute-start | bytes 552968 | tf_op jit(solution)/shard_map/ppermute | solution.py:736
  124.6 6.9 %collective-permute-start.40 = (bf16[2,24,1920]{2,1,0:T(8,128)(2,1)S(1)}, bf16[2,24,1920]{2,1,0:T(8,128)(2,1)S(1)}, u32[]{:S(2)}, u32[]{:S(2)}) collective-permute-start(bf16[2,24,1920]{2,1,0:T(8,128)(2,1)S(1)} %shard_map.217), channel_id=1, source_target_pairs={{0,8},{1,9},{2,10},{3,11},{4,12},{5,13},{6,14},{7,15},{8,0},{9,1},... | collective-permute-start | bytes 552968 | tf_op jit(solution)/shard_map/ppermute | solution.py:736
  124.6 8.0 %collective-permute-start.44 = (bf16[2,24,1280]{2,1,0:T(8,128)(2,1)S(1)}, bf16[2,24,1280]{2,1,0:T(8,128)(2,1)S(1)}, u32[]{:S(2)}, u32[]{:S(2)}) collective-permute-start(bf16[2,24,1280]{2,1,0:T(8,128)(2,1)S(1)} %get-tuple-element.158), channel_id=1, source_target_pairs={{0,4},{1,5},{2,6},{3,7},{4,0},{5,1},{6,2},{7,3},{8,12},{9,13},{10,... | collective-permute-start | bytes 368648 | tf_op jit(solution)/shard_map/ppermute | solution.py:736
  126.6 7.1 %collective-permute-start.46 = (bf16[2,24,1280]{2,1,0:T(8,128)(2,1)S(1)}, bf16[2,24,1280]{2,1,0:T(8,128)(2,1)S(1)}, u32[]{:S(2)}, u32[]{:S(2)}) collective-permute-start(bf16[2,24,1280]{2,1,0:T(8,128)(2,1)S(1)} %shard_map.220), channel_id=1, source_target_pairs={{0,8},{1,9},{2,10},{3,11},{4,12},{5,13},{6,14},{7,15},{8,0},{9,1},... | collective-permute-start | bytes 368648 | tf_op jit(solution)/shard_map/ppermute | solution.py:736
  131.6 6.3 %collective-permute-start.41 = (bf16[1,24,1920]{2,1,0:T(8,128)(2,1)S(1)}, bf16[1,24,1920]{2,1,0:T(8,128)(2,1)S(1)}, u32[]{:S(2)}, u32[]{:S(2)}) collective-permute-start(bf16[1,24,1920]{2,1,0:T(8,128)(2,1)S(1)} %get-tuple-element.155), channel_id=1, source_target_pairs={{0,16},{1,17},{2,18},{3,19},{4,20},{5,21},{6,22},{7,23},{8,24},{9,... | collective-permute-start | bytes 276488 | tf_op jit(solution)/shard_map/ppermute | solution.py:736
  133.7 5.8 %collective-permute-start.47 = (bf16[1,24,1280]{2,1,0:T(8,128)(2,1)S(1)}, bf16[1,24,1280]{2,1,0:T(8,128)(2,1)S(1)}, u32[]{:S(2)}, u32[]{:S(2)}) collective-permute-start(bf16[1,24,1280]{2,1,0:T(8,128)(2,1)S(1)} %get-tuple-element.161), channel_id=1, source_target_pairs={{0,16},{1,17},{2,18},{3,19},{4,20},{5,21},{6,22},{7,23},{8,24},{9,... | collective-permute-start | bytes 184328 | tf_op jit(solution)/shard_map/ppermute | solution.py:736
  (8 other events, 144.6 us)

commit v6 on v5

--- a/solution.py
+++ b/solution.py
@@ -475,10 +475,9 @@
     share = HEADS // 4
 
     def body(meta, cot_ref, par_ref, log_ref, sum_ref, r1_ref, r2_ref, r3_ref, xn_ref, dev_ref, n2_ref, w_in, xh_in,
-             joint_in, probs_in, mixed_in, res_in, block_ref, xgrad_ref, gm, gj, grads, sums_ref, xh_ref,
-             mixed_ref, joint_late, probs_late, *refs):
-        outs, (gn, gb, tile, small, w_ref, joint_ref, probs_ref, res_ref, sems) = refs[:-9], refs[-9:]
-        early = [pltpu.make_async_copy(res_in, res_ref, sems.at[0])]
+             joint_in, probs_in, mixed_in, small, grad_logs, xgrad_ref, gm, gj, grads, sums_ref, xh_ref,
+             mixed_ref, joint_late, probs_late, w_late, *refs):
+        outs, (gn, gb, tile, w_ref, joint_ref, probs_ref, sems) = refs[:-7], refs[-7:]
         late = [
             pltpu.make_async_copy(mixed_in, mixed_ref, sems.at[1]),
             pltpu.make_async_copy(w_in.at[:, 3 * width : 4 * width], w_ref, sems.at[2]),
@@ -486,7 +485,8 @@
         loads = half_loads(width, 0, joint_in, joint_ref, probs_in, probs_ref, sems.at[3:7])
         last = [pltpu.make_async_copy(xh_in, xh_ref, sems.at[7])]
         ahead = half_loads(width, 1, joint_in, joint_late, probs_in, probs_late, sems.at[8:12])
-        for load in early + late + loads + last + ahead:
+        ahead += weight_loads(width, w_in, w_late, sems.at[12:18])
+        for load in late + loads + last + ahead:
             load.start()
 
         def put(first, count):
@@ -499,7 +499,6 @@
         small[...] = sums.astype(bf16).astype(f32)
         slot_w = par_ref[4 : 4 + experts]
         column = lax.broadcasted_iota(jnp.int32, (1, rows), 1)
-        slot_grad = jnp.zeros((experts, width), f32)
         for img in range(images):
             span = slice(img * rows, (img + 1) * rows)
             live = column < meta[img]
@@ -513,17 +512,11 @@
             grad_log = grad_log + dispatch * (
                 grad_disp - jnp.sum(dispatch * grad_disp, axis=1, keepdims=True)
             )
-            slot_grad = slot_grad + nn(grad_log.astype(bf16), n2_ref[span])
+            grad_logs[img] = grad_log
             left = jnp.concatenate([dispatch, grad_log], axis=0).astype(bf16)
             right = jnp.concatenate([grad32, slot_w], axis=0).astype(bf16)
             gn[span] = tn(left, right)
-            live_row = lax.broadcasted_iota(jnp.int32, (rows, 1), 0) < meta[img]
-            expert_sum = tn(combine.astype(bf16), slot_out)
-            for load in early if img == 0 else []:
-                load.wait()
-            block_ref[span] = jnp.where(live_row, res_ref[span] + expert_sum, 0.0).astype(bf16)
-        grads[0:2] = jnp.zeros((2, width), f32)
-        grads[4 : 4 + experts] = slot_grad
+        grads[...] = jnp.zeros(grads.shape, f32)
 
         gain_m = par_ref[2:3]
         zero = jnp.zeros((8, width), f32)
@@ -564,9 +557,14 @@
 
 
 def heads_pull_kernel(sizes):
-    width = sizes[2]
-
-    def body(meta, gm_ref, joint_ref, probs_ref, mixed_ref, gj):
+    images, rows, width, experts, *_ = sizes
+
+    def body(meta, gm_ref, joint_ref, probs_ref, mixed_ref, grad_logs, n2_ref, gj, slot_ref):
+        total = jnp.zeros((experts, width), f32)
+        for img in range(images):
+            total = total + nn(grad_logs[img].astype(bf16), n2_ref[img * rows : (img + 1) * rows])
+        slot_ref[...] = jnp.zeros(slot_ref.shape, f32)
+        slot_ref[4 : 4 + experts] = total
         attend_pull(meta, sizes, 1, joint_ref, probs_ref, mixed_ref, gm_ref, gj)
 
     return body
@@ -576,14 +574,11 @@
     images, rows, width, experts, chips, part_rows, shares = sizes
     half = 3 * width // 2
 
-    def body(meta, gj, grads, sums_ref, xh_ref, w_in, w_ref, *refs):
-        outs, (tile, small, sems) = refs[:-3], refs[-3:]
-        loads = weight_loads(width, w_in, w_ref, sems)
-        for load in loads:
-            load.start()
+    def body(meta, gj, grads, slot_ref, sums_ref, xh_ref, *refs):
+        outs, (tile, small) = refs[:-2], refs[-2:]
         sums = [sums_ref[0:1], column_sums(gj)]
         wide = sums_lanes(width, part_rows)
-        small[:, :LANES] = jnp.concatenate([grads[...], jnp.zeros((LANES - 8, width), f32)], axis=0).T
+        small[:, :LANES] = jnp.concatenate([grads[...] + slot_ref[...], jnp.zeros((LANES - 8, width), f32)], axis=0).T
         each = 3 * width // part_rows
         for r in range(part_rows):
             row = [s[:, c0 - i * half : c1 - i * half] for i, s in enumerate(sums)
@@ -601,8 +596,6 @@
 
         put(tile, half, 0)
         put(small, small.shape[1], half)
-        for load in loads:
-            load.wait()
 
     return body
 
@@ -612,8 +605,19 @@
     total = images * rows
     half = 3 * width // 2
 
-    def body(meta, x_ref, par_ref, gj0_ref, gj1_ref, w_ref, part_ref, xgrad_ref, gn):
+    def body(meta, x_ref, par_ref, gj0_ref, gj1_ref, w_ref, part_ref, log_ref, small, res_in, xgrad_ref, block_ref,
+             gn, res_ref, sems):
+        load = pltpu.make_async_copy(res_in, res_ref, sems.at[0])
+        load.start()
         gn[...] = nt(gj0_ref[...], w_ref[:, :half]) + nt(gj1_ref[...], w_ref[:, half:])
+        column = lax.broadcasted_iota(jnp.int32, (1, rows), 1)
+        load.wait()
+        for img in range(images):
+            span = slice(img * rows, (img + 1) * rows)
+            _, combine = routing(log_ref[img], column < meta[img])
+            live_row = lax.broadcasted_iota(jnp.int32, (rows, 1), 0) < meta[img]
+            expert_sum = tn(combine.astype(bf16), small[img * experts : (img + 1) * experts].astype(bf16))
+            block_ref[span] = jnp.where(live_row, res_ref[span] + expert_sum, 0.0).astype(bf16)
         gain_a = par_ref[0:1]
 
         @pl.loop(0, total // CHUNK, unroll=UNROLL)
@@ -916,10 +920,11 @@
             far_in=range(2),
             sems=2,
         )(meta, res, n2)
-        block, part, gm, gj, early, sums, xh, mixed, joint1, probs1, *first = call(
+        slot_sums, grad_logs, part, gm, gj, early, sums, xh, mixed, joint1, probs1, w_all, *first = call(
             slots_pull_kernel(sizes),
             [
-                ((total, width), bf16),
+                ((2 * count * experts, width), f32),
+                ((count, experts, rows), f32),
                 ((total, width), f32),
                 ((total, width), bf16),
                 ((total, 3 * half), bf16),
@@ -929,47 +934,46 @@
                 ((total, width), bf16),
             ]
             + halves
+            + [((width, 3 * width), bf16)]
             + blocks(width + 3 * half),
             [
                 ((total, width), f32),
                 ((total, width), bf16),
                 ((width, 3 * half), f32),
-                ((2 * count * experts, width), f32),
                 ((width, width), bf16),
             ]
-            + halves
-            + [((total, width), f32)],
+            + halves,
             VMEM_MIB,
-            far_in=range(10, 16),
-            sems=12,
-        )(meta, cot, par, logs, *terms, xn, dev, n2, w, xh, joint, probs, mixed, res)
-        gj1 = call(
-            heads_pull_kernel(sizes), [((total, 3 * half), bf16)], [], VMEM_MIB, flops=3 * 10**9
-        )(meta, gm, joint1, probs1, mixed)[0]
+            far_in=range(10, 15),
+            sems=18,
+        )(meta, cot, par, logs, *terms, xn, dev, n2, w, xh, joint, probs, mixed)
+        gj1, slot_grads = call(
+            heads_pull_kernel(sizes), [((total, 3 * half), bf16), ((8, width), f32)], [], VMEM_MIB, flops=3 * 10**9
+        )(meta, gm, joint1, probs1, mixed, grad_logs, n2)
         gj_late = gj1
         if shares:
             first = scatter_begin(*first, devices)
             gj_late = after([gj1], first)[0]
         tiny = small_lanes(width, part_rows)
-        w_all, *second = call(
+        second = call(
             heads_grad_kernel(sizes),
-            [((width, 3 * width), bf16)] + blocks(3 * half + tiny),
+            blocks(3 * half + tiny),
             [((width, 3 * half), f32), ((width, tiny), f32)],
             VMEM_MIB,
             flops=4 * 10**9,
-            far_in=range(4, 5),
-            sems=6,
-        )(meta, gj_late, early, sums, xh, w)
+        )(meta, gj_late, early, slot_grads, sums, xh)
         if shares:
             second = scatter_begin(*second, devices)
             part = after([part], second)[0]
-        xgrad = call(
+        xgrad, block = call(
             inputs_pull_kernel(sizes),
-            [((total, width), f32)],
-            [((total, width), f32)],
+            [((total, width), f32), ((total, width), bf16)],
+            [((total, width), f32)] * 2,
             VMEM_MIB,
             flops=5 * 10**9,
-        )(meta, x, par, gj, gj1, w_all, part)[0]
+            far_in=(8,),
+            sems=1,
+        )(meta, x, par, gj, gj1, w_all, part, logs, slot_sums, res)
         if shares:
             first = scatter_middle(first, devices, [xgrad])
             second = scatter_middle(second, devices, first[2:4])

time: 141 us -> 139 us (0.986)
  waiting for transfers between devices: 55.9 us -> 53.8 us
    ppermute x48, waiting for transfers between devices: 55.9 us -> 53.8 us  [swap(): return lax.ppermute(value, 'fsdp', [(i, i ^ mask) for i in range(devices)])]
  transfers between devices with their start and end apart: 48 -> 48, of which waited for: 30 -> 30; matrix products, arithmetic and copies ran while one was open for 0% -> 0% of each run, Pallas kernels for 9% -> 11%
where the time goes in v6:
time: 139 us; the launch traced here: 138 us
  waiting for transfers between devices  53.8 us (39%)
  starting transfers between devices  42.1 us (30%)
  Pallas kernels  41.6 us (30%)
    ppermute x48, waiting for transfers between devices, swap(): return lax.ppermute(value, 'fsdp', [(i, i ^ mask) for i in range(devices)])  53.8 us
    ppermute x48, starting transfers between devices, swap(): return lax.ppermute(value, 'fsdp', [(i, i ^ mask) for i in range(devices)])  42.1 us
    pallas_call x8, Pallas kernels, run(): pl.pallas_call(body, out_shape=[pltpu.HBM(s, d) if i in far_out else jax....  38.3 us
  transfers between devices with their start and end apart: 48, of which 30 were waited for; matrix products, arithmetic and copies ran while one was open for 0% of the time, Pallas kernels for 11%

profile of v6, /device:TPU:0, one launch (start us, length us, event | category | flops | bytes accessed | tf_op | source)
XLA Modules:
  0.0 138.4 jit_solution(15506715235843649718)
XLA Ops:
  0.7 1.1 shard_map.203
  1.7 3.1 %collective-permute-start = (bf16[1,24,3200]{2,1,0:T(8,128)(2,1)S(1)}, bf16[1,24,3200]{2,1,0:T(8,128)(2,1)S(1)}, u32[]{:S(2)}, u32[]{:S(2)}) collective-permute-start(bf16[1,24,3200]{2,1,0:T(8,128)(2,1)S(1)} %bitcast.22), channel_id=1, source_target_pairs={{0,8},{1,9},{2,10},{3,11},{4,12},{5,13},{6,14},{7,15},{8,0},{9,1},... | collective-permute-start | bytes 460808 | tf_op jit(solution)/shard_map/ppermute | solution.py:740
  4.8 2.6 %collective-permute-start.1 = (bf16[1,24,3200]{2,1,0:T(8,128)(2,1)S(1)}, bf16[1,24,3200]{2,1,0:T(8,128)(2,1)S(1)}, u32[]{:S(2)}, u32[]{:S(2)}) collective-permute-start(bf16[1,24,3200]{2,1,0:T(8,128)(2,1)S(1)} %bitcast.23), channel_id=1, source_target_pairs={{0,16},{1,17},{2,18},{3,19},{4,20},{5,21},{6,22},{7,23},{8,24},{9,... | collective-permute-start | bytes 460808 | tf_op jit(solution)/shard_map/ppermute | solution.py:740
  7.4 4.2 %collective-permute-done = bf16[1,24,3200]{2,1,0:T(8,128)(2,1)S(1)} collective-permute-done((bf16[1,24,3200]{2,1,0:T(8,128)(2,1)S(1)}, bf16[1,24,3200]{2,1,0:T(8,128)(2,1)S(1)}, u32[]{:S(2)}, u32[]{:S(2)}) %collective-permute-start) | collective-permute-done | bytes 153632 | tf_op jit(solution)/shard_map/ppermute | solution.py:740
  11.7 1.9 %collective-permute-start.5 = (bf16[2,24,3200]{2,1,0:T(8,128)(2,1)S(1)}, bf16[2,24,3200]{2,1,0:T(8,128)(2,1)S(1)}, u32[]{:S(2)}, u32[]{:S(2)}) collective-permute-start(bf16[2,24,3200]{2,1,0:T(8,128)(2,1)S(1)} %pad_maximum_fusion.refs_0_), channel_id=1, source_target_pairs={{0,4},{1,5},{2,6},{3,7},{4,0},{5,1},{6,2},{7,3},{8,12},{9,13},{10,... | collective-permute-start | bytes 921608 | tf_op jit(solution)/shard_map/ppermute | solution.py:740
  13.6 1.5 %collective-permute-start.3 = (bf16[2,24,3200]{2,1,0:T(8,128)(2,1)S(1)}, bf16[2,24,3200]{2,1,0:T(8,128)(2,1)S(1)}, u32[]{:S(2)}, u32[]{:S(2)}) collective-permute-start(bf16[2,24,3200]{2,1,0:T(8,128)(2,1)S(1)} %pad_maximum_fusion.refs_0_), channel_id=1, source_target_pairs={{0,2},{1,3},{2,0},{3,1},{4,6},{5,7},{6,4},{7,5},{8,10},{9,11},{10,... | collective-permute-start | bytes 921608 | tf_op jit(solution)/shard_map/ppermute | solution.py:740
  15.2 5.8 %collective-permute-done.2 = bf16[1,24,3200]{2,1,0:T(8,128)(2,1)S(1)} collective-permute-done((bf16[1,24,3200]{2,1,0:T(8,128)(2,1)S(1)}, bf16[1,24,3200]{2,1,0:T(8,128)(2,1)S(1)}, u32[]{:S(2)}, u32[]{:S(2)}) %collective-permute-start.2) | collective-permute-done | bytes 153632 | tf_op jit(solution)/shard_map/ppermute | solution.py:740
  21.5 1.3 collective-permute-start.6
  23.3 2.0 %collective-permute-start.7 = (bf16[2,24,3200]{2,1,0:T(8,128)(2,1)S(1)}, bf16[2,24,3200]{2,1,0:T(8,128)(2,1)S(1)}, u32[]{:S(2)}, u32[]{:S(2)}) collective-permute-start(bf16[2,24,3200]{2,1,0:T(8,128)(2,1)S(1)} %collective-permute-done.5.refs_4_), channel_id=1, source_target_pairs={{0,2},{1,3},{2,0},{3,1},{4,6},{5,7},{6,4},{7,5},{8,10},{9,11},{10,... | collective-permute-start | bytes 921608 | tf_op jit(solution)/shard_map/ppermute | solution.py:740
  25.2 6.0 %collective-permute-done.4.refs_3_ = bf16[2,24,3200]{2,1,0:T(8,128)(2,1)S(1)} collective-permute-done((bf16[2,24,3200]{2,1,0:T(8,128)(2,1)S(1)}, bf16[2,24,3200]{2,1,0:T(8,128)(2,1)S(1)}, u32[]{:S(2)}, u32[]{:S(2)}) %collective-permute-start.4) | collective-permute-done | bytes 307232 | tf_op jit(solution)/shard_map/ppermute | solution.py:740
  32.3 3.9 %collective-permute-done.7.refs_6_ = bf16[2,24,3200]{2,1,0:T(8,128)(2,1)S(1)} collective-permute-done((bf16[2,24,3200]{2,1,0:T(8,128)(2,1)S(1)}, bf16[2,24,3200]{2,1,0:T(8,128)(2,1)S(1)}, u32[]{:S(2)}, u32[]{:S(2)}) %collective-permute-start.7) | collective-permute-done | bytes 307232 | tf_op jit(solution)/shard_map/ppermute | solution.py:740
  36.1 1.9 %collective-permute-done.8.refs_7_ = bf16[2,24,3200]{2,1,0:T(8,128)(2,1)S(1)} collective-permute-done((bf16[2,24,3200]{2,1,0:T(8,128)(2,1)S(1)}, bf16[2,24,3200]{2,1,0:T(8,128)(2,1)S(1)}, u32[]{:S(2)}, u32[]{:S(2)}) %collective-permute-start.8) | collective-permute-done | bytes 307232 | tf_op jit(solution)/shard_map/ppermute | solution.py:740
  38.1 1.6 %collective-permute-done.16.refs_15_ = bf16[2,24,3200]{2,1,0:T(8,128)(2,1)S(1)} collective-permute-done((bf16[2,24,3200]{2,1,0:T(8,128)(2,1)S(1)}, bf16[2,24,3200]{2,1,0:T(8,128)(2,1)S(1)}, u32[]{:S(2)}, u32[]{:S(2)}) %collective-permute-start.16) | collective-permute-done | bytes 307232 | tf_op jit(solution)/shard_map/ppermute | solution.py:740
  39.7 9.5 %shard_map.204 = (f32[8,768]{1,0:T(8,128)S(1)}, f32[2,4,208]{2,1,0:T(4,128)S(1)}, bf16[16,768]{1,0:T(8,128)(2,1)S(1)}, bf16[416,768]{1,0:T(8,128)(2,1)}, bf16[41...) custom-call(s32[2]{0:T(128)S(1)} %copy-done.5, ...), custom_call_target="tpu_custom_call" | custom-call | tf_op jit(solution)/shard_map/pallas_call | solution.py:57
  49.1 2.8 %collective-permute-start.19 = (bf16[1,16,768]{2,1,0:T(8,128)(2,1)S(1)}, bf16[1,16,768]{2,1,0:T(8,128)(2,1)S(1)}, u32[]{:S(2)}, u32[]{:S(2)}) collective-permute-start(bf16[1,16,768]{2,1,0:T(8,128)(2,1)S(1)} %bitcast.26), channel_id=1, source_target_pairs={{0,24},{1,25},{2,26},{3,27},{4,28},{5,29},{6,30},{7,31},{8,16},{9,... | collective-permute-start | bytes 73736 | tf_op jit(solution)/shard_map/ppermute | solution.py:740
  51.9 1.7 %collective-permute-start.17 = (bf16[1,16,768]{2,1,0:T(8,128)(2,1)S(1)}, bf16[1,16,768]{2,1,0:T(8,128)(2,1)S(1)}, u32[]{:S(2)}, u32[]{:S(2)}) collective-permute-start(bf16[1,16,768]{2,1,0:T(8,128)(2,1)S(1)} %bitcast.28), channel_id=1, source_target_pairs={{0,8},{1,9},{2,10},{3,11},{4,12},{5,13},{6,14},{7,15},{8,0},{9,1},... | collective-permute-start | bytes 73736 | tf_op jit(solution)/shard_map/ppermute | solution.py:740
  53.6 1.3 collective-permute-done.19
  54.9 1.7 %collective-permute-done.18 = bf16[1,16,768]{2,1,0:T(8,128)(2,1)S(1)} collective-permute-done((bf16[1,16,768]{2,1,0:T(8,128)(2,1)S(1)}, bf16[1,16,768]{2,1,0:T(8,128)(2,1)S(1)}, u32[]{:S(2)}, u32[]{:S(2)}) %collective-permute-start.18) | collective-permute-done | bytes 24608 | tf_op jit(solution)/shard_map/ppermute | solution.py:740
  56.7 1.3 collective-permute-start.22
  57.9 1.7 %collective-permute-start.21 = (bf16[4,16,768]{2,1,0:T(8,128)(2,1)S(1)}, bf16[4,16,768]{2,1,0:T(8,128)(2,1)S(1)}, u32[]{:S(2)}, u32[]{:S(2)}) collective-permute-start(bf16[4,16,768]{2,1,0:T(8,128)(2,1)S(1)} %pad_maximum_fusion.1.refs_0_), channel_id=1, source_target_pairs={{0,4},{1,5},{2,6},{3,7},{4,0},{5,1},{6,2},{7,3},{8,12},{9,13},{10,... | collective-permute-start | bytes 294920 | tf_op jit(solution)/shard_map/ppermute | solution.py:740
  60.2 2.3 %collective-permute-done.22.refs_3_ = bf16[4,16,768]{2,1,0:T(8,128)(2,1)S(1)} collective-permute-done((bf16[4,16,768]{2,1,0:T(8,128)(2,1)S(1)}, bf16[4,16,768]{2,1,0:T(8,128)(2,1)S(1)}, u32[]{:S(2)}, u32[]{:S(2)}) %collective-permute-start.22) | collective-permute-done | bytes 98336 | tf_op jit(solution)/shard_map/ppermute | solution.py:740
  65.6 2.6 %shard_map.205 = (bf16[16,16,768]{2,1,0:T(8,128)(2,1)S(1)}, bf16[16,16,768]{2,1,0:T(8,128)(2,1)S(1)}, bf16[256,768]{1,0:T(8,128)(2,1)S(1)}, bf16[256,768]{1,0:T(...) custom-call(s32[2]{0:T(128)S(1)} %copy-done.5, ...), custom_call_target="tpu_custom_call" | custom-call | tf_op jit(solution)/shard_map/pallas_call | solution.py:57
  68.4 1.6 %collective-permute-done.27.refs_1_ = bf16[16,16,768]{2,1,0:T(8,128)(2,1)S(1)} collective-permute-done((bf16[16,16,768]{2,1,0:T(8,128)(2,1)S(1)}, bf16[16,16,768]{2,1,0:T(8,128)(2,1)S(1)}, u32[]{:S(2)}, u32[]{:S(2)}) %collective-permute-start.27) | collective-permute-done | bytes 393248 | tf_op jit(solution)/shard_map/ppermute | solution.py:740
  71.5 2.2 %collective-permute-start.30 = (bf16[4,16,768]{2,1,0:T(8,128)(2,1)S(1)}, bf16[4,16,768]{2,1,0:T(8,128)(2,1)S(1)}, u32[]{:S(2)}, u32[]{:S(2)}) collective-permute-start(bf16[4,16,768]{2,1,0:T(8,128)(2,1)S(1)} %get-tuple-element.104), channel_id=1, source_target_pairs={{0,6},{1,7},{2,4},{3,5},{4,2},{5,3},{6,0},{7,1},{8,14},{9,15},{10,... | collective-permute-start | bytes 294920 | tf_op jit(solution)/shard_map/ppermute | solution.py:740
  73.7 2.4 %shard_map.209 = (f32[416,768]{1,0:T(8,128)S(1)}, f32[416,128]{1,0:T(8,128)S(1)}, bf16[416,768]{1,0:T(8,128)(2,1)S(1)}) custom-call(s32[2]{0:T(128)S(1)} %copy-done.5, f32[416,768]{1,0:T(8,128)} %get-tuple-element.116.res_in, bf16[416,768]{1,0:T(8,128)(2,1)} %get-tuple-element.117.n2_in), custom_call_target="tpu_custom_call" | custom-call | flops 1000000000 | tf_op jit(solution)/shard_map/pallas_call | solution.py:57
  76.1 1.5 %collective-permute-done.29.refs_2_ = bf16[4,16,768]{2,1,0:T(8,128)(2,1)S(1)} collective-permute-done((bf16[4,16,768]{2,1,0:T(8,128)(2,1)S(1)}, bf16[4,16,768]{2,1,0:T(8,128)(2,1)S(1)}, u32[]{:S(2)}, u32[]{:S(2)}) %collective-permute-start.29) | collective-permute-done | bytes 98336 | tf_op jit(solution)/shard_map/ppermute | solution.py:740
  77.7 1.0 collective-permute-start.31
  78.7 1.3 collective-permute-start.32
  80.0 2.1 %collective-permute-start.33 = (bf16[1,16,768]{2,1,0:T(8,128)(2,1)S(1)}, bf16[1,16,768]{2,1,0:T(8,128)(2,1)S(1)}, u32[]{:S(2)}, u32[]{:S(2)}) collective-permute-start(bf16[1,16,768]{2,1,0:T(8,128)(2,1)S(1)} %get-tuple-element.115), channel_id=1, source_target_pairs={{0,24},{1,25},{2,26},{3,27},{4,28},{5,29},{6,30},{7,31},{8,16},{9,... | collective-permute-start | bytes 73736 | tf_op jit(solution)/shard_map/ppermute | solution.py:740
  82.1 2.5 %shard_map.208 = (f32[4,96,768]{2,1,0:T(8,128)}, f32[4,96,768]{2,1,0:T(8,128)}) custom-call(s32[2]{0:T(128)S(1)} %copy-done.5, bf16[256,768]{1,0:T(8,128)(2,1)S(1)} %get-tuple-element.106.s_ref, bf16[256,768]{1,0:T(8,128)(2,1)S(1)} %get-tuple-element.107.g_ref, bf16[256,512]{1,0:T(8,128)(2,1)S(1)} %get-tuple-element.108.act_ref, ...), custom_call_target="tpu_custom_call" | custom-call | flops 2000000000 | tf_op jit(solution)/shard_map/pallas_call | solution.py:57
  84.6 1.0 collective-permute-done.33.r3_ref
  85.6 9.8 %shard_map.210 = (f32[16,768]{1,0:T(8,128)S(1)}, f32[2,4,208]{2,1,0:T(4,128)S(1)}, f32[416,768]{1,0:T(8,128)S(1)}, bf16[416,768]{1,0:T(8,128)(2,1)S(1)}, bf16[41...) custom-call(s32[2]{0:T(128)S(1)} %copy-done.5, ...), custom_call_target="tpu_custom_call" | custom-call | tf_op jit(solution)/shard_map/pallas_call | solution.py:57
  95.5 2.9 %shard_map.211 = (bf16[416,1152]{1,0:T(8,128)(2,1)S(1)}, f32[8,768]{1,0:T(8,128)S(1)}) custom-call(s32[2]{0:T(128)S(1)} %copy-done.5, bf16[416,768]{1,0:T(8,128)(2,1)S(1)} %get-tuple-element.127.gm_ref, bf16[416,1152]{1,0:T(8,128)(2,1)S(1)} %get-tuple-element.128.joint_ref, bf16[3,2,416,208]{3,2,1,0:T(8,128)(2,1)S(1)} %get-tuple-element.129.probs_ref, ...), custom_call_target="tpu_custom_call" | custom-call | flops 3000000000 | tf_op jit(solution)/shard_map/pallas_call | solution.py:57
  99.1 2.3 %shard_map.213 = (bf16[16,24,1280]{2,1,0:T(8,128)(2,1)S(1)}, bf16[16,24,1280]{2,1,0:T(8,128)(2,1)S(1)}) custom-call(s32[2]{0:T(128)S(1)} %copy-done.5, bf16[416,1152]{1,0:T(8,128)(2,1)S(1)} %get-tuple-element.143.gj.gj1_ref, f32[8,768]{1,0:T(8,128)S(1)} %get-tuple-element.144.grads, f32[8,768]{1,0:T(8,128)S(1)} %get-tuple-element.145.slot_ref, ...), custom_call_target="tpu_custom_call" | custom-call | flops 4000000000 | tf_op jit(solution)/shard_map/pallas_call | solution.py:57
  101.7 1.3 collective-permute-start.36
  104.3 1.3 collective-permute-start.42
  106.5 6.4 %shard_map.215 = (f32[416,768]{1,0:T(8,128)}, bf16[416,768]{1,0:T(8,128)(2,1)}) custom-call(s32[2]{0:T(128)S(1)} %copy-done.5, bf16[416,768]{1,0:T(8,128)(2,1)S(1)} %bitcast.21, f32[8,768]{1,0:T(8,128)S(1)} %get-tuple-element.96.par_ref, bf16[416,1152]{1,0:T(8,128)(2,1)S(1)} %get-tuple-element.126.gj0_ref, ...), custom_call_target="tpu_custom_call" | custom-call | flops 5000000000 | tf_op jit(solution)/shard_map/pallas_call | solution.py:57
  113.1 1.3 collective-permute-done.37.refs_2_
  115.3 3.0 %collective-permute-done.42.refs_3_.refs_1_ = bf16[4,24,1280]{2,1,0:T(8,128)(2,1)S(1)} collective-permute-done((bf16[4,24,1280]{2,1,0:T(8,128)(2,1)S(1)}, bf16[4,24,1280]{2,1,0:T(8,128)(2,1)S(1)}, u32[]{:S(2)}, u32[]{:S(2)}) %collective-permute-start.42) | collective-permute-done | bytes 245792 | tf_op jit(solution)/shard_map/ppermute | solution.py:740
  120.6 1.7 %collective-permute-done.39.refs_1_ = bf16[2,24,1920]{2,1,0:T(8,128)(2,1)S(1)} collective-permute-done((bf16[2,24,1920]{2,1,0:T(8,128)(2,1)S(1)}, bf16[2,24,1920]{2,1,0:T(8,128)(2,1)S(1)}, u32[]{:S(2)}, u32[]{:S(2)}) %collective-permute-start.39) | collective-permute-done | bytes 184352 | tf_op jit(solution)/shard_map/ppermute | solution.py:740
  122.5 1.0 collective-permute-start.44
  124.5 1.1 collective-permute-start.46
  126.5 2.9 %collective-permute-done.40.refs_3_ = bf16[2,24,1920]{2,1,0:T(8,128)(2,1)S(1)} collective-permute-done((bf16[2,24,1920]{2,1,0:T(8,128)(2,1)S(1)}, bf16[2,24,1920]{2,1,0:T(8,128)(2,1)S(1)}, u32[]{:S(2)}, u32[]{:S(2)}) %collective-permute-start.40) | collective-permute-done | bytes 184352 | tf_op jit(solution)/shard_map/ppermute | solution.py:740
  129.5 1.0 collective-permute-start.41
  130.5 1.0 collective-permute-done.46.refs_3_
  131.6 1.2 collective-permute-start.47
  132.8 3.0 %collective-permute-done.41.a1 = bf16[1,24,1920]{2,1,0:T(8,128)(2,1)S(1)} collective-permute-done((bf16[1,24,1920]{2,1,0:T(8,128)(2,1)S(1)}, bf16[1,24,1920]{2,1,0:T(8,128)(2,1)S(1)}, u32[]{:S(2)}, u32[]{:S(2)}) %collective-permute-start.41) | collective-permute-done | bytes 92192 | tf_op jit(solution)/shard_map/ppermute | solution.py:740
  135.8 1.7 %collective-permute-done.47.b1 = bf16[1,24,1280]{2,1,0:T(8,128)(2,1)S(1)} collective-permute-done((bf16[1,24,1280]{2,1,0:T(8,128)(2,1)S(1)}, bf16[1,24,1280]{2,1,0:T(8,128)(2,1)S(1)}, u32[]{:S(2)}, u32[]{:S(2)}) %collective-permute-start.47) | collective-permute-done | bytes 61472 | tf_op jit(solution)/shard_map/ppermute | solution.py:740
  (88 shorter events, 17.5 us)
Async XLA Ops:
  1.7 9.9 %collective-permute-start = (bf16[1,24,3200]{2,1,0:T(8,128)(2,1)S(1)}, bf16[1,24,3200]{2,1,0:T(8,128)(2,1)S(1)}, u32[]{:S(2)}, u32[]{:S(2)}) collective-permute-start(bf16[1,24,3200]{2,1,0:T(8,128)(2,1)S(1)} %bitcast.22), channel_id=1, source_target_pairs={{0,8},{1,9},{2,10},{3,11},{4,12},{5,13},{6,14},{7,15},{8,0},{9,1},... | collective-permute-start | bytes 460808 | tf_op jit(solution)/shard_map/ppermute | solution.py:740
  4.8 10.3 %collective-permute-start.1 = (bf16[1,24,3200]{2,1,0:T(8,128)(2,1)S(1)}, bf16[1,24,3200]{2,1,0:T(8,128)(2,1)S(1)}, u32[]{:S(2)}, u32[]{:S(2)}) collective-permute-start(bf16[1,24,3200]{2,1,0:T(8,128)(2,1)S(1)} %bitcast.23), channel_id=1, source_target_pairs={{0,16},{1,17},{2,18},{3,19},{4,20},{5,21},{6,22},{7,23},{8,24},{9,... | collective-permute-start | bytes 460808 | tf_op jit(solution)/shard_map/ppermute | solution.py:740
  11.6 9.9 %collective-permute-start.9 = (bf16[2,24,3200]{2,1,0:T(8,128)(2,1)S(1)}, bf16[2,24,3200]{2,1,0:T(8,128)(2,1)S(1)}, u32[]{:S(2)}, u32[]{:S(2)}) collective-permute-start(bf16[2,24,3200]{2,1,0:T(8,128)(2,1)S(1)} %pad_maximum_fusion.refs_0_), channel_id=1, source_target_pairs={{0,1},{1,0},{2,3},{3,2},{4,5},{5,4},{6,7},{7,6},{8,9},{9,8},{10,11... | collective-permute-start | bytes 921608 | tf_op jit(solution)/shard_map/ppermute | solution.py:740
  11.7 11.1 %collective-permute-start.5 = (bf16[2,24,3200]{2,1,0:T(8,128)(2,1)S(1)}, bf16[2,24,3200]{2,1,0:T(8,128)(2,1)S(1)}, u32[]{:S(2)}, u32[]{:S(2)}) collective-permute-start(bf16[2,24,3200]{2,1,0:T(8,128)(2,1)S(1)} %pad_maximum_fusion.refs_0_), channel_id=1, source_target_pairs={{0,4},{1,5},{2,6},{3,7},{4,0},{5,1},{6,2},{7,3},{8,12},{9,13},{10,... | collective-permute-start | bytes 921608 | tf_op jit(solution)/shard_map/ppermute | solution.py:740
  13.6 9.7 %collective-permute-start.3 = (bf16[2,24,3200]{2,1,0:T(8,128)(2,1)S(1)}, bf16[2,24,3200]{2,1,0:T(8,128)(2,1)S(1)}, u32[]{:S(2)}, u32[]{:S(2)}) collective-permute-start(bf16[2,24,3200]{2,1,0:T(8,128)(2,1)S(1)} %pad_maximum_fusion.refs_0_), channel_id=1, source_target_pairs={{0,2},{1,3},{2,0},{3,1},{4,6},{5,7},{6,4},{7,5},{8,10},{9,11},{10,... | collective-permute-start | bytes 921608 | tf_op jit(solution)/shard_map/ppermute | solution.py:740
  15.1 5.8 %collective-permute-start.2 = (bf16[1,24,3200]{2,1,0:T(8,128)(2,1)S(1)}, bf16[1,24,3200]{2,1,0:T(8,128)(2,1)S(1)}, u32[]{:S(2)}, u32[]{:S(2)}) collective-permute-start(bf16[1,24,3200]{2,1,0:T(8,128)(2,1)S(1)} %collective-permute-done.1), channel_id=1, source_target_pairs={{0,8},{1,9},{2,10},{3,11},{4,12},{5,13},{6,14},{7,15},{8,0},{9,1},... | collective-permute-start | bytes 460808 | tf_op jit(solution)/shard_map/ppermute | solution.py:740
  20.9 10.3 %collective-permute-start.4 = (bf16[2,24,3200]{2,1,0:T(8,128)(2,1)S(1)}, bf16[2,24,3200]{2,1,0:T(8,128)(2,1)S(1)}, u32[]{:S(2)}, u32[]{:S(2)}) collective-permute-start(bf16[2,24,3200]{2,1,0:T(8,128)(2,1)S(1)} %constant_dynamic-update-slice_fusion.refs_1_), channel_id=1, source_target_pairs={{0,2},{1,3},{2,0},{3,1},{4,6},{5,7},{6,4},{7,5},{8,10},{9,11},{10,... | collective-permute-start | bytes 921608 | tf_op jit(solution)/shard_map/ppermute | solution.py:740
  21.5 10.2 %collective-permute-start.10 = (bf16[2,24,3200]{2,1,0:T(8,128)(2,1)S(1)}, bf16[2,24,3200]{2,1,0:T(8,128)(2,1)S(1)}, u32[]{:S(2)}, u32[]{:S(2)}) collective-permute-start(bf16[2,24,3200]{2,1,0:T(8,128)(2,1)S(1)} %constant_dynamic-update-slice_fusion.refs_1_), channel_id=1, source_target_pairs={{0,1},{1,0},{2,3},{3,2},{4,5},{5,4},{6,7},{7,6},{8,9},{9,8},{10,11... | collective-permute-start | bytes 921608 | tf_op jit(solution)/shard_map/ppermute | solution.py:740
  21.5 10.2 %collective-permute-start.6 = (bf16[2,24,3200]{2,1,0:T(8,128)(2,1)S(1)}, bf16[2,24,3200]{2,1,0:T(8,128)(2,1)S(1)}, u32[]{:S(2)}, u32[]{:S(2)}) collective-permute-start(bf16[2,24,3200]{2,1,0:T(8,128)(2,1)S(1)} %constant_dynamic-update-slice_fusion.refs_1_), channel_id=1, source_target_pairs={{0,4},{1,5},{2,6},{3,7},{4,0},{5,1},{6,2},{7,3},{8,12},{9,13},{10,... | collective-permute-start | bytes 921608 | tf_op jit(solution)/shard_map/ppermute | solution.py:740
  22.8 9.4 %collective-permute-start.13 = (bf16[2,24,3200]{2,1,0:T(8,128)(2,1)S(1)}, bf16[2,24,3200]{2,1,0:T(8,128)(2,1)S(1)}, u32[]{:S(2)}, u32[]{:S(2)}) collective-permute-start(bf16[2,24,3200]{2,1,0:T(8,128)(2,1)S(1)} %collective-permute-done.5.refs_4_), channel_id=1, source_target_pairs={{0,1},{1,0},{2,3},{3,2},{4,5},{5,4},{6,7},{7,6},{8,9},{9,8},{10,11... | collective-permute-start | bytes 921608 | tf_op jit(solution)/shard_map/ppermute | solution.py:740
  23.3 12.9 %collective-permute-start.7 = (bf16[2,24,3200]{2,1,0:T(8,128)(2,1)S(1)}, bf16[2,24,3200]{2,1,0:T(8,128)(2,1)S(1)}, u32[]{:S(2)}, u32[]{:S(2)}) collective-permute-start(bf16[2,24,3200]{2,1,0:T(8,128)(2,1)S(1)} %collective-permute-done.5.refs_4_), channel_id=1, source_target_pairs={{0,2},{1,3},{2,0},{3,1},{4,6},{5,7},{6,4},{7,5},{8,10},{9,11},{10,... | collective-permute-start | bytes 921608 | tf_op jit(solution)/shard_map/ppermute | solution.py:740
  31.2 6.9 %collective-permute-start.8 = (bf16[2,24,3200]{2,1,0:T(8,128)(2,1)S(1)}, bf16[2,24,3200]{2,1,0:T(8,128)(2,1)S(1)}, u32[]{:S(2)}, u32[]{:S(2)}) collective-permute-start(bf16[2,24,3200]{2,1,0:T(8,128)(2,1)S(1)} %collective-permute-done.4.refs_3_), channel_id=1, source_target_pairs={{0,4},{1,5},{2,6},{3,7},{4,0},{5,1},{6,2},{7,3},{8,12},{9,13},{10,... | collective-permute-start | bytes 921608 | tf_op jit(solution)/shard_map/ppermute | solution.py:740
  31.7 6.4 %collective-permute-start.11 = (bf16[2,24,3200]{2,1,0:T(8,128)(2,1)S(1)}, bf16[2,24,3200]{2,1,0:T(8,128)(2,1)S(1)}, u32[]{:S(2)}, u32[]{:S(2)}) collective-permute-start(bf16[2,24,3200]{2,1,0:T(8,128)(2,1)S(1)} %collective-permute-done.3.refs_2_), channel_id=1, source_target_pairs={{0,1},{1,0},{2,3},{3,2},{4,5},{5,4},{6,7},{7,6},{8,9},{9,8},{10,11... | collective-permute-start | bytes 921608 | tf_op jit(solution)/shard_map/ppermute | solution.py:740
  31.7 6.4 %collective-permute-start.12 = (bf16[2,24,3200]{2,1,0:T(8,128)(2,1)S(1)}, bf16[2,24,3200]{2,1,0:T(8,128)(2,1)S(1)}, u32[]{:S(2)}, u32[]{:S(2)}) collective-permute-start(bf16[2,24,3200]{2,1,0:T(8,128)(2,1)S(1)} %collective-permute-done.4.refs_3_), channel_id=1, source_target_pairs={{0,1},{1,0},{2,3},{3,2},{4,5},{5,4},{6,7},{7,6},{8,9},{9,8},{10,11... | collective-permute-start | bytes 921608 | tf_op jit(solution)/shard_map/ppermute | solution.py:740
  32.2 5.8 %collective-permute-start.14 = (bf16[2,24,3200]{2,1,0:T(8,128)(2,1)S(1)}, bf16[2,24,3200]{2,1,0:T(8,128)(2,1)S(1)}, u32[]{:S(2)}, u32[]{:S(2)}) collective-permute-start(bf16[2,24,3200]{2,1,0:T(8,128)(2,1)S(1)} %collective-permute-done.6.refs_5_), channel_id=1, source_target_pairs={{0,1},{1,0},{2,3},{3,2},{4,5},{5,4},{6,7},{7,6},{8,9},{9,8},{10,11... | collective-permute-start | bytes 921608 | tf_op jit(solution)/shard_map/ppermute | solution.py:740
  36.1 1.9 %collective-permute-start.15 = (bf16[2,24,3200]{2,1,0:T(8,128)(2,1)S(1)}, bf16[2,24,3200]{2,1,0:T(8,128)(2,1)S(1)}, u32[]{:S(2)}, u32[]{:S(2)}) collective-permute-start(bf16[2,24,3200]{2,1,0:T(8,128)(2,1)S(1)} %collective-permute-done.7.refs_6_), channel_id=1, source_target_pairs={{0,1},{1,0},{2,3},{3,2},{4,5},{5,4},{6,7},{7,6},{8,9},{9,8},{10,11... | collective-permute-start | bytes 921608 | tf_op jit(solution)/shard_map/ppermute | solution.py:740
  38.1 1.6 %collective-permute-start.16 = (bf16[2,24,3200]{2,1,0:T(8,128)(2,1)S(1)}, bf16[2,24,3200]{2,1,0:T(8,128)(2,1)S(1)}, u32[]{:S(2)}, u32[]{:S(2)}) collective-permute-start(bf16[2,24,3200]{2,1,0:T(8,128)(2,1)S(1)} %collective-permute-done.8.refs_7_), channel_id=1, source_target_pairs={{0,1},{1,0},{2,3},{3,2},{4,5},{5,4},{6,7},{7,6},{8,9},{9,8},{10,11... | collective-permute-start | bytes 921608 | tf_op jit(solution)/shard_map/ppermute | solution.py:740
  49.1 5.7 %collective-permute-start.19 = (bf16[1,16,768]{2,1,0:T(8,128)(2,1)S(1)}, bf16[1,16,768]{2,1,0:T(8,128)(2,1)S(1)}, u32[]{:S(2)}, u32[]{:S(2)}) collective-permute-start(bf16[1,16,768]{2,1,0:T(8,128)(2,1)S(1)} %bitcast.26), channel_id=1, source_target_pairs={{0,24},{1,25},{2,26},{3,27},{4,28},{5,29},{6,30},{7,31},{8,16},{9,... | collective-permute-start | bytes 73736 | tf_op jit(solution)/shard_map/ppermute | solution.py:740
  51.9 4.7 %collective-permute-start.18 = (bf16[1,16,768]{2,1,0:T(8,128)(2,1)S(1)}, bf16[1,16,768]{2,1,0:T(8,128)(2,1)S(1)}, u32[]{:S(2)}, u32[]{:S(2)}) collective-permute-start(bf16[1,16,768]{2,1,0:T(8,128)(2,1)S(1)} %bitcast.27), channel_id=1, source_target_pairs={{0,16},{1,17},{2,18},{3,19},{4,20},{5,21},{6,22},{7,23},{8,24},{9,... | collective-permute-start | bytes 73736 | tf_op jit(solution)/shard_map/ppermute | solution.py:740
  51.9 4.7 %collective-permute-start.17 = (bf16[1,16,768]{2,1,0:T(8,128)(2,1)S(1)}, bf16[1,16,768]{2,1,0:T(8,128)(2,1)S(1)}, u32[]{:S(2)}, u32[]{:S(2)}) collective-permute-start(bf16[1,16,768]{2,1,0:T(8,128)(2,1)S(1)} %bitcast.28), channel_id=1, source_target_pairs={{0,8},{1,9},{2,10},{3,11},{4,12},{5,13},{6,14},{7,15},{8,0},{9,1},... | collective-permute-start | bytes 73736 | tf_op jit(solution)/shard_map/ppermute | solution.py:740
  56.7 5.8 %collective-permute-start.22 = (bf16[4,16,768]{2,1,0:T(8,128)(2,1)S(1)}, bf16[4,16,768]{2,1,0:T(8,128)(2,1)S(1)}, u32[]{:S(2)}, u32[]{:S(2)}) collective-permute-start(bf16[4,16,768]{2,1,0:T(8,128)(2,1)S(1)} %pad_maximum_fusion.1.refs_0_), channel_id=1, source_target_pairs={{0,6},{1,7},{2,4},{3,5},{4,2},{5,3},{6,0},{7,1},{8,14},{9,15},{10,... | collective-permute-start | bytes 294920 | tf_op jit(solution)/shard_map/ppermute | solution.py:740
  57.9 5.5 %collective-permute-start.21 = (bf16[4,16,768]{2,1,0:T(8,128)(2,1)S(1)}, bf16[4,16,768]{2,1,0:T(8,128)(2,1)S(1)}, u32[]{:S(2)}, u32[]{:S(2)}) collective-permute-start(bf16[4,16,768]{2,1,0:T(8,128)(2,1)S(1)} %pad_maximum_fusion.1.refs_0_), channel_id=1, source_target_pairs={{0,4},{1,5},{2,6},{3,7},{4,0},{5,1},{6,2},{7,3},{8,12},{9,13},{10,... | collective-permute-start | bytes 294920 | tf_op jit(solution)/shard_map/ppermute | solution.py:740
  59.7 4.6 %collective-permute-start.20 = (bf16[4,16,768]{2,1,0:T(8,128)(2,1)S(1)}, bf16[4,16,768]{2,1,0:T(8,128)(2,1)S(1)}, u32[]{:S(2)}, u32[]{:S(2)}) collective-permute-start(bf16[4,16,768]{2,1,0:T(8,128)(2,1)S(1)} %pad_maximum_fusion.1.refs_0_), channel_id=1, source_target_pairs={{0,2},{1,3},{2,0},{3,1},{4,6},{5,7},{6,4},{7,5},{8,10},{9,11},{10,... | collective-permute-start | bytes 294920 | tf_op jit(solution)/shard_map/ppermute | solution.py:740
  60.2 4.1 %collective-permute-start.23 = (bf16[4,16,768]{2,1,0:T(8,128)(2,1)S(1)}, bf16[4,16,768]{2,1,0:T(8,128)(2,1)S(1)}, u32[]{:S(2)}, u32[]{:S(2)}) collective-permute-start(bf16[4,16,768]{2,1,0:T(8,128)(2,1)S(1)} %pad_maximum_fusion.1.refs_0_), channel_id=1, source_target_pairs={{0,1},{1,0},{2,3},{3,2},{4,5},{5,4},{6,7},{7,6},{8,9},{9,8},{10,11... | collective-permute-start | bytes 294920 | tf_op jit(solution)/shard_map/ppermute | solution.py:740
  62.5 1.9 %collective-permute-start.26 = (bf16[4,16,768]{2,1,0:T(8,128)(2,1)S(1)}, bf16[4,16,768]{2,1,0:T(8,128)(2,1)S(1)}, u32[]{:S(2)}, u32[]{:S(2)}) collective-permute-start(bf16[4,16,768]{2,1,0:T(8,128)(2,1)S(1)} %collective-permute-done.22.refs_3_), channel_id=1, source_target_pairs={{0,1},{1,0},{2,3},{3,2},{4,5},{5,4},{6,7},{7,6},{8,9},{9,8},{10,11... | collective-permute-start | bytes 294920 | tf_op jit(solution)/shard_map/ppermute | solution.py:740
  63.4 1.3 collective-permute-start.25
  64.3 1.3 collective-permute-start.24
  68.2 1.8 %collective-permute-start.27 = (bf16[16,16,768]{2,1,0:T(8,128)(2,1)S(1)}, bf16[16,16,768]{2,1,0:T(8,128)(2,1)S(1)}, u32[]{:S(2)}, u32[]{:S(2)}) collective-permute-start(bf16[16,16,768]{2,1,0:T(8,128)(2,1)S(1)} %get-tuple-element.100), channel_id=1, source_target_pairs={{0,1},{1,0},{2,3},{3,2},{4,5},{5,4},{6,7},{7,6},{8,9},{9,8},{10,11... | collective-permute-start | bytes 1179656 | tf_op jit(solution)/shard_map/ppermute | solution.py:740
  70.2 5.9 %collective-permute-start.28 = (bf16[4,16,768]{2,1,0:T(8,128)(2,1)S(1)}, bf16[4,16,768]{2,1,0:T(8,128)(2,1)S(1)}, u32[]{:S(2)}, u32[]{:S(2)}) collective-permute-start(bf16[4,16,768]{2,1,0:T(8,128)(2,1)S(1)} %get-tuple-element.102), channel_id=1, source_target_pairs={{0,2},{1,3},{2,0},{3,1},{4,6},{5,7},{6,4},{7,5},{8,10},{9,11},{10,... | collective-permute-start | bytes 294920 | tf_op jit(solution)/shard_map/ppermute | solution.py:740
  70.7 6.9 %collective-permute-start.29 = (bf16[4,16,768]{2,1,0:T(8,128)(2,1)S(1)}, bf16[4,16,768]{2,1,0:T(8,128)(2,1)S(1)}, u32[]{:S(2)}, u32[]{:S(2)}) collective-permute-start(bf16[4,16,768]{2,1,0:T(8,128)(2,1)S(1)} %get-tuple-element.103), channel_id=1, source_target_pairs={{0,4},{1,5},{2,6},{3,7},{4,0},{5,1},{6,2},{7,3},{8,12},{9,13},{10,... | collective-permute-start | bytes 294920 | tf_op jit(solution)/shard_map/ppermute | solution.py:740
  71.5 6.1 %collective-permute-start.30 = (bf16[4,16,768]{2,1,0:T(8,128)(2,1)S(1)}, bf16[4,16,768]{2,1,0:T(8,128)(2,1)S(1)}, u32[]{:S(2)}, u32[]{:S(2)}) collective-permute-start(bf16[4,16,768]{2,1,0:T(8,128)(2,1)S(1)} %get-tuple-element.104), channel_id=1, source_target_pairs={{0,6},{1,7},{2,4},{3,5},{4,2},{5,3},{6,0},{7,1},{8,14},{9,15},{10,... | collective-permute-start | bytes 294920 | tf_op jit(solution)/shard_map/ppermute | solution.py:740
  77.7 7.0 %collective-permute-start.31 = (bf16[1,16,768]{2,1,0:T(8,128)(2,1)S(1)}, bf16[1,16,768]{2,1,0:T(8,128)(2,1)S(1)}, u32[]{:S(2)}, u32[]{:S(2)}) collective-permute-start(bf16[1,16,768]{2,1,0:T(8,128)(2,1)S(1)} %get-tuple-element.113), channel_id=1, source_target_pairs={{0,8},{1,9},{2,10},{3,11},{4,12},{5,13},{6,14},{7,15},{8,0},{9,1},... | collective-permute-start | bytes 73736 | tf_op jit(solution)/shard_map/ppermute | solution.py:740
  78.7 6.0 %collective-permute-start.32 = (bf16[1,16,768]{2,1,0:T(8,128)(2,1)S(1)}, bf16[1,16,768]{2,1,0:T(8,128)(2,1)S(1)}, u32[]{:S(2)}, u32[]{:S(2)}) collective-permute-start(bf16[1,16,768]{2,1,0:T(8,128)(2,1)S(1)} %get-tuple-element.114), channel_id=1, source_target_pairs={{0,16},{1,17},{2,18},{3,19},{4,20},{5,21},{6,22},{7,23},{8,24},{9,... | collective-permute-start | bytes 73736 | tf_op jit(solution)/shard_map/ppermute | solution.py:740
  80.0 5.6 %collective-permute-start.33 = (bf16[1,16,768]{2,1,0:T(8,128)(2,1)S(1)}, bf16[1,16,768]{2,1,0:T(8,128)(2,1)S(1)}, u32[]{:S(2)}, u32[]{:S(2)}) collective-permute-start(bf16[1,16,768]{2,1,0:T(8,128)(2,1)S(1)} %get-tuple-element.115), channel_id=1, source_target_pairs={{0,24},{1,25},{2,26},{3,27},{4,28},{5,29},{6,30},{7,31},{8,16},{9,... | collective-permute-start | bytes 73736 | tf_op jit(solution)/shard_map/ppermute | solution.py:740
  95.4 3.3 %collective-permute-start.34 = (bf16[16,24,1920]{2,1,0:T(8,128)(2,1)S(1)}, bf16[16,24,1920]{2,1,0:T(8,128)(2,1)S(1)}, u32[]{:S(2)}, u32[]{:S(2)}) collective-permute-start(bf16[16,24,1920]{2,1,0:T(8,128)(2,1)S(1)} %get-tuple-element.136), channel_id=1, source_target_pairs={{0,1},{1,0},{2,3},{3,2},{4,5},{5,4},{6,7},{7,6},{8,9},{9,8},{10,11... | collective-permute-start | bytes 4423688 | tf_op jit(solution)/shard_map/ppermute | solution.py:740
  101.5 2.6 %collective-permute-start.35 = (bf16[16,24,1280]{2,1,0:T(8,128)(2,1)S(1)}, bf16[16,24,1280]{2,1,0:T(8,128)(2,1)S(1)}, u32[]{:S(2)}, u32[]{:S(2)}) collective-permute-start(bf16[16,24,1280]{2,1,0:T(8,128)(2,1)S(1)} %get-tuple-element.149), channel_id=1, source_target_pairs={{0,1},{1,0},{2,3},{3,2},{4,5},{5,4},{6,7},{7,6},{8,9},{9,8},{10,11... | collective-permute-start | bytes 2949128 | tf_op jit(solution)/shard_map/ppermute | solution.py:740
  101.7 11.4 %collective-permute-start.36 = (bf16[4,24,1920]{2,1,0:T(8,128)(2,1)S(1)}, bf16[4,24,1920]{2,1,0:T(8,128)(2,1)S(1)}, u32[]{:S(2)}, u32[]{:S(2)}) collective-permute-start(bf16[4,24,1920]{2,1,0:T(8,128)(2,1)S(1)} %get-tuple-element.139), channel_id=1, source_target_pairs={{0,2},{1,3},{2,0},{3,1},{4,6},{5,7},{6,4},{7,5},{8,10},{9,11},{10,... | collective-permute-start | bytes 1105928 | tf_op jit(solution)/shard_map/ppermute | solution.py:740
  103.0 11.4 %collective-permute-start.37 = (bf16[4,24,1920]{2,1,0:T(8,128)(2,1)S(1)}, bf16[4,24,1920]{2,1,0:T(8,128)(2,1)S(1)}, u32[]{:S(2)}, u32[]{:S(2)}) collective-permute-start(bf16[4,24,1920]{2,1,0:T(8,128)(2,1)S(1)} %get-tuple-element.140), channel_id=1, source_target_pairs={{0,4},{1,5},{2,6},{3,7},{4,0},{5,1},{6,2},{7,3},{8,12},{9,13},{10,... | collective-permute-start | bytes 1105928 | tf_op jit(solution)/shard_map/ppermute | solution.py:740
  104.3 14.0 %collective-permute-start.42 = (bf16[4,24,1280]{2,1,0:T(8,128)(2,1)S(1)}, bf16[4,24,1280]{2,1,0:T(8,128)(2,1)S(1)}, u32[]{:S(2)}, u32[]{:S(2)}) collective-permute-start(bf16[4,24,1280]{2,1,0:T(8,128)(2,1)S(1)} %get-tuple-element.152), channel_id=1, source_target_pairs={{0,2},{1,3},{2,0},{3,1},{4,6},{5,7},{6,4},{7,5},{8,10},{9,11},{10,... | collective-permute-start | bytes 737288 | tf_op jit(solution)/shard_map/ppermute | solution.py:740
  105.7 13.1 %collective-permute-start.43 = (bf16[4,24,1280]{2,1,0:T(8,128)(2,1)S(1)}, bf16[4,24,1280]{2,1,0:T(8,128)(2,1)S(1)}, u32[]{:S(2)}, u32[]{:S(2)}) collective-permute-start(bf16[4,24,1280]{2,1,0:T(8,128)(2,1)S(1)} %get-tuple-element.153), channel_id=1, source_target_pairs={{0,4},{1,5},{2,6},{3,7},{4,0},{5,1},{6,2},{7,3},{8,12},{9,13},{10,... | collective-permute-start | bytes 737288 | tf_op jit(solution)/shard_map/ppermute | solution.py:740
  114.5 7.8 %collective-permute-start.39 = (bf16[2,24,1920]{2,1,0:T(8,128)(2,1)S(1)}, bf16[2,24,1920]{2,1,0:T(8,128)(2,1)S(1)}, u32[]{:S(2)}, u32[]{:S(2)}) collective-permute-start(bf16[2,24,1920]{2,1,0:T(8,128)(2,1)S(1)} %get-tuple-element.163), channel_id=1, source_target_pairs={{0,2},{1,3},{2,0},{3,1},{4,6},{5,7},{6,4},{7,5},{8,10},{9,11},{10,... | collective-permute-start | bytes 552968 | tf_op jit(solution)/shard_map/ppermute | solution.py:740
  118.9 5.5 %collective-permute-start.45 = (bf16[2,24,1280]{2,1,0:T(8,128)(2,1)S(1)}, bf16[2,24,1280]{2,1,0:T(8,128)(2,1)S(1)}, u32[]{:S(2)}, u32[]{:S(2)}) collective-permute-start(bf16[2,24,1280]{2,1,0:T(8,128)(2,1)S(1)} %get-tuple-element.169), channel_id=1, source_target_pairs={{0,2},{1,3},{2,0},{3,1},{4,6},{5,7},{6,4},{7,5},{8,10},{9,11},{10,... | collective-permute-start | bytes 368648 | tf_op jit(solution)/shard_map/ppermute | solution.py:740
  119.8 6.7 %collective-permute-start.38 = (bf16[2,24,1920]{2,1,0:T(8,128)(2,1)S(1)}, bf16[2,24,1920]{2,1,0:T(8,128)(2,1)S(1)}, u32[]{:S(2)}, u32[]{:S(2)}) collective-permute-start(bf16[2,24,1920]{2,1,0:T(8,128)(2,1)S(1)} %get-tuple-element.162), channel_id=1, source_target_pairs={{0,4},{1,5},{2,6},{3,7},{4,0},{5,1},{6,2},{7,3},{8,12},{9,13},{10,... | collective-permute-start | bytes 552968 | tf_op jit(solution)/shard_map/ppermute | solution.py:740
  122.4 6.9 %collective-permute-start.40 = (bf16[2,24,1920]{2,1,0:T(8,128)(2,1)S(1)}, bf16[2,24,1920]{2,1,0:T(8,128)(2,1)S(1)}, u32[]{:S(2)}, u32[]{:S(2)}) collective-permute-start(bf16[2,24,1920]{2,1,0:T(8,128)(2,1)S(1)} %shard_map.217), channel_id=1, source_target_pairs={{0,8},{1,9},{2,10},{3,11},{4,12},{5,13},{6,14},{7,15},{8,0},{9,1},... | collective-permute-start | bytes 552968 | tf_op jit(solution)/shard_map/ppermute | solution.py:740
  122.5 8.0 %collective-permute-start.44 = (bf16[2,24,1280]{2,1,0:T(8,128)(2,1)S(1)}, bf16[2,24,1280]{2,1,0:T(8,128)(2,1)S(1)}, u32[]{:S(2)}, u32[]{:S(2)}) collective-permute-start(bf16[2,24,1280]{2,1,0:T(8,128)(2,1)S(1)} %get-tuple-element.168), channel_id=1, source_target_pairs={{0,4},{1,5},{2,6},{3,7},{4,0},{5,1},{6,2},{7,3},{8,12},{9,13},{10,... | collective-permute-start | bytes 368648 | tf_op jit(solution)/shard_map/ppermute | solution.py:740
  124.5 7.1 %collective-permute-start.46 = (bf16[2,24,1280]{2,1,0:T(8,128)(2,1)S(1)}, bf16[2,24,1280]{2,1,0:T(8,128)(2,1)S(1)}, u32[]{:S(2)}, u32[]{:S(2)}) collective-permute-start(bf16[2,24,1280]{2,1,0:T(8,128)(2,1)S(1)} %shard_map.220), channel_id=1, source_target_pairs={{0,8},{1,9},{2,10},{3,11},{4,12},{5,13},{6,14},{7,15},{8,0},{9,1},... | collective-permute-start | bytes 368648 | tf_op jit(solution)/shard_map/ppermute | solution.py:740
  129.5 6.3 %collective-permute-start.41 = (bf16[1,24,1920]{2,1,0:T(8,128)(2,1)S(1)}, bf16[1,24,1920]{2,1,0:T(8,128)(2,1)S(1)}, u32[]{:S(2)}, u32[]{:S(2)}) collective-permute-start(bf16[1,24,1920]{2,1,0:T(8,128)(2,1)S(1)} %get-tuple-element.165), channel_id=1, source_target_pairs={{0,16},{1,17},{2,18},{3,19},{4,20},{5,21},{6,22},{7,23},{8,24},{9,... | collective-permute-start | bytes 276488 | tf_op jit(solution)/shard_map/ppermute | solution.py:740
  131.6 5.8 %collective-permute-start.47 = (bf16[1,24,1280]{2,1,0:T(8,128)(2,1)S(1)}, bf16[1,24,1280]{2,1,0:T(8,128)(2,1)S(1)}, u32[]{:S(2)}, u32[]{:S(2)}) collective-permute-start(bf16[1,24,1280]{2,1,0:T(8,128)(2,1)S(1)} %get-tuple-element.171), channel_id=1, source_target_pairs={{0,16},{1,17},{2,18},{3,19},{4,20},{5,21},{6,22},{7,23},{8,24},{9,... | collective-permute-start | bytes 184328 | tf_op jit(solution)/shard_map/ppermute | solution.py:740
  (8 other events, 144.5 us)

commit v7 on v6

--- a/solution.py
+++ b/solution.py
@@ -251,7 +251,7 @@
         for load in given:
             load.wait()
 
-        @pl.loop(0, total // CHUNK, unroll=UNROLL)
+        @pl.loop(0, total // CHUNK, unroll=2 * UNROLL)
         def _(i):
             at = rows_at(i, CHUNK)
             x = x_ref[at].astype(f32)
@@ -292,7 +292,7 @@
         res_ref[...] = x_ref[...].astype(f32) + nn(mixed_ref[...], w_ref[:, 3 * width : 4 * width])
         store(res_ref, res_out)
 
-        @pl.loop(0, total // CHUNK, unroll=UNROLL)
+        @pl.loop(0, total // CHUNK, unroll=2 * UNROLL)
         def _(i):
             at = rows_at(i, CHUNK)
             x = res_ref[at]
@@ -454,7 +454,7 @@
             load.start()
         loads[0].wait()
 
-        @pl.loop(0, images * rows // CHUNK, unroll=UNROLL)
+        @pl.loop(0, images * rows // CHUNK, unroll=2 * UNROLL)
         def _(i):
             at = rows_at(i, CHUNK)
             x = res_ref[at]
@@ -620,7 +620,7 @@
             block_ref[span] = jnp.where(live_row, res_ref[span] + expert_sum, 0.0).astype(bf16)
         gain_a = par_ref[0:1]
 
-        @pl.loop(0, total // CHUNK, unroll=UNROLL)
+        @pl.loop(0, total // CHUNK, unroll=2 * UNROLL)
         def _(i):
             at = rows_at(i, CHUNK)
             x = x_ref[at].astype(f32)

time: 139 us -> 139 us (level)
  transfers between devices with their start and end apart: 48 -> 48, of which waited for: 30 -> 30; matrix products, arithmetic and copies ran while one was open for 0% -> 0% of each run, Pallas kernels for 11% -> 10%
where the time goes in v7:
time: 139 us; the launch traced here: 138 us
  waiting for transfers between devices  54.3 us (39%)
  starting transfers between devices  42.1 us (30%)
  Pallas kernels  40.9 us (29%)
    ppermute x48, waiting for transfers between devices, swap(): return lax.ppermute(value, 'fsdp', [(i, i ^ mask) for i in range(devices)])  54.3 us
    ppermute x48, starting transfers between devices, swap(): return lax.ppermute(value, 'fsdp', [(i, i ^ mask) for i in range(devices)])  42.1 us
    pallas_call x8, Pallas kernels, run(): pl.pallas_call(body, out_shape=[pltpu.HBM(s, d) if i in far_out else jax....  37.7 us
  transfers between devices with their start and end apart: 48, of which 30 were waited for; matrix products, arithmetic and copies ran while one was open for 0% of the time, Pallas kernels for 10%

profile of v7, /device:TPU:0, one launch (start us, length us, event | category | flops | bytes accessed | tf_op | source)
XLA Modules:
  0.0 138.3 jit_solution(15712842157715161913)
XLA Ops:
  0.7 1.1 shard_map.203
  1.7 3.1 %collective-permute-start = (bf16[1,24,3200]{2,1,0:T(8,128)(2,1)S(1)}, bf16[1,24,3200]{2,1,0:T(8,128)(2,1)S(1)}, u32[]{:S(2)}, u32[]{:S(2)}) collective-permute-start(bf16[1,24,3200]{2,1,0:T(8,128)(2,1)S(1)} %bitcast.22), channel_id=1, source_target_pairs={{0,8},{1,9},{2,10},{3,11},{4,12},{5,13},{6,14},{7,15},{8,0},{9,1},... | collective-permute-start | bytes 460808 | tf_op jit(solution)/shard_map/ppermute | solution.py:740
  4.8 2.6 %collective-permute-start.1 = (bf16[1,24,3200]{2,1,0:T(8,128)(2,1)S(1)}, bf16[1,24,3200]{2,1,0:T(8,128)(2,1)S(1)}, u32[]{:S(2)}, u32[]{:S(2)}) collective-permute-start(bf16[1,24,3200]{2,1,0:T(8,128)(2,1)S(1)} %bitcast.23), channel_id=1, source_target_pairs={{0,16},{1,17},{2,18},{3,19},{4,20},{5,21},{6,22},{7,23},{8,24},{9,... | collective-permute-start | bytes 460808 | tf_op jit(solution)/shard_map/ppermute | solution.py:740
  7.4 4.2 %collective-permute-done = bf16[1,24,3200]{2,1,0:T(8,128)(2,1)S(1)} collective-permute-done((bf16[1,24,3200]{2,1,0:T(8,128)(2,1)S(1)}, bf16[1,24,3200]{2,1,0:T(8,128)(2,1)S(1)}, u32[]{:S(2)}, u32[]{:S(2)}) %collective-permute-start) | collective-permute-done | bytes 153632 | tf_op jit(solution)/shard_map/ppermute | solution.py:740
  11.7 1.9 %collective-permute-start.5 = (bf16[2,24,3200]{2,1,0:T(8,128)(2,1)S(1)}, bf16[2,24,3200]{2,1,0:T(8,128)(2,1)S(1)}, u32[]{:S(2)}, u32[]{:S(2)}) collective-permute-start(bf16[2,24,3200]{2,1,0:T(8,128)(2,1)S(1)} %pad_maximum_fusion.refs_0_), channel_id=1, source_target_pairs={{0,4},{1,5},{2,6},{3,7},{4,0},{5,1},{6,2},{7,3},{8,12},{9,13},{10,... | collective-permute-start | bytes 921608 | tf_op jit(solution)/shard_map/ppermute | solution.py:740
  13.6 1.5 %collective-permute-start.3 = (bf16[2,24,3200]{2,1,0:T(8,128)(2,1)S(1)}, bf16[2,24,3200]{2,1,0:T(8,128)(2,1)S(1)}, u32[]{:S(2)}, u32[]{:S(2)}) collective-permute-start(bf16[2,24,3200]{2,1,0:T(8,128)(2,1)S(1)} %pad_maximum_fusion.refs_0_), channel_id=1, source_target_pairs={{0,2},{1,3},{2,0},{3,1},{4,6},{5,7},{6,4},{7,5},{8,10},{9,11},{10,... | collective-permute-start | bytes 921608 | tf_op jit(solution)/shard_map/ppermute | solution.py:740
  15.2 5.8 %collective-permute-done.2 = bf16[1,24,3200]{2,1,0:T(8,128)(2,1)S(1)} collective-permute-done((bf16[1,24,3200]{2,1,0:T(8,128)(2,1)S(1)}, bf16[1,24,3200]{2,1,0:T(8,128)(2,1)S(1)}, u32[]{:S(2)}, u32[]{:S(2)}) %collective-permute-start.2) | collective-permute-done | bytes 153632 | tf_op jit(solution)/shard_map/ppermute | solution.py:740
  21.5 1.3 collective-permute-start.6
  23.3 2.0 %collective-permute-start.7 = (bf16[2,24,3200]{2,1,0:T(8,128)(2,1)S(1)}, bf16[2,24,3200]{2,1,0:T(8,128)(2,1)S(1)}, u32[]{:S(2)}, u32[]{:S(2)}) collective-permute-start(bf16[2,24,3200]{2,1,0:T(8,128)(2,1)S(1)} %collective-permute-done.5.refs_4_), channel_id=1, source_target_pairs={{0,2},{1,3},{2,0},{3,1},{4,6},{5,7},{6,4},{7,5},{8,10},{9,11},{10,... | collective-permute-start | bytes 921608 | tf_op jit(solution)/shard_map/ppermute | solution.py:740
  25.2 6.0 %collective-permute-done.4.refs_3_ = bf16[2,24,3200]{2,1,0:T(8,128)(2,1)S(1)} collective-permute-done((bf16[2,24,3200]{2,1,0:T(8,128)(2,1)S(1)}, bf16[2,24,3200]{2,1,0:T(8,128)(2,1)S(1)}, u32[]{:S(2)}, u32[]{:S(2)}) %collective-permute-start.4) | collective-permute-done | bytes 307232 | tf_op jit(solution)/shard_map/ppermute | solution.py:740
  32.3 3.9 %collective-permute-done.7.refs_6_ = bf16[2,24,3200]{2,1,0:T(8,128)(2,1)S(1)} collective-permute-done((bf16[2,24,3200]{2,1,0:T(8,128)(2,1)S(1)}, bf16[2,24,3200]{2,1,0:T(8,128)(2,1)S(1)}, u32[]{:S(2)}, u32[]{:S(2)}) %collective-permute-start.7) | collective-permute-done | bytes 307232 | tf_op jit(solution)/shard_map/ppermute | solution.py:740
  36.1 1.9 %collective-permute-done.8.refs_7_ = bf16[2,24,3200]{2,1,0:T(8,128)(2,1)S(1)} collective-permute-done((bf16[2,24,3200]{2,1,0:T(8,128)(2,1)S(1)}, bf16[2,24,3200]{2,1,0:T(8,128)(2,1)S(1)}, u32[]{:S(2)}, u32[]{:S(2)}) %collective-permute-start.8) | collective-permute-done | bytes 307232 | tf_op jit(solution)/shard_map/ppermute | solution.py:740
  38.1 1.6 %collective-permute-done.16.refs_15_ = bf16[2,24,3200]{2,1,0:T(8,128)(2,1)S(1)} collective-permute-done((bf16[2,24,3200]{2,1,0:T(8,128)(2,1)S(1)}, bf16[2,24,3200]{2,1,0:T(8,128)(2,1)S(1)}, u32[]{:S(2)}, u32[]{:S(2)}) %collective-permute-start.16) | collective-permute-done | bytes 307232 | tf_op jit(solution)/shard_map/ppermute | solution.py:740
  39.7 9.2 %shard_map.204 = (f32[8,768]{1,0:T(8,128)S(1)}, f32[2,4,208]{2,1,0:T(4,128)S(1)}, bf16[16,768]{1,0:T(8,128)(2,1)S(1)}, bf16[416,768]{1,0:T(8,128)(2,1)}, bf16[41...) custom-call(s32[2]{0:T(128)S(1)} %copy-done.5, ...), custom_call_target="tpu_custom_call" | custom-call | tf_op jit(solution)/shard_map/pallas_call | solution.py:57
  48.8 2.8 %collective-permute-start.19 = (bf16[1,16,768]{2,1,0:T(8,128)(2,1)S(1)}, bf16[1,16,768]{2,1,0:T(8,128)(2,1)S(1)}, u32[]{:S(2)}, u32[]{:S(2)}) collective-permute-start(bf16[1,16,768]{2,1,0:T(8,128)(2,1)S(1)} %bitcast.26), channel_id=1, source_target_pairs={{0,24},{1,25},{2,26},{3,27},{4,28},{5,29},{6,30},{7,31},{8,16},{9,... | collective-permute-start | bytes 73736 | tf_op jit(solution)/shard_map/ppermute | solution.py:740
  51.6 1.7 %collective-permute-start.17 = (bf16[1,16,768]{2,1,0:T(8,128)(2,1)S(1)}, bf16[1,16,768]{2,1,0:T(8,128)(2,1)S(1)}, u32[]{:S(2)}, u32[]{:S(2)}) collective-permute-start(bf16[1,16,768]{2,1,0:T(8,128)(2,1)S(1)} %bitcast.28), channel_id=1, source_target_pairs={{0,8},{1,9},{2,10},{3,11},{4,12},{5,13},{6,14},{7,15},{8,0},{9,1},... | collective-permute-start | bytes 73736 | tf_op jit(solution)/shard_map/ppermute | solution.py:740
  53.3 1.3 collective-permute-done.19
  54.5 1.7 %collective-permute-done.18 = bf16[1,16,768]{2,1,0:T(8,128)(2,1)S(1)} collective-permute-done((bf16[1,16,768]{2,1,0:T(8,128)(2,1)S(1)}, bf16[1,16,768]{2,1,0:T(8,128)(2,1)S(1)}, u32[]{:S(2)}, u32[]{:S(2)}) %collective-permute-start.18) | collective-permute-done | bytes 24608 | tf_op jit(solution)/shard_map/ppermute | solution.py:740
  56.3 1.3 collective-permute-start.22
  57.6 1.7 %collective-permute-start.21 = (bf16[4,16,768]{2,1,0:T(8,128)(2,1)S(1)}, bf16[4,16,768]{2,1,0:T(8,128)(2,1)S(1)}, u32[]{:S(2)}, u32[]{:S(2)}) collective-permute-start(bf16[4,16,768]{2,1,0:T(8,128)(2,1)S(1)} %pad_maximum_fusion.1.refs_0_), channel_id=1, source_target_pairs={{0,4},{1,5},{2,6},{3,7},{4,0},{5,1},{6,2},{7,3},{8,12},{9,13},{10,... | collective-permute-start | bytes 294920 | tf_op jit(solution)/shard_map/ppermute | solution.py:740
  59.9 2.3 %collective-permute-done.22.refs_3_ = bf16[4,16,768]{2,1,0:T(8,128)(2,1)S(1)} collective-permute-done((bf16[4,16,768]{2,1,0:T(8,128)(2,1)S(1)}, bf16[4,16,768]{2,1,0:T(8,128)(2,1)S(1)}, u32[]{:S(2)}, u32[]{:S(2)}) %collective-permute-start.22) | collective-permute-done | bytes 98336 | tf_op jit(solution)/shard_map/ppermute | solution.py:740
  65.3 2.6 %shard_map.205 = (bf16[16,16,768]{2,1,0:T(8,128)(2,1)S(1)}, bf16[16,16,768]{2,1,0:T(8,128)(2,1)S(1)}, bf16[256,768]{1,0:T(8,128)(2,1)S(1)}, bf16[256,768]{1,0:T(...) custom-call(s32[2]{0:T(128)S(1)} %copy-done.5, ...), custom_call_target="tpu_custom_call" | custom-call | tf_op jit(solution)/shard_map/pallas_call | solution.py:57
  68.1 1.6 %collective-permute-done.27.refs_1_ = bf16[16,16,768]{2,1,0:T(8,128)(2,1)S(1)} collective-permute-done((bf16[16,16,768]{2,1,0:T(8,128)(2,1)S(1)}, bf16[16,16,768]{2,1,0:T(8,128)(2,1)S(1)}, u32[]{:S(2)}, u32[]{:S(2)}) %collective-permute-start.27) | collective-permute-done | bytes 393248 | tf_op jit(solution)/shard_map/ppermute | solution.py:740
  71.2 2.2 %collective-permute-start.30 = (bf16[4,16,768]{2,1,0:T(8,128)(2,1)S(1)}, bf16[4,16,768]{2,1,0:T(8,128)(2,1)S(1)}, u32[]{:S(2)}, u32[]{:S(2)}) collective-permute-start(bf16[4,16,768]{2,1,0:T(8,128)(2,1)S(1)} %get-tuple-element.104), channel_id=1, source_target_pairs={{0,6},{1,7},{2,4},{3,5},{4,2},{5,3},{6,0},{7,1},{8,14},{9,15},{10,... | collective-permute-start | bytes 294920 | tf_op jit(solution)/shard_map/ppermute | solution.py:740
  73.4 2.2 %shard_map.209 = (f32[416,768]{1,0:T(8,128)S(1)}, f32[416,128]{1,0:T(8,128)S(1)}, bf16[416,768]{1,0:T(8,128)(2,1)S(1)}) custom-call(s32[2]{0:T(128)S(1)} %copy-done.5, f32[416,768]{1,0:T(8,128)} %get-tuple-element.116.res_in, bf16[416,768]{1,0:T(8,128)(2,1)} %get-tuple-element.117.n2_in), custom_call_target="tpu_custom_call" | custom-call | flops 1000000000 | tf_op jit(solution)/shard_map/pallas_call | solution.py:57
  75.6 1.7 %collective-permute-done.29.refs_2_ = bf16[4,16,768]{2,1,0:T(8,128)(2,1)S(1)} collective-permute-done((bf16[4,16,768]{2,1,0:T(8,128)(2,1)S(1)}, bf16[4,16,768]{2,1,0:T(8,128)(2,1)S(1)}, u32[]{:S(2)}, u32[]{:S(2)}) %collective-permute-start.29) | collective-permute-done | bytes 98336 | tf_op jit(solution)/shard_map/ppermute | solution.py:740
  77.3 1.0 collective-permute-start.31
  78.3 1.3 collective-permute-start.32
  79.7 2.1 %collective-permute-start.33 = (bf16[1,16,768]{2,1,0:T(8,128)(2,1)S(1)}, bf16[1,16,768]{2,1,0:T(8,128)(2,1)S(1)}, u32[]{:S(2)}, u32[]{:S(2)}) collective-permute-start(bf16[1,16,768]{2,1,0:T(8,128)(2,1)S(1)} %get-tuple-element.115), channel_id=1, source_target_pairs={{0,24},{1,25},{2,26},{3,27},{4,28},{5,29},{6,30},{7,31},{8,16},{9,... | collective-permute-start | bytes 73736 | tf_op jit(solution)/shard_map/ppermute | solution.py:740
  81.8 2.5 %shard_map.208 = (f32[4,96,768]{2,1,0:T(8,128)}, f32[4,96,768]{2,1,0:T(8,128)}) custom-call(s32[2]{0:T(128)S(1)} %copy-done.5, bf16[256,768]{1,0:T(8,128)(2,1)S(1)} %get-tuple-element.106.s_ref, bf16[256,768]{1,0:T(8,128)(2,1)S(1)} %get-tuple-element.107.g_ref, bf16[256,512]{1,0:T(8,128)(2,1)S(1)} %get-tuple-element.108.act_ref, ...), custom_call_target="tpu_custom_call" | custom-call | flops 2000000000 | tf_op jit(solution)/shard_map/pallas_call | solution.py:57
  84.3 1.0 collective-permute-done.33.r3_ref
  85.3 9.8 %shard_map.210 = (f32[16,768]{1,0:T(8,128)S(1)}, f32[2,4,208]{2,1,0:T(4,128)S(1)}, f32[416,768]{1,0:T(8,128)S(1)}, bf16[416,768]{1,0:T(8,128)(2,1)S(1)}, bf16[41...) custom-call(s32[2]{0:T(128)S(1)} %copy-done.5, ...), custom_call_target="tpu_custom_call" | custom-call | tf_op jit(solution)/shard_map/pallas_call | solution.py:57
  95.2 2.9 %shard_map.211 = (bf16[416,1152]{1,0:T(8,128)(2,1)S(1)}, f32[8,768]{1,0:T(8,128)S(1)}) custom-call(s32[2]{0:T(128)S(1)} %copy-done.5, bf16[416,768]{1,0:T(8,128)(2,1)S(1)} %get-tuple-element.127.gm_ref, bf16[416,1152]{1,0:T(8,128)(2,1)S(1)} %get-tuple-element.128.joint_ref, bf16[3,2,416,208]{3,2,1,0:T(8,128)(2,1)S(1)} %get-tuple-element.129.probs_ref, ...), custom_call_target="tpu_custom_call" | custom-call | flops 3000000000 | tf_op jit(solution)/shard_map/pallas_call | solution.py:57
  98.8 2.6 %shard_map.213 = (bf16[16,24,1280]{2,1,0:T(8,128)(2,1)S(1)}, bf16[16,24,1280]{2,1,0:T(8,128)(2,1)S(1)}) custom-call(s32[2]{0:T(128)S(1)} %copy-done.5, bf16[416,1152]{1,0:T(8,128)(2,1)S(1)} %get-tuple-element.143.gj.gj1_ref, f32[8,768]{1,0:T(8,128)S(1)} %get-tuple-element.144.grads, f32[8,768]{1,0:T(8,128)S(1)} %get-tuple-element.145.slot_ref, ...), custom_call_target="tpu_custom_call" | custom-call | flops 4000000000 | tf_op jit(solution)/shard_map/pallas_call | solution.py:57
  101.6 1.3 collective-permute-start.36
  104.3 1.3 collective-permute-start.42
  106.4 6.0 %shard_map.215 = (f32[416,768]{1,0:T(8,128)}, bf16[416,768]{1,0:T(8,128)(2,1)}) custom-call(s32[2]{0:T(128)S(1)} %copy-done.5, bf16[416,768]{1,0:T(8,128)(2,1)S(1)} %bitcast.21, f32[8,768]{1,0:T(8,128)S(1)} %get-tuple-element.96.par_ref, bf16[416,1152]{1,0:T(8,128)(2,1)S(1)} %get-tuple-element.126.gj0_ref, ...), custom_call_target="tpu_custom_call" | custom-call | flops 5000000000 | tf_op jit(solution)/shard_map/pallas_call | solution.py:57
  113.0 1.3 collective-permute-done.37.refs_2_
  115.3 3.0 %collective-permute-done.42.refs_3_.refs_1_ = bf16[4,24,1280]{2,1,0:T(8,128)(2,1)S(1)} collective-permute-done((bf16[4,24,1280]{2,1,0:T(8,128)(2,1)S(1)}, bf16[4,24,1280]{2,1,0:T(8,128)(2,1)S(1)}, u32[]{:S(2)}, u32[]{:S(2)}) %collective-permute-start.42) | collective-permute-done | bytes 245792 | tf_op jit(solution)/shard_map/ppermute | solution.py:740
  120.6 1.7 %collective-permute-done.39.refs_1_ = bf16[2,24,1920]{2,1,0:T(8,128)(2,1)S(1)} collective-permute-done((bf16[2,24,1920]{2,1,0:T(8,128)(2,1)S(1)}, bf16[2,24,1920]{2,1,0:T(8,128)(2,1)S(1)}, u32[]{:S(2)}, u32[]{:S(2)}) %collective-permute-start.39) | collective-permute-done | bytes 184352 | tf_op jit(solution)/shard_map/ppermute | solution.py:740
  122.5 1.0 collective-permute-start.44
  124.4 1.1 collective-permute-start.46
  126.4 2.9 %collective-permute-done.40.refs_3_ = bf16[2,24,1920]{2,1,0:T(8,128)(2,1)S(1)} collective-permute-done((bf16[2,24,1920]{2,1,0:T(8,128)(2,1)S(1)}, bf16[2,24,1920]{2,1,0:T(8,128)(2,1)S(1)}, u32[]{:S(2)}, u32[]{:S(2)}) %collective-permute-start.40) | collective-permute-done | bytes 184352 | tf_op jit(solution)/shard_map/ppermute | solution.py:740
  129.4 1.0 collective-permute-start.41
  130.4 1.0 collective-permute-done.46.refs_3_
  131.5 1.2 collective-permute-start.47
  132.7 3.0 %collective-permute-done.41.a1 = bf16[1,24,1920]{2,1,0:T(8,128)(2,1)S(1)} collective-permute-done((bf16[1,24,1920]{2,1,0:T(8,128)(2,1)S(1)}, bf16[1,24,1920]{2,1,0:T(8,128)(2,1)S(1)}, u32[]{:S(2)}, u32[]{:S(2)}) %collective-permute-start.41) | collective-permute-done | bytes 92192 | tf_op jit(solution)/shard_map/ppermute | solution.py:740
  135.7 1.7 %collective-permute-done.47.b1 = bf16[1,24,1280]{2,1,0:T(8,128)(2,1)S(1)} collective-permute-done((bf16[1,24,1280]{2,1,0:T(8,128)(2,1)S(1)}, bf16[1,24,1280]{2,1,0:T(8,128)(2,1)S(1)}, u32[]{:S(2)}, u32[]{:S(2)}) %collective-permute-start.47) | collective-permute-done | bytes 61472 | tf_op jit(solution)/shard_map/ppermute | solution.py:740
  (88 shorter events, 17.9 us)
Async XLA Ops:
  1.7 9.9 %collective-permute-start = (bf16[1,24,3200]{2,1,0:T(8,128)(2,1)S(1)}, bf16[1,24,3200]{2,1,0:T(8,128)(2,1)S(1)}, u32[]{:S(2)}, u32[]{:S(2)}) collective-permute-start(bf16[1,24,3200]{2,1,0:T(8,128)(2,1)S(1)} %bitcast.22), channel_id=1, source_target_pairs={{0,8},{1,9},{2,10},{3,11},{4,12},{5,13},{6,14},{7,15},{8,0},{9,1},... | collective-permute-start | bytes 460808 | tf_op jit(solution)/shard_map/ppermute | solution.py:740
  4.8 10.3 %collective-permute-start.1 = (bf16[1,24,3200]{2,1,0:T(8,128)(2,1)S(1)}, bf16[1,24,3200]{2,1,0:T(8,128)(2,1)S(1)}, u32[]{:S(2)}, u32[]{:S(2)}) collective-permute-start(bf16[1,24,3200]{2,1,0:T(8,128)(2,1)S(1)} %bitcast.23), channel_id=1, source_target_pairs={{0,16},{1,17},{2,18},{3,19},{4,20},{5,21},{6,22},{7,23},{8,24},{9,... | collective-permute-start | bytes 460808 | tf_op jit(solution)/shard_map/ppermute | solution.py:740
  11.6 9.9 %collective-permute-start.9 = (bf16[2,24,3200]{2,1,0:T(8,128)(2,1)S(1)}, bf16[2,24,3200]{2,1,0:T(8,128)(2,1)S(1)}, u32[]{:S(2)}, u32[]{:S(2)}) collective-permute-start(bf16[2,24,3200]{2,1,0:T(8,128)(2,1)S(1)} %pad_maximum_fusion.refs_0_), channel_id=1, source_target_pairs={{0,1},{1,0},{2,3},{3,2},{4,5},{5,4},{6,7},{7,6},{8,9},{9,8},{10,11... | collective-permute-start | bytes 921608 | tf_op jit(solution)/shard_map/ppermute | solution.py:740
  11.7 11.1 %collective-permute-start.5 = (bf16[2,24,3200]{2,1,0:T(8,128)(2,1)S(1)}, bf16[2,24,3200]{2,1,0:T(8,128)(2,1)S(1)}, u32[]{:S(2)}, u32[]{:S(2)}) collective-permute-start(bf16[2,24,3200]{2,1,0:T(8,128)(2,1)S(1)} %pad_maximum_fusion.refs_0_), channel_id=1, source_target_pairs={{0,4},{1,5},{2,6},{3,7},{4,0},{5,1},{6,2},{7,3},{8,12},{9,13},{10,... | collective-permute-start | bytes 921608 | tf_op jit(solution)/shard_map/ppermute | solution.py:740
  13.6 9.7 %collective-permute-start.3 = (bf16[2,24,3200]{2,1,0:T(8,128)(2,1)S(1)}, bf16[2,24,3200]{2,1,0:T(8,128)(2,1)S(1)}, u32[]{:S(2)}, u32[]{:S(2)}) collective-permute-start(bf16[2,24,3200]{2,1,0:T(8,128)(2,1)S(1)} %pad_maximum_fusion.refs_0_), channel_id=1, source_target_pairs={{0,2},{1,3},{2,0},{3,1},{4,6},{5,7},{6,4},{7,5},{8,10},{9,11},{10,... | collective-permute-start | bytes 921608 | tf_op jit(solution)/shard_map/ppermute | solution.py:740
  15.1 5.8 %collective-permute-start.2 = (bf16[1,24,3200]{2,1,0:T(8,128)(2,1)S(1)}, bf16[1,24,3200]{2,1,0:T(8,128)(2,1)S(1)}, u32[]{:S(2)}, u32[]{:S(2)}) collective-permute-start(bf16[1,24,3200]{2,1,0:T(8,128)(2,1)S(1)} %collective-permute-done.1), channel_id=1, source_target_pairs={{0,8},{1,9},{2,10},{3,11},{4,12},{5,13},{6,14},{7,15},{8,0},{9,1},... | collective-permute-start | bytes 460808 | tf_op jit(solution)/shard_map/ppermute | solution.py:740
  20.9 10.3 %collective-permute-start.4 = (bf16[2,24,3200]{2,1,0:T(8,128)(2,1)S(1)}, bf16[2,24,3200]{2,1,0:T(8,128)(2,1)S(1)}, u32[]{:S(2)}, u32[]{:S(2)}) collective-permute-start(bf16[2,24,3200]{2,1,0:T(8,128)(2,1)S(1)} %constant_dynamic-update-slice_fusion.refs_1_), channel_id=1, source_target_pairs={{0,2},{1,3},{2,0},{3,1},{4,6},{5,7},{6,4},{7,5},{8,10},{9,11},{10,... | collective-permute-start | bytes 921608 | tf_op jit(solution)/shard_map/ppermute | solution.py:740
  21.5 10.2 %collective-permute-start.10 = (bf16[2,24,3200]{2,1,0:T(8,128)(2,1)S(1)}, bf16[2,24,3200]{2,1,0:T(8,128)(2,1)S(1)}, u32[]{:S(2)}, u32[]{:S(2)}) collective-permute-start(bf16[2,24,3200]{2,1,0:T(8,128)(2,1)S(1)} %constant_dynamic-update-slice_fusion.refs_1_), channel_id=1, source_target_pairs={{0,1},{1,0},{2,3},{3,2},{4,5},{5,4},{6,7},{7,6},{8,9},{9,8},{10,11... | collective-permute-start | bytes 921608 | tf_op jit(solution)/shard_map/ppermute | solution.py:740
  21.5 10.2 %collective-permute-start.6 = (bf16[2,24,3200]{2,1,0:T(8,128)(2,1)S(1)}, bf16[2,24,3200]{2,1,0:T(8,128)(2,1)S(1)}, u32[]{:S(2)}, u32[]{:S(2)}) collective-permute-start(bf16[2,24,3200]{2,1,0:T(8,128)(2,1)S(1)} %constant_dynamic-update-slice_fusion.refs_1_), channel_id=1, source_target_pairs={{0,4},{1,5},{2,6},{3,7},{4,0},{5,1},{6,2},{7,3},{8,12},{9,13},{10,... | collective-permute-start | bytes 921608 | tf_op jit(solution)/shard_map/ppermute | solution.py:740
  22.8 9.4 %collective-permute-start.13 = (bf16[2,24,3200]{2,1,0:T(8,128)(2,1)S(1)}, bf16[2,24,3200]{2,1,0:T(8,128)(2,1)S(1)}, u32[]{:S(2)}, u32[]{:S(2)}) collective-permute-start(bf16[2,24,3200]{2,1,0:T(8,128)(2,1)S(1)} %collective-permute-done.5.refs_4_), channel_id=1, source_target_pairs={{0,1},{1,0},{2,3},{3,2},{4,5},{5,4},{6,7},{7,6},{8,9},{9,8},{10,11... | collective-permute-start | bytes 921608 | tf_op jit(solution)/shard_map/ppermute | solution.py:740
  23.3 12.9 %collective-permute-start.7 = (bf16[2,24,3200]{2,1,0:T(8,128)(2,1)S(1)}, bf16[2,24,3200]{2,1,0:T(8,128)(2,1)S(1)}, u32[]{:S(2)}, u32[]{:S(2)}) collective-permute-start(bf16[2,24,3200]{2,1,0:T(8,128)(2,1)S(1)} %collective-permute-done.5.refs_4_), channel_id=1, source_target_pairs={{0,2},{1,3},{2,0},{3,1},{4,6},{5,7},{6,4},{7,5},{8,10},{9,11},{10,... | collective-permute-start | bytes 921608 | tf_op jit(solution)/shard_map/ppermute | solution.py:740
  31.2 6.9 %collective-permute-start.8 = (bf16[2,24,3200]{2,1,0:T(8,128)(2,1)S(1)}, bf16[2,24,3200]{2,1,0:T(8,128)(2,1)S(1)}, u32[]{:S(2)}, u32[]{:S(2)}) collective-permute-start(bf16[2,24,3200]{2,1,0:T(8,128)(2,1)S(1)} %collective-permute-done.4.refs_3_), channel_id=1, source_target_pairs={{0,4},{1,5},{2,6},{3,7},{4,0},{5,1},{6,2},{7,3},{8,12},{9,13},{10,... | collective-permute-start | bytes 921608 | tf_op jit(solution)/shard_map/ppermute | solution.py:740
  31.7 6.4 %collective-permute-start.11 = (bf16[2,24,3200]{2,1,0:T(8,128)(2,1)S(1)}, bf16[2,24,3200]{2,1,0:T(8,128)(2,1)S(1)}, u32[]{:S(2)}, u32[]{:S(2)}) collective-permute-start(bf16[2,24,3200]{2,1,0:T(8,128)(2,1)S(1)} %collective-permute-done.3.refs_2_), channel_id=1, source_target_pairs={{0,1},{1,0},{2,3},{3,2},{4,5},{5,4},{6,7},{7,6},{8,9},{9,8},{10,11... | collective-permute-start | bytes 921608 | tf_op jit(solution)/shard_map/ppermute | solution.py:740
  31.7 6.4 %collective-permute-start.12 = (bf16[2,24,3200]{2,1,0:T(8,128)(2,1)S(1)}, bf16[2,24,3200]{2,1,0:T(8,128)(2,1)S(1)}, u32[]{:S(2)}, u32[]{:S(2)}) collective-permute-start(bf16[2,24,3200]{2,1,0:T(8,128)(2,1)S(1)} %collective-permute-done.4.refs_3_), channel_id=1, source_target_pairs={{0,1},{1,0},{2,3},{3,2},{4,5},{5,4},{6,7},{7,6},{8,9},{9,8},{10,11... | collective-permute-start | bytes 921608 | tf_op jit(solution)/shard_map/ppermute | solution.py:740
  32.2 5.8 %collective-permute-start.14 = (bf16[2,24,3200]{2,1,0:T(8,128)(2,1)S(1)}, bf16[2,24,3200]{2,1,0:T(8,128)(2,1)S(1)}, u32[]{:S(2)}, u32[]{:S(2)}) collective-permute-start(bf16[2,24,3200]{2,1,0:T(8,128)(2,1)S(1)} %collective-permute-done.6.refs_5_), channel_id=1, source_target_pairs={{0,1},{1,0},{2,3},{3,2},{4,5},{5,4},{6,7},{7,6},{8,9},{9,8},{10,11... | collective-permute-start | bytes 921608 | tf_op jit(solution)/shard_map/ppermute | solution.py:740
  36.1 1.9 %collective-permute-start.15 = (bf16[2,24,3200]{2,1,0:T(8,128)(2,1)S(1)}, bf16[2,24,3200]{2,1,0:T(8,128)(2,1)S(1)}, u32[]{:S(2)}, u32[]{:S(2)}) collective-permute-start(bf16[2,24,3200]{2,1,0:T(8,128)(2,1)S(1)} %collective-permute-done.7.refs_6_), channel_id=1, source_target_pairs={{0,1},{1,0},{2,3},{3,2},{4,5},{5,4},{6,7},{7,6},{8,9},{9,8},{10,11... | collective-permute-start | bytes 921608 | tf_op jit(solution)/shard_map/ppermute | solution.py:740
  38.1 1.6 %collective-permute-start.16 = (bf16[2,24,3200]{2,1,0:T(8,128)(2,1)S(1)}, bf16[2,24,3200]{2,1,0:T(8,128)(2,1)S(1)}, u32[]{:S(2)}, u32[]{:S(2)}) collective-permute-start(bf16[2,24,3200]{2,1,0:T(8,128)(2,1)S(1)} %collective-permute-done.8.refs_7_), channel_id=1, source_target_pairs={{0,1},{1,0},{2,3},{3,2},{4,5},{5,4},{6,7},{7,6},{8,9},{9,8},{10,11... | collective-permute-start | bytes 921608 | tf_op jit(solution)/shard_map/ppermute | solution.py:740
  48.8 5.7 %collective-permute-start.19 = (bf16[1,16,768]{2,1,0:T(8,128)(2,1)S(1)}, bf16[1,16,768]{2,1,0:T(8,128)(2,1)S(1)}, u32[]{:S(2)}, u32[]{:S(2)}) collective-permute-start(bf16[1,16,768]{2,1,0:T(8,128)(2,1)S(1)} %bitcast.26), channel_id=1, source_target_pairs={{0,24},{1,25},{2,26},{3,27},{4,28},{5,29},{6,30},{7,31},{8,16},{9,... | collective-permute-start | bytes 73736 | tf_op jit(solution)/shard_map/ppermute | solution.py:740
  51.6 4.7 %collective-permute-start.18 = (bf16[1,16,768]{2,1,0:T(8,128)(2,1)S(1)}, bf16[1,16,768]{2,1,0:T(8,128)(2,1)S(1)}, u32[]{:S(2)}, u32[]{:S(2)}) collective-permute-start(bf16[1,16,768]{2,1,0:T(8,128)(2,1)S(1)} %bitcast.27), channel_id=1, source_target_pairs={{0,16},{1,17},{2,18},{3,19},{4,20},{5,21},{6,22},{7,23},{8,24},{9,... | collective-permute-start | bytes 73736 | tf_op jit(solution)/shard_map/ppermute | solution.py:740
  51.6 4.7 %collective-permute-start.17 = (bf16[1,16,768]{2,1,0:T(8,128)(2,1)S(1)}, bf16[1,16,768]{2,1,0:T(8,128)(2,1)S(1)}, u32[]{:S(2)}, u32[]{:S(2)}) collective-permute-start(bf16[1,16,768]{2,1,0:T(8,128)(2,1)S(1)} %bitcast.28), channel_id=1, source_target_pairs={{0,8},{1,9},{2,10},{3,11},{4,12},{5,13},{6,14},{7,15},{8,0},{9,1},... | collective-permute-start | bytes 73736 | tf_op jit(solution)/shard_map/ppermute | solution.py:740
  56.3 5.8 %collective-permute-start.22 = (bf16[4,16,768]{2,1,0:T(8,128)(2,1)S(1)}, bf16[4,16,768]{2,1,0:T(8,128)(2,1)S(1)}, u32[]{:S(2)}, u32[]{:S(2)}) collective-permute-start(bf16[4,16,768]{2,1,0:T(8,128)(2,1)S(1)} %pad_maximum_fusion.1.refs_0_), channel_id=1, source_target_pairs={{0,6},{1,7},{2,4},{3,5},{4,2},{5,3},{6,0},{7,1},{8,14},{9,15},{10,... | collective-permute-start | bytes 294920 | tf_op jit(solution)/shard_map/ppermute | solution.py:740
  57.6 5.5 %collective-permute-start.21 = (bf16[4,16,768]{2,1,0:T(8,128)(2,1)S(1)}, bf16[4,16,768]{2,1,0:T(8,128)(2,1)S(1)}, u32[]{:S(2)}, u32[]{:S(2)}) collective-permute-start(bf16[4,16,768]{2,1,0:T(8,128)(2,1)S(1)} %pad_maximum_fusion.1.refs_0_), channel_id=1, source_target_pairs={{0,4},{1,5},{2,6},{3,7},{4,0},{5,1},{6,2},{7,3},{8,12},{9,13},{10,... | collective-permute-start | bytes 294920 | tf_op jit(solution)/shard_map/ppermute | solution.py:740
  59.4 4.6 %collective-permute-start.20 = (bf16[4,16,768]{2,1,0:T(8,128)(2,1)S(1)}, bf16[4,16,768]{2,1,0:T(8,128)(2,1)S(1)}, u32[]{:S(2)}, u32[]{:S(2)}) collective-permute-start(bf16[4,16,768]{2,1,0:T(8,128)(2,1)S(1)} %pad_maximum_fusion.1.refs_0_), channel_id=1, source_target_pairs={{0,2},{1,3},{2,0},{3,1},{4,6},{5,7},{6,4},{7,5},{8,10},{9,11},{10,... | collective-permute-start | bytes 294920 | tf_op jit(solution)/shard_map/ppermute | solution.py:740
  59.9 4.1 %collective-permute-start.23 = (bf16[4,16,768]{2,1,0:T(8,128)(2,1)S(1)}, bf16[4,16,768]{2,1,0:T(8,128)(2,1)S(1)}, u32[]{:S(2)}, u32[]{:S(2)}) collective-permute-start(bf16[4,16,768]{2,1,0:T(8,128)(2,1)S(1)} %pad_maximum_fusion.1.refs_0_), channel_id=1, source_target_pairs={{0,1},{1,0},{2,3},{3,2},{4,5},{5,4},{6,7},{7,6},{8,9},{9,8},{10,11... | collective-permute-start | bytes 294920 | tf_op jit(solution)/shard_map/ppermute | solution.py:740
  62.1 1.8 %collective-permute-start.26 = (bf16[4,16,768]{2,1,0:T(8,128)(2,1)S(1)}, bf16[4,16,768]{2,1,0:T(8,128)(2,1)S(1)}, u32[]{:S(2)}, u32[]{:S(2)}) collective-permute-start(bf16[4,16,768]{2,1,0:T(8,128)(2,1)S(1)} %collective-permute-done.22.refs_3_), channel_id=1, source_target_pairs={{0,1},{1,0},{2,3},{3,2},{4,5},{5,4},{6,7},{7,6},{8,9},{9,8},{10,11... | collective-permute-start | bytes 294920 | tf_op jit(solution)/shard_map/ppermute | solution.py:740
  63.1 1.3 collective-permute-start.25
  64.0 1.3 collective-permute-start.24
  67.9 1.8 %collective-permute-start.27 = (bf16[16,16,768]{2,1,0:T(8,128)(2,1)S(1)}, bf16[16,16,768]{2,1,0:T(8,128)(2,1)S(1)}, u32[]{:S(2)}, u32[]{:S(2)}) collective-permute-start(bf16[16,16,768]{2,1,0:T(8,128)(2,1)S(1)} %get-tuple-element.100), channel_id=1, source_target_pairs={{0,1},{1,0},{2,3},{3,2},{4,5},{5,4},{6,7},{7,6},{8,9},{9,8},{10,11... | collective-permute-start | bytes 1179656 | tf_op jit(solution)/shard_map/ppermute | solution.py:740
  69.8 5.8 %collective-permute-start.28 = (bf16[4,16,768]{2,1,0:T(8,128)(2,1)S(1)}, bf16[4,16,768]{2,1,0:T(8,128)(2,1)S(1)}, u32[]{:S(2)}, u32[]{:S(2)}) collective-permute-start(bf16[4,16,768]{2,1,0:T(8,128)(2,1)S(1)} %get-tuple-element.102), channel_id=1, source_target_pairs={{0,2},{1,3},{2,0},{3,1},{4,6},{5,7},{6,4},{7,5},{8,10},{9,11},{10,... | collective-permute-start | bytes 294920 | tf_op jit(solution)/shard_map/ppermute | solution.py:740
  70.4 6.9 %collective-permute-start.29 = (bf16[4,16,768]{2,1,0:T(8,128)(2,1)S(1)}, bf16[4,16,768]{2,1,0:T(8,128)(2,1)S(1)}, u32[]{:S(2)}, u32[]{:S(2)}) collective-permute-start(bf16[4,16,768]{2,1,0:T(8,128)(2,1)S(1)} %get-tuple-element.103), channel_id=1, source_target_pairs={{0,4},{1,5},{2,6},{3,7},{4,0},{5,1},{6,2},{7,3},{8,12},{9,13},{10,... | collective-permute-start | bytes 294920 | tf_op jit(solution)/shard_map/ppermute | solution.py:740
  71.2 6.1 %collective-permute-start.30 = (bf16[4,16,768]{2,1,0:T(8,128)(2,1)S(1)}, bf16[4,16,768]{2,1,0:T(8,128)(2,1)S(1)}, u32[]{:S(2)}, u32[]{:S(2)}) collective-permute-start(bf16[4,16,768]{2,1,0:T(8,128)(2,1)S(1)} %get-tuple-element.104), channel_id=1, source_target_pairs={{0,6},{1,7},{2,4},{3,5},{4,2},{5,3},{6,0},{7,1},{8,14},{9,15},{10,... | collective-permute-start | bytes 294920 | tf_op jit(solution)/shard_map/ppermute | solution.py:740
  77.3 7.0 %collective-permute-start.31 = (bf16[1,16,768]{2,1,0:T(8,128)(2,1)S(1)}, bf16[1,16,768]{2,1,0:T(8,128)(2,1)S(1)}, u32[]{:S(2)}, u32[]{:S(2)}) collective-permute-start(bf16[1,16,768]{2,1,0:T(8,128)(2,1)S(1)} %get-tuple-element.113), channel_id=1, source_target_pairs={{0,8},{1,9},{2,10},{3,11},{4,12},{5,13},{6,14},{7,15},{8,0},{9,1},... | collective-permute-start | bytes 73736 | tf_op jit(solution)/shard_map/ppermute | solution.py:740
  78.3 6.0 %collective-permute-start.32 = (bf16[1,16,768]{2,1,0:T(8,128)(2,1)S(1)}, bf16[1,16,768]{2,1,0:T(8,128)(2,1)S(1)}, u32[]{:S(2)}, u32[]{:S(2)}) collective-permute-start(bf16[1,16,768]{2,1,0:T(8,128)(2,1)S(1)} %get-tuple-element.114), channel_id=1, source_target_pairs={{0,16},{1,17},{2,18},{3,19},{4,20},{5,21},{6,22},{7,23},{8,24},{9,... | collective-permute-start | bytes 73736 | tf_op jit(solution)/shard_map/ppermute | solution.py:740
  79.7 5.6 %collective-permute-start.33 = (bf16[1,16,768]{2,1,0:T(8,128)(2,1)S(1)}, bf16[1,16,768]{2,1,0:T(8,128)(2,1)S(1)}, u32[]{:S(2)}, u32[]{:S(2)}) collective-permute-start(bf16[1,16,768]{2,1,0:T(8,128)(2,1)S(1)} %get-tuple-element.115), channel_id=1, source_target_pairs={{0,24},{1,25},{2,26},{3,27},{4,28},{5,29},{6,30},{7,31},{8,16},{9,... | collective-permute-start | bytes 73736 | tf_op jit(solution)/shard_map/ppermute | solution.py:740
  95.1 3.3 %collective-permute-start.34 = (bf16[16,24,1920]{2,1,0:T(8,128)(2,1)S(1)}, bf16[16,24,1920]{2,1,0:T(8,128)(2,1)S(1)}, u32[]{:S(2)}, u32[]{:S(2)}) collective-permute-start(bf16[16,24,1920]{2,1,0:T(8,128)(2,1)S(1)} %get-tuple-element.136), channel_id=1, source_target_pairs={{0,1},{1,0},{2,3},{3,2},{4,5},{5,4},{6,7},{7,6},{8,9},{9,8},{10,11... | collective-permute-start | bytes 4423688 | tf_op jit(solution)/shard_map/ppermute | solution.py:740
  101.4 2.6 %collective-permute-start.35 = (bf16[16,24,1280]{2,1,0:T(8,128)(2,1)S(1)}, bf16[16,24,1280]{2,1,0:T(8,128)(2,1)S(1)}, u32[]{:S(2)}, u32[]{:S(2)}) collective-permute-start(bf16[16,24,1280]{2,1,0:T(8,128)(2,1)S(1)} %get-tuple-element.149), channel_id=1, source_target_pairs={{0,1},{1,0},{2,3},{3,2},{4,5},{5,4},{6,7},{7,6},{8,9},{9,8},{10,11... | collective-permute-start | bytes 2949128 | tf_op jit(solution)/shard_map/ppermute | solution.py:740
  101.6 11.4 %collective-permute-start.36 = (bf16[4,24,1920]{2,1,0:T(8,128)(2,1)S(1)}, bf16[4,24,1920]{2,1,0:T(8,128)(2,1)S(1)}, u32[]{:S(2)}, u32[]{:S(2)}) collective-permute-start(bf16[4,24,1920]{2,1,0:T(8,128)(2,1)S(1)} %get-tuple-element.139), channel_id=1, source_target_pairs={{0,2},{1,3},{2,0},{3,1},{4,6},{5,7},{6,4},{7,5},{8,10},{9,11},{10,... | collective-permute-start | bytes 1105928 | tf_op jit(solution)/shard_map/ppermute | solution.py:740
  102.9 11.4 %collective-permute-start.37 = (bf16[4,24,1920]{2,1,0:T(8,128)(2,1)S(1)}, bf16[4,24,1920]{2,1,0:T(8,128)(2,1)S(1)}, u32[]{:S(2)}, u32[]{:S(2)}) collective-permute-start(bf16[4,24,1920]{2,1,0:T(8,128)(2,1)S(1)} %get-tuple-element.140), channel_id=1, source_target_pairs={{0,4},{1,5},{2,6},{3,7},{4,0},{5,1},{6,2},{7,3},{8,12},{9,13},{10,... | collective-permute-start | bytes 1105928 | tf_op jit(solution)/shard_map/ppermute | solution.py:740
  104.3 14.0 %collective-permute-start.42 = (bf16[4,24,1280]{2,1,0:T(8,128)(2,1)S(1)}, bf16[4,24,1280]{2,1,0:T(8,128)(2,1)S(1)}, u32[]{:S(2)}, u32[]{:S(2)}) collective-permute-start(bf16[4,24,1280]{2,1,0:T(8,128)(2,1)S(1)} %get-tuple-element.152), channel_id=1, source_target_pairs={{0,2},{1,3},{2,0},{3,1},{4,6},{5,7},{6,4},{7,5},{8,10},{9,11},{10,... | collective-permute-start | bytes 737288 | tf_op jit(solution)/shard_map/ppermute | solution.py:740
  105.6 13.1 %collective-permute-start.43 = (bf16[4,24,1280]{2,1,0:T(8,128)(2,1)S(1)}, bf16[4,24,1280]{2,1,0:T(8,128)(2,1)S(1)}, u32[]{:S(2)}, u32[]{:S(2)}) collective-permute-start(bf16[4,24,1280]{2,1,0:T(8,128)(2,1)S(1)} %get-tuple-element.153), channel_id=1, source_target_pairs={{0,4},{1,5},{2,6},{3,7},{4,0},{5,1},{6,2},{7,3},{8,12},{9,13},{10,... | collective-permute-start | bytes 737288 | tf_op jit(solution)/shard_map/ppermute | solution.py:740
  114.5 7.8 %collective-permute-start.39 = (bf16[2,24,1920]{2,1,0:T(8,128)(2,1)S(1)}, bf16[2,24,1920]{2,1,0:T(8,128)(2,1)S(1)}, u32[]{:S(2)}, u32[]{:S(2)}) collective-permute-start(bf16[2,24,1920]{2,1,0:T(8,128)(2,1)S(1)} %get-tuple-element.163), channel_id=1, source_target_pairs={{0,2},{1,3},{2,0},{3,1},{4,6},{5,7},{6,4},{7,5},{8,10},{9,11},{10,... | collective-permute-start | bytes 552968 | tf_op jit(solution)/shard_map/ppermute | solution.py:740
  118.8 5.5 %collective-permute-start.45 = (bf16[2,24,1280]{2,1,0:T(8,128)(2,1)S(1)}, bf16[2,24,1280]{2,1,0:T(8,128)(2,1)S(1)}, u32[]{:S(2)}, u32[]{:S(2)}) collective-permute-start(bf16[2,24,1280]{2,1,0:T(8,128)(2,1)S(1)} %get-tuple-element.169), channel_id=1, source_target_pairs={{0,2},{1,3},{2,0},{3,1},{4,6},{5,7},{6,4},{7,5},{8,10},{9,11},{10,... | collective-permute-start | bytes 368648 | tf_op jit(solution)/shard_map/ppermute | solution.py:740
  119.7 6.7 %collective-permute-start.38 = (bf16[2,24,1920]{2,1,0:T(8,128)(2,1)S(1)}, bf16[2,24,1920]{2,1,0:T(8,128)(2,1)S(1)}, u32[]{:S(2)}, u32[]{:S(2)}) collective-permute-start(bf16[2,24,1920]{2,1,0:T(8,128)(2,1)S(1)} %get-tuple-element.162), channel_id=1, source_target_pairs={{0,4},{1,5},{2,6},{3,7},{4,0},{5,1},{6,2},{7,3},{8,12},{9,13},{10,... | collective-permute-start | bytes 552968 | tf_op jit(solution)/shard_map/ppermute | solution.py:740
  122.4 6.9 %collective-permute-start.40 = (bf16[2,24,1920]{2,1,0:T(8,128)(2,1)S(1)}, bf16[2,24,1920]{2,1,0:T(8,128)(2,1)S(1)}, u32[]{:S(2)}, u32[]{:S(2)}) collective-permute-start(bf16[2,24,1920]{2,1,0:T(8,128)(2,1)S(1)} %shard_map.217), channel_id=1, source_target_pairs={{0,8},{1,9},{2,10},{3,11},{4,12},{5,13},{6,14},{7,15},{8,0},{9,1},... | collective-permute-start | bytes 552968 | tf_op jit(solution)/shard_map/ppermute | solution.py:740
  122.5 8.0 %collective-permute-start.44 = (bf16[2,24,1280]{2,1,0:T(8,128)(2,1)S(1)}, bf16[2,24,1280]{2,1,0:T(8,128)(2,1)S(1)}, u32[]{:S(2)}, u32[]{:S(2)}) collective-permute-start(bf16[2,24,1280]{2,1,0:T(8,128)(2,1)S(1)} %get-tuple-element.168), channel_id=1, source_target_pairs={{0,4},{1,5},{2,6},{3,7},{4,0},{5,1},{6,2},{7,3},{8,12},{9,13},{10,... | collective-permute-start | bytes 368648 | tf_op jit(solution)/shard_map/ppermute | solution.py:740
  124.4 7.1 %collective-permute-start.46 = (bf16[2,24,1280]{2,1,0:T(8,128)(2,1)S(1)}, bf16[2,24,1280]{2,1,0:T(8,128)(2,1)S(1)}, u32[]{:S(2)}, u32[]{:S(2)}) collective-permute-start(bf16[2,24,1280]{2,1,0:T(8,128)(2,1)S(1)} %shard_map.220), channel_id=1, source_target_pairs={{0,8},{1,9},{2,10},{3,11},{4,12},{5,13},{6,14},{7,15},{8,0},{9,1},... | collective-permute-start | bytes 368648 | tf_op jit(solution)/shard_map/ppermute | solution.py:740
  129.4 6.3 %collective-permute-start.41 = (bf16[1,24,1920]{2,1,0:T(8,128)(2,1)S(1)}, bf16[1,24,1920]{2,1,0:T(8,128)(2,1)S(1)}, u32[]{:S(2)}, u32[]{:S(2)}) collective-permute-start(bf16[1,24,1920]{2,1,0:T(8,128)(2,1)S(1)} %get-tuple-element.165), channel_id=1, source_target_pairs={{0,16},{1,17},{2,18},{3,19},{4,20},{5,21},{6,22},{7,23},{8,24},{9,... | collective-permute-start | bytes 276488 | tf_op jit(solution)/shard_map/ppermute | solution.py:740
  131.5 5.8 %collective-permute-start.47 = (bf16[1,24,1280]{2,1,0:T(8,128)(2,1)S(1)}, bf16[1,24,1280]{2,1,0:T(8,128)(2,1)S(1)}, u32[]{:S(2)}, u32[]{:S(2)}) collective-permute-start(bf16[1,24,1280]{2,1,0:T(8,128)(2,1)S(1)} %get-tuple-element.171), channel_id=1, source_target_pairs={{0,16},{1,17},{2,18},{3,19},{4,20},{5,21},{6,22},{7,23},{8,24},{9,... | collective-permute-start | bytes 184328 | tf_op jit(solution)/shard_map/ppermute | solution.py:740
  (8 other events, 143.8 us)
